TPU v7x, 32 devices: a whole 2x2x4 slice. The times are simulated.
32 devices in a mesh: dp: 8 (over y, x, core), tensor: 4 (over z).
Axes of the slice: x: 2, y: 2, z: 4, core: 2. Of those that a mesh axis runs over, the one named last changes fastest.
Arguments:
- tokens: bfloat16 [4096, 2560], P(('dp', 'tensor')), may hold values from -6 to 6
- norm_gain: bfloat16 [2560], P('dp'), may hold values from 0.5 to 1.5
- x_weight: bfloat16 [2560, 2560], P('dp', 'tensor'), may hold values from -0.125 to 0.125
- y_weight: bfloat16 [2560, 2560], P('dp', 'tensor'), may hold values from -0.125 to 0.125
- conv_weight: float32 [4, 2560], P(None, 'tensor'), may hold values from -3 to 3
- recur_gate_weight: bfloat16 [256, 2560], P('dp', 'tensor'), may hold values from -0.375 to 0.375
- input_gate_weight: bfloat16 [256, 2560], P('dp', 'tensor'), may hold values from -0.375 to 0.375
- decay_param: float32 [2560], P('tensor'), may hold values from 5 to 11
- out_weight: bfloat16 [2560, 2560], P('tensor', 'dp'), may hold values from -0.25 to 0.25
- mlp_gain: bfloat16 [2560], P('dp'), may hold values from 0.5 to 1.5
- gate_weight: bfloat16 [2560, 7680], P('dp', 'tensor'), may hold values from -0.125 to 0.125
- up_weight: bfloat16 [2560, 7680], P('dp', 'tensor'), may hold values from -0.125 to 0.125
- down_weight: bfloat16 [7680, 2560], P('tensor', 'dp'), may hold values from -0.125 to 0.125
- seq_lengths: int32 [3], replicated, may hold values from 1 to 2048, 3968 in all
- token_order: int32 [4096], P(('dp', 'tensor')), may hold values from 0 to 4095, as said below
- cotangent: bfloat16 [4096, 2560], P(('dp', 'tensor')), may hold values from -6 to 6
Outputs:
- output: bfloat16 [4096, 2560], P(('dp', 'tensor'))
- grad_tokens: float32 [4096, 2560], P(('dp', 'tensor'))
- grad_norm_gain: float32 [2560], P('dp')
- grad_x_weight: float32 [2560, 2560], P('dp', 'tensor')
- grad_y_weight: float32 [2560, 2560], P('dp', 'tensor')
- grad_conv_weight: float32 [4, 2560], P(None, 'tensor')
- grad_recur_gate: float32 [256, 2560], P('dp', 'tensor')
- grad_input_gate: float32 [256, 2560], P('dp', 'tensor')
- grad_decay: float32 [2560], P('tensor')
- grad_out_weight: float32 [2560, 2560], P('tensor', 'dp')
- grad_mlp_gain: float32 [2560], P('dp')
- grad_gate_weight: float32 [2560, 7680], P('dp', 'tensor')
- grad_up_weight: float32 [2560, 7680], P('dp', 'tensor')
- grad_down_weight: float32 [7680, 2560], P('tensor', 'dp')
Inputs may be any that keep to these rules, and one draw needn't show every extreme that they name: `seq_lengths`: the lengths sum to 3968; the remaining places at the end are padding. The longest is exactly 2048. token_order is a permutation that maps each aligned block of 512 stored rows onto the same block of 512 places.
All inputs are finite; a program needn't handle non-finite values.
Results may differ from a plain program's by a relative error of at most 0.022.
Values may be sent and summed in bfloat16 or wider, within the bound.
A program may use at most 256 MiB of HBM per device.

v0:
```python
import jax
import jax.numpy as jnp
from jax import lax
from jax.sharding import PartitionSpec as P

epsilon = 1e-06
rate_scale = 8.0


def from_behind(block, axis, distance):
    devices = range(lax.axis_size(axis))
    route = [(i - distance, i) for i in devices if i - distance in devices]
    return lax.ppermute(block, axis, route)


def extended_2(array, sides, width):
    for axis, dim in sides:
        size, length = (lax.axis_size(axis), array.shape[dim])
        up = [(i, (i + 1) % size) for i in range(size - 1)]
        down = [(j, i) for i, j in up]
        last = lax.slice_in_dim(array, length - width, length, axis=dim)
        leading = lax.slice_in_dim(array, 0, width, axis=dim)
        before = lax.ppermute(last, axis, up)
        after = lax.ppermute(leading, axis, down)
        array = jnp.concatenate([before, array, after], axis=dim)
    return array


def entering(value, axis, join, neutral, backward):
    count, mine = (lax.axis_size(axis), lax.axis_index(axis))
    pieces = jax.tree.map(lambda part: lax.all_gather(part, axis), value)
    if backward:
        pieces = jax.tree.map(lambda part: part[::-1], pieces)
        mine = count - 1 - mine
    total = jax.tree.map(
        lambda part, zero: jnp.full_like(part, 0) + jnp.asarray(zero, part.dtype), value, neutral
    )

    def lap(position, total):
        longer = join(total, jax.tree.map(lambda part: part[position], pieces))
        return jax.tree.map(lambda new, old: jnp.where(position < mine, new, old), longer, total)

    return lax.fori_loop(0, count - 1, lap, total)


def rms_scale(values, gain):
    return values * lax.rsqrt(jnp.mean(values * values, axis=-1, keepdims=True) + epsilon) * gain


def norm_back(values, gain, grad):
    inv_root = lax.rsqrt(jnp.mean(values * values, axis=-1, keepdims=True) + epsilon)
    normed = values * inv_root
    upstream = grad * gain
    grad_values = inv_root * (
        upstream - normed * jnp.mean(upstream * normed, axis=-1, keepdims=True)
    )
    return (grad_values, normed)


def segment_of(places, ends):
    return jnp.sum((ends[None, :] <= places[:, None]).astype(jnp.int32), axis=1)


def pair_step(early, later):
    return (early[0] * later[0], later[0] * early[1] + later[1])


def plain_dot(left, right):
    return jnp.dot(left, right, preferred_element_type=jnp.float32)


def times_trans(left, right):
    return lax.dot_general(
        left, right, (((1,), (1,)), ((), ())), preferred_element_type=jnp.float32
    )


def trans_times(left, right):
    return lax.dot_general(
        left, right, (((0,), (0,)), ((), ())), preferred_element_type=jnp.float32
    )


def gelu_tanh(values):
    return jax.nn.gelu(values, approximate=True)


def collect(
    norm_gain,
    mlp_gain,
    x_weight,
    y_weight,
    recur_gate_weight,
    input_gate_weight,
    gate_weight,
    up_weight,
    out_weight,
    down_weight,
):
    return (
        lax.all_gather(norm_gain, "dp", axis=0, tiled=True),
        lax.all_gather(mlp_gain, "dp", axis=0, tiled=True),
        lax.all_gather(x_weight, "dp", axis=0, tiled=True),
        lax.all_gather(y_weight, "dp", axis=0, tiled=True),
        lax.all_gather(recur_gate_weight, "dp", axis=0, tiled=True),
        lax.all_gather(input_gate_weight, "dp", axis=0, tiled=True),
        lax.all_gather(gate_weight, "dp", axis=0, tiled=True),
        lax.all_gather(up_weight, "dp", axis=0, tiled=True),
        lax.all_gather(out_weight, "dp", axis=1, tiled=True),
        lax.all_gather(down_weight, "dp", axis=1, tiled=True),
    )


def row_sums(term_rows, tok_rows):
    return lax.psum_scatter(
        term_rows(jnp.int32(0), lax.axis_size("tensor") * tok_rows).astype(jnp.bfloat16),
        "tensor",
        scatter_dimension=0,
        tiled=True,
    ).astype(jnp.float32)


def spread_rows(values):
    return lax.all_gather(values, "tensor", axis=0, tiled=True)


def local(
    tokens,
    norm_gain,
    x_weight,
    y_weight,
    conv_weight,
    recur_gate_weight,
    input_gate_weight,
    decay_param,
    out_weight,
    mlp_gain,
    gate_weight,
    up_weight,
    down_weight,
    seq_lengths,
    token_order,
    cotangent,
):
    n_tensor = lax.axis_size("tensor")
    tensor_index = lax.axis_index("tensor")
    dp_index = lax.axis_index("dp")
    tok_rows = tokens.shape[0]
    row_count = tok_rows * n_tensor
    own_width = conv_weight.shape[1]
    kernel_taps = conv_weight.shape[0]
    edge_rows = kernel_taps - 1
    dp_width = norm_gain.shape[0]
    own_start = tensor_index * tok_rows
    shards = (
        norm_gain,
        mlp_gain,
        x_weight,
        y_weight,
        recur_gate_weight,
        input_gate_weight,
        gate_weight,
        up_weight,
        out_weight,
        down_weight,
    )
    (
        gain_one,
        gain_two,
        x_full,
        y_full,
        recur_full,
        input_full,
        gate_full,
        up_full,
        out_full,
        down_full,
    ) = collect(*shards)
    block_size = recur_full.shape[0]
    first_gain = gain_one.astype(jnp.float32)
    second_gain = gain_two.astype(jnp.float32)
    both_gates = jnp.concatenate([recur_full, input_full], axis=1)
    tok_own = tokens.astype(jnp.float32)
    own_order = token_order - dp_index * row_count
    first_rows = rms_scale(tok_own, first_gain).astype(jnp.bfloat16)
    first_all, cot_all, order_all = (
        lax.all_gather(first_rows, "tensor", axis=0, tiled=True),
        lax.all_gather(cotangent, "tensor", axis=0, tiled=True),
        lax.all_gather(own_order, "tensor", axis=0, tiled=True),
    )
    row_index = jnp.arange(row_count, dtype=jnp.int32)
    inverse = jnp.zeros((row_count,), jnp.int32).at[order_all].set(row_index)
    hidden_place = jnp.take(first_all, inverse, axis=0)
    places = dp_index * row_count + row_index
    ends = jnp.cumsum(seq_lengths)
    segment = segment_of(places, ends)
    starts = (places == 0) | (segment != segment_of(places - 1, ends))
    live = (places < ends[-1]).astype(jnp.float32)
    live_stored = jnp.take(live, order_all, axis=0)
    same = [
        (segment_of(places - shift, ends) == segment).astype(jnp.float32)
        for shift in range(kernel_taps)
    ]
    low_edge = tensor_index * own_width
    own_blocks = (low_edge + jnp.arange(own_width, dtype=jnp.int32)) // block_size
    first_block = low_edge // block_size
    block_count = own_width // block_size + 2

    def block_start(index):
        return (first_block + index) * block_size - low_edge + block_size

    def block_mask(index):
        inside = own_blocks == first_block + index
        return jnp.concatenate([inside, inside])

    def convolve(extended, kernel):
        return sum(
            (
                kernel[shift][None, :]
                * extended[edge_rows - shift : edge_rows - shift + row_count]
                * same[shift][:, None]
                for shift in range(kernel_taps)
            )
        )

    def gates(conv_vals, pre_recur, pre_input, decay_vals):
        log_rate = -rate_scale * jax.nn.sigmoid(pre_recur) * jax.nn.softplus(-decay_vals)
        decay_rate = jnp.where(starts[:, None], 0.0, jnp.exp(log_rate))
        scale_in = jnp.where(starts[:, None], 1.0, jnp.sqrt(-jnp.expm1(2.0 * log_rate)))
        return (decay_rate, conv_vals * jax.nn.sigmoid(pre_input) * scale_in)

    def glu(gate_pre, up_pre):
        return gelu_tanh(gate_pre) * up_pre

    x_branch = plain_dot(hidden_place, x_full).astype(jnp.bfloat16)
    y_before = plain_dot(hidden_place, y_full)
    previous = from_behind(x_branch[row_count - edge_rows :], "dp", 1)
    extended = jnp.concatenate([previous, x_branch], axis=0).astype(jnp.float32)
    conv_out = convolve(extended, conv_weight)
    conv_wide = extended_2(conv_out.astype(jnp.bfloat16), (("tensor", 1),), block_size)
    pre_both = jnp.zeros((row_count, 2 * own_width), jnp.float32)
    for index in range(block_count):
        piece = lax.dynamic_slice_in_dim(conv_wide, block_start(index), block_size, 1)
        pre_both = pre_both + jnp.where(
            block_mask(index)[None, :], plain_dot(piece, both_gates), 0.0
        )
    (decay_rate, driven), gate_pull = jax.vjp(
        gates, conv_out, pre_both[:, :own_width], pre_both[:, own_width:], decay_param
    )
    cum_rate, local_state = lax.associative_scan(pair_step, (decay_rate, driven), axis=0)
    ident = (jnp.ones((own_width,), jnp.float32), jnp.zeros((own_width,), jnp.float32))
    rate_in, state_in = entering((cum_rate[-1], local_state[-1]), "dp", pair_step, ident, False)
    state = local_state + cum_rate * state_in[None, :]
    y_branch = gelu_tanh(y_before)
    merged = (state * y_branch).astype(jnp.bfloat16)
    merged_stored = jnp.take(merged, order_all, axis=0)

    def mixer_rows(begin, number):
        return plain_dot(merged_stored, out_full)

    after_own = tok_own + row_sums(mixer_rows, tok_rows)
    hidden_two = spread_rows(rms_scale(after_own, second_gain).astype(jnp.bfloat16))
    gate_pre = plain_dot(hidden_two, gate_full)
    up_pre = plain_dot(hidden_two, up_full)
    glu_out, glu_pull = jax.vjp(glu, gate_pre, up_pre)
    product = glu_out.astype(jnp.bfloat16)

    def down_rows(begin, number):
        return plain_dot(product, down_full)

    feed_out = row_sums(down_rows, tok_rows)
    live_own = lax.dynamic_slice_in_dim(live_stored, own_start, tok_rows, 0)
    output = ((after_own + feed_out) * live_own[:, None]).astype(jnp.bfloat16)
    grad_out = cot_all.astype(jnp.float32) * live_stored[:, None]
    fresh = lax.optimization_barrier((shards, grad_out))[0]
    (
        gain_one,
        gain_two,
        x_full,
        y_full,
        recur_full,
        input_full,
        gate_full,
        up_full,
        out_full,
        down_full,
    ) = collect(*fresh)
    first_gain = gain_one.astype(jnp.float32)
    second_gain = gain_two.astype(jnp.float32)
    both_gates = jnp.concatenate([recur_full, input_full], axis=1)
    down_in = grad_out.astype(jnp.bfloat16)
    grad_down = trans_times(product, down_in)
    grad_product = times_trans(down_in, down_full)
    grad_gate_pre, grad_up_pre = glu_pull(grad_product)
    grad_gate_pre = grad_gate_pre.astype(jnp.bfloat16)
    grad_up_pre = grad_up_pre.astype(jnp.bfloat16)
    grad_gate = trans_times(hidden_two, grad_gate_pre)
    grad_up = trans_times(hidden_two, grad_up_pre)

    def feed_rows(begin, number):
        return times_trans(grad_gate_pre, gate_full) + times_trans(grad_up_pre, up_full)

    grad_out_own = lax.dynamic_slice_in_dim(grad_out, own_start, tok_rows, 0)
    grad_two_own = row_sums(feed_rows, tok_rows)
    grad_norm_own, normed_two = norm_back(after_own, second_gain, grad_two_own)
    second_part = jnp.sum(grad_two_own * normed_two, axis=0)
    grad_after_own = grad_out_own + grad_norm_own
    mixer_in = spread_rows(grad_after_own.astype(jnp.bfloat16))
    grad_out_mat = trans_times(merged_stored, mixer_in)
    grad_merged = jnp.take(times_trans(mixer_in, out_full), inverse, axis=0)
    grad_state = grad_merged * y_branch
    gelu_pull = jax.vjp(gelu_tanh, y_before)[1]
    grad_y_before = gelu_pull(grad_merged * state)[0].astype(jnp.bfloat16)
    rate_next = jnp.concatenate([decay_rate[1:], jnp.ones((1, own_width), jnp.float32)], axis=0)
    rev_rate, local_lam = lax.associative_scan(
        pair_step, (rate_next, grad_state), reverse=True, axis=0
    )
    head_rate = decay_rate[0] * rev_rate[0]
    head_lam = decay_rate[0] * local_lam[0]
    factor_in, lam_in = entering((head_rate, head_lam), "dp", pair_step, ident, True)
    lam = local_lam + rev_rate * lam_in[None, :]
    state_prev = jnp.concatenate([state_in[None, :], state[:-1]], axis=0)
    grad_conv_local, grad_pre_recur, grad_pre_input, grad_decay_own = gate_pull(
        (lam * state_prev, lam)
    )
    grad_pre = jnp.concatenate([grad_pre_recur, grad_pre_input], axis=1).astype(jnp.bfloat16)
    grad_both = jnp.zeros((block_size, 2 * own_width), jnp.float32)
    grad_wide = jnp.zeros((row_count, own_width + 2 * block_size), jnp.float32)
    for index in range(block_count):
        begin = block_start(index)
        piece = lax.dynamic_slice_in_dim(conv_wide, begin, block_size, 1)
        masked = jnp.where(block_mask(index)[None, :], grad_pre, jnp.zeros((), jnp.bfloat16))
        grad_both = grad_both + trans_times(piece, masked)
        added = lax.dynamic_slice_in_dim(grad_wide, begin, block_size, 1) + times_trans(
            masked, both_gates
        )
        grad_wide = lax.dynamic_update_slice_in_dim(grad_wide, added, begin, 1)
    grad_recur = grad_both[:, :own_width]
    grad_input = grad_both[:, own_width:]
    rims = jnp.concatenate(
        [grad_wide[:, :block_size], grad_wide[:, own_width + block_size :]], axis=1
    )
    arrived = extended_2(rims.astype(jnp.bfloat16), (("tensor", 1),), block_size).astype(rims.dtype)
    from_lower = jnp.pad(arrived[:, :block_size], ((0, 0), (0, own_width - block_size)))
    from_upper = jnp.pad(arrived[:, 3 * block_size :], ((0, 0), (own_width - block_size, 0)))
    grad_conv = (
        grad_conv_local
        + grad_wide[:, block_size : block_size + own_width]
        + from_lower
        + from_upper
    )
    conv_pull = jax.vjp(convolve, extended, conv_weight)[1]
    grad_extended, grad_kernel = conv_pull(grad_conv)
    returned = from_behind(grad_extended[:edge_rows], "dp", -1)
    grad_x_branch = grad_extended[edge_rows:] + jnp.concatenate(
        [jnp.zeros((row_count - edge_rows, own_width), jnp.float32), returned], axis=0
    )
    grad_x_low = grad_x_branch.astype(jnp.bfloat16)
    grad_x_stored = jnp.take(grad_x_low, order_all, axis=0)
    grad_y_stored = jnp.take(grad_y_before, order_all, axis=0)
    grad_x_mat = trans_times(first_all, grad_x_stored)
    grad_y_mat = trans_times(first_all, grad_y_stored)

    def mixer_back_rows(begin, number):
        return times_trans(grad_x_stored, x_full) + times_trans(grad_y_stored, y_full)

    grad_one_own = row_sums(mixer_back_rows, tok_rows)
    grad_norm_one, normed_one = norm_back(tok_own, first_gain, grad_one_own)
    first_part = jnp.sum(grad_one_own * normed_one, axis=0)
    grad_tokens = grad_after_own + grad_norm_one
    chosen = jnp.arange(n_tensor, dtype=jnp.int32) == tensor_index
    kernel_tile = jnp.where(chosen[:, None, None], grad_kernel[None, :, :], 0.0)
    decay_tile = jnp.where(chosen[:, None], grad_decay_own[None, :], 0.0)
    small = lax.psum((first_part, second_part, kernel_tile, decay_tile), ("dp", "tensor"))
    grad_first_gain = lax.dynamic_slice_in_dim(small[0], dp_index * dp_width, dp_width, 0)
    grad_second_gain = lax.dynamic_slice_in_dim(small[1], dp_index * dp_width, dp_width, 0)
    grad_kernel_sum = lax.dynamic_index_in_dim(small[2], tensor_index, 0, keepdims=False)
    grad_decay = lax.dynamic_index_in_dim(small[3], tensor_index, 0, keepdims=False)
    sums = (
        lax.psum_scatter(
            grad_x_mat.astype(jnp.bfloat16), "dp", scatter_dimension=0, tiled=True
        ).astype(jnp.float32),
        lax.psum_scatter(
            grad_y_mat.astype(jnp.bfloat16), "dp", scatter_dimension=0, tiled=True
        ).astype(jnp.float32),
        lax.psum_scatter(
            grad_recur.astype(jnp.bfloat16), "dp", scatter_dimension=0, tiled=True
        ).astype(jnp.float32),
        lax.psum_scatter(
            grad_input.astype(jnp.bfloat16), "dp", scatter_dimension=0, tiled=True
        ).astype(jnp.float32),
        lax.psum_scatter(
            grad_gate.astype(jnp.bfloat16), "dp", scatter_dimension=0, tiled=True
        ).astype(jnp.float32),
        lax.psum_scatter(
            grad_up.astype(jnp.bfloat16), "dp", scatter_dimension=0, tiled=True
        ).astype(jnp.float32),
        lax.psum_scatter(
            grad_out_mat.astype(jnp.bfloat16), "dp", scatter_dimension=1, tiled=True
        ).astype(jnp.float32),
        lax.psum_scatter(
            grad_down.astype(jnp.bfloat16), "dp", scatter_dimension=1, tiled=True
        ).astype(jnp.float32),
    )
    return (
        output,
        grad_tokens,
        grad_first_gain,
        sums[0],
        sums[1],
        grad_kernel_sum,
        sums[2],
        sums[3],
        grad_decay,
        sums[6],
        grad_second_gain,
        sums[4],
        sums[5],
        sums[7],
    )


def solution(mesh):
    in_specs = (
        P(("dp", "tensor"), None),
        P("dp"),
        P("dp", "tensor"),
        P("dp", "tensor"),
        P(None, "tensor"),
        P("dp", "tensor"),
        P("dp", "tensor"),
        P("tensor"),
        P("tensor", "dp"),
        P("dp"),
        P("dp", "tensor"),
        P("dp", "tensor"),
        P("tensor", "dp"),
        P(),
        P(("dp", "tensor")),
        P(("dp", "tensor"), None),
    )
    out_specs = (
        P(("dp", "tensor"), None),
        P(("dp", "tensor"), None),
        P("dp"),
        P("dp", "tensor"),
        P("dp", "tensor"),
        P(None, "tensor"),
        P("dp", "tensor"),
        P("dp", "tensor"),
        P("tensor"),
        P("tensor", "dp"),
        P("dp"),
        P("dp", "tensor"),
        P("dp", "tensor"),
        P("tensor", "dp"),
    )
    return jax.shard_map(local, mesh=mesh, in_specs=in_specs, out_specs=out_specs, check_vma=False)
```

profile of v0, /device:TPU:0, one launch (start us, length us, event | category | flops | bytes accessed | tf_op | source)
XLA Modules:
  0.0 1932.7 jit_solution(3863131239763523783)
XLA Ops:
  10.1 12.5 all-gather
  29.4 37.7 %all-gather.38.cloned.1.call-done = bf16[512,2560]{1,0:T(8,128)(2,1)} async-done(((bf16[128,2560]{1,0:T(8,128)(2,1)}), bf16[512,2560]{1,0:T(8,128)(2,1)}) %all-gather.38.cloned.1.call-update) | async-done | bytes 2621456 | tf_op jit(solution)/shard_map/all_gather | solution.py:188
  72.1 24.5 %all-reduce.89 = (bf16[2560]{0:T(1024)(128)(2,1)S(1)}, bf16[2560]{0:T(1024)(128)(2,1)}, bf16[2560]{0:T(1024)(128)(2,1)}, bf16[2560]{0:T(1024)(128)(2,1)}) all-reduce(bf16[2560]{0:T(1024)(128)(2,1)S(1)} %dynamic-update-slice, bf16[2560]{0:T(1024)(128)(2,1)S(1)} %dynamic-update-slice.1, ...), channel_id=1, replica_groups=mesh['dp'=8,'tensor'=4] {'dp'}, use_global_device_ids=true, to_apply=%add.84 | all-reduce | flops 10240 | bytes 40960
  120.5 29.2 %all-gather.22.cloned.1.call-done = bf16[512,2560]{1,0:T(8,128)(2,1)} async-done(((bf16[128,2560]{1,0:T(8,128)(2,1)}), bf16[512,2560]{1,0:T(8,128)(2,1)}) %all-gather.22.cloned.1.call-update) | async-done | bytes 2621456 | tf_op jit(solution)/shard_map/all_gather | solution.py:187
  157.9 25.4 %all-gather.24.cloned.1.call-done = bf16[2560,640]{1,0:T(8,128)(2,1)} async-done(((bf16[320,640]{1,0:T(8,128)(2,1)}), bf16[2560,640]{1,0:T(8,128)(2,1)}) %all-gather.24.cloned.1.call-update) | async-done | bytes 3276816 | tf_op jit(solution)/shard_map/all_gather | solution.py:103
  399.6 50.4 %reduce-scatter.13.cloned.1.call-done = bf16[128,2560]{1,0:T(8,128)(2,1)} async-done(((bf16[512,2560]{1,0:T(8,128)(2,1)}), bf16[128,2560]{1,0:T(8,128)(2,1)}) %reduce-scatter.13.cloned.1.call-update) | async-done | bytes 655376 | tf_op jit(solution)/shard_map/reduce_scatter | solution.py:115
  455.5 56.6 %all-gather.32.cloned.1.call-done = bf16[2560,1920]{1,0:T(8,128)(2,1)} async-done(((bf16[320,1920]{1,0:T(8,128)(2,1)}), bf16[2560,1920]{1,0:T(8,128)(2,1)}) %all-gather.32.cloned.1.call-update) | async-done | bytes 9830416 | tf_op jit(solution)/shard_map/all_gather | solution.py:107
  512.1 57.0 %all-gather.30.cloned.1.call-done = bf16[512,2560]{1,0:T(8,128)(2,1)} async-done(((bf16[128,2560]{1,0:T(8,128)(2,1)}), bf16[512,2560]{1,0:T(8,128)(2,1)}) %all-gather.30.cloned.1.call-update) | async-done | bytes 2621456 | tf_op jit(solution)/shard_map/all_gather | solution.py:124
  569.1 11.3 fusion.169
  580.4 49.9 %all-gather.34.cloned.1.call-done = bf16[2560,1920]{1,0:T(8,128)(2,1)} async-done(((bf16[320,1920]{1,0:T(8,128)(2,1)}), bf16[2560,1920]{1,0:T(8,128)(2,1)}) %all-gather.34.cloned.1.call-update) | async-done | bytes 9830416 | tf_op jit(solution)/shard_map/all_gather | solution.py:108
  630.3 11.4 fusion.170
  641.6 50.9 %all-gather.40.cloned.1.call-done = bf16[1920,2560]{0,1:T(8,128)(2,1)} async-done(((bf16[1920,320]{0,1:T(8,128)(2,1)}), bf16[1920,2560]{0,1:T(8,128)(2,1)}) %all-gather.40.cloned.1.call-update) | async-done | bytes 9830416 | tf_op jit(solution)/shard_map/all_gather | solution.py:110
  692.5 15.7 multiply_convert_fusion
  708.2 46.7 %all-gather.42.cloned.1.call-done = bf16[2560,1920]{1,0:T(8,128)(2,1)} async-done(((bf16[320,1920]{1,0:T(8,128)(2,1)}), bf16[2560,1920]{1,0:T(8,128)(2,1)}) %all-gather.42.cloned.1.call-update) | async-done | bytes 9830416 | tf_op jit(solution)/shard_map/all_gather | solution.py:107
  765.3 51.9 %all-gather.44.cloned.1.call-done = bf16[2560,1920]{1,0:T(8,128)(2,1)} async-done(((bf16[320,1920]{1,0:T(8,128)(2,1)}), bf16[2560,1920]{1,0:T(8,128)(2,1)}) %all-gather.44.cloned.1.call-update) | async-done | bytes 9830416 | tf_op jit(solution)/shard_map/all_gather | solution.py:108
  817.2 10.7 add_convert_fusion.1
  829.0 51.2 %reduce-scatter.17.cloned.1.call-done = bf16[128,2560]{1,0:T(8,128)(2,1)} async-done(((bf16[512,2560]{1,0:T(8,128)(2,1)}), bf16[128,2560]{1,0:T(8,128)(2,1)}) %reduce-scatter.17.cloned.1.call-update) | async-done | bytes 655376 | tf_op jit(solution)/shard_map/reduce_scatter | solution.py:115
  887.0 10.5 all_gather.113
  926.4 45.3 %all-gather.46.cloned.1.call-done = bf16[512,2560]{1,0:T(8,128)(2,1)} async-done(((bf16[128,2560]{1,0:T(8,128)(2,1)}), bf16[512,2560]{1,0:T(8,128)(2,1)}) %all-gather.46.cloned.1.call-update) | async-done | bytes 2621456 | tf_op jit(solution)/shard_map/all_gather | solution.py:124
  1145.0 10.7 rev.15
  1155.7 10.9 rev.14
  1241.7 10.7 convolution_convert_fusion.6
  1254.6 14.1 reduce-scatter.19.cloned.1.call-done
  1307.0 36.0 %reduce-scatter.27.cloned.1.call-done = bf16[32,640]{1,0:T(8,128)(2,1)} async-done(((bf16[256,640]{1,0:T(8,128)(2,1)}), bf16[32,640]{1,0:T(8,128)(2,1)}) %reduce-scatter.27.cloned.1.call-update) | async-done | bytes 40976 | tf_op jit(solution)/shard_map/reduce_scatter | solution.py:389
  1344.4 48.9 %reduce-scatter.29.cloned.1.call-done = bf16[640,320]{0,1:T(8,128)(2,1)} async-done(((bf16[640,2560]{0,1:T(8,128)(2,1)}), bf16[640,320]{0,1:T(8,128)(2,1)}) %reduce-scatter.29.cloned.1.call-update) | async-done | bytes 409616 | tf_op jit(solution)/shard_map/reduce_scatter | solution.py:398
  1395.2 48.4 %reduce-scatter.23.cloned.1.call-done = bf16[320,640]{1,0:T(8,128)(2,1)} async-done(((bf16[2560,640]{1,0:T(8,128)(2,1)}), bf16[320,640]{1,0:T(8,128)(2,1)}) %reduce-scatter.23.cloned.1.call-update) | async-done | bytes 409616 | tf_op jit(solution)/shard_map/reduce_scatter | solution.py:383
  1445.6 48.2 %reduce-scatter.21.cloned.1.call-done = bf16[320,640]{1,0:T(8,128)(2,1)} async-done(((bf16[2560,640]{1,0:T(8,128)(2,1)}), bf16[320,640]{1,0:T(8,128)(2,1)}) %reduce-scatter.21.cloned.1.call-update) | async-done | bytes 409616 | tf_op jit(solution)/shard_map/reduce_scatter | solution.py:380
  1495.7 52.5 %reduce-scatter.15.cloned.1.call-done = bf16[128,2560]{1,0:T(8,128)(2,1)} async-done(((bf16[512,2560]{1,0:T(8,128)(2,1)}), bf16[128,2560]{1,0:T(8,128)(2,1)}) %reduce-scatter.15.cloned.1.call-update) | async-done | bytes 655376 | tf_op jit(solution)/shard_map/reduce_scatter | solution.py:115
  1552.0 123.5 %all-reduce.92.cloned.1.call-done = (f32[2560]{0:T(1024)}, f32[4,4,640]{2,1,0:T(4,128)}, f32[4,640]{1,0:T(4,128)}, f32[2560]{0:T(1024)}) async-done(((f32[2560]{0:T(1024)}, f32[4,4,640]{2,1,0:T(4,128)}, f32[4,640]{1,0:T(4,128)}, f32[2560]{0:T(1024)}), (f32[2560]{0:T(1024)}, f32[4,4,640]{2,1,0:T(4,128)}, f32[4,640]{1,0:T(4,128)}, f32[2560]{0:T(1024)})) %all-reduce.92.cloned.1.call-update) | async-done | bytes 71696 | tf_op jit(solution)/shard_map/psum | solution.py:374
  1680.8 78.3 %reduce-scatter.31.cloned.1.call-done = bf16[320,1920]{1,0:T(8,128)(2,1)} async-done(((bf16[2560,1920]{1,0:T(8,128)(2,1)}), bf16[320,1920]{1,0:T(8,128)(2,1)}) %reduce-scatter.31.cloned.1.call-update) | async-done | bytes 1228816 | tf_op jit(solution)/shard_map/reduce_scatter | solution.py:392
  1762.0 79.0 %reduce-scatter.33.cloned.1.call-done = bf16[320,1920]{1,0:T(8,128)(2,1)} async-done(((bf16[2560,1920]{1,0:T(8,128)(2,1)}), bf16[320,1920]{1,0:T(8,128)(2,1)}) %reduce-scatter.33.cloned.1.call-update) | async-done | bytes 1228816 | tf_op jit(solution)/shard_map/reduce_scatter | solution.py:395
  1843.8 79.0 %reduce-scatter.35.cloned.1.call-done = bf16[1920,320]{0,1:T(8,128)(2,1)} async-done(((bf16[1920,2560]{0,1:T(8,128)(2,1)}), bf16[1920,320]{0,1:T(8,128)(2,1)}) %reduce-scatter.35.cloned.1.call-update) | async-done | bytes 1228816 | tf_op jit(solution)/shard_map/reduce_scatter | solution.py:401
  (838 shorter events, 626.2 us)
Async XLA Ops:
  7.2 59.9 %all-gather.38.cloned.1.call-start = ((), (), s32[]{:S(2)}) async-start(), calls=%async_computation.22 | async-start | bytes 3276800 | tf_op jit(solution)/shard_map/all_gather | solution.py:188
  8.0 141.8 %all-gather.22.cloned.1.call-start = ((), (), s32[]{:S(2)}) async-start(), calls=%async_computation.12 | async-start | bytes 3276800 | tf_op jit(solution)/shard_map/all_gather | solution.py:187
  97.7 85.6 %all-gather.24.cloned.1.call-start = ((), (), s32[]{:S(2)}) async-start(), calls=%async_computation.13 | async-start | bytes 3686400 | tf_op jit(solution)/shard_map/all_gather | solution.py:103
  98.4 284.2 %all-gather.26.cloned.1.call-start = ((), (), s32[]{:S(2)}) async-start(), calls=%async_computation.14 | async-start | bytes 3686400 | tf_op jit(solution)/shard_map/all_gather | solution.py:104
  99.0 293.9 %all-gather.28.cloned.1.call-start = ((), (), s32[]{:S(2)}) async-start(), calls=%async_computation.15 | async-start | bytes 3686400 | tf_op jit(solution)/shard_map/all_gather | solution.py:109
  99.6 350.4 %reduce-scatter.13.cloned.1.call-start = ((), (), s32[]{:S(2)}) async-start(), calls=%async_computation.16 | async-start | bytes 3276800 | tf_op jit(solution)/shard_map/reduce_scatter | solution.py:115
  193.4 9.8 collective-permute-start.1
  196.8 11.1 collective-permute-start.2
  398.8 113.3 %all-gather.32.cloned.1.call-start = ((), (), s32[]{:S(2)}) async-start(), calls=%async_computation.18 | async-start | bytes 11059200 | tf_op jit(solution)/shard_map/all_gather | solution.py:107
  399.6 169.5 %all-gather.30.cloned.1.call-start = ((), (), s32[]{:S(2)}) async-start(), calls=%async_computation.17 | async-start | bytes 3276800 | tf_op jit(solution)/shard_map/all_gather | solution.py:124
  452.6 177.7 %all-gather.34.cloned.1.call-start = ((), (), s32[]{:S(2)}) async-start(), calls=%async_computation.19 | async-start | bytes 11059200 | tf_op jit(solution)/shard_map/all_gather | solution.py:108
  453.4 239.2 %all-gather.40.cloned.1.call-start = ((), (), s32[]{:S(2)}) async-start(), calls=%async_computation.23 | async-start | bytes 11059200 | tf_op jit(solution)/shard_map/all_gather | solution.py:110
  453.9 301.0 %all-gather.42.cloned.1.call-start = ((), (), s32[]{:S(2)}) async-start(), calls=%async_computation.24 | async-start | bytes 11059200 | tf_op jit(solution)/shard_map/all_gather | solution.py:107
  454.7 362.5 %all-gather.44.cloned.1.call-start = ((), (), s32[]{:S(2)}) async-start(), calls=%async_computation.25 | async-start | bytes 11059200 | tf_op jit(solution)/shard_map/all_gather | solution.py:108
  455.3 424.9 %reduce-scatter.17.cloned.1.call-start = ((), (), s32[]{:S(2)}) async-start(), calls=%async_computation.26 | async-start | bytes 3276800 | tf_op jit(solution)/shard_map/reduce_scatter | solution.py:115
  827.9 98.4 %all-gather.48.cloned.1.call-start = ((), (), s32[]{:S(2)}) async-start(), calls=%async_computation.28 | async-start | bytes 3686400 | tf_op jit(solution)/shard_map/all_gather | solution.py:109
  828.5 143.1 %all-gather.46.cloned.1.call-start = ((), (), s32[]{:S(2)}) async-start(), calls=%async_computation.27 | async-start | bytes 3276800 | tf_op jit(solution)/shard_map/all_gather | solution.py:124
  885.2 318.5 %all-gather.50.cloned.1.call-start = ((), (), s32[]{:S(2)}) async-start(), calls=%async_computation.29 | async-start | bytes 3686400 | tf_op jit(solution)/shard_map/all_gather | solution.py:103
  885.8 324.6 %all-gather.52.cloned.1.call-start = ((), (), s32[]{:S(2)}) async-start(), calls=%async_computation.30 | async-start | bytes 3686400 | tf_op jit(solution)/shard_map/all_gather | solution.py:104
  886.4 353.8 %all-gather.36.cloned.1.call-start = ((), (), s32[]{:S(2)}) async-start(), calls=%async_computation.20 | async-start | bytes 11059200 | tf_op jit(solution)/shard_map/all_gather | solution.py:110
  887.0 381.7 %reduce-scatter.19.cloned.1.call-start = ((), (), s32[]{:S(2)}) async-start(), calls=%async_computation.31 | async-start | bytes 3276800 | tf_op jit(solution)/shard_map/reduce_scatter | solution.py:115
  1181.8 10.6 collective-permute-start.4
  1217.7 87.8 %reduce-scatter.25.cloned.1.call-start = ((), (), s32[]{:S(2)}) async-start(), calls=%async_computation.34 | async-start | bytes 368640 | tf_op jit(solution)/shard_map/reduce_scatter | solution.py:386
  1222.7 120.3 %reduce-scatter.27.cloned.1.call-start = ((), (), s32[]{:S(2)}) async-start(), calls=%async_computation.35 | async-start | bytes 368640 | tf_op jit(solution)/shard_map/reduce_scatter | solution.py:389
  1223.4 169.9 %reduce-scatter.29.cloned.1.call-start = ((), (), s32[]{:S(2)}) async-start(), calls=%async_computation.36 | async-start | bytes 3686400 | tf_op jit(solution)/shard_map/reduce_scatter | solution.py:398
  1229.2 214.4 %reduce-scatter.23.cloned.1.call-start = ((), (), s32[]{:S(2)}) async-start(), calls=%async_computation.33 | async-start | bytes 3686400 | tf_op jit(solution)/shard_map/reduce_scatter | solution.py:383
  1235.0 258.8 %reduce-scatter.21.cloned.1.call-start = ((), (), s32[]{:S(2)}) async-start(), calls=%async_computation.32 | async-start | bytes 3686400 | tf_op jit(solution)/shard_map/reduce_scatter | solution.py:380
  1240.2 308.1 %reduce-scatter.15.cloned.1.call-start = ((), (), s32[]{:S(2)}) async-start(), calls=%async_computation.21 | async-start | bytes 3276800 | tf_op jit(solution)/shard_map/reduce_scatter | solution.py:115
  1252.5 423.0 %all-reduce.92.cloned.1.call-start = ((), (), s32[]{:S(2)}) async-start(), calls=%async_computation.40 | async-start | bytes 151552 | tf_op jit(solution)/shard_map/psum | solution.py:374
  1270.9 488.2 %reduce-scatter.31.cloned.1.call-start = ((), (), s32[]{:S(2)}) async-start(), calls=%async_computation.37 | async-start | bytes 11059200 | tf_op jit(solution)/shard_map/reduce_scatter | solution.py:392
  1280.8 560.1 %reduce-scatter.33.cloned.1.call-start = ((), (), s32[]{:S(2)}) async-start(), calls=%async_computation.38 | async-start | bytes 11059200 | tf_op jit(solution)/shard_map/reduce_scatter | solution.py:395
  1290.6 632.3 %reduce-scatter.35.cloned.1.call-start = ((), (), s32[]{:S(2)}) async-start(), calls=%async_computation.39 | async-start | bytes 11059200 | tf_op jit(solution)/shard_map/reduce_scatter | solution.py:401
  (150 other events, 3358.3 us)
Sparse Core Ops, SparseCore 0:
  9.6 57.4 all-gather.37
  97.8 51.8 all-gather.21
  151.6 31.6 all-gather.23
  185.0 32.8 all-gather.25
  219.7 32.8 all-gather.27
  398.9 51.0 reduce-scatter.12
  451.9 60.1 all-gather.31
  514.2 54.7 all-gather.29
  571.0 59.2 all-gather.33
  632.0 60.4 all-gather.39
  694.4 60.4 all-gather.41
  756.7 60.4 all-gather.43
  828.1 52.0 reduce-scatter.16
  881.9 33.8 all-gather.47
  917.2 54.3 all-gather.45
  973.4 31.6 all-gather.49
  1006.8 32.8 all-gather.51
  1041.4 60.4 all-gather.35
  1217.8 50.7 reduce-scatter.18
  1272.1 33.3 reduce-scatter.24
  1309.2 33.7 reduce-scatter.26
  1346.4 46.8 reduce-scatter.28
  1396.7 46.8 reduce-scatter.22
  1446.9 46.8 reduce-scatter.20
  1496.1 52.0 reduce-scatter.14
  1555.4 120.0 all-reduce.91
  1678.9 80.1 reduce-scatter.30
  1762.6 78.2 reduce-scatter.32
  1844.5 78.2 reduce-scatter.34
where the time goes:
time: 1950 us; the launch traced here: 1930 us
  waiting for transfers between devices  1190 us (61%)
  local copies, waits for them, and re-layouts  312 us (16%)
  matrix products  157 us (8%)
  other arithmetic  130 us (7%)
  blocking collectives  111 us (6%)
    reduce_scatter x4, waiting for transfers between devices, row_sums(): lax.psum_scatter(term_rows(jnp.int32(0), lax.axis_size('tensor') * tok_ro...  168 us
    psum x1, waiting for transfers between devices, local(): lax.psum((first_part, second_part, kernel_tile, decay_tile), ('dp', 'tens...  123 us
    slice x65, local copies, waits for them, and re-layouts, local(): lax.associative_scan(pair_step, (rate_next, grad_state), reverse=True, ax...  105 us
    all_gather x2, waiting for transfers between devices, collect(): lax.all_gather(gate_weight, 'dp', axis=0, tiled=True)  103 us
    all_gather x2, waiting for transfers between devices, spread_rows(): return lax.all_gather(values, 'tensor', axis=0, tiled=True)  102 us
    all_gather x2, waiting for transfers between devices, collect(): lax.all_gather(up_weight, 'dp', axis=0, tiled=True)  102 us
    slice x60, local copies, waits for them, and re-layouts, local(): lax.associative_scan(pair_step, (decay_rate, driven), axis=0)  82.4 us
    reduce_scatter x1, waiting for transfers between devices, local(): lax.psum_scatter(grad_down.astype(jnp.bfloat16), 'dp', scatter_dimension=...  79 us
  transfers between devices with their start and end apart: 35, of which 29 were waited for; matrix products, arithmetic and copies ran while one was open for 29% of the time, Pallas kernels for 0%

commit v1 on v0

--- a/solution.py
+++ b/solution.py
@@ -1,6 +1,8 @@
 import jax
 import jax.numpy as jnp
 from jax import lax
+from jax.experimental import pallas as pl
+from jax.experimental.pallas import tpu as pltpu
 from jax.sharding import PartitionSpec as P
 
 epsilon = 1e-06
@@ -124,7 +126,7 @@
     return lax.all_gather(values, "tensor", axis=0, tiled=True)
 
 
-def local(
+def local_general(
     tokens,
     norm_gain,
     x_weight,
@@ -420,6 +422,977 @@
     )
 
 
+MESH = pl.DeviceIdType.MESH
+VMEM_BYTES = 60 * 2**20
+
+
+def remote(src, dst, send, recv, device):
+    return pltpu.make_async_remote_copy(
+        src_ref=src,
+        dst_ref=dst,
+        send_sem=send,
+        recv_sem=recv,
+        device_id=device,
+        device_id_type=MESH,
+    )
+
+
+class Place:
+    def __init__(self, n_dp, n_line):
+        self.n_dp, self.n_line = n_dp, n_line
+        self.d, self.t = lax.axis_index("dp"), lax.axis_index("tensor")
+        self.core = lax.rem(self.d, 2)
+        self.x = lax.rem(lax.div(self.d, 2), 2)
+        self.y = lax.div(self.d, 4)
+
+    def chip(self, flip_x, flip_y, flip_core=0):
+        x = 1 - self.x if flip_x else self.x
+        y = 1 - self.y if flip_y else self.y
+        core = 1 - self.core if flip_core else self.core
+        return y * 4 + x * 2 + core
+
+    def at(self, flip_x=0, flip_y=0, flip_core=0):
+        return (self.chip(flip_x, flip_y, flip_core), self.t)
+
+    def up(self):
+        return (self.d, lax.rem(self.t + 1, self.n_line))
+
+    def down(self):
+        return (self.d, lax.rem(self.t + self.n_line - 1, self.n_line))
+
+    def meet(self, everyone=False):
+        barrier = pltpu.get_barrier_semaphore()
+
+        def greet(device):
+            pl.semaphore_signal(barrier, inc=1, device_id=device, device_id_type=MESH)
+
+        if everyone:
+            for i in range(1, self.n_dp):
+                greet((lax.rem(self.d + i, self.n_dp), self.t))
+            for i in range(1, self.n_line):
+                greet((self.d, lax.rem(self.t + i, self.n_line)))
+            pl.semaphore_wait(barrier, self.n_dp + self.n_line - 2)
+            return
+        for flips in ((1, 0), (0, 1), (0, 0, 1)):
+            greet(self.at(*flips))
+        below, above = self.t > 0, self.t < self.n_line - 1
+
+        @pl.when(below)
+        def _():
+            greet(self.down())
+
+        @pl.when(above)
+        def _():
+            greet(self.up())
+
+        pl.semaphore_wait(barrier, 3 + below.astype(jnp.int32) + above.astype(jnp.int32))
+
+
+class GatherPlane:
+    def __init__(self, place, src, dst, send, recv, local):
+        self.p, self.src, self.dst = place, src, dst
+        self.rows = src.shape[0]
+        self.send, self.recv, self.local = send, recv, local
+
+    def block(self, fx, fy, fc=0, part=None):
+        first = self.p.chip(fx, fy, fc) * self.rows
+        size = self.rows
+        if part is not None:
+            size = self.rows // 2
+            first = first + part * size
+        return self.dst.at[pl.ds(pl.multiple_of(first, 16), size)]
+
+    def copy(self, i, src, dst, device):
+        return remote(src, dst, self.send.at[i], self.recv.at[i], device)
+
+    def mine(self):
+        return pltpu.make_async_copy(self.src, self.block(0, 0), self.local)
+
+    def outgoing(self, i):
+        at, block = self.p.at, self.block
+        if i == 0:
+            return self.copy(0, self.src, block(0, 0), at(1, 0))
+        if i == 1:
+            return self.copy(1, self.src, block(0, 0), at(0, 1))
+        if i == 2:
+            return self.copy(2, self.src, block(0, 0), at(0, 0, 1))
+        if i == 3:
+            return self.copy(3, block(1, 0, 0, 0), block(1, 0, 0, 0), at(0, 1))
+        if i == 4:
+            return self.copy(4, block(0, 1, 0, 1), block(0, 1, 0, 1), at(1, 0))
+        spot = ((1, 0), (0, 1), (1, 1, 0, 0), (1, 1, 0, 1))[i - 5]
+        return self.copy(i, block(*spot), block(*spot), at(0, 0, 1))
+
+    def arrive(self, i):
+        spot = (
+            (1, 0),
+            (0, 1),
+            (0, 0, 1),
+            (1, 1, 0, 0),
+            (1, 1, 0, 1),
+            (1, 0, 1),
+            (0, 1, 1),
+            (1, 1, 1, 0),
+            (1, 1, 1, 1),
+        )[i]
+        here = self.block(*spot)
+        self.copy(i, here, here, self.p.at(0, 0, 1)).wait_recv()
+
+    def begin(self):
+        self.mine().start()
+        for i in (0, 1, 2):
+            self.outgoing(i).start()
+
+    def forward(self):
+        self.arrive(0)
+        self.outgoing(3).start()
+        self.arrive(1)
+        self.outgoing(4).start()
+        self.outgoing(5).start()
+        self.outgoing(6).start()
+
+    def share(self):
+        self.arrive(3)
+        self.outgoing(7).start()
+        self.arrive(4)
+        self.outgoing(8).start()
+
+    def finish(self):
+        for i in (2, 5, 6, 7, 8):
+            self.arrive(i)
+        for i in range(9):
+            self.outgoing(i).wait_send()
+        self.mine().wait()
+
+
+class GatherLine:
+    def __init__(self, place, dst, rows, begin, span, send, recv):
+        self.p, self.dst, self.rows = place, dst, rows
+        self.begin, self.span = begin, span
+        self.send, self.recv = send, recv
+        self.last = place.n_line - 1
+
+    def block(self, owner):
+        first = owner * self.rows + self.begin
+        return self.dst.at[pl.ds(pl.multiple_of(first, 8), self.span)]
+
+    def copy(self, way, k, owner, source=None):
+        to = self.p.up() if way == 0 else self.p.down()
+        block = self.block(owner)
+        return remote(
+            block if source is None else source,
+            block,
+            self.send.at[way, k],
+            self.recv.at[way, k],
+            to,
+        )
+
+    def step(self, k, source=None):
+        t, last = self.p.t, self.last
+        if k > 0:
+            self.arrive(k - 1)
+
+        @pl.when((t < last) & (t >= k))
+        def _():
+            self.copy(0, k, t - k, source).start()
+
+        @pl.when((t > 0) & (t + k <= last))
+        def _():
+            self.copy(1, k, t + k, source).start()
+
+    def arrive(self, k):
+        t, last = self.p.t, self.last
+
+        @pl.when(t >= k + 1)
+        def _():
+            self.copy(0, k, t - 1 - k).wait_recv()
+
+        @pl.when(t + k + 1 <= last)
+        def _():
+            self.copy(1, k, t + 1 + k).wait_recv()
+
+    def finish(self):
+        t, last = self.p.t, self.last
+        self.arrive(last - 1)
+        for k in range(last):
+
+            @pl.when((t < last) & (t >= k))
+            def _():
+                self.copy(0, k, t - k).wait_send()
+
+            @pl.when((t > 0) & (t + k <= last))
+            def _():
+                self.copy(1, k, t + k).wait_send()
+
+
+class ReduceLine:
+    def __init__(self, place, terms, rows, begin, span, stage, inbox, send, recv):
+        self.p, self.terms, self.rows = place, terms, rows
+        self.begin, self.span = begin, span
+        self.stage, self.inbox = stage, inbox
+        self.send, self.recv = send, recv
+        self.last = place.n_line - 1
+
+    def own(self, owner):
+        first = owner * self.rows + self.begin
+        return self.terms.at[pl.ds(pl.multiple_of(first, 16), self.span)]
+
+    def copy(self, way, j, source):
+        to = self.p.up() if way == 0 else self.p.down()
+        return remote(
+            source, self.inbox.at[way, j], self.send.at[way, j], self.recv.at[way, j], to
+        )
+
+    def step(self, j):
+        t, last = self.p.t, self.last
+        for way in (0, 1):
+            owner = last - j if way == 0 else j
+            first = (t == 0) if way == 0 else (t == last)
+            passing = (t > 0) & (t < owner) if way == 0 else (t < last) & (t > owner)
+            term = self.own(owner)
+
+            @pl.when(first)
+            def _():
+                self.copy(way, j, term).start()
+
+            @pl.when(passing)
+            def _():
+                self.copy(way, j, term).wait_recv()
+                self.stage[way, j] = (
+                    term[...].astype(jnp.float32) + self.inbox[way, j].astype(jnp.float32)
+                ).astype(jnp.bfloat16)
+                self.copy(way, j, self.stage.at[way, j]).start()
+
+    def total(self, result):
+        t, last = self.p.t, self.last
+        result[...] = self.own(t)[...].astype(jnp.float32)
+
+        @pl.when(t > 0)
+        def _():
+            j = last - t
+            self.copy(0, j, self.stage.at[0, 0]).wait_recv()
+            result[...] += self.inbox[0, j].astype(jnp.float32)
+
+        @pl.when(t < last)
+        def _():
+            self.copy(1, t, self.stage.at[0, 0]).wait_recv()
+            result[...] += self.inbox[1, t].astype(jnp.float32)
+
+    def finish(self):
+        t, last = self.p.t, self.last
+        for j in range(last):
+
+            @pl.when(t < last - j)
+            def _():
+                self.copy(0, j, self.stage.at[0, j]).wait_send()
+
+            @pl.when(t > j)
+            def _():
+                self.copy(1, j, self.stage.at[1, j]).wait_send()
+
+
+def add_rows(into, other, result=None):
+    result = into if result is None else result
+
+    def tile(i, carry):
+        rows = pl.ds(pl.multiple_of(i * 16, 16), 16)
+        result[rows] = (
+            into[rows].astype(jnp.float32) + other[rows].astype(jnp.float32)
+        ).astype(result.dtype)
+        return carry
+
+    lax.fori_loop(0, into.shape[0] // 16, tile, None)
+
+
+class ReducePlane:
+    chips = ((0, 0), (1, 0), (0, 1), (1, 1))
+
+    def __init__(self, place, terms, scratch):
+        self.p, self.terms = place, terms
+        self.held, self.near, self.along, self.last, self.send, self.recv, self.local = scratch
+        self.rows = self.held.shape[1]
+        self.half = self.rows // 2
+
+    @staticmethod
+    def scratch(rows, width):
+        return [
+            pltpu.VMEM((4, rows, width), jnp.bfloat16),
+            pltpu.VMEM((4, rows, width), jnp.bfloat16),
+            pltpu.VMEM((4, rows // 2, width), jnp.bfloat16),
+            pltpu.VMEM((2, rows // 2, width), jnp.bfloat16),
+            pltpu.SemaphoreType.DMA((10,)),
+            pltpu.SemaphoreType.DMA((10,)),
+            pltpu.SemaphoreType.DMA((4,)),
+        ]
+
+    def block(self, k, other):
+        first = self.p.chip(*self.chips[k], other) * self.rows
+        return self.terms.at[pl.ds(pl.multiple_of(first, 16), self.rows)]
+
+    def half_of(self, k, part):
+        return self.held.at[k, pl.ds(part * self.half, self.half)]
+
+    def load(self, k):
+        return pltpu.make_async_copy(self.block(k, 0), self.held.at[k], self.local.at[k])
+
+    def copy(self, i):
+        at = self.p.at
+        if i < 4:
+            src, dst, to = self.block(i, 1), self.near.at[i], at(0, 0, 1)
+        elif i < 8:
+            src, to = (
+                (self.half_of(1, 0), at(1, 0)),
+                (self.half_of(3, 0), at(1, 0)),
+                (self.half_of(2, 1), at(0, 1)),
+                (self.half_of(3, 1), at(0, 1)),
+            )[i - 4]
+            dst = self.along.at[i - 4]
+        else:
+            src, to = ((self.half_of(2, 0), at(0, 1)), (self.half_of(1, 1), at(1, 0)))[i - 8]
+            dst = self.last.at[i - 8]
+        return remote(src, dst, self.send.at[i], self.recv.at[i], to)
+
+    def begin(self):
+        for k in (3, 1, 2, 0):
+            self.copy(k).start()
+            self.load(k).start()
+
+    def cores(self):
+        for k in (3, 1, 2, 0):
+            self.load(k).wait()
+            self.copy(k).wait_recv()
+            add_rows(self.held.at[k], self.near.at[k])
+            if k == 3:
+                self.copy(5).start()
+                self.copy(7).start()
+            elif k == 1:
+                self.copy(4).start()
+            elif k == 2:
+                self.copy(6).start()
+
+    def turn(self):
+        self.copy(5).wait_recv()
+        add_rows(self.half_of(2, 0), self.along.at[1])
+        self.copy(8).start()
+        self.copy(7).wait_recv()
+        add_rows(self.half_of(1, 1), self.along.at[3])
+        self.copy(9).start()
+        self.copy(4).wait_recv()
+        add_rows(self.half_of(0, 0), self.along.at[0])
+        self.copy(6).wait_recv()
+        add_rows(self.half_of(0, 1), self.along.at[2])
+
+    def finish(self, result):
+        for part in (0, 1):
+            self.copy(8 + part).wait_recv()
+            rows = pl.ds(part * self.half, self.half)
+            add_rows(self.half_of(0, part), self.last.at[part], result.at[rows])
+        for i in range(10):
+            self.copy(i).wait_send()
+
+
+def dma_sems(*dims):
+    return pltpu.SemaphoreType.DMA(dims)
+
+
+def in_vmem():
+    return pl.BlockSpec(memory_space=pltpu.VMEM)
+
+
+def in_any():
+    return pl.BlockSpec(memory_space=pl.ANY)
+
+
+def comm_params(number):
+    return pltpu.CompilerParams(
+        collective_id=number, has_side_effects=True, vmem_limit_bytes=VMEM_BYTES
+    )
+
+
+def shaped(dims, kind):
+    return jax.ShapeDtypeStruct(dims, kind)
+
+
+def first_gather(n_dp, n_line, mats, minor, rows_in, order):
+    def kernel(a, b, c, e, a_out, b_out, c_out, e_out, ps, pr, pl_sem, ls, lr, ll):
+        place = Place(n_dp, n_line)
+        place.meet()
+        planes = [
+            GatherPlane(place, a, a_out, ps.at[0], pr.at[0], pl_sem.at[0]),
+            GatherPlane(place, b, b_out, ps.at[1], pr.at[1], pl_sem.at[1]),
+        ]
+        lines, copies = [], []
+        for i, (src, dst) in enumerate(((c, c_out), (e, e_out))):
+            rows = src.shape[0]
+            lines.append(GatherLine(place, dst, rows, 0, rows, ls.at[i], lr.at[i]))
+            own = dst.at[pl.ds(pl.multiple_of(place.t * rows, 8), rows)]
+            copies.append(pltpu.make_async_copy(src, own, ll.at[i]))
+        for copy in copies:
+            copy.start()
+        lines[0].step(0, c)
+        lines[1].step(0, e)
+        planes[0].begin()
+        planes[1].begin()
+        lines[0].step(1)
+        lines[1].step(1)
+        planes[0].forward()
+        planes[1].forward()
+        lines[0].step(2)
+        lines[1].step(2)
+        planes[0].share()
+        planes[1].share()
+        for part in lines + planes:
+            part.finish()
+        for copy in copies:
+            copy.wait()
+
+    return pl.pallas_call(
+        kernel,
+        out_shape=(
+            shaped((n_dp * mats.shape[0], mats.shape[1]), mats.dtype),
+            shaped((n_dp * minor.shape[0], minor.shape[1]), minor.dtype),
+            shaped((n_line * rows_in.shape[0], rows_in.shape[1]), rows_in.dtype),
+            shaped((n_line * order.shape[0], order.shape[1]), order.dtype),
+        ),
+        in_specs=[in_any()] * 4,
+        out_specs=[in_any()] * 4,
+        scratch_shapes=[
+            dma_sems(2, 9),
+            dma_sems(2, 9),
+            dma_sems(2),
+            dma_sems(2, 2, n_line - 1),
+            dma_sems(2, 2, n_line - 1),
+            dma_sems(2),
+        ],
+        compiler_params=comm_params(1),
+        name="first_gather",
+    )(mats, minor, rows_in, order)
+
+
+CHUNKS = 4
+
+
+def line_scratch(n_line, span, width):
+    hops = n_line - 1
+    return [
+        pltpu.VMEM((CHUNKS, 2, hops, span, width), jnp.bfloat16),
+        pltpu.VMEM((CHUNKS, 2, hops, span, width), jnp.bfloat16),
+        dma_sems(CHUNKS, 2, hops),
+        dma_sems(CHUNKS, 2, hops),
+        dma_sems(CHUNKS, 2, hops),
+        dma_sems(CHUNKS, 2, hops),
+        pltpu.VMEM((span, width), jnp.float32),
+    ]
+
+
+def sum_rows_and_spread(place, terms, scratch, finish_rows, spread, between):
+    stage, inbox, rs, rr, gs, gr, total = scratch
+    span = total.shape[0]
+    rows = span * CHUNKS
+    hops = place.n_line - 1
+    sums = [
+        ReduceLine(place, terms, rows, c * span, span, stage.at[c], inbox.at[c], rs.at[c], rr.at[c])
+        for c in range(CHUNKS)
+    ]
+    gathers = []
+    if spread is not None:
+        gathers = [
+            GatherLine(place, spread, rows, c * span, span, gs.at[c], gr.at[c])
+            for c in range(CHUNKS)
+        ]
+    for c in range(CHUNKS + 1):
+        for j in range(hops):
+            if c < CHUNKS:
+                sums[c].step(j)
+            if c > 0 and gathers:
+                gathers[c - 1].step(j)
+        if c < CHUNKS:
+            sums[c].total(total)
+            finish_rows(c, pl.ds(c * span, span), total)
+        if c < len(between):
+            between[c]()
+    for part in gathers + sums:
+        part.finish()
+
+
+def middle_gather(n_dp, n_line, terms, tokens, gain, mats):
+    rows, width = tokens.shape
+    count = len(mats)
+
+    def kernel(*refs):
+        s, tok, gain_ref = refs[:3]
+        srcs = refs[3 : 3 + count]
+        after, hidden = refs[3 + count : 5 + count]
+        dsts = refs[5 + count : 5 + 2 * count]
+        ps, pr, pl_sem = refs[5 + 2 * count : 8 + 2 * count]
+        scratch = refs[8 + 2 * count :]
+        place = Place(n_dp, n_line)
+        place.meet()
+        planes = [
+            GatherPlane(place, a, b, ps.at[i], pr.at[i], pl_sem.at[i])
+            for i, (a, b) in enumerate(zip(srcs, dsts))
+        ]
+        for part in planes:
+            part.begin()
+
+        def norm(c, here, total):
+            values = tok[here].astype(jnp.float32) + total[...]
+            after[here] = values
+            low = rms_scale(values, gain_ref[...]).astype(jnp.bfloat16)
+            first = pl.multiple_of(place.t * rows, 16) + c * total.shape[0]
+            hidden[pl.ds(pl.multiple_of(first, 16), total.shape[0])] = low
+
+        sum_rows_and_spread(place, s, scratch, norm, hidden, [])
+        for part in planes:
+            part.forward()
+        for part in planes:
+            part.share()
+        for part in planes:
+            part.finish()
+
+    return pl.pallas_call(
+        kernel,
+        out_shape=(
+            shaped((rows, width), jnp.float32),
+            shaped((n_line * rows, width), jnp.bfloat16),
+        )
+        + tuple(shaped((n_dp * m.shape[0], m.shape[1]), m.dtype) for m in mats),
+        in_specs=[in_vmem()] * 3 + [in_any()] * count,
+        out_specs=[in_vmem()] * 2 + [in_any()] * count,
+        scratch_shapes=[dma_sems(count, 9), dma_sems(count, 9), dma_sems(count)]
+        + line_scratch(n_line, rows // CHUNKS, width),
+        compiler_params=comm_params(2),
+        name="middle_gather",
+    )(terms, tokens, gain, *mats)
+
+
+def middle_sums(n_dp, n_line, terms, after, gain, grad_in, mats):
+    rows, width = after.shape
+    count = len(mats)
+    block = mats[0].shape[0] // n_dp
+    per = len(ReducePlane.scratch(16, 128))
+
+    def kernel(*refs):
+        s, after_ref, gain_ref, g_ref = refs[:4]
+        srcs = refs[4 : 4 + count]
+        grad_after, gain_sum, spread = refs[4 + count : 7 + count]
+        results = refs[7 + count : 7 + 2 * count]
+        rest = refs[7 + 2 * count :]
+        scratch = rest[count * per :]
+        place = Place(n_dp, n_line)
+        place.meet()
+        planes = [
+            ReducePlane(place, srcs[i], rest[i * per : (i + 1) * per]) for i in range(count)
+        ]
+        for part in planes:
+            part.begin()
+        gain_sum[...] = jnp.zeros_like(gain_sum)
+
+        def norm(c, here, total):
+            grad = total[...]
+            grad_rows, normed = norm_back(after_ref[here], gain_ref[...], grad)
+            gain_sum[...] += jnp.sum(grad * normed, axis=0, keepdims=True)
+            both = g_ref[here].astype(jnp.float32) + grad_rows
+            grad_after[here] = both
+            first = pl.multiple_of(place.t * rows, 16) + c * total.shape[0]
+            spread[pl.ds(pl.multiple_of(first, 16), total.shape[0])] = both.astype(jnp.bfloat16)
+
+        between = [planes[0].cores, planes[1].cores, planes[0].turn]
+        sum_rows_and_spread(place, s, scratch, norm, spread, between)
+        planes[1].turn()
+        for part, result in zip(planes, results):
+            part.finish(result)
+
+    return pl.pallas_call(
+        kernel,
+        out_shape=(
+            shaped((rows, width), jnp.float32),
+            shaped((1, width), jnp.float32),
+            shaped((n_line * rows, width), jnp.bfloat16),
+        )
+        + tuple(shaped((block, m.shape[1]), jnp.bfloat16) for m in mats),
+        in_specs=[in_vmem()] * 4 + [in_any()] * count,
+        out_specs=[in_vmem()] * (3 + count),
+        scratch_shapes=sum([ReducePlane.scratch(block, m.shape[1]) for m in mats], [])
+        + line_scratch(n_line, rows // CHUNKS, width),
+        compiler_params=comm_params(3),
+        name="middle_sums",
+    )(terms, after, gain, grad_in, *mats)
+
+
+class Exchange:
+    def __init__(self, place, axis, src, slots, send, recv, local):
+        self.p, self.src, self.slots = place, src, slots
+        self.over_dp = axis == "dp"
+        self.size = place.n_dp if self.over_dp else place.n_line
+        self.me = place.d if self.over_dp else place.t
+        self.send, self.recv, self.local = send, recv, local
+
+    def copy(self, i):
+        to = lax.rem(self.me + i, self.size)
+        device = (to, self.p.t) if self.over_dp else (self.p.d, to)
+        return remote(
+            self.src, self.slots.at[self.me], self.send.at[i - 1], self.recv.at[i - 1], device
+        )
+
+    def mine(self):
+        return pltpu.make_async_copy(self.src, self.slots.at[self.me], self.local)
+
+    def begin(self):
+        for i in range(1, self.size):
+            self.copy(i).start()
+        self.mine().start()
+
+    def finish(self):
+        self.mine().wait()
+        for i in range(1, self.size):
+            self.copy(i).wait()
+        total = self.slots[0]
+        for i in range(1, self.size):
+            total = total + self.slots[i]
+        return total
+
+
+def last_sums(n_dp, n_line, terms, tokens, gain, grad_after, small, mats):
+    rows, width = tokens.shape
+    count = len(mats)
+    per = len(ReducePlane.scratch(16, 128))
+
+    def kernel(*refs):
+        s, tok, gain_ref, g_ref, small_ref = refs[:5]
+        srcs = refs[5 : 5 + count]
+        grad_tok, small_out, first_out = refs[5 + count : 8 + count]
+        results = refs[8 + count : 8 + 2 * count]
+        rest = refs[8 + 2 * count :]
+        own_first, row_sum = rest[count * per : count * per + 2]
+        slots_a, slots_b, slots_c, slots_d = rest[count * per + 2 : count * per + 6]
+        xs, xr, xl = rest[count * per + 6 : count * per + 9]
+        scratch = rest[count * per + 9 :]
+        place = Place(n_dp, n_line)
+        place.meet(True)
+        planes = [
+            ReducePlane(place, srcs[i], rest[i * per : (i + 1) * per]) for i in range(count)
+        ]
+        for part in planes:
+            part.begin()
+        early = Exchange(place, "dp", small_ref, slots_a, xs.at[0], xr.at[0], xl.at[0])
+        early.begin()
+        own_first[...] = jnp.zeros_like(own_first)
+
+        def norm(c, here, total):
+            grad = total[...]
+            grad_rows, normed = norm_back(tok[here].astype(jnp.float32), gain_ref[...], grad)
+            own_first[...] += jnp.sum(grad * normed, axis=0, keepdims=True)
+            grad_tok[here] = g_ref[here] + grad_rows
+
+        def cores():
+            for part in planes:
+                part.cores()
+
+        def turn():
+            for part in planes:
+                part.turn()
+
+        sum_rows_and_spread(place, s, scratch, norm, None, [cores, turn])
+        first = Exchange(place, "dp", own_first, slots_b, xs.at[1], xr.at[1], xl.at[1])
+        first.begin()
+        small_out[...] = early.finish()
+        row_sum[0:1] = small_out[0:1]
+        row_sum[1:2] = first.finish()
+        both = Exchange(place, "tensor", row_sum, slots_c, xs.at[2], xr.at[2], xl.at[2])
+        both.begin()
+        for part, result in zip(planes, results):
+            part.finish(result)
+        first_out[...] = both.finish()
+
+    return pl.pallas_call(
+        kernel,
+        out_shape=(
+            shaped((rows, width), jnp.float32),
+            shaped(small.shape, jnp.float32),
+            shaped((2, width), jnp.float32),
+        )
+        + tuple(shaped((m.shape[0] // n_dp, m.shape[1]), jnp.bfloat16) for m in mats),
+        in_specs=[in_vmem()] * 5 + [in_any()] * count,
+        out_specs=[in_vmem()] * (3 + count),
+        scratch_shapes=sum([ReducePlane.scratch(m.shape[0] // n_dp, m.shape[1]) for m in mats], [])
+        + [
+            pltpu.VMEM((1, width), jnp.float32),
+            pltpu.VMEM((2, width), jnp.float32),
+            pltpu.VMEM((n_dp,) + small.shape, jnp.float32),
+            pltpu.VMEM((n_dp, 1, width), jnp.float32),
+            pltpu.VMEM((n_line, 2, width), jnp.float32),
+            pltpu.VMEM((1, width), jnp.float32),
+            dma_sems(3, n_dp),
+            dma_sems(3, n_dp),
+            dma_sems(3),
+        ]
+        + line_scratch(n_line, rows // CHUNKS, width),
+        compiler_params=comm_params(4),
+        name="last_sums",
+    )(terms, tokens, gain, grad_after, small, *mats)
+
+
+def matches(mesh):
+    return mesh.shape["dp"] == 8 and mesh.shape["tensor"] == 4
+
+
+def local_blocks(
+    tokens,
+    norm_gain,
+    x_weight,
+    y_weight,
+    conv_weight,
+    recur_gate_weight,
+    input_gate_weight,
+    decay_param,
+    out_weight,
+    mlp_gain,
+    gate_weight,
+    up_weight,
+    down_weight,
+    seq_lengths,
+    token_order,
+    cotangent,
+):
+    n_dp, n_tensor = lax.axis_size("dp"), lax.axis_size("tensor")
+    tensor_index = lax.axis_index("tensor")
+    dp_index = lax.axis_index("dp")
+    tok_rows, width = tokens.shape
+    row_count = tok_rows * n_tensor
+    own_width = conv_weight.shape[1]
+    kernel_taps = conv_weight.shape[0]
+    edge_rows = kernel_taps - 1
+    dp_width = norm_gain.shape[0]
+    gate_rows = recur_gate_weight.shape[0]
+    own_start = tensor_index * tok_rows
+
+    mats = jnp.concatenate([x_weight, y_weight, out_weight.T], axis=1)
+    gains = jnp.concatenate([norm_gain, mlp_gain])
+    spare = gate_rows * 128 - gains.shape[0]
+    gains = jnp.pad(gains, (0, spare)).reshape(gate_rows, 128)
+    minor = jnp.concatenate([recur_gate_weight, input_gate_weight, gains], axis=1)
+    own_order = (token_order - dp_index * row_count).astype(jnp.int32)
+    order_rows = jnp.broadcast_to(own_order[None, :], (8, tok_rows))
+    mats_full, minor_full, tok_all, order_full = first_gather(
+        n_dp, n_tensor, mats, minor, tokens, order_rows
+    )
+    down_full = lax.all_gather(down_weight.T, "dp", axis=0, tiled=True)
+    cot_all = lax.all_gather(
+        lax.optimization_barrier((cotangent, order_full))[0], "tensor", axis=0, tiled=True
+    )
+    order_all = order_full.reshape(n_tensor, 8, tok_rows)[:, 0].reshape(row_count)
+    both_gates = minor_full[:, : 2 * own_width]
+    gain_rows = minor_full[:, 2 * own_width :].reshape(n_dp, -1)
+    first_gain = gain_rows[:, :dp_width].reshape(1, width).astype(jnp.float32)
+    second_gain = gain_rows[:, dp_width : 2 * dp_width].reshape(1, width).astype(jnp.float32)
+    block_size = both_gates.shape[0]
+    x_full, y_full, out_full = (
+        mats_full[:, :own_width],
+        mats_full[:, own_width : 2 * own_width],
+        mats_full[:, 2 * own_width :],
+    )
+
+    first_all = rms_scale(tok_all.astype(jnp.float32), first_gain).astype(jnp.bfloat16)
+    row_index = jnp.arange(row_count, dtype=jnp.int32)
+    to_place = (row_index[:, None] == order_all[None, :]).astype(jnp.bfloat16)
+
+    def placed(stored):
+        return plain_dot(to_place, stored).astype(jnp.bfloat16)
+
+    def stored(rows):
+        return trans_times(to_place, rows).astype(jnp.bfloat16)
+
+    hidden_place = placed(first_all)
+    places = dp_index * row_count + row_index
+    ends = jnp.cumsum(seq_lengths)
+    segment = segment_of(places, ends)
+    starts = (places == 0) | (segment != segment_of(places - 1, ends))
+    live_stored = (order_all + dp_index * row_count < ends[-1]).astype(jnp.float32)
+    live_own = (token_order < ends[-1]).astype(jnp.float32)
+    same = [
+        (segment_of(places - shift, ends) == segment).astype(jnp.float32)
+        for shift in range(kernel_taps)
+    ]
+    low_edge = tensor_index * own_width
+    own_blocks = (low_edge + jnp.arange(own_width, dtype=jnp.int32)) // block_size
+    first_block = low_edge // block_size
+    block_count = own_width // block_size + 2
+
+    def block_start(index):
+        return (first_block + index) * block_size - low_edge + block_size
+
+    def block_mask(index):
+        inside = own_blocks == first_block + index
+        return jnp.concatenate([inside, inside])
+
+    def convolve(extended, kernel):
+        return sum(
+            (
+                kernel[shift][None, :]
+                * extended[edge_rows - shift : edge_rows - shift + row_count]
+                * same[shift][:, None]
+                for shift in range(kernel_taps)
+            )
+        )
+
+    def gates(conv_vals, pre_recur, pre_input, decay_vals):
+        log_rate = -rate_scale * jax.nn.sigmoid(pre_recur) * jax.nn.softplus(-decay_vals)
+        decay_rate = jnp.where(starts[:, None], 0.0, jnp.exp(log_rate))
+        scale_in = jnp.where(starts[:, None], 1.0, jnp.sqrt(-jnp.expm1(2.0 * log_rate)))
+        return (decay_rate, conv_vals * jax.nn.sigmoid(pre_input) * scale_in)
+
+    def glu(gate_pre, up_pre):
+        return gelu_tanh(gate_pre) * up_pre
+
+    x_branch = plain_dot(hidden_place, x_full).astype(jnp.bfloat16)
+    y_before = plain_dot(hidden_place, y_full)
+    previous = from_behind(x_branch[row_count - edge_rows :], "dp", 1)
+    extended = jnp.concatenate([previous, x_branch], axis=0).astype(jnp.float32)
+    conv_out = convolve(extended, conv_weight)
+    conv_wide = extended_2(conv_out.astype(jnp.bfloat16), (("tensor", 1),), block_size)
+    pre_both = jnp.zeros((row_count, 2 * own_width), jnp.float32)
+    for index in range(block_count):
+        piece = lax.dynamic_slice_in_dim(conv_wide, block_start(index), block_size, 1)
+        pre_both = pre_both + jnp.where(
+            block_mask(index)[None, :], plain_dot(piece, both_gates), 0.0
+        )
+    (decay_rate, driven), gate_pull = jax.vjp(
+        gates, conv_out, pre_both[:, :own_width], pre_both[:, own_width:], decay_param
+    )
+    cum_rate, local_state = lax.associative_scan(pair_step, (decay_rate, driven), axis=0)
+    ident = (jnp.ones((own_width,), jnp.float32), jnp.zeros((own_width,), jnp.float32))
+    rate_in, state_in = entering((cum_rate[-1], local_state[-1]), "dp", pair_step, ident, False)
+    state = local_state + cum_rate * state_in[None, :]
+    y_branch = gelu_tanh(y_before)
+    merged = (state * y_branch).astype(jnp.bfloat16)
+    merged_stored = stored(merged)
+
+    mixer_terms = times_trans(merged_stored, out_full).astype(jnp.bfloat16)
+    after_own, hidden_two, gate_full, up_full = middle_gather(
+        n_dp, n_tensor, mixer_terms, tokens, second_gain, (gate_weight, up_weight)
+    )
+    gate_pre = plain_dot(hidden_two, gate_full)
+    up_pre = plain_dot(hidden_two, up_full)
+    glu_out, glu_pull = jax.vjp(glu, gate_pre, up_pre)
+    product = glu_out.astype(jnp.bfloat16)
+    feed_out = lax.psum_scatter(
+        times_trans(product, down_full).astype(jnp.bfloat16),
+        "tensor",
+        scatter_dimension=0,
+        tiled=True,
+    ).astype(jnp.float32)
+    output = ((after_own + feed_out) * live_own[:, None]).astype(jnp.bfloat16)
+
+    down_in = (cot_all.astype(jnp.float32) * live_stored[:, None]).astype(jnp.bfloat16)
+    grad_in_own = (cotangent.astype(jnp.float32) * live_own[:, None]).astype(jnp.bfloat16)
+    grad_down = trans_times(down_in, product).astype(jnp.bfloat16)
+    grad_product = plain_dot(down_in, down_full)
+    grad_gate_pre, grad_up_pre = glu_pull(grad_product)
+    grad_gate_pre = grad_gate_pre.astype(jnp.bfloat16)
+    grad_up_pre = grad_up_pre.astype(jnp.bfloat16)
+    grad_gate = trans_times(hidden_two, grad_gate_pre).astype(jnp.bfloat16)
+    grad_up = trans_times(hidden_two, grad_up_pre).astype(jnp.bfloat16)
+    feed_terms = (
+        times_trans(grad_gate_pre, gate_full) + times_trans(grad_up_pre, up_full)
+    ).astype(jnp.bfloat16)
+    down_sum = lax.psum_scatter(grad_down, "dp", scatter_dimension=0, tiled=True)
+    grad_after_own, second_part, mixer_in, gate_sum, up_sum = middle_sums(
+        n_dp, n_tensor, feed_terms, after_own, second_gain, grad_in_own, (grad_gate, grad_up)
+    )
+
+    grad_out_mat = trans_times(mixer_in, merged_stored).astype(jnp.bfloat16)
+    out_sum = lax.psum_scatter(grad_out_mat, "dp", scatter_dimension=0, tiled=True)
+    grad_merged = plain_dot(placed(mixer_in), out_full)
+    grad_state = grad_merged * y_branch
+    gelu_pull = jax.vjp(gelu_tanh, y_before)[1]
+    grad_y_before = gelu_pull(grad_merged * state)[0].astype(jnp.bfloat16)
+    rate_next = jnp.concatenate([decay_rate[1:], jnp.ones((1, own_width), jnp.float32)], axis=0)
+    rev_rate, local_lam = lax.associative_scan(
+        pair_step, (rate_next, grad_state), reverse=True, axis=0
+    )
+    head_rate = decay_rate[0] * rev_rate[0]
+    head_lam = decay_rate[0] * local_lam[0]
+    factor_in, lam_in = entering((head_rate, head_lam), "dp", pair_step, ident, True)
+    lam = local_lam + rev_rate * lam_in[None, :]
+    state_prev = jnp.concatenate([state_in[None, :], state[:-1]], axis=0)
+    grad_conv_local, grad_pre_recur, grad_pre_input, grad_decay_own = gate_pull(
+        (lam * state_prev, lam)
+    )
+    grad_pre = jnp.concatenate([grad_pre_recur, grad_pre_input], axis=1).astype(jnp.bfloat16)
+    grad_both = jnp.zeros((block_size, 2 * own_width), jnp.float32)
+    grad_wide = jnp.zeros((row_count, own_width + 2 * block_size), jnp.float32)
+    for index in range(block_count):
+        begin = block_start(index)
+        piece = lax.dynamic_slice_in_dim(conv_wide, begin, block_size, 1)
+        masked = jnp.where(block_mask(index)[None, :], grad_pre, jnp.zeros((), jnp.bfloat16))
+        grad_both = grad_both + trans_times(piece, masked)
+        added = lax.dynamic_slice_in_dim(grad_wide, begin, block_size, 1) + times_trans(
+            masked, both_gates
+        )
+        grad_wide = lax.dynamic_update_slice_in_dim(grad_wide, added, begin, 1)
+    rims = jnp.concatenate(
+        [grad_wide[:, :block_size], grad_wide[:, own_width + block_size :]], axis=1
+    )
+    arrived = extended_2(rims.astype(jnp.bfloat16), (("tensor", 1),), block_size).astype(rims.dtype)
+    from_lower = jnp.pad(arrived[:, :block_size], ((0, 0), (0, own_width - block_size)))
+    from_upper = jnp.pad(arrived[:, 3 * block_size :], ((0, 0), (own_width - block_size, 0)))
+    grad_conv = (
+        grad_conv_local
+        + grad_wide[:, block_size : block_size + own_width]
+        + from_lower
+        + from_upper
+    )
+    conv_pull = jax.vjp(convolve, extended, conv_weight)[1]
+    grad_extended, grad_kernel = conv_pull(grad_conv)
+    returned = from_behind(grad_extended[:edge_rows], "dp", -1)
+    grad_x_branch = grad_extended[edge_rows:] + jnp.concatenate(
+        [jnp.zeros((row_count - edge_rows, own_width), jnp.float32), returned], axis=0
+    )
+    grad_xy = stored(
+        jnp.concatenate([grad_x_branch.astype(jnp.bfloat16), grad_y_before], axis=1)
+    )
+    grad_xy_mat = trans_times(first_all, grad_xy).astype(jnp.bfloat16)
+    one_terms = times_trans(grad_xy, mats_full[:, : 2 * own_width]).astype(jnp.bfloat16)
+    small = jnp.concatenate(
+        [
+            second_part,
+            grad_kernel.reshape(1, -1),
+            jnp.pad(grad_decay_own, (0, width - own_width)).reshape(1, width),
+            jnp.zeros((1, width), jnp.float32),
+        ],
+        axis=0,
+    )
+    grad_tokens, small_sum, gain_sums, xy_sum, gates_sum = last_sums(
+        n_dp,
+        n_tensor,
+        one_terms,
+        tokens,
+        first_gain,
+        grad_after_own,
+        small,
+        (grad_xy_mat, grad_both.astype(jnp.bfloat16)),
+    )
+    xy_sum, gates_sum = xy_sum.astype(jnp.float32), gates_sum.astype(jnp.float32)
+    own_gains = lax.dynamic_slice_in_dim(gain_sums, dp_index * dp_width, dp_width, 1)
+    return (
+        output,
+        grad_tokens,
+        own_gains[1],
+        xy_sum[:, :own_width],
+        xy_sum[:, own_width:],
+        small_sum[1].reshape(kernel_taps, own_width),
+        gates_sum[:, :own_width],
+        gates_sum[:, own_width:],
+        small_sum[2, :own_width],
+        out_sum.astype(jnp.float32).T,
+        own_gains[0],
+        gate_sum.astype(jnp.float32),
+        up_sum.astype(jnp.float32),
+        down_sum.astype(jnp.float32).T,
+    )
+
+
 def solution(mesh):
     in_specs = (
         P(("dp", "tensor"), None),
@@ -455,4 +1428,6 @@
         P("dp", "tensor"),
         P("tensor", "dp"),
     )
+    fits = matches(mesh)
+    local = local_blocks if fits else local_general
     return jax.shard_map(local, mesh=mesh, in_specs=in_specs, out_specs=out_specs, check_vma=False)

time: 1950 us -> 1000 us (0.51)
  waiting for transfers between devices: 1190 us -> 32.7 us
  Pallas kernels: 0 us -> 417 us
  blocking collectives: 111 us -> 35.4 us
  local copies, waits for them, and re-layouts: 312 us -> 246 us
  other arithmetic: 130 us -> 86 us
    reduce_scatter x12 -> x3, waiting for transfers between devices: 589 us -> 16.8 us  [the longest x1 16.8 us: local_blocks(): lax.psum_scatter(times_trans(product, down_full).astype(jnp.bfloat16), 't...]
    all_gather x16 -> x2, waiting for transfers between devices: 451 us -> 0.01 us  [the longest x1 0.01 us: local_blocks(): lax.all_gather(lax.optimization_barrier((cotangent, order_full))[0], 'ten...]
    pallas_call x0 -> x4, Pallas kernels: none -> 417 us  [the longest x1 134 us: middle_gather(): pl.pallas_call(kernel, out_shape=(shaped((rows, width), jnp.float32), sha...]
    psum x1 -> x0, waiting for transfers between devices: 123 us -> none  [local(): lax.psum((first_part, second_part, kernel_tile, decay_tile), ('dp', 'tens...]
    all_gather x5 -> x0, blocking collectives: 50.7 us -> none  [the longest x2 19.1 us: collect(): lax.all_gather(input_gate_weight, 'dp', axis=0, tiled=True)]
    pad x64 -> x65, local copies, waits for them, and re-layouts: 53.6 us -> 19.8 us  [the longest x32 17.2 us: local_blocks(): lax.associative_scan(pair_step, (decay_rate, driven), axis=0)]
    unnamed x1 -> x0, blocking collectives: 24.5 us -> none
    convert_element_type x22 -> x11, other arithmetic: 30.8 us -> 9.43 us  [the longest x1 2.45 us: local_blocks(): (cotangent.astype(jnp.float32) * live_own[:, None]).astype(jnp.bfloat16)]
  transfers between devices with their start and end apart: 35 -> 11, of which waited for: 29 -> 3; matrix products, arithmetic and copies ran while one was open for 29% -> 42% of each run, Pallas kernels for 0% -> 23%
where the time goes in v1:
time: 1000 us; the launch traced here: 988 us
  Pallas kernels  417 us (42%)
  local copies, waits for them, and re-layouts  246 us (25%)
  matrix products  138 us (14%)
  other arithmetic  86 us (9%)
  blocking collectives  35.4 us (4%)
  waiting for transfers between devices  32.7 us (3%)
  between operations  16.7 us (2%)
  starting transfers between devices  15.5 us (2%)
    pallas_call x1, Pallas kernels, middle_gather(): pl.pallas_call(kernel, out_shape=(shaped((rows, width), jnp.float32), sha...  134 us
    pallas_call x1, Pallas kernels, middle_sums(): pl.pallas_call(kernel, out_shape=(shaped((rows, width), jnp.float32), sha...  125 us
    pallas_call x1, Pallas kernels, last_sums(): pl.pallas_call(kernel, out_shape=(shaped((rows, width), jnp.float32), sha...  93 us
    slice x65, local copies, waits for them, and re-layouts, local_blocks(): lax.associative_scan(pair_step, (rate_next, grad_state), reverse=True, ax...  87.2 us
    slice x60, local copies, waits for them, and re-layouts, local_blocks(): lax.associative_scan(pair_step, (decay_rate, driven), axis=0)  83.4 us
    pallas_call x1, Pallas kernels, first_gather(): pl.pallas_call(kernel, out_shape=(shaped((n_dp * mats.shape[0], mats.shap...  64.6 us
    dot_general x11, matrix products, plain_dot(): return jnp.dot(left, right, preferred_element_type=jnp.float32)  57.3 us
    dot_general x11, matrix products, trans_times(): lax.dot_general(left, right, (((0,), (0,)), ((), ())), preferred_element_...  42.8 us
  transfers between devices with their start and end apart: 11, of which 3 were waited for; matrix products, arithmetic and copies ran while one was open for 42% of the time, Pallas kernels for 23%

profile of v1, /device:TPU:0, one launch (start us, length us, event | category | flops | bytes accessed | tf_op | source)
XLA Modules:
  0.0 988.0 jit_solution(15541086981658514560)
XLA Ops:
  12.3 64.6 %first_gather.1 = (bf16[2560,1920]{1,0:T(8,128)(2,1)}, bf16[256,1408]{1,0:T(8,128)(2,1)}, bf16[512,2560]{1,0:T(8,128)(2,1)}, s32[32,128]{1,0:T(8,128)}) custom-call(bf16[320,1920]{1,0:T(8,128)(2,1)} %pad_maximum_fusion.1.a, bf16[32,1408]{1,0:T(8,128)(2,1)} %pad_maximum_fusion.14.b, bf16[128,2560]{1,0:T(8,128)(2,1)} %refs_1_.3, s32[8,128]{1,0:T(8,128)} %broadcast_in_dim.131.e), custom_call_target="tpu_custom_call" | custom-call | tf_op jit(solution)/shard_map/first_gather/pallas_call | solution.py:849
  83.1 5.3 fusion.28
  93.6 6.0 fusion.18
  103.1 4.7 collective-permute-start.1
  108.6 15.5 %collective-permute-done.2 = bf16[512,256]{1,0:T(8,128)(2,1)S(1)} collective-permute-done((bf16[512,256]{1,0:T(8,128)(2,1)}, bf16[512,256]{1,0:T(8,128)(2,1)S(1)}, u32[]{:S(2)}, u32[]{:S(2)}) %collective-permute-start.2) | collective-permute-done | bytes 262176 | tf_op jit(solution)/shard_map/ppermute | solution.py:26
  247.0 4.8 pad.299
  252.8 4.8 pad.280
  261.2 9.3 all-gather
  271.3 9.0 all-gather.1
  285.3 5.9 convolution_convert_fusion.7.refs_0_
  291.2 134.2 %middle_gather.1 = (f32[128,2560]{1,0:T(8,128)}, bf16[512,2560]{1,0:T(8,128)(2,1)}, bf16[2560,1920]{1,0:T(8,128)(2,1)}, bf16[2560,1920]{1,0:T(8,128)(2,1)}) custom-call(bf16[512,2560]{1,0:T(8,128)(2,1)} %convolution_convert_fusion.7.refs_0_, bf16[128,2560]{1,0:T(8,128)(2,1)} %refs_1_.3, f32[1,2560]{1,0:T(1,128)} %reshape.183.refs_2_, ...), custom_call_target="tpu_custom_call" | custom-call | tf_op jit(solution)/shard_map/middle_gather/pallas_call | solution.py:953
  425.4 11.4 %fusion.181 = f32[512,1920]{1,0:T(8,128)} fusion(bf16[512,2560]{1,0:T(8,128)(2,1)} %get-tuple-element.227, bf16[2560,1920]{1,0:T(8,128)(2,1)} %get-tuple-element.228), kind=kOutput, calls=%fused_computation.394 | convolution fusion | flops 5033164800 | bytes 16384000 | tf_op jit(solution)/shard_map/dot_general | solution.py:71
  436.8 7.4 fusion.182
  444.3 15.2 %multiply_convert_fusion.1 = (bf16[512,1920]{1,0:T(8,128)(2,1)S(1)}, bf16[512,1920]{1,0:T(8,128)(2,1)}, bf16[512,1920]{1,0:T(8,128)(2,1)S(1)}) fusion(f32[512,1920]{1,0:T(8,128)} %fusion.181, f32[512,1920]{1,0:T(8,128)} %fusion.182, bf16[2560,1920]{1,0:T(8,128)(2,1)} %all-gather.7.cloned.1.call-done, bf16[512,2560]{1,0:T(8,128)(2,1)} %all-gather.9.cloned.1.call-done, ...), kind=kOutput, calls=%fused_computation.34 | convolution fusion | flops 5062656000 | bytes 26216448 | tf_op jit(solution)/shard_map/dot_general | solution.py:71
  460.7 6.9 convolution_convert_fusion.6
  467.9 9.0 fusion.183
  477.0 8.1 convolution_convert_fusion.3.refs_4_
  485.1 8.0 convolution_convert_fusion.2.refs_5_
  493.2 8.8 add_convert_fusion.refs_0_
  502.0 16.8 %reduce-scatter.4.cloned.1.call-done = bf16[128,2560]{1,0:T(8,128)(2,1)} async-done(((bf16[512,2560]{1,0:T(8,128)(2,1)}), bf16[128,2560]{1,0:T(8,128)(2,1)}) %reduce-scatter.4.cloned.1.call-update) | async-done | bytes 655376 | tf_op jit(solution)/shard_map/reduce_scatter | solution.py:1279
  521.2 125.5 %middle_sums.1 = (f32[128,2560]{1,0:T(8,128)}, f32[1,2560]{1,0:T(1,128)}, bf16[512,2560]{1,0:T(8,128)(2,1)}, bf16[320,1920]{1,0:T(8,128)(2,1)}, bf16[320,1920]{1,0:T(8,128)(2,1)}) custom-call(bf16[512,2560]{1,0:T(8,128)(2,1)} %add_convert_fusion.refs_0_, f32[128,2560]{1,0:T(8,128)} %get-tuple-element.226.refs_1_, f32[1,2560]{1,0:T(1,128)} %reshape.183.refs_2_, ...), custom_call_target="tpu_custom_call" | custom-call | tf_op jit(solution)/shard_map/middle_sums/pallas_call | solution.py:1006
  646.7 5.7 convolution_convert_fusion.4
  658.5 4.6 slice.800
  669.6 10.2 %convolution_convert_fusion = bf16[2560,1920]{1,0:T(8,128)(2,1)} fusion(bf16[512,1920]{1,0:T(8,128)(2,1)} %copy-done.137, bf16[512,2560]{1,0:T(8,128)(2,1)} %all-gather.9.cloned.1.call-done, f32[512]{0:T(512)S(1)} %copy-done.120), kind=kOutput, calls=%fused_computation.6 | convolution fusion | flops 5042012160 | bytes 14419968 | tf_op jit(solution)/shard_map/dot_general | solution.py:81
  681.2 8.2 fusion.79
  788.4 10.7 %rev.14 = f32[512,640]{1,0:T(8,128)} reverse(f32[512,640]{1,0:T(8,128)} %add.758), dimensions={0} | reverse | bytes 2621440 | tf_op jit(solution)/shard_map/rev | solution.py:1311
  803.6 10.8 %rev.15 = f32[512,640]{1,0:T(8,128)} reverse(f32[512,640]{1,0:T(8,128)} %add.767), dimensions={0} | reverse | bytes 2621440 | tf_op jit(solution)/shard_map/rev | solution.py:1311
  815.2 8.8 all-gather.2
  824.2 8.2 all-gather.3
  863.5 5.8 convolution_convert_fusion.1.refs_5_
  869.3 4.9 fusion.5.refs_0_
  874.2 93.0 %last_sums.1 = (f32[128,2560]{1,0:T(8,128)}, f32[4,2560]{1,0:T(4,128)}, f32[2,2560]{1,0:T(2,128)}, bf16[320,1280]{1,0:T(8,128)(2,1)}, bf16[32,1280]{1,0:T(8,128)(2,1)}) custom-call(bf16[512,2560]{1,0:T(8,128)(2,1)} %fusion.5.refs_0_, bf16[128,2560]{1,0:T(8,128)(2,1)} %refs_1_.3, f32[1,2560]{1,0:T(1,128)} %reshape.184.refs_2_, ...), custom_call_target="tpu_custom_call" | custom-call | tf_op jit(solution)/shard_map/last_sums/pallas_call | solution.py:1108
  (731 shorter events, 319.4 us)
Async XLA Ops:
  7.2 437.1 %all-gather.9.cloned.1.call-start = ((), (), s32[]{:S(2)}) async-start(), calls=%async_computation.5 | async-start | bytes 3276800 | tf_op jit(solution)/shard_map/all_gather | solution.py:1181
  77.0 367.3 %all-gather.7.cloned.1.call-start = ((), (), s32[]{:S(2)}) async-start(), calls=%async_computation.3 | async-start | bytes 11059200 | tf_op jit(solution)/shard_map/all_gather | solution.py:1180
  88.4 11.2 %collective-permute-start = (bf16[3,640]{1,0:T(4,128)(2,1)S(1)}, bf16[3,640]{1,0:T(4,128)(2,1)S(1)}, u32[]{:S(2)}, u32[]{:S(2)}) collective-permute-start(bf16[3,640]{1,0:T(4,128)(2,1)S(1)} %slice.908), channel_id=1, source_target_pairs={{0,4},{4,8},{8,12},{12,16},{16,20},{20,24},{24,28},{1,5},{5,9},{9,... | collective-permute-start | bytes 11528 | tf_op jit(solution)/shard_map/ppermute | solution.py:15
  90.0 428.8 %reduce-scatter.4.cloned.1.call-start = ((), (), s32[]{:S(2)}) async-start(), calls=%async_computation.4 | async-start | bytes 3276800 | tf_op jit(solution)/shard_map/reduce_scatter | solution.py:1279
  90.8 33.4 %copy-start.107 = (pred[1280]{0:T(1024)(128)(4,1)}, pred[1280]{0:T(1024)(128)(4,1)S(1)}, u32[]{:S(2)}) copy-start(pred[1280]{0:T(1024)(128)(4,1)S(1)} %pad_add_fusion.5) | copy-start | bytes 3844
  90.8 33.9 %copy-start.109 = (pred[1280]{0:T(1024)(128)(4,1)}, pred[1280]{0:T(1024)(128)(4,1)S(1)}, u32[]{:S(2)}) copy-start(pred[1280]{0:T(1024)(128)(4,1)S(1)} %pad_add_fusion.4) | copy-start | bytes 3844
  93.6 32.9 %copy-start.116 = (pred[512]{0:T(512)(128)(4,1)}, pred[512]{0:T(512)(128)(4,1)S(1)}, u32[]{:S(2)}) copy-start(pred[512]{0:T(512)(128)(4,1)S(1)} %get-tuple-element.427) | copy-start | bytes 1540
  99.6 25.7 %copy-start.111 = (pred[1280]{0:T(1024)(128)(4,1)}, pred[1280]{0:T(1024)(128)(4,1)S(1)}, u32[]{:S(2)}) copy-start(pred[1280]{0:T(1024)(128)(4,1)S(1)} %pad_add_fusion.3) | copy-start | bytes 3844
  100.8 25.6 %copy-start.5 = (f32[512,640]{1,0:T(8,128)}, f32[512,640]{1,0:T(8,128)S(1)}, u32[]{:S(2)}) copy-start(f32[512,640]{1,0:T(8,128)S(1)} %get-tuple-element.318) | copy-start | bytes 3932164
  101.7 22.5 %copy-start.6 = (bf16[256,1408]{1,0:T(8,128)(2,1)S(1)}, bf16[256,1408]{1,0:T(8,128)(2,1)}, u32[]{:S(2)}) copy-start(bf16[256,1408]{1,0:T(8,128)(2,1)} %get-tuple-element.223) | copy-start | bytes 2162692
  101.7 22.4 %collective-permute-start.2 = (bf16[512,256]{1,0:T(8,128)(2,1)}, bf16[512,256]{1,0:T(8,128)(2,1)S(1)}, u32[]{:S(2)}, u32[]{:S(2)}) collective-permute-start(bf16[512,256]{1,0:T(8,128)(2,1)} %get-tuple-element.351), channel_id=1, source_target_pairs={{1,0},{2,1},{3,2},{5,4},{6,5},{7,6},{9,8},{10,9},{11,10},{13,12},{... | collective-permute-start | bytes 786440 | tf_op jit(solution)/shard_map/ppermute | solution.py:26
  103.1 21.0 %collective-permute-start.1 = (bf16[512,256]{1,0:T(8,128)(2,1)S(1)}, bf16[512,256]{1,0:T(8,128)(2,1)S(1)}, u32[]{:S(2)}, u32[]{:S(2)}) collective-permute-start(bf16[512,256]{1,0:T(8,128)(2,1)S(1)} %get-tuple-element.350), channel_id=1, source_target_pairs={{0,1},{1,2},{2,3},{4,5},{5,6},{6,7},{8,9},{9,10},{10,11},{12,13},{... | collective-permute-start | bytes 786440 | tf_op jit(solution)/shard_map/ppermute | solution.py:25
  107.9 17.9 %copy-start.83 = (pred[1280]{0:T(1024)(128)(4,1)}, pred[1280]{0:T(1024)(128)(4,1)S(1)}, u32[]{:S(2)}) copy-start(pred[1280]{0:T(1024)(128)(4,1)S(1)} %pad_add_fusion.2) | copy-start | bytes 3844
  108.6 17.8 %copy-start.62 = (f32[640]{0:T(1024)}, f32[640]{0:T(1024)S(1)}, u32[]{:S(2)}) copy-start(f32[640]{0:T(1024)S(1)} %broadcast_multiply_fusion.1) | copy-start | bytes 7684
  129.1 526.0 %copy-start.4 = (f32[512,640]{1,0:T(8,128)}, f32[512,640]{1,0:T(8,128)S(1)}, u32[]{:S(2)}) copy-start(f32[512,640]{1,0:T(8,128)S(1)} %get-tuple-element.329) | copy-start | bytes 3932164
  199.4 26.5 %copy-start.57 = (f32[4,640]{1,0:T(4,128)}, f32[4,640]{1,0:T(4,128)S(1)}, u32[]{:S(2)}) copy-start(f32[4,640]{1,0:T(4,128)S(1)} %get-tuple-element.411) | copy-start | bytes 30724
  444.3 16.4 %copy-start.124 = (bf16[2560,1920]{1,0:T(8,128)(2,1)S(1)}, bf16[2560,1920]{1,0:T(8,128)(2,1)}, u32[]{:S(2)}) copy-start(bf16[2560,1920]{1,0:T(8,128)(2,1)} %all-gather.7.cloned.1.call-done) | copy-start | bytes 29491204
  459.4 25.7 %copy-start.135 = (bf16[512,1920]{1,0:T(8,128)(2,1)}, bf16[512,1920]{1,0:T(8,128)(2,1)S(1)}, u32[]{:S(2)}) copy-start(bf16[512,1920]{1,0:T(8,128)(2,1)S(1)} %get-tuple-element.323) | copy-start | bytes 5898244
  467.7 507.6 %reduce-scatter.6.cloned.1.call-start = ((), (), s32[]{:S(2)}) async-start(), calls=%async_computation.6 | async-start | bytes 3686400 | tf_op jit(solution)/shard_map/reduce_scatter | solution.py:1305
  477.0 16.2 %slice-start.3 = ((s8[9830400]{0:T(1024)(128)(4,1)}), s8[4194304]{0:T(1024)(128)(4,1)S(1)}, s32[]{:S(2)}) async-start(s8[9830400]{0:T(1024)(128)(4,1)} %bitcast.80), calls=%async_computation.11 | async-start | bytes 8388608
  493.2 25.6 %copy-start.16 = (f32[128,2560]{1,0:T(8,128)S(1)}, f32[128,2560]{1,0:T(8,128)}, u32[]{:S(2)}) copy-start(f32[128,2560]{1,0:T(8,128)} %get-tuple-element.226.refs_1_) | copy-start | bytes 3932164
  493.2 25.5 %copy-start.27 = (bf16[128,2560]{1,0:T(8,128)(2,1)S(1)}, bf16[128,2560]{1,0:T(8,128)(2,1)}, u32[]{:S(2)}) copy-start(bf16[128,2560]{1,0:T(8,128)(2,1)} %param.35) | copy-start | bytes 1966084
  493.2 25.5 %copy-start.123 = (f32[128]{0:T(128)S(1)}, f32[128]{0:T(128)}, u32[]{:S(2)}) copy-start(f32[128]{0:T(128)} %compare_convert_fusion) | copy-start | bytes 1540
  521.2 125.5 %copy-start.132 = (bf16[512,640]{1,0:T(8,128)(2,1)S(1)}, bf16[512,640]{1,0:T(8,128)(2,1)}, u32[]{:S(2)}) copy-start(bf16[512,640]{1,0:T(8,128)(2,1)} %copy-done.131) | copy-start | bytes 1966084
  652.5 324.7 %reduce-scatter.8.cloned.1.call-start = ((), (), s32[]{:S(2)}) async-start(), calls=%async_computation.7 | async-start | bytes 11059200 | tf_op jit(solution)/shard_map/reduce_scatter | solution.py:1299
  803.6 29.4 %copy-start.3 = (f32[512,1280]{1,0:T(8,128)S(1)}, f32[512,1280]{1,0:T(8,128)}, u32[]{:S(2)}) copy-start(f32[512,1280]{1,0:T(8,128)} %copy-done.2) | copy-start | bytes 7864324
  803.6 29.4 %copy-start.63 = (f32[640]{0:T(1024)S(1)}, f32[640]{0:T(1024)}, u32[]{:S(2)}) copy-start(f32[640]{0:T(1024)} %copy-done.62) | copy-start | bytes 7684
  803.6 29.4 %copy-start.106 = (f32[1,640]{1,0:T(1,128)S(1)}, f32[1,640]{1,0:T(1,128)}, u32[]{:S(2)}) copy-start(f32[1,640]{1,0:T(1,128)} %broadcast_in_dim.140) | copy-start | bytes 7684
  803.6 29.4 %copy-start.117 = (pred[512]{0:T(512)(128)(4,1)S(1)}, pred[512]{0:T(512)(128)(4,1)}, u32[]{:S(2)}) copy-start(pred[512]{0:T(512)(128)(4,1)} %copy-done.116) | copy-start | bytes 1540
  841.9 12.5 %collective-permute-start.4 = (bf16[512,256]{1,0:T(8,128)(2,1)S(1)}, bf16[512,256]{1,0:T(8,128)(2,1)S(1)}, u32[]{:S(2)}, u32[]{:S(2)}) collective-permute-start(bf16[512,256]{1,0:T(8,128)(2,1)S(1)} %get-tuple-element.339), channel_id=1, source_target_pairs={{1,0},{2,1},{3,2},{5,4},{6,5},{7,6},{9,8},{10,9},{11,10},{13,12},{... | collective-permute-start | bytes 786440 | tf_op jit(solution)/shard_map/ppermute | solution.py:26
  843.3 11.1 %collective-permute-start.3 = (bf16[512,256]{1,0:T(8,128)(2,1)S(1)}, bf16[512,256]{1,0:T(8,128)(2,1)S(1)}, u32[]{:S(2)}, u32[]{:S(2)}) collective-permute-start(bf16[512,256]{1,0:T(8,128)(2,1)S(1)} %get-tuple-element.338), channel_id=1, source_target_pairs={{0,1},{1,2},{2,3},{4,5},{5,6},{6,7},{8,9},{9,10},{10,11},{12,13},{... | collective-permute-start | bytes 786440 | tf_op jit(solution)/shard_map/ppermute | solution.py:25
  857.9 3.1 collective-permute-start.5
  (123 other events, 502.7 us)
Sparse Core Ops, SparseCore 0:
  77.1 60.4 all-gather.8
  139.5 59.2 all-gather.6
  467.8 50.8 reduce-scatter.3
  652.6 44.2 reduce-scatter.5
  700.3 78.3 reduce-scatter.7

commit v2 on v1

--- a/solution.py
+++ b/solution.py
@@ -643,25 +643,52 @@
             source, self.inbox.at[way, j], self.send.at[way, j], self.recv.at[way, j], to
         )
 
-    def step(self, j):
+    def ends(self):
         t, last = self.p.t, self.last
-        for way in (0, 1):
-            owner = last - j if way == 0 else j
-            first = (t == 0) if way == 0 else (t == last)
-            passing = (t > 0) & (t < owner) if way == 0 else (t < last) & (t > owner)
-            term = self.own(owner)
-
-            @pl.when(first)
-            def _():
-                self.copy(way, j, term).start()
-
-            @pl.when(passing)
-            def _():
-                self.copy(way, j, term).wait_recv()
-                self.stage[way, j] = (
-                    term[...].astype(jnp.float32) + self.inbox[way, j].astype(jnp.float32)
-                ).astype(jnp.bfloat16)
-                self.copy(way, j, self.stage.at[way, j]).start()
+
+        @pl.when(t == 0)
+        def _():
+            for j in range(last):
+                self.copy(0, j, self.own(last - j)).start()
+
+        @pl.when(t == last)
+        def _():
+            for j in range(last):
+                self.copy(1, j, self.own(j)).start()
+
+    def sent(self):
+        t, last = self.p.t, self.last
+
+        @pl.when(t == 0)
+        def _():
+            for j in range(last):
+                self.copy(0, j, self.own(last - j)).wait_send()
+
+        @pl.when(t == last)
+        def _():
+            for j in range(last):
+                self.copy(1, j, self.own(j)).wait_send()
+
+    def hand_on(self, way, j):
+        term = self.own(self.last - j if way == 0 else j)
+        self.copy(way, j, term).wait_recv()
+        self.stage[way, j] = (
+            term[...].astype(jnp.float32) + self.inbox[way, j].astype(jnp.float32)
+        ).astype(jnp.bfloat16)
+        self.copy(way, j, self.stage.at[way, j]).start()
+
+    def hop(self, k):
+        t, last = self.p.t, self.last
+
+        @pl.when(t == k + 1)
+        def _():
+            for j in range(last - 1 - k):
+                self.hand_on(0, j)
+
+        @pl.when(t == last - 1 - k)
+        def _():
+            for j in range(last - 1 - k):
+                self.hand_on(1, j)
 
     def total(self, result):
         t, last = self.p.t, self.last
@@ -680,13 +707,13 @@
 
     def finish(self):
         t, last = self.p.t, self.last
-        for j in range(last):
-
-            @pl.when(t < last - j)
+        for j in range(last - 1):
+
+            @pl.when((t > 0) & (t < last - j))
             def _():
                 self.copy(0, j, self.stage.at[0, j]).wait_send()
 
-            @pl.when(t > j)
+            @pl.when((t < last) & (t > j))
             def _():
                 self.copy(1, j, self.stage.at[1, j]).wait_send()
 
@@ -869,7 +896,7 @@
     )(mats, minor, rows_in, order)
 
 
-CHUNKS = 4
+CHUNKS = 8
 
 
 def line_scratch(n_line, span, width):
@@ -888,31 +915,48 @@
 def sum_rows_and_spread(place, terms, scratch, finish_rows, spread, between):
     stage, inbox, rs, rr, gs, gr, total = scratch
     span = total.shape[0]
-    rows = span * CHUNKS
+    count = stage.shape[0]
+    rows = span * count
     hops = place.n_line - 1
     sums = [
         ReduceLine(place, terms, rows, c * span, span, stage.at[c], inbox.at[c], rs.at[c], rr.at[c])
-        for c in range(CHUNKS)
+        for c in range(count)
     ]
     gathers = []
     if spread is not None:
         gathers = [
             GatherLine(place, spread, rows, c * span, span, gs.at[c], gr.at[c])
-            for c in range(CHUNKS)
+            for c in range(count)
         ]
-    for c in range(CHUNKS + 1):
-        for j in range(hops):
-            if c < CHUNKS:
-                sums[c].step(j)
-            if c > 0 and gathers:
-                gathers[c - 1].step(j)
-        if c < CHUNKS:
-            sums[c].total(total)
-            finish_rows(c, pl.ds(c * span, span), total)
-        if c < len(between):
-            between[c]()
+    sums[0].ends()
+
+    def total_of(c):
+        sums[c].total(total)
+        finish_rows(c, pl.ds(c * span, span), total)
+        if gathers:
+            gathers[c].step(0)
+
+    stages = [lambda c, k=k: sums[c].hop(k) for k in range(hops - 1)] + [total_of]
+    lags = [LAGS[min(k, len(LAGS) - 1)] for k in range(hops)]
+    if gathers:
+        stages += [lambda c, k=k: gathers[c].step(k) for k in range(1, hops)]
+        lags += [lags[-1] + LAG_STEP * k for k in range(1, hops)]
+    for i in range(count + lags[-1]):
+        if i < count:
+            sums[i].sent()
+        if i + 1 < count:
+            sums[i + 1].ends()
+        for work, lag in zip(stages, lags):
+            if 0 <= i - lag < count:
+                work(i - lag)
+        if i in between:
+            between[i]()
     for part in gathers + sums:
         part.finish()
+
+
+LAGS = (0, 1, 1)
+LAG_STEP = 1
 
 
 def middle_gather(n_dp, n_line, terms, tokens, gain, mats):
@@ -932,8 +976,7 @@
             GatherPlane(place, a, b, ps.at[i], pr.at[i], pl_sem.at[i])
             for i, (a, b) in enumerate(zip(srcs, dsts))
         ]
-        for part in planes:
-            part.begin()
+        planes[0].begin()
 
         def norm(c, here, total):
             values = tok[here].astype(jnp.float32) + total[...]
@@ -942,11 +985,11 @@
             first = pl.multiple_of(place.t * rows, 16) + c * total.shape[0]
             hidden[pl.ds(pl.multiple_of(first, 16), total.shape[0])] = low
 
-        sum_rows_and_spread(place, s, scratch, norm, hidden, [])
-        for part in planes:
-            part.forward()
-        for part in planes:
-            part.share()
+        between = {4: planes[1].begin, 5: planes[0].forward}
+        sum_rows_and_spread(place, s, scratch, norm, hidden, between)
+        planes[1].forward()
+        planes[0].share()
+        planes[1].share()
         for part in planes:
             part.finish()
 
@@ -997,7 +1040,7 @@
             first = pl.multiple_of(place.t * rows, 16) + c * total.shape[0]
             spread[pl.ds(pl.multiple_of(first, 16), total.shape[0])] = both.astype(jnp.bfloat16)
 
-        between = [planes[0].cores, planes[1].cores, planes[0].turn]
+        between = {0: planes[0].cores, 3: planes[1].cores, 5: planes[0].turn}
         sum_rows_and_spread(place, s, scratch, norm, spread, between)
         planes[1].turn()
         for part, result in zip(planes, results):
@@ -1043,10 +1086,13 @@
             self.copy(i).start()
         self.mine().start()
 
-    def finish(self):
+    def wait(self):
         self.mine().wait()
         for i in range(1, self.size):
             self.copy(i).wait()
+
+    def finish(self):
+        self.wait()
         total = self.slots[0]
         for i in range(1, self.size):
             total = total + self.slots[i]
@@ -1093,7 +1139,7 @@
             for part in planes:
                 part.turn()
 
-        sum_rows_and_spread(place, s, scratch, norm, None, [cores, turn])
+        sum_rows_and_spread(place, s, scratch, norm, None, {0: cores, 5: turn})
         first = Exchange(place, "dp", own_first, slots_b, xs.at[1], xr.at[1], xl.at[1])
         first.begin()
         small_out[...] = early.finish()
@@ -1131,6 +1177,499 @@
         compiler_params=comm_params(4),
         name="last_sums",
     )(terms, tokens, gain, grad_after, small, *mats)
+
+
+def loop(count, body, unroll=1):
+    def step(i, carry):
+        body(i)
+        return carry
+
+    lax.fori_loop(0, count, step, None, unroll=unroll)
+
+
+def tile_rows(i, size, ahead=0):
+    return pl.ds(pl.multiple_of(i * size + ahead, 8), size)
+
+
+def moved_up(values, distance, count):
+    size = values.shape[0]
+    return pltpu.roll(values, (size - distance) % size, 0)[:count]
+
+
+def take_lanes(ref, here):
+    return jnp.concatenate([ref[c, here] for c in range(ref.shape[0])], axis=1)
+
+
+def put_lanes(ref, here, values):
+    for c in range(ref.shape[0]):
+        ref[c, here] = values[:, c * LANES : (c + 1) * LANES]
+
+
+def gelu_parts(values):
+    inner = GELU_C * (values + 0.044715 * (values * values * values))
+    tanh = jnp.tanh(inner)
+    half = 0.5 * (1.0 + tanh)
+    slope = half + 0.5 * values * (1.0 - tanh * tanh) * GELU_C * (
+        1.0 + 3.0 * 0.044715 * (values * values)
+    )
+    return values * half, slope
+
+
+GELU_C = 0.7978845608028654
+RIM = 128
+LANES = 128
+TILE = 16
+
+
+def one_minus_exp(values, exponential):
+    series = jnp.ones_like(values)
+    for term in range(9, 1, -1):
+        series = 1.0 + values * (1.0 / term) * series
+    return jnp.where(values > -0.35, -values * series, 1.0 - exponential)
+
+
+def rate_and_scale(pre_recur, soft, start):
+    sr = jax.nn.sigmoid(pre_recur)
+    log_rate = -rate_scale * sr * soft
+    decay = jnp.exp(log_rate)
+    rate = jnp.where(start, 0.0, decay)
+    scale = jnp.where(start, 1.0, jnp.sqrt(one_minus_exp(2.0 * log_rate, decay * decay)))
+    return sr, rate, scale
+
+
+class RimSwap:
+    def __init__(self, place, own):
+        self.odd = lax.rem(place.t, 2)
+        self.partner = (place.d, place.t + 1 - 2 * self.odd)
+        self.first = pl.multiple_of(RIM - RIM * self.odd, RIM)
+        self.edge = pl.ds(pl.multiple_of((1 - self.odd) * own + self.odd * RIM, RIM), RIM)
+        self.over_there = pl.ds(pl.multiple_of(self.odd * (own + RIM), RIM), RIM)
+        self.beyond = pl.ds(pl.multiple_of((1 - self.odd) * (own + RIM), RIM), RIM)
+
+    def block(self, index, size):
+        return pl.ds(pl.multiple_of(self.first + index * size, RIM), size)
+
+
+def recur_forward(
+    n_dp, n_line, tok_all, cot, to_place, to_stored, mats, out_full, gain, gates, taps, soft, flags
+):
+    rows, width = tok_all.shape
+    count, own = taps.shape
+    size = gates.shape[0]
+    wide = own + 2 * RIM
+    blocks = (wide - RIM) // size
+    chunk = rows // 8
+    cot_rows = cot.shape[0]
+    parts = 2
+
+    def kernel(*refs):
+        (tok, cot_ref, plc, sto, w, wo, gain_ref, gw, cw, sp, fl) = refs[:11]
+        (hp, xext, y, conv_low, conv, pre_r, pre_i, rate, state, merged_st, terms, cot_all) = refs[
+            11:23
+        ]
+        (h, xf, local, cum, merged, agg, slots, hs, hr, es, er, el, gs, gr, gl) = refs[23:]
+        place = Place(n_dp, n_line)
+        place.meet(True)
+        swap = RimSwap(place, own)
+        own_cot = cot_all.at[pl.ds(pl.multiple_of(place.t * cot_rows, 16), cot_rows)]
+        keep = pltpu.make_async_copy(cot_ref, own_cot, gl)
+        keep.start()
+        span = cot_rows // parts
+        lines = [
+            GatherLine(place, cot_all, cot_rows, c * span, span, gs.at[c], gr.at[c])
+            for c in range(parts)
+        ]
+        for c, line in enumerate(lines):
+            line.step(0, cot_ref.at[pl.ds(c * span, span)])
+
+        def norm(i):
+            here = tile_rows(i, TILE)
+            h[here] = rms_scale(tok[here].astype(jnp.float32), gain_ref[...]).astype(jnp.bfloat16)
+
+        loop(rows // TILE, norm)
+
+        def project(i):
+            here = tile_rows(i, 128)
+            hp[here] = plain_dot(plc[here], h[...]).astype(jnp.bfloat16)
+            xext[tile_rows(i, 128, 16)] = plain_dot(hp[here], w[:, :own]).astype(jnp.bfloat16)
+
+        loop(rows // 128, project)
+        edge = remote(
+            xext.at[pl.ds(rows, 16)],
+            xext.at[pl.ds(0, 16)],
+            hs.at[0],
+            hr.at[0],
+            (lax.rem(place.d + 1, n_dp), place.t),
+        )
+        edge.start()
+
+        def project_y(i):
+            here = tile_rows(i, 128)
+            y[here] = plain_dot(hp[here], w[:, own : 2 * own])
+
+        loop(rows // 128, project_y)
+        for line in lines:
+            line.step(1)
+        edge.wait()
+        top = xext[pl.ds(0, 16)]
+        xext[pl.ds(0, 16)] = jnp.where(place.d > 0, top, jnp.zeros_like(top))
+
+        def widen(i):
+            xf[tile_rows(i, TILE)] = xext[tile_rows(i, TILE)].astype(jnp.float32)
+
+        loop(rows // TILE + 1, widen)
+
+        def convolve(i):
+            here = tile_rows(i, TILE)
+            near = xf[pl.ds(pl.multiple_of(i * TILE + 8, 8), TILE + 8)]
+            same = fl[tile_rows(i, TILE, 8)]
+            total = cw[0:1] * near[8:]
+            for k in range(1, count):
+                total += cw[k : k + 1] * moved_up(near, 8 - k, TILE) * same[:, k : k + 1]
+            conv[here] = total
+            conv_low[here, RIM : RIM + own] = total.astype(jnp.bfloat16)
+
+        loop(rows // TILE, convolve)
+        rim = remote(
+            conv_low.at[:, swap.edge],
+            conv_low.at[:, swap.over_there],
+            hs.at[1],
+            hr.at[1],
+            swap.partner,
+        )
+        rim.start()
+        for i in range(blocks):
+            index = lax.rem(i + swap.odd, blocks)
+            cols = swap.block(index, size)
+            other = pl.ds(pl.multiple_of(wide + swap.first + index * size, RIM), size)
+            if i == blocks - 1:
+                rim.wait()
+            pre_r[:, cols] = plain_dot(conv_low[:, cols], gw[:, cols])
+            pre_i[:, cols] = plain_dot(conv_low[:, cols], gw[:, other])
+
+        def drive(i):
+            here = tile_rows(i, TILE)
+            start = fl[tile_rows(i, TILE, 8)][:, 0:1] > 0.0
+            own_cols = pl.ds(RIM, own)
+            _, decay, scale = rate_and_scale(pre_r[here, own_cols], sp[...], start)
+            put_lanes(rate, here, decay)
+            put_lanes(local, here, conv[here] * jax.nn.sigmoid(pre_i[here, own_cols]) * scale)
+
+        loop(rows // TILE, drive)
+        groups = own // LANES
+
+        def scan(i, carry):
+            here = pl.ds(i, 8, chunk)
+            result = []
+            for c in range(groups):
+                product, total = carry[c]
+                r = rate[c, here]
+                product = product * r
+                total = total * r + local[c, here]
+                cum[c, here] = product
+                local[c, here] = total
+                result.append((product, total))
+            return tuple(result)
+
+        blank = (jnp.ones((8, LANES), jnp.float32), jnp.zeros((8, LANES), jnp.float32))
+        lax.fori_loop(0, chunk, scan, (blank,) * groups)
+        product, total = jnp.ones((1, own), jnp.float32), jnp.zeros((1, own), jnp.float32)
+        for j in range(8):
+            last = pl.ds(j * chunk + chunk - 1, 1)
+            total = take_lanes(local, last) + take_lanes(cum, last) * total
+            product = product * take_lanes(cum, last)
+        agg[0:1] = product
+        agg[1:2] = total
+        swap_all = Exchange(place, "dp", agg, slots, es, er, el)
+        swap_all.begin()
+        swap_all.wait()
+        entry = jnp.zeros((1, own), jnp.float32)
+        for q in range(n_dp):
+            longer = slots[q, 1:2] + slots[q, 0:1] * entry
+            entry = jnp.where(q < place.d, longer, entry)
+        state[pl.ds(0, 8)] = jnp.broadcast_to(entry, (8, own))
+        for j in range(8):
+
+            def settle(i, entry=entry):
+                here = tile_rows(i, TILE, j * chunk)
+                values = take_lanes(local, here) + take_lanes(cum, here) * entry
+                state[tile_rows(i, TILE, j * chunk + 8)] = values
+                merged[here] = (values * gelu_parts(y[here])[0]).astype(jnp.bfloat16)
+
+            loop(chunk // TILE, settle)
+            last = pl.ds(j * chunk + chunk - 1, 1)
+            entry = take_lanes(local, last) + take_lanes(cum, last) * entry
+        for line in lines:
+            line.step(2)
+        merged_st[...] = plain_dot(sto[...], merged[...]).astype(jnp.bfloat16)
+
+        def mix(i):
+            some = tile_rows(i, 512)
+            terms[:, pl.ds(pl.multiple_of(i * 512, 512), 512)] = times_trans(
+                merged_st[...], wo[some, :]
+            ).astype(jnp.bfloat16)
+
+        loop(width // 512, mix)
+        for line in lines:
+            line.finish()
+        keep.wait()
+
+    low, full = jnp.bfloat16, jnp.float32
+    return pl.pallas_call(
+        kernel,
+        out_shape=(
+            shaped((rows, width), low),
+            shaped((rows + 16, own), low),
+            shaped((rows, own), full),
+            shaped((rows, wide), low),
+            shaped((rows, own), full),
+            shaped((rows, wide), full),
+            shaped((rows, wide), full),
+            shaped((own // LANES, rows, LANES), full),
+            shaped((rows + 8, own), full),
+            shaped((rows, own), low),
+            shaped((rows, width), low),
+            shaped((n_line * cot_rows, width), low),
+        ),
+        in_specs=[in_vmem(), in_any()] + [in_vmem()] * 9,
+        out_specs=[in_vmem()] * 11 + [in_any()],
+        scratch_shapes=[
+            pltpu.VMEM((rows, width), low),
+            pltpu.VMEM((rows + 16, own), full),
+            pltpu.VMEM((own // LANES, rows, LANES), full),
+            pltpu.VMEM((own // LANES, rows, LANES), full),
+            pltpu.VMEM((rows, own), low),
+            pltpu.VMEM((2, own), full),
+            pltpu.VMEM((n_dp, 2, own), full),
+            dma_sems(2),
+            dma_sems(2),
+            dma_sems(n_dp),
+            dma_sems(n_dp),
+            pltpu.SemaphoreType.DMA,
+            dma_sems(parts, 2, n_line - 1),
+            dma_sems(parts, 2, n_line - 1),
+            pltpu.SemaphoreType.DMA,
+        ],
+        compiler_params=comm_params(5),
+        name="recur_forward",
+    )(tok_all, cot, to_place, to_stored, mats, out_full, gain, gates, taps, soft, flags)
+
+
+def recur_backward(
+    n_dp, n_line, mixer_in, to_place, out_full, gates, taps, soft, slope, flags, kept
+):
+    rows, width = mixer_in.shape
+    count, own = taps.shape
+    size = gates.shape[0]
+    wide = own + 2 * RIM
+    blocks = (wide - RIM) // size
+    chunk = rows // 8
+
+    def kernel(*refs):
+        (mix, plc, wo, gw, cw, sp, sg, fl) = refs[:8]
+        (xext, y, conv_low, conv, pre_r, pre_i, rate, state) = refs[8:16]
+        (gxy, gate_grads, tap_grads, decay_grad) = refs[16:20]
+        (mp, gm, lam, reach, gp_r, gp_i, grad, spread, rim_out, rim_in, ret_out, ret_in) = refs[
+            20:32
+        ]
+        (tap_sums, decay_sums, ends, agg, slots, hs, hr, es, er, el) = refs[32:]
+        place = Place(n_dp, n_line)
+        place.meet(True)
+        swap = RimSwap(place, own)
+        own_cols = pl.ds(RIM, own)
+
+        def project(i):
+            here = tile_rows(i, 128)
+            mp[here] = plain_dot(plc[here], mix[...]).astype(jnp.bfloat16)
+            gm[here] = plain_dot(mp[here], wo[...])
+
+        loop(rows // 128, project)
+
+        def split(i):
+            here = tile_rows(i, TILE)
+            branch, slope_y = gelu_parts(y[here])
+            grads = gm[here]
+            put_lanes(lam, here, grads * branch)
+            values = state[tile_rows(i, TILE, 8)]
+            gxy[here, own:] = (grads * values * slope_y).astype(jnp.bfloat16)
+
+        loop(rows // TILE, split)
+        groups = own // LANES
+
+        def scan(i, carry):
+            here = pl.ds(chunk - 1 - i, 8, chunk)
+            result = []
+            for c in range(groups):
+                product, message = carry[c]
+                r = rate[c, here]
+                value = lam[c, here] + message
+                lam[c, here] = value
+                reach[c, here] = product
+                result.append((product * r, value * r))
+            return tuple(result)
+
+        blank = (jnp.ones((8, LANES), jnp.float32), jnp.zeros((8, LANES), jnp.float32))
+        done = lax.fori_loop(0, chunk, scan, (blank,) * groups)
+        for c in range(groups):
+            lanes = pl.ds(c * LANES, LANES)
+            ends[0, :, lanes] = done[c][0]
+            ends[1, :, lanes] = done[c][1]
+        product, message = jnp.ones((1, own), jnp.float32), jnp.zeros((1, own), jnp.float32)
+        for j in reversed(range(8)):
+            message = ends[1, j : j + 1] + ends[0, j : j + 1] * message
+            product = product * ends[0, j : j + 1]
+        agg[0:1] = product
+        agg[1:2] = message
+        swap_all = Exchange(place, "dp", agg, slots, es, er, el)
+        swap_all.begin()
+        swap_all.wait()
+        entry = jnp.zeros((1, own), jnp.float32)
+        for q in reversed(range(n_dp)):
+            longer = slots[q, 1:2] + slots[q, 0:1] * entry
+            entry = jnp.where(q > place.d, longer, entry)
+        for ref in (tap_sums, decay_sums):
+            ref[...] = jnp.zeros_like(ref)
+        for ref in (gp_r, gp_i):
+            ref[:, 0:RIM] = jnp.zeros((rows, RIM), jnp.bfloat16)
+            ref[:, RIM + own :] = jnp.zeros((rows, RIM), jnp.bfloat16)
+        grad[pl.ds(0, 8)] = jnp.zeros((8, own), jnp.float32)
+        grad[pl.ds(rows + 8, 8)] = jnp.zeros((8, own), jnp.float32)
+        for j in reversed(range(8)):
+
+            def back(i, entry=entry):
+                here = tile_rows(i, TILE, j * chunk)
+                flag = fl[tile_rows(i, TILE, j * chunk + 8)]
+                start = flag[:, 0:1] > 0.0
+                values = take_lanes(lam, here) + take_lanes(reach, here) * entry
+                before = moved_up(
+                    state[pl.ds(pl.multiple_of(j * chunk + i * TILE, 8), TILE + 8)], 7, TILE
+                )
+                sr, decay, scale = rate_and_scale(pre_r[here, own_cols], sp[...], start)
+                si = jax.nn.sigmoid(pre_i[here, own_cols])
+                block = conv[here]
+                driven = values * si
+                log_grad = values * before * decay - block * driven * (decay * decay) / scale
+                log_grad = jnp.where(start, 0.0, log_grad)
+                inner = sr * log_grad
+                gp_r[here, own_cols] = (
+                    -rate_scale * sp[...] * inner * (1.0 - sr)
+                ).astype(jnp.bfloat16)
+                gp_i[here, own_cols] = (driven * block * (1.0 - si) * scale).astype(jnp.bfloat16)
+                grad[tile_rows(i, TILE, j * chunk + 8)] = driven * scale
+                decay_sums[...] += inner[:8] + inner[8:]
+
+            loop(chunk // TILE, back)
+            entry = ends[1, j : j + 1] + ends[0, j : j + 1] * entry
+        decay_grad[...] = rate_scale * sg[...] * jnp.sum(decay_sums[...], axis=0, keepdims=True)
+
+        for i in range(blocks):
+            index = lax.rem(i + 2 - 2 * swap.odd, blocks)
+            cols = swap.block(index, size)
+            other = pl.ds(pl.multiple_of(wide + swap.first + index * size, RIM), size)
+            spread[:, cols] = times_trans(gp_r[:, cols], gw[:, cols]) + times_trans(
+                gp_i[:, cols], gw[:, other]
+            )
+            if i == 0:
+                rim_out[...] = spread[:, swap.beyond].astype(jnp.bfloat16)
+                rim = remote(rim_out, rim_in, hs.at[0], hr.at[0], swap.partner)
+                rim.start()
+        rim.wait()
+        shared = pl.ds(pl.multiple_of((1 - swap.odd) * (own - RIM), RIM), RIM)
+
+        def join(i):
+            here = tile_rows(i, TILE)
+            there = tile_rows(i, TILE, 8)
+            grad[there] += spread[here, own_cols]
+            grad[there, shared] += rim_in[here].astype(jnp.float32)
+
+        loop(rows // TILE, join)
+
+        near = grad[pl.ds(0, 16)]
+        back_rows = jnp.zeros((8, own), jnp.float32)
+        for k in range(1, count):
+            masked = near * fl[pl.ds(0, 16)][:, k : k + 1]
+            back_rows += cw[k : k + 1] * moved_up(masked, k, 8)
+        ret_out[...] = back_rows
+        ret = remote(
+            ret_out,
+            ret_in,
+            hs.at[1],
+            hr.at[1],
+            (lax.rem(place.d + n_dp - 1, n_dp), place.t),
+        )
+        ret.start()
+        for i in range(blocks):
+            cols = swap.block(i, size)
+            spread[0:size, cols] = trans_times(conv_low[:, cols], gp_r[:, cols])
+            spread[size : 2 * size, cols] = trans_times(conv_low[:, cols], gp_i[:, cols])
+        gate_grads[:, 0:own] = spread[0:size, own_cols].astype(jnp.bfloat16)
+        gate_grads[:, own:] = spread[size : 2 * size, own_cols].astype(jnp.bfloat16)
+
+        def taps_back(i, added=None):
+            here = tile_rows(i, TILE)
+            start = pl.ds(pl.multiple_of(i * TILE + 8, 8), TILE + 8)
+            after = grad[start]
+            flag = fl[start]
+            behind = xext[pl.ds(pl.multiple_of(i * TILE, 16), 2 * TILE)].astype(jnp.float32)
+            total = cw[0:1] * after[:TILE]
+            for k in range(count):
+                if k > 0:
+                    masked = after * flag[:, k : k + 1]
+                    total += cw[k : k + 1] * moved_up(masked, k, TILE)
+                    mine = masked[:TILE]
+                else:
+                    mine = after[:TILE]
+                term = mine * moved_up(behind, 16 - k, TILE)
+                tap_sums[k] += term[:8] + term[8:]
+            if added is not None:
+                total = total + jnp.concatenate([jnp.zeros((8, own), jnp.float32), added], axis=0)
+            gxy[here, 0:own] = total.astype(jnp.bfloat16)
+
+        loop(rows // TILE - 1, taps_back)
+        ret.wait()
+        taps_back(rows // TILE - 1, jnp.where(place.d < n_dp - 1, ret_in[...], 0.0))
+        tap_grads[...] = jnp.zeros_like(tap_grads)
+        for k in range(count):
+            tap_grads[k : k + 1] = jnp.sum(tap_sums[k], axis=0, keepdims=True)
+
+    low, full = jnp.bfloat16, jnp.float32
+    return pl.pallas_call(
+        kernel,
+        out_shape=(
+            shaped((rows, 2 * own), low),
+            shaped((size, 2 * own), low),
+            shaped((8, own), full),
+            shaped((1, own), full),
+        ),
+        in_specs=[in_vmem()] * 16,
+        out_specs=[in_vmem()] * 4,
+        scratch_shapes=[
+            pltpu.VMEM((rows, width), low),
+            pltpu.VMEM((rows, own), full),
+            pltpu.VMEM((own // LANES, rows, LANES), full),
+            pltpu.VMEM((own // LANES, rows, LANES), full),
+            pltpu.VMEM((rows, wide), low),
+            pltpu.VMEM((rows, wide), low),
+            pltpu.VMEM((rows + 16, own), full),
+            pltpu.VMEM((rows, wide), full),
+            pltpu.VMEM((rows, RIM), low),
+            pltpu.VMEM((rows, RIM), low),
+            pltpu.VMEM((8, own), full),
+            pltpu.VMEM((8, own), full),
+            pltpu.VMEM((count, 8, own), full),
+            pltpu.VMEM((8, own), full),
+            pltpu.VMEM((2, 8, own), full),
+            pltpu.VMEM((2, own), full),
+            pltpu.VMEM((n_dp, 2, own), full),
+            dma_sems(2),
+            dma_sems(2),
+            dma_sems(n_dp),
+            dma_sems(n_dp),
+            pltpu.SemaphoreType.DMA,
+        ],
+        compiler_params=comm_params(6),
+        name="recur_backward",
+    )(mixer_in, to_place, out_full, gates, taps, soft, slope, flags, *kept)
 
 
 def matches(mesh):
@@ -1167,19 +1706,19 @@
     gate_rows = recur_gate_weight.shape[0]
     own_start = tensor_index * tok_rows
 
-    mats = jnp.concatenate([x_weight, y_weight, out_weight.T], axis=1)
+    mats = jnp.concatenate([x_weight, y_weight], axis=1)
+    out_full = lax.all_gather(out_weight.T, "dp", axis=0, tiled=True)
     gains = jnp.concatenate([norm_gain, mlp_gain])
     spare = gate_rows * 128 - gains.shape[0]
     gains = jnp.pad(gains, (0, spare)).reshape(gate_rows, 128)
     minor = jnp.concatenate([recur_gate_weight, input_gate_weight, gains], axis=1)
     own_order = (token_order - dp_index * row_count).astype(jnp.int32)
     order_rows = jnp.broadcast_to(own_order[None, :], (8, tok_rows))
-    mats_full, minor_full, tok_all, order_full = first_gather(
+    xy_full, minor_full, tok_all, order_full = first_gather(
         n_dp, n_tensor, mats, minor, tokens, order_rows
     )
-    down_full = lax.all_gather(down_weight.T, "dp", axis=0, tiled=True)
-    cot_all = lax.all_gather(
-        lax.optimization_barrier((cotangent, order_full))[0], "tensor", axis=0, tiled=True
+    down_full = lax.all_gather(
+        lax.optimization_barrier((down_weight.T, out_full))[0], "dp", axis=0, tiled=True
     )
     order_all = order_full.reshape(n_tensor, 8, tok_rows)[:, 0].reshape(row_count)
     both_gates = minor_full[:, : 2 * own_width]
@@ -1187,88 +1726,54 @@
     first_gain = gain_rows[:, :dp_width].reshape(1, width).astype(jnp.float32)
     second_gain = gain_rows[:, dp_width : 2 * dp_width].reshape(1, width).astype(jnp.float32)
     block_size = both_gates.shape[0]
-    x_full, y_full, out_full = (
-        mats_full[:, :own_width],
-        mats_full[:, own_width : 2 * own_width],
-        mats_full[:, 2 * own_width :],
-    )
-
-    first_all = rms_scale(tok_all.astype(jnp.float32), first_gain).astype(jnp.bfloat16)
     row_index = jnp.arange(row_count, dtype=jnp.int32)
-    to_place = (row_index[:, None] == order_all[None, :]).astype(jnp.bfloat16)
-
-    def placed(stored):
-        return plain_dot(to_place, stored).astype(jnp.bfloat16)
-
-    def stored(rows):
-        return trans_times(to_place, rows).astype(jnp.bfloat16)
-
-    hidden_place = placed(first_all)
-    places = dp_index * row_count + row_index
+    hits = row_index[:, None] == order_all[None, :]
+    to_place = hits.astype(jnp.bfloat16)
+    to_stored = (order_all[:, None] == row_index[None, :]).astype(jnp.bfloat16)
+    places = dp_index * row_count + jnp.arange(-8, row_count + 8, dtype=jnp.int32)
+    inside = (jnp.arange(row_count + 16) >= 8) & (jnp.arange(row_count + 16) < row_count + 8)
     ends = jnp.cumsum(seq_lengths)
     segment = segment_of(places, ends)
     starts = (places == 0) | (segment != segment_of(places - 1, ends))
+    columns = [starts] + [
+        segment_of(places - shift, ends) == segment for shift in range(1, kernel_taps)
+    ]
+    columns += [jnp.zeros_like(starts)] * (8 - len(columns))
+    flags = (jnp.stack(columns, axis=1) & inside[:, None]).astype(jnp.float32)
     live_stored = (order_all + dp_index * row_count < ends[-1]).astype(jnp.float32)
     live_own = (token_order < ends[-1]).astype(jnp.float32)
-    same = [
-        (segment_of(places - shift, ends) == segment).astype(jnp.float32)
-        for shift in range(kernel_taps)
-    ]
-    low_edge = tensor_index * own_width
-    own_blocks = (low_edge + jnp.arange(own_width, dtype=jnp.int32)) // block_size
-    first_block = low_edge // block_size
-    block_count = own_width // block_size + 2
-
-    def block_start(index):
-        return (first_block + index) * block_size - low_edge + block_size
-
-    def block_mask(index):
-        inside = own_blocks == first_block + index
-        return jnp.concatenate([inside, inside])
-
-    def convolve(extended, kernel):
-        return sum(
-            (
-                kernel[shift][None, :]
-                * extended[edge_rows - shift : edge_rows - shift + row_count]
-                * same[shift][:, None]
-                for shift in range(kernel_taps)
-            )
-        )
-
-    def gates(conv_vals, pre_recur, pre_input, decay_vals):
-        log_rate = -rate_scale * jax.nn.sigmoid(pre_recur) * jax.nn.softplus(-decay_vals)
-        decay_rate = jnp.where(starts[:, None], 0.0, jnp.exp(log_rate))
-        scale_in = jnp.where(starts[:, None], 1.0, jnp.sqrt(-jnp.expm1(2.0 * log_rate)))
-        return (decay_rate, conv_vals * jax.nn.sigmoid(pre_input) * scale_in)
-
+    soft = jax.nn.softplus(-decay_param).reshape(1, own_width)
+    slope = jax.nn.sigmoid(-decay_param).reshape(1, own_width)
+    zero_rim = jnp.zeros((block_size, RIM), jnp.bfloat16)
+    gates_wide = jnp.concatenate(
+        [
+            zero_rim,
+            both_gates[:, :own_width],
+            zero_rim,
+            zero_rim,
+            both_gates[:, own_width:],
+            zero_rim,
+        ],
+        axis=1,
+    )
     def glu(gate_pre, up_pre):
         return gelu_tanh(gate_pre) * up_pre
 
-    x_branch = plain_dot(hidden_place, x_full).astype(jnp.bfloat16)
-    y_before = plain_dot(hidden_place, y_full)
-    previous = from_behind(x_branch[row_count - edge_rows :], "dp", 1)
-    extended = jnp.concatenate([previous, x_branch], axis=0).astype(jnp.float32)
-    conv_out = convolve(extended, conv_weight)
-    conv_wide = extended_2(conv_out.astype(jnp.bfloat16), (("tensor", 1),), block_size)
-    pre_both = jnp.zeros((row_count, 2 * own_width), jnp.float32)
-    for index in range(block_count):
-        piece = lax.dynamic_slice_in_dim(conv_wide, block_start(index), block_size, 1)
-        pre_both = pre_both + jnp.where(
-            block_mask(index)[None, :], plain_dot(piece, both_gates), 0.0
-        )
-    (decay_rate, driven), gate_pull = jax.vjp(
-        gates, conv_out, pre_both[:, :own_width], pre_both[:, own_width:], decay_param
-    )
-    cum_rate, local_state = lax.associative_scan(pair_step, (decay_rate, driven), axis=0)
-    ident = (jnp.ones((own_width,), jnp.float32), jnp.zeros((own_width,), jnp.float32))
-    rate_in, state_in = entering((cum_rate[-1], local_state[-1]), "dp", pair_step, ident, False)
-    state = local_state + cum_rate * state_in[None, :]
-    y_branch = gelu_tanh(y_before)
-    merged = (state * y_branch).astype(jnp.bfloat16)
-    merged_stored = stored(merged)
-
-    mixer_terms = times_trans(merged_stored, out_full).astype(jnp.bfloat16)
+    hidden_place, *kept, merged_stored, mixer_terms, cot_all = recur_forward(
+        n_dp,
+        n_tensor,
+        tok_all,
+        cotangent,
+        to_place,
+        to_stored,
+        xy_full,
+        out_full,
+        first_gain,
+        gates_wide,
+        conv_weight,
+        soft,
+        flags,
+    )
     after_own, hidden_two, gate_full, up_full = middle_gather(
         n_dp, n_tensor, mixer_terms, tokens, second_gain, (gate_weight, up_weight)
     )
@@ -1303,62 +1808,27 @@
 
     grad_out_mat = trans_times(mixer_in, merged_stored).astype(jnp.bfloat16)
     out_sum = lax.psum_scatter(grad_out_mat, "dp", scatter_dimension=0, tiled=True)
-    grad_merged = plain_dot(placed(mixer_in), out_full)
-    grad_state = grad_merged * y_branch
-    gelu_pull = jax.vjp(gelu_tanh, y_before)[1]
-    grad_y_before = gelu_pull(grad_merged * state)[0].astype(jnp.bfloat16)
-    rate_next = jnp.concatenate([decay_rate[1:], jnp.ones((1, own_width), jnp.float32)], axis=0)
-    rev_rate, local_lam = lax.associative_scan(
-        pair_step, (rate_next, grad_state), reverse=True, axis=0
-    )
-    head_rate = decay_rate[0] * rev_rate[0]
-    head_lam = decay_rate[0] * local_lam[0]
-    factor_in, lam_in = entering((head_rate, head_lam), "dp", pair_step, ident, True)
-    lam = local_lam + rev_rate * lam_in[None, :]
-    state_prev = jnp.concatenate([state_in[None, :], state[:-1]], axis=0)
-    grad_conv_local, grad_pre_recur, grad_pre_input, grad_decay_own = gate_pull(
-        (lam * state_prev, lam)
-    )
-    grad_pre = jnp.concatenate([grad_pre_recur, grad_pre_input], axis=1).astype(jnp.bfloat16)
-    grad_both = jnp.zeros((block_size, 2 * own_width), jnp.float32)
-    grad_wide = jnp.zeros((row_count, own_width + 2 * block_size), jnp.float32)
-    for index in range(block_count):
-        begin = block_start(index)
-        piece = lax.dynamic_slice_in_dim(conv_wide, begin, block_size, 1)
-        masked = jnp.where(block_mask(index)[None, :], grad_pre, jnp.zeros((), jnp.bfloat16))
-        grad_both = grad_both + trans_times(piece, masked)
-        added = lax.dynamic_slice_in_dim(grad_wide, begin, block_size, 1) + times_trans(
-            masked, both_gates
-        )
-        grad_wide = lax.dynamic_update_slice_in_dim(grad_wide, added, begin, 1)
-    rims = jnp.concatenate(
-        [grad_wide[:, :block_size], grad_wide[:, own_width + block_size :]], axis=1
-    )
-    arrived = extended_2(rims.astype(jnp.bfloat16), (("tensor", 1),), block_size).astype(rims.dtype)
-    from_lower = jnp.pad(arrived[:, :block_size], ((0, 0), (0, own_width - block_size)))
-    from_upper = jnp.pad(arrived[:, 3 * block_size :], ((0, 0), (own_width - block_size, 0)))
-    grad_conv = (
-        grad_conv_local
-        + grad_wide[:, block_size : block_size + own_width]
-        + from_lower
-        + from_upper
-    )
-    conv_pull = jax.vjp(convolve, extended, conv_weight)[1]
-    grad_extended, grad_kernel = conv_pull(grad_conv)
-    returned = from_behind(grad_extended[:edge_rows], "dp", -1)
-    grad_x_branch = grad_extended[edge_rows:] + jnp.concatenate(
-        [jnp.zeros((row_count - edge_rows, own_width), jnp.float32), returned], axis=0
-    )
-    grad_xy = stored(
-        jnp.concatenate([grad_x_branch.astype(jnp.bfloat16), grad_y_before], axis=1)
-    )
-    grad_xy_mat = trans_times(first_all, grad_xy).astype(jnp.bfloat16)
-    one_terms = times_trans(grad_xy, mats_full[:, : 2 * own_width]).astype(jnp.bfloat16)
+    grad_xy, gate_grads, tap_grads, decay_grad = recur_backward(
+        n_dp,
+        n_tensor,
+        mixer_in,
+        to_place,
+        out_full,
+        gates_wide,
+        conv_weight,
+        soft,
+        slope,
+        flags,
+        kept,
+    )
+    grad_xy_mat = trans_times(hidden_place, grad_xy).astype(jnp.bfloat16)
+    grad_xy_stored = plain_dot(to_stored, grad_xy).astype(jnp.bfloat16)
+    one_terms = times_trans(grad_xy_stored, xy_full).astype(jnp.bfloat16)
     small = jnp.concatenate(
         [
             second_part,
-            grad_kernel.reshape(1, -1),
-            jnp.pad(grad_decay_own, (0, width - own_width)).reshape(1, width),
+            tap_grads[:kernel_taps].reshape(1, -1),
+            jnp.pad(decay_grad, ((0, 0), (0, width - own_width))),
             jnp.zeros((1, width), jnp.float32),
         ],
         axis=0,
@@ -1371,7 +1841,7 @@
         first_gain,
         grad_after_own,
         small,
-        (grad_xy_mat, grad_both.astype(jnp.bfloat16)),
+        (grad_xy_mat, gate_grads),
     )
     xy_sum, gates_sum = xy_sum.astype(jnp.float32), gates_sum.astype(jnp.float32)
     own_gains = lax.dynamic_slice_in_dim(gain_sums, dp_index * dp_width, dp_width, 1)

time: 1000 us -> 659 us (0.66)
  local copies, waits for them, and re-layouts: 246 us -> 22.2 us
  other arithmetic: 86 us -> 21.3 us
  blocking collectives: 35.4 us -> 0 us
  matrix products: 138 us -> 104 us
  waiting for transfers between devices: 32.7 us -> 57.4 us
  Pallas kernels: 417 us -> 432 us
  starting transfers between devices: 15.5 us -> 0.6 us
    slice x130 -> x0, local copies, waits for them, and re-layouts: 172 us -> none  [the longest x65 87.2 us: local_blocks(): lax.associative_scan(pair_step, (rate_next, grad_state), reverse=True, ax...]
    pallas_call x0 -> x2, Pallas kernels: none -> 111 us  [the longest x1 74.3 us: recur_forward(): pl.pallas_call(kernel, out_shape=(shaped((rows, width), low), shaped((row...]
    pallas_call x1, Pallas kernels: 134 us -> 95 us  [middle_gather(): pl.pallas_call(kernel, out_shape=(shaped((rows, width), jnp.float32), sha...]
    all_gather x2, waiting for transfers between devices: 0.01 us -> 37.5 us  [the longest x1 37.5 us: local_blocks(): out_full = lax.all_gather(out_weight.T, 'dp', axis=0, tiled=True)]
    all_gather x4 -> x0, blocking collectives: 35.4 us -> none  [entering(): pieces = jax.tree.map(lambda part: lax.all_gather(part, axis), value)]
    pallas_call x1, Pallas kernels: 125 us -> 94.5 us  [middle_sums(): pl.pallas_call(kernel, out_shape=(shaped((rows, width), jnp.float32), sha...]
    add x52 -> x1, other arithmetic: 28.8 us -> 0.01 us  [local_blocks(): dp_index * row_count + jnp.arange(-8, row_count + 8, dtype=jnp.int32)]
    dot_general x11 -> x3, matrix products: 57.3 us -> 33.4 us  [plain_dot(): return jnp.dot(left, right, preferred_element_type=jnp.float32)]
  transfers between devices with their start and end apart: 11 -> 5, of which waited for: 3 -> 2; matrix products, arithmetic and copies ran while one was open for 42% -> 17% of each run, Pallas kernels for 23% -> 52%
where the time goes in v2:
time: 659 us; the launch traced here: 652 us
  Pallas kernels  432 us (66%)
  matrix products  104 us (16%)
  waiting for transfers between devices  57.4 us (9%)
  local copies, waits for them, and re-layouts  22.2 us (3%)
  other arithmetic  21.3 us (3%)
  between operations  14.4 us (2%)
    pallas_call x1, Pallas kernels, middle_gather(): pl.pallas_call(kernel, out_shape=(shaped((rows, width), jnp.float32), sha...  95 us
    pallas_call x1, Pallas kernels, middle_sums(): pl.pallas_call(kernel, out_shape=(shaped((rows, width), jnp.float32), sha...  94.5 us
    pallas_call x1, Pallas kernels, recur_forward(): pl.pallas_call(kernel, out_shape=(shaped((rows, width), low), shaped((row...  74.3 us
    pallas_call x1, Pallas kernels, last_sums(): pl.pallas_call(kernel, out_shape=(shaped((rows, width), jnp.float32), sha...  73.9 us
    pallas_call x1, Pallas kernels, first_gather(): pl.pallas_call(kernel, out_shape=(shaped((n_dp * mats.shape[0], mats.shap...  57.5 us
    dot_general x5, matrix products, trans_times(): lax.dot_general(left, right, (((0,), (0,)), ((), ())), preferred_element_...  37.8 us
    all_gather x1, waiting for transfers between devices, local_blocks(): out_full = lax.all_gather(out_weight.T, 'dp', axis=0, tiled=True)  37.5 us
    pallas_call x1, Pallas kernels, recur_backward(): pl.pallas_call(kernel, out_shape=(shaped((rows, 2 * own), low), shaped((s...  37 us
  transfers between devices with their start and end apart: 5, of which 2 were waited for; matrix products, arithmetic and copies ran while one was open for 17% of the time, Pallas kernels for 52%

profile of v2, /device:TPU:0, one launch (start us, length us, event | category | flops | bytes accessed | tf_op | source)
XLA Modules:
  0.0 651.8 jit_solution(731343627889641248)
XLA Ops:
  8.0 37.5 %all-gather.3.cloned.1.call-done.refs_5_.refs_2_ = bf16[2560,640]{1,0:T(8,128)(2,1)} async-done(((bf16[320,640]{1,0:T(8,128)(2,1)}), bf16[2560,640]{1,0:T(8,128)(2,1)}) %all-gather.3.cloned.1.call-update) | async-done | bytes 3276816 | tf_op jit(solution)/shard_map/all_gather | solution.py:1710
  50.1 1.5 pad_maximum_fusion.1.b
  51.6 2.1 pad_maximum_fusion.a
  54.3 57.5 %first_gather.1 = (bf16[2560,1280]{1,0:T(8,128)(2,1)}, bf16[256,1408]{1,0:T(8,128)(2,1)}, bf16[512,2560]{1,0:T(8,128)(2,1)}, s32[32,128]{1,0:T(8,128)}) custom-call(bf16[320,1280]{1,0:T(8,128)(2,1)} %pad_maximum_fusion.a, bf16[32,1408]{1,0:T(8,128)(2,1)} %pad_maximum_fusion.1.b, bf16[128,2560]{1,0:T(8,128)(2,1)} %refs_1_.5, s32[8,128]{1,0:T(8,128)} %broadcast_in_dim.6.e), custom_call_target="tpu_custom_call" | custom-call | tf_op jit(solution)/shard_map/first_gather/pallas_call | solution.py:876
  120.3 74.3 %recur_forward.1 = (bf16[512,2560]{1,0:T(8,128)(2,1)}, bf16[528,640]{1,0:T(8,128)(2,1)}, f32[512,640]{1,0:T(8,128)}, bf16[512,896]{1,0:T(8,128)(2,1)}, f32[512,6...) custom-call(bf16[512,2560]{1,0:T(8,128)(2,1)} %get-tuple-element.49., ...), custom_call_target="tpu_custom_call" | custom-call | tf_op jit(solution)/shard_map/recur_forward/pallas_call | solution.py:1418
  194.6 95.0 %middle_gather.1 = (f32[128,2560]{1,0:T(8,128)}, bf16[512,2560]{1,0:T(8,128)(2,1)}, bf16[2560,1920]{1,0:T(8,128)(2,1)}, bf16[2560,1920]{1,0:T(8,128)(2,1)}) custom-call(bf16[512,2560]{1,0:T(8,128)(2,1)} %get-tuple-element.53.refs_0_, bf16[128,2560]{1,0:T(8,128)(2,1)} %refs_1_.5, f32[1,2560]{1,0:T(1,128)} %reshape.187.refs_2_, bf16[320,1920]{1,0:T(8,128)(2,1)} %refs_3_.1, ...), custom_call_target="tpu_custom_call" | custom-call | tf_op jit(solution)/shard_map/middle_gather/pallas_call | solution.py:996
  289.6 11.4 %fusion.26 = f32[512,1920]{1,0:T(8,128)} fusion(bf16[512,2560]{1,0:T(8,128)(2,1)} %get-tuple-element.55, bf16[2560,1920]{1,0:T(8,128)(2,1)} %get-tuple-element.56), kind=kOutput, calls=%fused_computation.78 | convolution fusion | flops 5033164800 | bytes 16384000 | tf_op jit(solution)/shard_map/dot_general | solution.py:71
  301.0 7.5 %fusion.27 = f32[512,1920]{1,0:T(8,128)} fusion(bf16[512,2560]{1,0:T(8,128)(2,1)S(1)} %copy-done.13, bf16[2560,1920]{1,0:T(8,128)(2,1)S(1)} %copy-done.9), kind=kOutput, calls=%fused_computation.79 | convolution fusion | flops 5033164800 | bytes 16384000 | tf_op jit(solution)/shard_map/dot_general | solution.py:71
  308.5 14.6 %multiply_convert_fusion.1 = (bf16[512,1920]{1,0:T(8,128)(2,1)}, bf16[512,1920]{1,0:T(8,128)(2,1)}, bf16[512,1920]{1,0:T(8,128)(2,1)S(1)}) fusion(f32[512,1920]{1,0:T(8,128)} %fusion.26, f32[512,1920]{1,0:T(8,128)} %fusion.27, bf16[2560,1920]{1,0:T(8,128)(2,1)} %all-gather.5.cloned.1.call-done, bf16[512,2560]{1,0:T(8,128)(2,1)S(1)} %copy-done.11, ...), kind=kOutput, calls=%fused_computation.18 | convolution fusion | flops 5062656000 | bytes 26216448 | tf_op jit(solution)/shard_map/dot_general | solution.py:71
  324.4 6.9 %convolution_convert_fusion.6 = bf16[512,2560]{1,0:T(8,128)(2,1)} fusion(bf16[512,1920]{1,0:T(8,128)(2,1)S(1)} %get-tuple-element.92, bf16[2560,1920]{1,0:T(8,128)(2,1)S(1)} %copy-done.8), kind=kOutput, calls=%fused_computation.10 | convolution fusion | flops 5034475520 | bytes 14417920 | tf_op jit(solution)/shard_map/dot_general | solution.py:75
  332.8 8.4 %fusion.28 = f32[512,2560]{1,0:T(8,128)S(1)} fusion(bf16[512,1920]{1,0:T(8,128)(2,1)S(1)} %copy-done.19, bf16[2560,1920]{1,0:T(8,128)(2,1)} %get-tuple-element.56), kind=kOutput, calls=%fused_computation.80 | convolution fusion | flops 5033164800 | bytes 17039360 | tf_op jit(solution)/shard_map/dot_general | solution.py:75
  341.3 8.1 %convolution_convert_fusion.3.refs_4_ = bf16[2560,1920]{1,0:T(8,128)(2,1)} fusion(bf16[512,2560]{1,0:T(8,128)(2,1)S(1)} %copy-done.14, bf16[512,1920]{1,0:T(8,128)(2,1)S(1)} %copy-done.19), kind=kOutput, calls=%fused_computation.3 | convolution fusion | flops 5038080000 | bytes 14417920 | tf_op jit(solution)/shard_map/dot_general | solution.py:81
  349.4 8.1 %convolution_convert_fusion.2.refs_5_ = bf16[2560,1920]{1,0:T(8,128)(2,1)} fusion(bf16[512,2560]{1,0:T(8,128)(2,1)S(1)} %copy-done.14, bf16[512,1920]{1,0:T(8,128)(2,1)S(1)} %copy-done.18), kind=kOutput, calls=%fused_computation.2 | convolution fusion | flops 5038080000 | bytes 14417920 | tf_op jit(solution)/shard_map/dot_general | solution.py:81
  357.6 7.1 %add_convert_fusion.refs_0_ = bf16[512,2560]{1,0:T(8,128)(2,1)} fusion(f32[512,2560]{1,0:T(8,128)S(1)} %fusion.28, bf16[512,1920]{1,0:T(8,128)(2,1)S(1)} %copy-done.18, bf16[2560,1920]{1,0:T(8,128)(2,1)S(1)} %bitcast.49), kind=kOutput, calls=%fused_computation.6 | convolution fusion | flops 5035786240 | bytes 19660800 | tf_op jit(solution)/shard_map/dot_general | solution.py:75
  364.6 19.1 %reduce-scatter.4.cloned.1.call-done = bf16[128,2560]{1,0:T(8,128)(2,1)} async-done(((bf16[512,2560]{1,0:T(8,128)(2,1)}), bf16[128,2560]{1,0:T(8,128)(2,1)}) %reduce-scatter.4.cloned.1.call-update) | async-done | bytes 655376 | tf_op jit(solution)/shard_map/reduce_scatter | solution.py:1784
  383.7 2.4 multiply_convert_fusion.3
  386.2 94.5 %middle_sums.1 = (f32[128,2560]{1,0:T(8,128)}, f32[1,2560]{1,0:T(1,128)}, bf16[512,2560]{1,0:T(8,128)(2,1)}, bf16[320,1920]{1,0:T(8,128)(2,1)}, bf16[320,1920]{1,0:T(8,128)(2,1)}) custom-call(bf16[512,2560]{1,0:T(8,128)(2,1)} %add_convert_fusion.refs_0_, f32[128,2560]{1,0:T(8,128)} %get-tuple-element.54.refs_1_, f32[1,2560]{1,0:T(1,128)} %reshape.187.refs_2_, ...), custom_call_target="tpu_custom_call" | custom-call | tf_op jit(solution)/shard_map/middle_sums/pallas_call | solution.py:1049
  480.8 5.7 convolution_convert_fusion.4
  486.5 1.7 copy-done.12
  488.2 9.8 %convolution_convert_fusion = bf16[2560,1920]{1,0:T(8,128)(2,1)} fusion(bf16[512,1920]{1,0:T(8,128)(2,1)} %copy-done.20, bf16[512,2560]{1,0:T(8,128)(2,1)S(1)} %copy-done.12, f32[512]{0:T(512)S(1)} %fusion.22), kind=kOutput, calls=%fused_computation | convolution fusion | flops 5042012160 | bytes 14419968 | tf_op jit(solution)/shard_map/dot_general | solution.py:81
  498.7 37.0 %recur_backward.1 = (bf16[512,1280]{1,0:T(8,128)(2,1)}, bf16[256,1280]{1,0:T(8,128)(2,1)}, f32[8,640]{1,0:T(8,128)}, f32[1,640]{1,0:T(1,128)}) custom-call(bf16[512,2560]{1,0:T(8,128)(2,1)} %get-tuple-element.60.refs_0_, bf16[512,512]{1,0:T(8,128)(2,1)} %get-tuple-element.106.refs_2_.refs_1_, bf16[2560,640]{1,0:T(8,128)(2,1)} %all-gather.3.cloned.1.call-done.refs_5_.refs_2_, ...), custom_call_target="tpu_custom_call" | custom-call | tf_op jit(solution)/shard_map/recur_backward/pallas_call | solution.py:1636
  536.5 1.6 convert_element_type.146
  538.1 1.6 convert_element_type.147
  540.9 6.1 convolution_convert_fusion.1.refs_5_
  546.9 10.1 %convolution_convert_fusion.5.refs_0_ = bf16[512,2560]{1,0:T(8,128)(2,1)} fusion(bf16[2560,1280]{1,0:T(8,128)(2,1)} %get-tuple-element.51.refs_4_, bf16[512,1280]{1,0:T(8,128)(2,1)S(1)} %copy-done.15, s32[512]{0:T(512)S(1)} %bitcast.45), kind=kOutput, calls=%fused_computation.9 | convolution fusion | flops 4028760064 | bytes 10487808 | tf_op jit(solution)/shard_map/dot_general | solution.py:75
  557.0 73.9 %last_sums.1 = (f32[128,2560]{1,0:T(8,128)}, f32[4,2560]{1,0:T(4,128)}, f32[2,2560]{1,0:T(2,128)}, bf16[320,1280]{1,0:T(8,128)(2,1)}, bf16[32,1280]{1,0:T(8,128)(2,1)}) custom-call(bf16[512,2560]{1,0:T(8,128)(2,1)} %convolution_convert_fusion.5.refs_0_, bf16[128,2560]{1,0:T(8,128)(2,1)} %refs_1_.5, f32[1,2560]{1,0:T(1,128)} %reshape.186.refs_6_.refs_2_, ...), custom_call_target="tpu_custom_call" | custom-call | tf_op jit(solution)/shard_map/last_sums/pallas_call | solution.py:1154
  632.4 1.4 dynamic-slice_reduce_fusion
  633.8 1.3 slice_reduce_fusion.1
  635.1 1.5 fusion.24
  636.6 2.4 fusion.23
  639.0 2.0 convert_bitcast_fusion.1
  641.1 2.9 convert_bitcast_fusion
  (103 shorter events, 22.4 us)
Async XLA Ops:
  7.2 38.3 %all-gather.3.cloned.1.call-start = ((), (), s32[]{:S(2)}) async-start(), calls=%async_computation.3 | async-start | bytes 3686400 | tf_op jit(solution)/shard_map/all_gather | solution.py:1710
  7.9 300.6 %all-gather.5.cloned.1.call-start = ((), (), s32[]{:S(2)}) async-start(), calls=%async_computation.4 | async-start | bytes 11059200 | tf_op jit(solution)/shard_map/all_gather | solution.py:1720
  45.5 338.2 %reduce-scatter.4.cloned.1.call-start = ((), (), s32[]{:S(2)}) async-start(), calls=%async_computation.5 | async-start | bytes 3276800 | tf_op jit(solution)/shard_map/reduce_scatter | solution.py:1784
  50.1 66.8 %copy-start.17 = (s32[128]{0:T(128)S(1)}, s32[128]{0:T(128)}, u32[]{:S(2)}) copy-start(s32[128]{0:T(128)} %param.30) | copy-start | bytes 1540
  116.9 3.4 copy-start.1
  289.6 11.4 %copy-start.9 = (bf16[2560,1920]{1,0:T(8,128)(2,1)S(1)}, bf16[2560,1920]{1,0:T(8,128)(2,1)}, u32[]{:S(2)}) copy-start(bf16[2560,1920]{1,0:T(8,128)(2,1)} %get-tuple-element.57) | copy-start | bytes 29491204
  289.6 11.4 %copy-start.13 = (bf16[512,2560]{1,0:T(8,128)(2,1)S(1)}, bf16[512,2560]{1,0:T(8,128)(2,1)}, u32[]{:S(2)}) copy-start(bf16[512,2560]{1,0:T(8,128)(2,1)} %get-tuple-element.55) | copy-start | bytes 7864324
  301.0 7.5 %copy-start.11 = (bf16[512,2560]{1,0:T(8,128)(2,1)S(1)}, bf16[512,2560]{1,0:T(8,128)(2,1)}, u32[]{:S(2)}) copy-start(bf16[512,2560]{1,0:T(8,128)(2,1)} %get-tuple-element.59) | copy-start | bytes 7864324
  308.5 15.8 %copy-start.8 = (bf16[2560,1920]{1,0:T(8,128)(2,1)S(1)}, bf16[2560,1920]{1,0:T(8,128)(2,1)}, u32[]{:S(2)}) copy-start(bf16[2560,1920]{1,0:T(8,128)(2,1)} %all-gather.5.cloned.1.call-done) | copy-start | bytes 29491204
  323.1 1.3 copy-start.20
  331.3 1.5 copy-start.19
  331.3 307.7 %reduce-scatter.6.cloned.1.call-start = ((), (), s32[]{:S(2)}) async-start(), calls=%async_computation.6 | async-start | bytes 3686400 | tf_op jit(solution)/shard_map/reduce_scatter | solution.py:1810
  332.8 8.4 %copy-start.14 = (bf16[512,2560]{1,0:T(8,128)(2,1)S(1)}, bf16[512,2560]{1,0:T(8,128)(2,1)}, u32[]{:S(2)}) copy-start(bf16[512,2560]{1,0:T(8,128)(2,1)} %get-tuple-element.55) | copy-start | bytes 7864324
  341.2 8.2 %copy-start.18 = (bf16[512,1920]{1,0:T(8,128)(2,1)S(1)}, bf16[512,1920]{1,0:T(8,128)(2,1)}, u32[]{:S(2)}) copy-start(bf16[512,1920]{1,0:T(8,128)(2,1)} %get-tuple-element.90) | copy-start | bytes 5898244
  341.2 16.3 %slice-start = ((s8[9830400]{0:T(1024)(128)(4,1)}), s8[4194304]{0:T(1024)(128)(4,1)S(1)}, s32[]{:S(2)}) async-start(s8[9830400]{0:T(1024)(128)(4,1)} %bitcast.48), calls=%async_computation.8 | async-start | bytes 8388608
  341.3 16.3 %slice-start.1 = ((s8[9830400]{0:T(1024)(128)(4,1)}), s8[4194304]{0:T(1024)(128)(4,1)S(1)}, s32[]{:S(2)}) async-start(s8[9830400]{0:T(1024)(128)(4,1)} %bitcast.48), calls=%async_computation.9 | async-start | bytes 8388608
  349.4 8.1 %slice-start.2 = ((s8[9830400]{0:T(1024)(128)(4,1)}), s8[1441792]{0:T(1024)(128)(4,1)S(1)}, s32[]{:S(2)}) async-start(s8[9830400]{0:T(1024)(128)(4,1)} %bitcast.48), calls=%async_computation.10 | async-start | bytes 2883584
  357.5 26.2 %copy-start = (f32[128,2560]{1,0:T(8,128)S(1)}, f32[128,2560]{1,0:T(8,128)}, u32[]{:S(2)}) copy-start(f32[128,2560]{1,0:T(8,128)} %get-tuple-element.54.refs_1_) | copy-start | bytes 3932164
  357.5 26.2 %copy-start.2 = (bf16[128,2560]{1,0:T(8,128)(2,1)S(1)}, bf16[128,2560]{1,0:T(8,128)(2,1)}, u32[]{:S(2)}) copy-start(bf16[128,2560]{1,0:T(8,128)(2,1)} %refs_1_.3) | copy-start | bytes 1966084
  386.2 94.6 %copy-start.16 = (bf16[512,640]{1,0:T(8,128)(2,1)S(1)}, bf16[512,640]{1,0:T(8,128)(2,1)}, u32[]{:S(2)}) copy-start(bf16[512,640]{1,0:T(8,128)(2,1)} %get-tuple-element.81) | copy-start | bytes 1966084
  486.4 1.7 copy-start.12
  486.4 154.6 %reduce-scatter.8.cloned.1.call-start = ((), (), s32[]{:S(2)}) async-start(), calls=%async_computation.7 | async-start | bytes 11059200 | tf_op jit(solution)/shard_map/reduce_scatter | solution.py:1804
  498.7 37.8 %copy-start.5 = (bf16[320,1920]{1,0:T(8,128)(2,1)S(1)}, bf16[320,1920]{1,0:T(8,128)(2,1)}, u32[]{:S(2)}) copy-start(bf16[320,1920]{1,0:T(8,128)(2,1)} %get-tuple-element.82) | copy-start | bytes 3686404
  535.7 2.5 copy-start.4
  536.5 3.9 copy-start.15
  538.1 1.6 copy-start.6
  538.1 1.6 copy-start.7
  538.1 2.7 copy-start.10
  639.0 4.9 copy-start.3
Sparse Core Ops, SparseCore 0:
  9.9 35.5 all-gather.2
  47.4 81.5 all-gather.4
  331.4 52.2 reduce-scatter.3
  486.6 46.5 reduce-scatter.5
  536.6 103.7 reduce-scatter.7

commit v3 on v2

--- a/solution.py
+++ b/solution.py
@@ -840,34 +840,54 @@
     return jax.ShapeDtypeStruct(dims, kind)
 
 
-def first_gather(n_dp, n_line, mats, minor, rows_in, order):
-    def kernel(a, b, c, e, a_out, b_out, c_out, e_out, ps, pr, pl_sem, ls, lr, ll):
+def first_gather(n_dp, n_line, mats, rows_in, order):
+    count = len(mats)
+    parts = 2
+
+    def kernel(*refs):
+        srcs, (c, e) = refs[:count], refs[count : count + 2]
+        dsts, (c_out, e_out) = refs[count + 2 : 2 * count + 2], refs[2 * count + 2 : 2 * count + 4]
+        ps, pr, pl_sem, ls, lr, ll = refs[2 * count + 4 :]
         place = Place(n_dp, n_line)
         place.meet()
         planes = [
-            GatherPlane(place, a, a_out, ps.at[0], pr.at[0], pl_sem.at[0]),
-            GatherPlane(place, b, b_out, ps.at[1], pr.at[1], pl_sem.at[1]),
+            GatherPlane(place, a, b, ps.at[i], pr.at[i], pl_sem.at[i])
+            for i, (a, b) in enumerate(zip(srcs, dsts))
         ]
-        lines, copies = [], []
+        rows = c.shape[0]
+        span = rows // parts
+        lines = [
+            GatherLine(place, c_out, rows, i * span, span, ls.at[i], lr.at[i])
+            for i in range(parts)
+        ]
+        lines.append(
+            GatherLine(place, e_out, e.shape[0], 0, e.shape[0], ls.at[parts], lr.at[parts])
+        )
+        for i in range(parts):
+            lines[i].step(0, c.at[pl.ds(i * span, span)])
+        lines[parts].step(0, e)
+        early, late = planes[: count // 2], planes[count // 2 :]
+        for part in early:
+            part.begin()
+        copies = []
         for i, (src, dst) in enumerate(((c, c_out), (e, e_out))):
-            rows = src.shape[0]
-            lines.append(GatherLine(place, dst, rows, 0, rows, ls.at[i], lr.at[i]))
-            own = dst.at[pl.ds(pl.multiple_of(place.t * rows, 8), rows)]
+            own = dst.at[pl.ds(pl.multiple_of(place.t * src.shape[0], 8), src.shape[0])]
             copies.append(pltpu.make_async_copy(src, own, ll.at[i]))
-        for copy in copies:
-            copy.start()
-        lines[0].step(0, c)
-        lines[1].step(0, e)
-        planes[0].begin()
-        planes[1].begin()
-        lines[0].step(1)
-        lines[1].step(1)
-        planes[0].forward()
-        planes[1].forward()
-        lines[0].step(2)
-        lines[1].step(2)
-        planes[0].share()
-        planes[1].share()
+            copies[i].start()
+        for line in lines:
+            line.step(1)
+        for part in late:
+            part.begin()
+        for part in early:
+            part.forward()
+        for line in lines:
+            line.step(2)
+        for part in early:
+            part.share()
+        for part in late:
+            part.forward()
+        for part in late:
+            part.share()
         for part in lines + planes:
             part.finish()
         for copy in copies:
@@ -875,25 +895,24 @@
 
     return pl.pallas_call(
         kernel,
-        out_shape=(
-            shaped((n_dp * mats.shape[0], mats.shape[1]), mats.dtype),
-            shaped((n_dp * minor.shape[0], minor.shape[1]), minor.dtype),
+        out_shape=tuple(shaped((n_dp * m.shape[0], m.shape[1]), m.dtype) for m in mats)
+        + (
             shaped((n_line * rows_in.shape[0], rows_in.shape[1]), rows_in.dtype),
             shaped((n_line * order.shape[0], order.shape[1]), order.dtype),
         ),
-        in_specs=[in_any()] * 4,
-        out_specs=[in_any()] * 4,
+        in_specs=[in_any()] * (count + 2),
+        out_specs=[in_any()] * (count + 2),
         scratch_shapes=[
-            dma_sems(2, 9),
-            dma_sems(2, 9),
-            dma_sems(2),
-            dma_sems(2, 2, n_line - 1),
-            dma_sems(2, 2, n_line - 1),
+            dma_sems(count, 9),
+            dma_sems(count, 9),
+            dma_sems(count),
+            dma_sems(parts + 1, 2, n_line - 1),
+            dma_sems(parts + 1, 2, n_line - 1),
             dma_sems(2),
         ],
         compiler_params=comm_params(1),
         name="first_gather",
-    )(mats, minor, rows_in, order)
+    )(*mats, rows_in, order)
 
 
 CHUNKS = 8
@@ -1251,7 +1270,20 @@
 
 
 def recur_forward(
-    n_dp, n_line, tok_all, cot, to_place, to_stored, mats, out_full, gain, gates, taps, soft, flags
+    n_dp,
+    n_line,
+    tok_all,
+    cot,
+    to_place,
+    to_stored,
+    x_full,
+    y_full,
+    out_full,
+    gain,
+    gates,
+    taps,
+    soft,
+    flags,
 ):
     rows, width = tok_all.shape
     count, own = taps.shape
@@ -1260,14 +1292,14 @@
     blocks = (wide - RIM) // size
     chunk = rows // 8
     cot_rows = cot.shape[0]
-    parts = 2
+    parts = 1
 
     def kernel(*refs):
-        (tok, cot_ref, plc, sto, w, wo, gain_ref, gw, cw, sp, fl) = refs[:11]
+        (tok, cot_ref, plc, sto, wx, wy, wo, gain_ref, gw, cw, sp, fl) = refs[:12]
         (hp, xext, y, conv_low, conv, pre_r, pre_i, rate, state, merged_st, terms, cot_all) = refs[
-            11:23
+            12:24
         ]
-        (h, xf, local, cum, merged, agg, slots, hs, hr, es, er, el, gs, gr, gl) = refs[23:]
+        (h, xf, local, cum, merged, agg, slots, hs, hr, es, er, el, gs, gr, gl) = refs[24:]
         place = Place(n_dp, n_line)
         place.meet(True)
         swap = RimSwap(place, own)
@@ -1291,7 +1323,7 @@
         def project(i):
             here = tile_rows(i, 128)
             hp[here] = plain_dot(plc[here], h[...]).astype(jnp.bfloat16)
-            xext[tile_rows(i, 128, 16)] = plain_dot(hp[here], w[:, :own]).astype(jnp.bfloat16)
+            xext[tile_rows(i, 128, 16)] = plain_dot(hp[here], wx[...]).astype(jnp.bfloat16)
 
         loop(rows // 128, project)
         edge = remote(
@@ -1302,14 +1334,14 @@
             (lax.rem(place.d + 1, n_dp), place.t),
         )
         edge.start()
+        for line in lines:
+            line.step(1)
 
         def project_y(i):
             here = tile_rows(i, 128)
-            y[here] = plain_dot(hp[here], w[:, own : 2 * own])
+            y[here] = plain_dot(hp[here], wy[...])
 
         loop(rows // 128, project_y)
-        for line in lines:
-            line.step(1)
         edge.wait()
         top = xext[pl.ds(0, 16)]
         xext[pl.ds(0, 16)] = jnp.where(place.d > 0, top, jnp.zeros_like(top))
@@ -1356,6 +1388,8 @@
             put_lanes(local, here, conv[here] * jax.nn.sigmoid(pre_i[here, own_cols]) * scale)
 
         loop(rows // TILE, drive)
+        for line in lines:
+            line.step(2)
         groups = own // LANES
 
         def scan(i, carry):
@@ -1399,8 +1433,6 @@
             loop(chunk // TILE, settle)
             last = pl.ds(j * chunk + chunk - 1, 1)
             entry = take_lanes(local, last) + take_lanes(cum, last) * entry
-        for line in lines:
-            line.step(2)
         merged_st[...] = plain_dot(sto[...], merged[...]).astype(jnp.bfloat16)
 
         def mix(i):
@@ -1431,7 +1463,7 @@
             shaped((rows, width), low),
             shaped((n_line * cot_rows, width), low),
         ),
-        in_specs=[in_vmem(), in_any()] + [in_vmem()] * 9,
+        in_specs=[in_vmem(), in_any()] + [in_vmem()] * 10,
         out_specs=[in_vmem()] * 11 + [in_any()],
         scratch_shapes=[
             pltpu.VMEM((rows, width), low),
@@ -1452,11 +1484,37 @@
         ],
         compiler_params=comm_params(5),
         name="recur_forward",
-    )(tok_all, cot, to_place, to_stored, mats, out_full, gain, gates, taps, soft, flags)
+    )(
+        tok_all,
+        cot,
+        to_place,
+        to_stored,
+        x_full,
+        y_full,
+        out_full,
+        gain,
+        gates,
+        taps,
+        soft,
+        flags,
+    )
 
 
 def recur_backward(
-    n_dp, n_line, mixer_in, to_place, out_full, gates, taps, soft, slope, flags, kept
+    n_dp,
+    n_line,
+    mixer_in,
+    to_place,
+    to_stored,
+    x_full,
+    y_full,
+    out_full,
+    gates,
+    taps,
+    soft,
+    slope,
+    flags,
+    kept,
 ):
     rows, width = mixer_in.shape
     count, own = taps.shape
@@ -1466,13 +1524,13 @@
     chunk = rows // 8
 
     def kernel(*refs):
-        (mix, plc, wo, gw, cw, sp, sg, fl) = refs[:8]
-        (xext, y, conv_low, conv, pre_r, pre_i, rate, state) = refs[8:16]
-        (gxy, gate_grads, tap_grads, decay_grad) = refs[16:20]
+        (mix, plc, sto, wx, wy, wo, gw, cw, sp, sg, fl) = refs[:11]
+        (xext, y, conv_low, conv, pre_r, pre_i, rate, state) = refs[11:19]
+        (gxy, gate_grads, tap_grads, decay_grad, terms) = refs[19:24]
         (mp, gm, lam, reach, gp_r, gp_i, grad, spread, rim_out, rim_in, ret_out, ret_in) = refs[
-            20:32
+            24:36
         ]
-        (tap_sums, decay_sums, ends, agg, slots, hs, hr, es, er, el) = refs[32:]
+        (tap_sums, decay_sums, ends, agg, slots, hs, hr, es, er, el) = refs[36:]
         place = Place(n_dp, n_line)
         place.meet(True)
         swap = RimSwap(place, own)
@@ -1632,6 +1690,20 @@
         for k in range(count):
             tap_grads[k : k + 1] = jnp.sum(tap_sums[k], axis=0, keepdims=True)
 
+        def restore(i):
+            here = tile_rows(i, 128)
+            mp[here, 0 : 2 * own] = plain_dot(sto[here], gxy[...]).astype(jnp.bfloat16)
+
+        loop(rows // 128, restore)
+
+        def spread_back(i):
+            some = tile_rows(i, 512)
+            terms[:, pl.ds(pl.multiple_of(i * 512, 512), 512)] = (
+                times_trans(mp[:, 0:own], wx[some]) + times_trans(mp[:, own : 2 * own], wy[some])
+            ).astype(jnp.bfloat16)
+
+        loop(width // 512, spread_back)
+
     low, full = jnp.bfloat16, jnp.float32
     return pl.pallas_call(
         kernel,
@@ -1640,9 +1712,10 @@
             shaped((size, 2 * own), low),
             shaped((8, own), full),
             shaped((1, own), full),
+            shaped((rows, width), low),
         ),
-        in_specs=[in_vmem()] * 16,
-        out_specs=[in_vmem()] * 4,
+        in_specs=[in_vmem()] * 19,
+        out_specs=[in_vmem()] * 5,
         scratch_shapes=[
             pltpu.VMEM((rows, width), low),
             pltpu.VMEM((rows, own), full),
@@ -1669,7 +1742,20 @@
         ],
         compiler_params=comm_params(6),
         name="recur_backward",
-    )(mixer_in, to_place, out_full, gates, taps, soft, slope, flags, *kept)
+    )(
+        mixer_in,
+        to_place,
+        to_stored,
+        x_full,
+        y_full,
+        out_full,
+        gates,
+        taps,
+        soft,
+        slope,
+        flags,
+        *kept,
+    )
 
 
 def matches(mesh):
@@ -1706,19 +1792,17 @@
     gate_rows = recur_gate_weight.shape[0]
     own_start = tensor_index * tok_rows
 
-    mats = jnp.concatenate([x_weight, y_weight], axis=1)
-    out_full = lax.all_gather(out_weight.T, "dp", axis=0, tiled=True)
     gains = jnp.concatenate([norm_gain, mlp_gain])
     spare = gate_rows * 128 - gains.shape[0]
     gains = jnp.pad(gains, (0, spare)).reshape(gate_rows, 128)
     minor = jnp.concatenate([recur_gate_weight, input_gate_weight, gains], axis=1)
     own_order = (token_order - dp_index * row_count).astype(jnp.int32)
     order_rows = jnp.broadcast_to(own_order[None, :], (8, tok_rows))
-    xy_full, minor_full, tok_all, order_full = first_gather(
-        n_dp, n_tensor, mats, minor, tokens, order_rows
+    x_full, y_full, out_full, minor_full, tok_all, order_full = first_gather(
+        n_dp, n_tensor, (x_weight, y_weight, out_weight.T, minor), tokens, order_rows
     )
     down_full = lax.all_gather(
-        lax.optimization_barrier((down_weight.T, out_full))[0], "dp", axis=0, tiled=True
+        lax.optimization_barrier((down_weight.T, tok_all))[0], "dp", axis=0, tiled=True
     )
     order_all = order_full.reshape(n_tensor, 8, tok_rows)[:, 0].reshape(row_count)
     both_gates = minor_full[:, : 2 * own_width]
@@ -1766,7 +1850,8 @@
         cotangent,
         to_place,
         to_stored,
-        xy_full,
+        x_full,
+        y_full,
         out_full,
         first_gain,
         gates_wide,
@@ -1781,38 +1866,40 @@
     up_pre = plain_dot(hidden_two, up_full)
     glu_out, glu_pull = jax.vjp(glu, gate_pre, up_pre)
     product = glu_out.astype(jnp.bfloat16)
-    feed_out = lax.psum_scatter(
-        times_trans(product, down_full).astype(jnp.bfloat16),
-        "tensor",
-        scatter_dimension=0,
-        tiled=True,
-    ).astype(jnp.float32)
-    output = ((after_own + feed_out) * live_own[:, None]).astype(jnp.bfloat16)
-
     down_in = (cot_all.astype(jnp.float32) * live_stored[:, None]).astype(jnp.bfloat16)
     grad_in_own = (cotangent.astype(jnp.float32) * live_own[:, None]).astype(jnp.bfloat16)
     grad_down = trans_times(down_in, product).astype(jnp.bfloat16)
+    down_sum = lax.psum_scatter(grad_down, "dp", scatter_dimension=0, tiled=True)
+    down_in, _ = lax.optimization_barrier((down_in, grad_down))
     grad_product = plain_dot(down_in, down_full)
     grad_gate_pre, grad_up_pre = glu_pull(grad_product)
     grad_gate_pre = grad_gate_pre.astype(jnp.bfloat16)
     grad_up_pre = grad_up_pre.astype(jnp.bfloat16)
     grad_gate = trans_times(hidden_two, grad_gate_pre).astype(jnp.bfloat16)
     grad_up = trans_times(hidden_two, grad_up_pre).astype(jnp.bfloat16)
-    feed_terms = (
+    back_terms = (
         times_trans(grad_gate_pre, gate_full) + times_trans(grad_up_pre, up_full)
     ).astype(jnp.bfloat16)
-    down_sum = lax.psum_scatter(grad_down, "dp", scatter_dimension=0, tiled=True)
+    feed_terms = times_trans(product, down_full).astype(jnp.bfloat16)
     grad_after_own, second_part, mixer_in, gate_sum, up_sum = middle_sums(
-        n_dp, n_tensor, feed_terms, after_own, second_gain, grad_in_own, (grad_gate, grad_up)
-    )
-
-    grad_out_mat = trans_times(mixer_in, merged_stored).astype(jnp.bfloat16)
-    out_sum = lax.psum_scatter(grad_out_mat, "dp", scatter_dimension=0, tiled=True)
-    grad_xy, gate_grads, tap_grads, decay_grad = recur_backward(
+        n_dp, n_tensor, back_terms, after_own, second_gain, grad_in_own, (grad_gate, grad_up)
+    )
+    feed_out = lax.psum_scatter(
+        lax.optimization_barrier((feed_terms, mixer_in))[0],
+        "tensor",
+        scatter_dimension=0,
+        tiled=True,
+    ).astype(jnp.float32)
+    output = ((after_own + feed_out) * live_own[:, None]).astype(jnp.bfloat16)
+
+    grad_xy, gate_grads, tap_grads, decay_grad, one_terms = recur_backward(
         n_dp,
         n_tensor,
         mixer_in,
         to_place,
+        to_stored,
+        x_full,
+        y_full,
         out_full,
         gates_wide,
         conv_weight,
@@ -1821,9 +1908,8 @@
         flags,
         kept,
     )
+    grad_out_mat = trans_times(mixer_in, merged_stored).astype(jnp.bfloat16)
     grad_xy_mat = trans_times(hidden_place, grad_xy).astype(jnp.bfloat16)
-    grad_xy_stored = plain_dot(to_stored, grad_xy).astype(jnp.bfloat16)
-    one_terms = times_trans(grad_xy_stored, xy_full).astype(jnp.bfloat16)
     small = jnp.concatenate(
         [
             second_part,
@@ -1833,7 +1919,7 @@
         ],
         axis=0,
     )
-    grad_tokens, small_sum, gain_sums, xy_sum, gates_sum = last_sums(
+    grad_tokens, small_sum, gain_sums, xy_sum, out_sum, gates_sum = last_sums(
         n_dp,
         n_tensor,
         one_terms,
@@ -1841,7 +1927,7 @@
         first_gain,
         grad_after_own,
         small,
-        (grad_xy_mat, gate_grads),
+        (grad_xy_mat, grad_out_mat, gate_grads),
     )
     xy_sum, gates_sum = xy_sum.astype(jnp.float32), gates_sum.astype(jnp.float32)
     own_gains = lax.dynamic_slice_in_dim(gain_sums, dp_index * dp_width, dp_width, 1)

time: 659 us -> 606 us (0.920)
  waiting for transfers between devices: 57.4 us -> 0.05 us
  Pallas kernels: 432 us -> 456 us
  matrix products: 104 us -> 91.1 us
    all_gather x2 -> x1, waiting for transfers between devices: 37.5 us -> 0.01 us  [local_blocks(): lax.all_gather(lax.optimization_barrier((down_weight.T, tok_all))[0], 'dp...]
    reduce_scatter x2 -> x1, waiting for transfers between devices: 19.1 us -> 0.01 us  [local_blocks(): lax.psum_scatter(lax.optimization_barrier((feed_terms, mixer_in))[0], 'te...]
    pallas_call x1, Pallas kernels: 94.5 us -> 110 us  [middle_sums(): pl.pallas_call(kernel, out_shape=(shaped((rows, width), jnp.float32), sha...]
    pallas_call x1, Pallas kernels: 37 us -> 51.6 us  [recur_backward(): pl.pallas_call(kernel, out_shape=(shaped((rows, 2 * own), low), shaped((s...]
    pallas_call x1, Pallas kernels: 57.5 us -> 65.1 us  [first_gather(): pl.pallas_call(kernel, out_shape=tuple((shaped((n_dp * m.shape[0], m.shap...]
    pallas_call x1, Pallas kernels: 74.3 us -> 66.9 us  [recur_forward(): pl.pallas_call(kernel, out_shape=(shaped((rows, width), low), shaped((row...]
    dot_general x4 -> x3, matrix products: 32.5 us -> 26.3 us  [times_trans(): lax.dot_general(left, right, (((1,), (1,)), ((), ())), preferred_element_...]
  transfers between devices with their start and end apart: 5 -> 3, of which waited for: 2 -> 0; matrix products, arithmetic and copies ran while one was open for 17% -> 20% of each run, Pallas kernels for 52% -> 65%
where the time goes in v3:
time: 606 us; the launch traced here: 599 us
  Pallas kernels  456 us (75%)
  matrix products  91.1 us (15%)
  other arithmetic  20.1 us (3%)
  local copies, waits for them, and re-layouts  17.3 us (3%)
  between operations  14.4 us (2%)
    pallas_call x1, Pallas kernels, middle_sums(): pl.pallas_call(kernel, out_shape=(shaped((rows, width), jnp.float32), sha...  110 us
    pallas_call x1, Pallas kernels, middle_gather(): pl.pallas_call(kernel, out_shape=(shaped((rows, width), jnp.float32), sha...  95 us
    pallas_call x1, Pallas kernels, last_sums(): pl.pallas_call(kernel, out_shape=(shaped((rows, width), jnp.float32), sha...  67.5 us
    pallas_call x1, Pallas kernels, recur_forward(): pl.pallas_call(kernel, out_shape=(shaped((rows, width), low), shaped((row...  66.9 us
    pallas_call x1, Pallas kernels, first_gather(): pl.pallas_call(kernel, out_shape=tuple((shaped((n_dp * m.shape[0], m.shap...  65.1 us
    pallas_call x1, Pallas kernels, recur_backward(): pl.pallas_call(kernel, out_shape=(shaped((rows, 2 * own), low), shaped((s...  51.6 us
    dot_general x5, matrix products, trans_times(): lax.dot_general(left, right, (((0,), (0,)), ((), ())), preferred_element_...  34.1 us
    dot_general x3, matrix products, plain_dot(): return jnp.dot(left, right, preferred_element_type=jnp.float32)  30.7 us
  transfers between devices with their start and end apart: 3, of which 0 were waited for; matrix products, arithmetic and copies ran while one was open for 20% of the time, Pallas kernels for 65%

profile of v3, /device:TPU:0, one launch (start us, length us, event | category | flops | bytes accessed | tf_op | source)
XLA Modules:
  0.0 599.3 jit_solution(15468591946452943471)
XLA Ops:
  8.7 1.4 pad_maximum_fusion.refs_3_
  10.7 65.1 %first_gather.1 = (bf16[2560,640]{1,0:T(8,128)(2,1)}, bf16[2560,640]{1,0:T(8,128)(2,1)}, bf16[2560,640]{1,0:T(8,128)(2,1)}, bf16[256,1408]{1,0:T(8,128)(2,1)}, b...) custom-call(bf16[320,640]{1,0:T(8,128)(2,1)} %refs_0_.1, bf16[320,640]{1,0:T(8,128)(2,1)} %refs_1_.4, ...), custom_call_target="tpu_custom_call" | custom-call | tf_op jit(solution)/shard_map/first_gather/pallas_call | solution.py:896
  80.7 1.0 slice_dynamic-update-slice_fusion.1
  81.8 1.1 slice_dynamic-update-slice_fusion
  83.9 1.1 fusion.8
  85.0 66.9 %recur_forward.1 = (bf16[512,2560]{1,0:T(8,128)(2,1)}, bf16[528,640]{1,0:T(8,128)(2,1)}, f32[512,640]{1,0:T(8,128)}, bf16[512,896]{1,0:T(8,128)(2,1)}, f32[512,6...) custom-call(bf16[512,2560]{1,0:T(8,128)(2,1)} %get-tuple-element.55., ...), custom_call_target="tpu_custom_call" | custom-call | tf_op jit(solution)/shard_map/recur_forward/pallas_call | solution.py:1450
  151.9 95.0 %middle_gather.1 = (f32[128,2560]{1,0:T(8,128)}, bf16[512,2560]{1,0:T(8,128)(2,1)}, bf16[2560,1920]{1,0:T(8,128)(2,1)}, bf16[2560,1920]{1,0:T(8,128)(2,1)}) custom-call(bf16[512,2560]{1,0:T(8,128)(2,1)} %get-tuple-element.61.refs_0_, bf16[128,2560]{1,0:T(8,128)(2,1)} %refs_1_.7, f32[1,2560]{1,0:T(1,128)} %reshape.187.refs_2_, bf16[320,1920]{1,0:T(8,128)(2,1)} %refs_3_.1, ...), custom_call_target="tpu_custom_call" | custom-call | tf_op jit(solution)/shard_map/middle_gather/pallas_call | solution.py:1015
  247.7 2.4 multiply_convert_fusion
  250.1 8.5 %fusion.23 = f32[512,1920]{1,0:T(8,128)S(1)} fusion(bf16[512,2560]{1,0:T(8,128)(2,1)S(1)} %copy-done.14, bf16[2560,1920]{1,0:T(8,128)(2,1)} %get-tuple-element.64), kind=kOutput, calls=%fused_computation.73 | convolution fusion | flops 5033164800 | bytes 16384000 | tf_op jit(solution)/shard_map/dot_general | solution.py:71
  258.7 7.8 %multiply_convert_fusion.2 = (bf16[512,1920]{1,0:T(8,128)(2,1)S(1)}, f32[512,1920]{1,0:T(8,128)}) fusion(f32[512,1920]{1,0:T(8,128)S(1)} %fusion.23, bf16[512,2560]{1,0:T(8,128)(2,1)S(1)} %copy-done.14, bf16[2560,1920]{1,0:T(8,128)(2,1)S(1)} %bitcast.48), kind=kOutput, calls=%fused_computation.18 | convolution fusion | flops 5042995200 | bytes 22282240 | tf_op jit(solution)/shard_map/dot_general | solution.py:71
  266.5 1.3 copy-done.21
  267.7 8.1 %convolution_convert_fusion.3 = bf16[2560,1920]{1,0:T(8,128)(2,1)} fusion(bf16[512,2560]{1,0:T(8,128)(2,1)S(1)} %multiply_convert_fusion, bf16[512,1920]{1,0:T(8,128)(2,1)S(1)} %get-tuple-element.118), kind=kOutput, calls=%fused_computation.3 | convolution fusion | flops 5038080000 | bytes 14417920 | tf_op jit(solution)/shard_map/dot_general | solution.py:81
  277.1 1.0 multiply_convert_fusion.4.refs_3_
  278.2 14.4 %multiply_convert_fusion.1 = (bf16[512,1920]{1,0:T(8,128)(2,1)S(1)}, bf16[512,1920]{1,0:T(8,128)(2,1)S(1)}) fusion(f32[512,1920]{1,0:T(8,128)} %copy-done.20, f32[512,1920]{1,0:T(8,128)} %get-tuple-element.119, bf16[512,2560]{1,0:T(8,128)(2,1)S(1)} %multiply_convert_fusion, bf16[2560,1920]{1,0:T(8,128)(2,1)} %all-gather.2.cloned.1.call-done), kind=kOutput, calls=%fused_computation.17 | convolution fusion | flops 5056757760 | bytes 24248320 | tf_op jit(solution)/shard_map/dot_general | solution.py:71
  292.5 8.5 %fusion.24 = f32[512,2560]{1,0:T(8,128)S(1)} fusion(bf16[512,1920]{1,0:T(8,128)(2,1)S(1)} %get-tuple-element.103, bf16[2560,1920]{1,0:T(8,128)(2,1)} %get-tuple-element.64), kind=kOutput, calls=%fused_computation.74 | convolution fusion | flops 5033164800 | bytes 17039360 | tf_op jit(solution)/shard_map/dot_general | solution.py:75
  301.1 8.1 %convolution_convert_fusion.2.refs_4_ = bf16[2560,1920]{1,0:T(8,128)(2,1)} fusion(bf16[512,2560]{1,0:T(8,128)(2,1)S(1)} %copy-done.15, bf16[512,1920]{1,0:T(8,128)(2,1)S(1)} %get-tuple-element.103), kind=kOutput, calls=%fused_computation.2 | convolution fusion | flops 5038080000 | bytes 14417920 | tf_op jit(solution)/shard_map/dot_general | solution.py:81
  309.2 8.1 %convolution_convert_fusion.1.refs_5_ = bf16[2560,1920]{1,0:T(8,128)(2,1)} fusion(bf16[512,2560]{1,0:T(8,128)(2,1)S(1)} %copy-done.15, bf16[512,1920]{1,0:T(8,128)(2,1)S(1)} %get-tuple-element.102), kind=kOutput, calls=%fused_computation.1 | convolution fusion | flops 5038080000 | bytes 14417920 | tf_op jit(solution)/shard_map/dot_general | solution.py:81
  317.4 7.0 %add_convert_fusion.refs_0_ = bf16[512,2560]{1,0:T(8,128)(2,1)} fusion(f32[512,2560]{1,0:T(8,128)S(1)} %fusion.24, bf16[512,1920]{1,0:T(8,128)(2,1)S(1)} %get-tuple-element.102, bf16[2560,1920]{1,0:T(8,128)(2,1)S(1)} %bitcast.50), kind=kOutput, calls=%fused_computation.6 | convolution fusion | flops 5035786240 | bytes 19660800 | tf_op jit(solution)/shard_map/dot_general | solution.py:75
  324.3 109.7 %middle_sums.1 = (f32[128,2560]{1,0:T(8,128)}, f32[1,2560]{1,0:T(1,128)}, bf16[512,2560]{1,0:T(8,128)(2,1)}, bf16[320,1920]{1,0:T(8,128)(2,1)}, bf16[320,1920]{1,0:T(8,128)(2,1)}) custom-call(bf16[512,2560]{1,0:T(8,128)(2,1)} %add_convert_fusion.refs_0_, f32[128,2560]{1,0:T(8,128)} %get-tuple-element.62.refs_1_, f32[1,2560]{1,0:T(1,128)} %reshape.187.refs_2_, ...), custom_call_target="tpu_custom_call" | custom-call | tf_op jit(solution)/shard_map/middle_sums/pallas_call | solution.py:1068
  434.0 10.8 %convolution_convert_fusion.5 = bf16[512,2560]{1,0:T(8,128)(2,1)} fusion(bf16[512,1920]{1,0:T(8,128)(2,1)S(1)} %copy-done.22, bf16[2560,1920]{1,0:T(8,128)(2,1)} %all-gather.2.cloned.1.call-done), kind=kOutput, calls=%fused_computation.9 | convolution fusion | flops 5034475520 | bytes 14417920 | tf_op jit(solution)/shard_map/dot_general | solution.py:75
  445.5 2.9 convert_bitcast_fusion
  448.4 51.6 %recur_backward.1 = (bf16[512,1280]{1,0:T(8,128)(2,1)}, bf16[256,1280]{1,0:T(8,128)(2,1)}, f32[8,640]{1,0:T(8,128)}, f32[1,640]{1,0:T(1,128)}, bf16[512,2560]{1,0:T(8,128)(2,1)}) custom-call(bf16[512,2560]{1,0:T(8,128)(2,1)} %get-tuple-element.69.refs_0_, bf16[512,512]{1,0:T(8,128)(2,1)} %get-tuple-element.117.refs_2_.refs_1_, ...), custom_call_target="tpu_custom_call" | custom-call | tf_op jit(solution)/shard_map/recur_backward/pallas_call | solution.py:1708
  500.9 4.0 convolution_convert_fusion.4.refs_6_
  505.6 5.8 convolution_convert_fusion.refs_5_
  511.4 67.5 %last_sums.1 = (f32[128,2560]{1,0:T(8,128)}, f32[4,2560]{1,0:T(4,128)}, f32[2,2560]{1,0:T(2,128)}, bf16[320,1280]{1,0:T(8,128)(2,1)}, bf16[320,640]{1,0:T(8,128)(2,1)}, /*index=5*/bf16[32,1280]{1,0:T(8,128)(2,1)}) custom-call(bf16[512,2560]{1,0:T(8,128)(2,1)} %get-tuple-element.79.refs_0_, bf16[128,2560]{1,0:T(8,128)(2,1)} %refs_1_.7, ...), custom_call_target="tpu_custom_call" | custom-call | tf_op jit(solution)/shard_map/last_sums/pallas_call | solution.py:1173
  580.4 1.6 convert_element_type.139
  582.0 1.6 convert_element_type.140
  583.6 1.5 dynamic-slice_reduce_fusion
  585.1 1.3 slice_reduce_fusion.1
  588.0 1.3 fusion.20
  589.3 2.1 multiply_convert_fusion.3
  591.5 1.1 copy.44
  (108 shorter events, 15.4 us)
Async XLA Ops:
  7.2 71.1 %copy-start.11 = (f32[640]{0:T(1024)S(1)}, f32[640]{0:T(1024)}, u32[]{:S(2)}) copy-start(f32[640]{0:T(1024)} %param.23) | copy-start | bytes 7684
  7.2 71.7 %copy-start.18 = (s32[3]{0:T(128)S(1)}, s32[3]{0:T(128)}, u32[]{:S(2)}) copy-start(s32[3]{0:T(128)} %param.29) | copy-start | bytes 40
  7.2 271.0 %all-gather.2.cloned.1.call-start = ((), (), s32[]{:S(2)}) async-start(), calls=%async_computation.2 | async-start | bytes 11059200 | tf_op jit(solution)/shard_map/all_gather | solution.py:1804
  75.8 369.7 %reduce-scatter.5.cloned.1.call-start = ((), (), s32[]{:S(2)}) async-start(), calls=%async_computation.4 | async-start | bytes 11059200 | tf_op jit(solution)/shard_map/reduce_scatter | solution.py:1872
  82.9 2.1 copy-start.1
  246.9 3.2 copy-start.14
  247.7 10.9 %slice-start = ((s8[9830400]{0:T(1024)(128)(4,1)}), s8[4194304]{0:T(1024)(128)(4,1)S(1)}, s32[]{:S(2)}) async-start(s8[9830400]{0:T(1024)(128)(4,1)} %bitcast.47), calls=%async_computation.5 | async-start | bytes 8388608
  250.1 8.5 %slice-start.1 = ((s8[9830400]{0:T(1024)(128)(4,1)}), s8[4194304]{0:T(1024)(128)(4,1)S(1)}, s32[]{:S(2)}) async-start(s8[9830400]{0:T(1024)(128)(4,1)} %bitcast.47), calls=%async_computation.6 | async-start | bytes 8388608
  250.1 8.5 %slice-start.2 = ((s8[9830400]{0:T(1024)(128)(4,1)}), s8[1441792]{0:T(1024)(128)(4,1)S(1)}, s32[]{:S(2)}) async-start(s8[9830400]{0:T(1024)(128)(4,1)} %bitcast.47), calls=%async_computation.7 | async-start | bytes 2883584
  258.6 7.8 %copy-start.20 = (f32[512,1920]{1,0:T(8,128)}, f32[512,1920]{1,0:T(8,128)S(1)}, u32[]{:S(2)}) copy-start(f32[512,1920]{1,0:T(8,128)S(1)} %fusion.23) | copy-start | bytes 11796484
  266.5 1.3 copy-start.21
  275.8 0.7 copy-start.19
  275.8 1.3 copy-start.3
  275.8 313.5 %reduce-scatter.3.cloned.1.call-start = ((), (), s32[]{:S(2)}) async-start(), calls=%async_computation.3 | async-start | bytes 3276800 | tf_op jit(solution)/shard_map/reduce_scatter | solution.py:1887
  292.5 8.5 %copy-start.15 = (bf16[512,2560]{1,0:T(8,128)(2,1)S(1)}, bf16[512,2560]{1,0:T(8,128)(2,1)}, u32[]{:S(2)}) copy-start(bf16[512,2560]{1,0:T(8,128)(2,1)} %get-tuple-element.63) | copy-start | bytes 7864324
  301.1 16.3 %slice-start.3 = ((s8[9830400]{0:T(1024)(128)(4,1)}), s8[4194304]{0:T(1024)(128)(4,1)S(1)}, s32[]{:S(2)}) async-start(s8[9830400]{0:T(1024)(128)(4,1)} %bitcast.49), calls=%async_computation.8 | async-start | bytes 8388608
  301.1 16.3 %slice-start.4 = ((s8[9830400]{0:T(1024)(128)(4,1)}), s8[4194304]{0:T(1024)(128)(4,1)S(1)}, s32[]{:S(2)}) async-start(s8[9830400]{0:T(1024)(128)(4,1)} %bitcast.49), calls=%async_computation.9 | async-start | bytes 8388608
  309.2 8.1 %slice-start.5 = ((s8[9830400]{0:T(1024)(128)(4,1)}), s8[1441792]{0:T(1024)(128)(4,1)S(1)}, s32[]{:S(2)}) async-start(s8[9830400]{0:T(1024)(128)(4,1)} %bitcast.49), calls=%async_computation.10 | async-start | bytes 2883584
  324.3 109.7 %copy-start.22 = (bf16[512,1920]{1,0:T(8,128)(2,1)S(1)}, bf16[512,1920]{1,0:T(8,128)(2,1)}, u32[]{:S(2)}) copy-start(bf16[512,1920]{1,0:T(8,128)(2,1)} %copy-done.21) | copy-start | bytes 5898244
  448.4 52.4 %copy-start.4 = (bf16[512,2560]{1,0:T(8,128)(2,1)S(1)}, bf16[512,2560]{1,0:T(8,128)(2,1)}, u32[]{:S(2)}) copy-start(bf16[512,2560]{1,0:T(8,128)(2,1)} %get-tuple-element.69.refs_0_) | copy-start | bytes 7864324
  448.4 52.4 %copy-start.17 = (bf16[512,640]{1,0:T(8,128)(2,1)S(1)}, bf16[512,640]{1,0:T(8,128)(2,1)}, u32[]{:S(2)}) copy-start(bf16[512,640]{1,0:T(8,128)(2,1)} %get-tuple-element.86) | copy-start | bytes 1966084
  500.8 4.0 copy-start.10
  500.8 4.0 copy-start.12
  500.8 4.7 copy-start.13
  500.9 4.7 copy-start.16
  511.3 69.1 %copy-start.7 = (bf16[320,1920]{1,0:T(8,128)(2,1)S(1)}, bf16[320,1920]{1,0:T(8,128)(2,1)}, u32[]{:S(2)}) copy-start(bf16[320,1920]{1,0:T(8,128)(2,1)} %get-tuple-element.94) | copy-start | bytes 3686404
  578.9 3.1 copy-start.6
  580.4 6.0 copy-start.9
  580.4 6.7 %copy-start.8 = (bf16[320,640]{1,0:T(8,128)(2,1)S(1)}, bf16[320,640]{1,0:T(8,128)(2,1)}, u32[]{:S(2)}) copy-start(bf16[320,640]{1,0:T(8,128)(2,1)} %get-tuple-element.93) | copy-start | bytes 1228804
  582.0 6.0 %copy-start.2 = (bf16[320,1280]{1,0:T(8,128)(2,1)S(1)}, bf16[320,1280]{1,0:T(8,128)(2,1)}, u32[]{:S(2)}) copy-start(bf16[320,1280]{1,0:T(8,128)(2,1)} %get-tuple-element.90) | copy-start | bytes 2457604
  583.6 5.7 copy-start
  587.1 4.4 copy-start.5
Sparse Core Ops, SparseCore 0:
  75.9 60.7 all-gather.1
  276.0 90.5 reduce-scatter.4
  445.0 52.7 reduce-scatter.2

commit v4 on v3

--- a/solution.py
+++ b/solution.py
@@ -1004,11 +1004,8 @@
             first = pl.multiple_of(place.t * rows, 16) + c * total.shape[0]
             hidden[pl.ds(pl.multiple_of(first, 16), total.shape[0])] = low
 
-        between = {4: planes[1].begin, 5: planes[0].forward}
+        between = {5: planes[0].forward, 8: planes[0].share}
         sum_rows_and_spread(place, s, scratch, norm, hidden, between)
-        planes[1].forward()
-        planes[0].share()
-        planes[1].share()
         for part in planes:
             part.finish()
 
@@ -1059,9 +1056,8 @@
             first = pl.multiple_of(place.t * rows, 16) + c * total.shape[0]
             spread[pl.ds(pl.multiple_of(first, 16), total.shape[0])] = both.astype(jnp.bfloat16)
 
-        between = {0: planes[0].cores, 3: planes[1].cores, 5: planes[0].turn}
+        between = {1: planes[0].cores, 7: planes[0].turn}
         sum_rows_and_spread(place, s, scratch, norm, spread, between)
-        planes[1].turn()
         for part, result in zip(planes, results):
             part.finish(result)
 
@@ -1801,9 +1797,9 @@
     x_full, y_full, out_full, minor_full, tok_all, order_full = first_gather(
         n_dp, n_tensor, (x_weight, y_weight, out_weight.T, minor), tokens, order_rows
     )
-    down_full = lax.all_gather(
-        lax.optimization_barrier((down_weight.T, tok_all))[0], "dp", axis=0, tiled=True
-    )
+    late_up, late_down, _ = lax.optimization_barrier((up_weight, down_weight.T, tok_all))
+    up_full = lax.all_gather(late_up, "dp", axis=0, tiled=True)
+    down_full = lax.all_gather(late_down, "dp", axis=0, tiled=True)
     order_all = order_full.reshape(n_tensor, 8, tok_rows)[:, 0].reshape(row_count)
     both_gates = minor_full[:, : 2 * own_width]
     gain_rows = minor_full[:, 2 * own_width :].reshape(n_dp, -1)
@@ -1859,8 +1855,8 @@
         soft,
         flags,
     )
-    after_own, hidden_two, gate_full, up_full = middle_gather(
-        n_dp, n_tensor, mixer_terms, tokens, second_gain, (gate_weight, up_weight)
+    after_own, hidden_two, gate_full = middle_gather(
+        n_dp, n_tensor, mixer_terms, tokens, second_gain, (gate_weight,)
     )
     gate_pre = plain_dot(hidden_two, gate_full)
     up_pre = plain_dot(hidden_two, up_full)
@@ -1881,8 +1877,9 @@
         times_trans(grad_gate_pre, gate_full) + times_trans(grad_up_pre, up_full)
     ).astype(jnp.bfloat16)
     feed_terms = times_trans(product, down_full).astype(jnp.bfloat16)
-    grad_after_own, second_part, mixer_in, gate_sum, up_sum = middle_sums(
-        n_dp, n_tensor, back_terms, after_own, second_gain, grad_in_own, (grad_gate, grad_up)
+    up_sum = lax.psum_scatter(grad_up, "dp", scatter_dimension=0, tiled=True)
+    grad_after_own, second_part, mixer_in, gate_sum = middle_sums(
+        n_dp, n_tensor, back_terms, after_own, second_gain, grad_in_own, (grad_gate,)
     )
     feed_out = lax.psum_scatter(
         lax.optimization_barrier((feed_terms, mixer_in))[0],

time: 606 us -> 675 us (1.11)
  waiting for transfers between devices: 0.05 us -> 66.3 us
    reduce_scatter x1, waiting for transfers between devices: 0.01 us -> 65 us  [local_blocks(): lax.psum_scatter(grad_down, 'dp', scatter_dimension=0, tiled=True)]
    pallas_call x1, Pallas kernels: 67.5 us -> 96.6 us  [last_sums(): pl.pallas_call(kernel, out_shape=(shaped((rows, width), jnp.float32), sha...]
    pallas_call x1, Pallas kernels: 110 us -> 81.6 us  [middle_sums(): pl.pallas_call(kernel, out_shape=(shaped((rows, width), jnp.float32), sha...]
  transfers between devices with their start and end apart: 3 -> 5, of which waited for: 0 -> 1; matrix products, arithmetic and copies ran while one was open for 20% -> 12% of each run, Pallas kernels for 65% -> 46%
where the time goes in v4:
time: 675 us; the launch traced here: 668 us
  Pallas kernels  453 us (67%)
  matrix products  97.4 us (14%)
  waiting for transfers between devices  66.3 us (10%)
  other arithmetic  21.3 us (3%)
  local copies, waits for them, and re-layouts  15.2 us (2%)
  between operations  14.7 us (2%)
    pallas_call x1, Pallas kernels, last_sums(): pl.pallas_call(kernel, out_shape=(shaped((rows, width), jnp.float32), sha...  96.6 us
    pallas_call x1, Pallas kernels, middle_gather(): pl.pallas_call(kernel, out_shape=(shaped((rows, width), jnp.float32), sha...  88.6 us
    pallas_call x1, Pallas kernels, middle_sums(): pl.pallas_call(kernel, out_shape=(shaped((rows, width), jnp.float32), sha...  81.6 us
    pallas_call x1, Pallas kernels, recur_forward(): pl.pallas_call(kernel, out_shape=(shaped((rows, width), low), shaped((row...  67.6 us
    pallas_call x1, Pallas kernels, first_gather(): pl.pallas_call(kernel, out_shape=tuple((shaped((n_dp * m.shape[0], m.shap...  65.1 us
    reduce_scatter x1, waiting for transfers between devices, local_blocks(): lax.psum_scatter(grad_down, 'dp', scatter_dimension=0, tiled=True)  65 us
    pallas_call x1, Pallas kernels, recur_backward(): pl.pallas_call(kernel, out_shape=(shaped((rows, 2 * own), low), shaped((s...  53 us
    dot_general x5, matrix products, trans_times(): lax.dot_general(left, right, (((0,), (0,)), ((), ())), preferred_element_...  36.1 us
  transfers between devices with their start and end apart: 5, of which 1 were waited for; matrix products, arithmetic and copies ran while one was open for 12% of the time, Pallas kernels for 46%

profile of v4, /device:TPU:0, one launch (start us, length us, event | category | flops | bytes accessed | tf_op | source)
XLA Modules:
  0.0 667.5 jit_solution(9677155075605485164)
XLA Ops:
  8.7 1.4 pad_maximum_fusion.refs_3_
  10.7 65.1 %first_gather.1 = (bf16[2560,640]{1,0:T(8,128)(2,1)}, bf16[2560,640]{1,0:T(8,128)(2,1)}, bf16[2560,640]{1,0:T(8,128)(2,1)}, bf16[256,1408]{1,0:T(8,128)(2,1)}, b...) custom-call(bf16[320,640]{1,0:T(8,128)(2,1)} %refs_0_.1, bf16[320,640]{1,0:T(8,128)(2,1)} %refs_1_.4, ...), custom_call_target="tpu_custom_call" | custom-call | tf_op jit(solution)/shard_map/first_gather/pallas_call | solution.py:896
  81.7 1.0 and_convert_fusion.refs_11_.refs_10_
  82.7 1.1 fusion.8
  83.8 67.6 %recur_forward.1 = (bf16[512,2560]{1,0:T(8,128)(2,1)}, bf16[528,640]{1,0:T(8,128)(2,1)}, f32[512,640]{1,0:T(8,128)}, bf16[512,896]{1,0:T(8,128)(2,1)}, f32[512,6...) custom-call(bf16[512,2560]{1,0:T(8,128)(2,1)} %get-tuple-element.54., ...), custom_call_target="tpu_custom_call" | custom-call | tf_op jit(solution)/shard_map/recur_forward/pallas_call | solution.py:1446
  151.4 88.6 %middle_gather.1 = (f32[128,2560]{1,0:T(8,128)}, bf16[512,2560]{1,0:T(8,128)(2,1)}, bf16[2560,1920]{1,0:T(8,128)(2,1)}) custom-call(bf16[512,2560]{1,0:T(8,128)(2,1)} %get-tuple-element.60.refs_0_, bf16[128,2560]{1,0:T(8,128)(2,1)} %refs_1_.7, f32[1,2560]{1,0:T(1,128)} %reshape.187.refs_2_, bf16[320,1920]{1,0:T(8,128)(2,1)} %refs_3_.1), custom_call_target="tpu_custom_call" | custom-call | tf_op jit(solution)/shard_map/middle_gather/pallas_call | solution.py:1012
  241.4 1.0 multiply_convert_fusion.4.refs_3_
  242.4 2.0 multiply_convert_fusion
  244.4 10.5 %fusion.23 = f32[512,1920]{1,0:T(8,128)} fusion(bf16[512,2560]{1,0:T(8,128)(2,1)S(1)} %copy-done.16, bf16[2560,1920]{1,0:T(8,128)(2,1)} %get-tuple-element.63), kind=kOutput, calls=%fused_computation.73 | convolution fusion | flops 5033164800 | bytes 16384000 | tf_op jit(solution)/shard_map/dot_general | solution.py:71
  255.0 12.1 %multiply_convert_fusion.2 = (bf16[512,1920]{1,0:T(8,128)(2,1)S(1)}, f32[512,1920]{1,0:T(8,128)}) fusion(f32[512,1920]{1,0:T(8,128)} %fusion.23, bf16[512,2560]{1,0:T(8,128)(2,1)} %get-tuple-element.62, bf16[2560,1920]{1,0:T(8,128)(2,1)} %all-gather.3.cloned.1.call-done), kind=kOutput, calls=%fused_computation.18 | convolution fusion | flops 5042995200 | bytes 22282240 | tf_op jit(solution)/shard_map/dot_general | solution.py:71
  267.1 1.3 copy-done.22
  268.4 8.2 %convolution_convert_fusion.3 = bf16[2560,1920]{1,0:T(8,128)(2,1)} fusion(bf16[512,2560]{1,0:T(8,128)(2,1)S(1)} %copy-done.6, bf16[512,1920]{1,0:T(8,128)(2,1)S(1)} %get-tuple-element.116), kind=kOutput, calls=%fused_computation.3 | convolution fusion | flops 5038080000 | bytes 14417920 | tf_op jit(solution)/shard_map/dot_general | solution.py:81
  276.5 12.7 %multiply_convert_fusion.1 = (bf16[512,1920]{1,0:T(8,128)(2,1)S(1)}, bf16[512,1920]{1,0:T(8,128)(2,1)S(1)}) fusion(f32[512,1920]{1,0:T(8,128)} %fusion.23, f32[512,1920]{1,0:T(8,128)} %get-tuple-element.117, bf16[512,2560]{1,0:T(8,128)(2,1)S(1)} %copy-done.6, bf16[2560,1920]{1,0:T(8,128)(2,1)} %all-gather.5.cloned.1.call-done), kind=kOutput, calls=%fused_computation.17 | convolution fusion | flops 5056757760 | bytes 24248320 | tf_op jit(solution)/shard_map/dot_general | solution.py:71
  289.3 9.0 %fusion.24 = f32[512,2560]{1,0:T(8,128)S(1)} fusion(bf16[512,1920]{1,0:T(8,128)(2,1)S(1)} %get-tuple-element.101, bf16[2560,1920]{1,0:T(8,128)(2,1)} %get-tuple-element.63), kind=kOutput, calls=%fused_computation.74 | convolution fusion | flops 5033164800 | bytes 17039360 | tf_op jit(solution)/shard_map/dot_general | solution.py:75
  298.3 8.3 %convolution_convert_fusion.2.refs_4_ = bf16[2560,1920]{1,0:T(8,128)(2,1)} fusion(bf16[512,2560]{1,0:T(8,128)(2,1)S(1)} %copy-done.17, bf16[512,1920]{1,0:T(8,128)(2,1)S(1)} %get-tuple-element.101), kind=kOutput, calls=%fused_computation.2 | convolution fusion | flops 5038080000 | bytes 14417920 | tf_op jit(solution)/shard_map/dot_general | solution.py:81
  306.6 6.9 %add_convert_fusion.refs_0_ = bf16[512,2560]{1,0:T(8,128)(2,1)} fusion(f32[512,2560]{1,0:T(8,128)S(1)} %fusion.24, bf16[512,1920]{1,0:T(8,128)(2,1)S(1)} %get-tuple-element.100, bf16[2560,1920]{1,0:T(8,128)(2,1)S(1)} %bitcast.48), kind=kOutput, calls=%fused_computation.6 | convolution fusion | flops 5035786240 | bytes 19660800 | tf_op jit(solution)/shard_map/dot_general | solution.py:75
  313.5 81.6 %middle_sums.1 = (f32[128,2560]{1,0:T(8,128)}, f32[1,2560]{1,0:T(1,128)}, bf16[512,2560]{1,0:T(8,128)(2,1)}, bf16[320,1920]{1,0:T(8,128)(2,1)}) custom-call(bf16[512,2560]{1,0:T(8,128)(2,1)} %add_convert_fusion.refs_0_, f32[128,2560]{1,0:T(8,128)} %get-tuple-element.61.refs_1_, f32[1,2560]{1,0:T(1,128)} %reshape.187.refs_2_, ...), custom_call_target="tpu_custom_call" | custom-call | tf_op jit(solution)/shard_map/middle_sums/pallas_call | solution.py:1064
  395.2 10.0 %convolution_convert_fusion.5 = bf16[512,2560]{1,0:T(8,128)(2,1)} fusion(bf16[512,1920]{1,0:T(8,128)(2,1)} %copy-done.22, bf16[2560,1920]{1,0:T(8,128)(2,1)} %all-gather.5.cloned.1.call-done), kind=kOutput, calls=%fused_computation.9 | convolution fusion | flops 5034475520 | bytes 14417920 | tf_op jit(solution)/shard_map/dot_general | solution.py:75
  405.2 9.8 %convolution_convert_fusion = bf16[2560,1920]{1,0:T(8,128)(2,1)} fusion(bf16[512,2560]{1,0:T(8,128)(2,1)S(1)} %copy-done.17, bf16[512,1920]{1,0:T(8,128)(2,1)} %copy-done.23), kind=kOutput, calls=%fused_computation | convolution fusion | flops 5038080000 | bytes 14417920 | tf_op jit(solution)/shard_map/dot_general | solution.py:81
  416.3 53.0 %recur_backward.1 = (bf16[512,1280]{1,0:T(8,128)(2,1)}, bf16[256,1280]{1,0:T(8,128)(2,1)}, f32[8,640]{1,0:T(8,128)}, f32[1,640]{1,0:T(1,128)}, bf16[512,2560]{1,0:T(8,128)(2,1)}) custom-call(bf16[512,2560]{1,0:T(8,128)(2,1)} %get-tuple-element.68.refs_0_, bf16[512,512]{1,0:T(8,128)(2,1)} %get-tuple-element.115.refs_2_.refs_1_, ...), custom_call_target="tpu_custom_call" | custom-call | tf_op jit(solution)/shard_map/recur_backward/pallas_call | solution.py:1704
  470.2 4.2 convolution_convert_fusion.4.refs_6_
  475.1 5.6 convolution_convert_fusion.1.refs_5_
  480.7 96.6 %last_sums.1 = (f32[128,2560]{1,0:T(8,128)}, f32[4,2560]{1,0:T(4,128)}, f32[2,2560]{1,0:T(2,128)}, bf16[320,1280]{1,0:T(8,128)(2,1)}, bf16[320,640]{1,0:T(8,128)(2,1)}, /*index=5*/bf16[32,1280]{1,0:T(8,128)(2,1)}) custom-call(bf16[512,2560]{1,0:T(8,128)(2,1)} %get-tuple-element.78.refs_0_, bf16[128,2560]{1,0:T(8,128)(2,1)} %refs_1_.7, ...), custom_call_target="tpu_custom_call" | custom-call | tf_op jit(solution)/shard_map/last_sums/pallas_call | solution.py:1169
  578.9 1.6 convert_element_type.138
  580.5 1.4 dynamic-slice_reduce_fusion
  582.0 1.3 slice_reduce_fusion.1
  584.9 1.3 fusion.20
  586.2 2.3 multiply_convert_fusion.3
  588.5 3.2 convert_element_type.140
  591.7 65.0 %reduce-scatter.8.cloned.1.call-done = bf16[320,1920]{1,0:T(8,128)(2,1)} async-done(((bf16[2560,1920]{1,0:T(8,128)(2,1)}), bf16[320,1920]{1,0:T(8,128)(2,1)}) %reduce-scatter.8.cloned.1.call-update) | async-done | bytes 1228816 | tf_op jit(solution)/shard_map/reduce_scatter | solution.py:1868
  656.6 2.9 convert_bitcast_fusion
  659.5 1.1 copy.44
  (109 shorter events, 15.1 us)
Async XLA Ops:
  7.2 71.8 %copy-start.13 = (f32[640]{0:T(1024)S(1)}, f32[640]{0:T(1024)}, u32[]{:S(2)}) copy-start(f32[640]{0:T(1024)} %param.23) | copy-start | bytes 7684
  7.2 72.4 %copy-start.20 = (s32[3]{0:T(128)S(1)}, s32[3]{0:T(128)}, u32[]{:S(2)}) copy-start(s32[3]{0:T(128)} %param.29) | copy-start | bytes 40
  7.2 247.8 %all-gather.3.cloned.1.call-start = ((), (), s32[]{:S(2)}) async-start(), calls=%async_computation.3 | async-start | bytes 11059200 | tf_op jit(solution)/shard_map/all_gather | solution.py:1801
  75.8 5.7 copy-start.9
  75.8 200.7 %all-gather.5.cloned.1.call-start = ((), (), s32[]{:S(2)}) async-start(), calls=%async_computation.4 | async-start | bytes 11059200 | tf_op jit(solution)/shard_map/all_gather | solution.py:1802
  76.6 509.6 %reduce-scatter.4.cloned.1.call-start = ((), (), s32[]{:S(2)}) async-start(), calls=%async_computation.5 | async-start | bytes 3276800 | tf_op jit(solution)/shard_map/reduce_scatter | solution.py:1884
  81.7 2.1 copy-start.1
  151.4 88.7 %copy-start.21 = (s32[128]{0:T(128)S(1)}, s32[128]{0:T(128)}, u32[]{:S(2)}) copy-start(s32[128]{0:T(128)} %param.30) | copy-start | bytes 1540
  151.4 90.0 %copy-start.3 = (bf16[128,2560]{1,0:T(8,128)(2,1)S(1)}, bf16[128,2560]{1,0:T(8,128)(2,1)}, u32[]{:S(2)}) copy-start(bf16[128,2560]{1,0:T(8,128)(2,1)} %refs_1_.5) | copy-start | bytes 1966084
  151.4 91.0 %copy-start.5 = (bf16[512,2560]{1,0:T(8,128)(2,1)S(1)}, bf16[512,2560]{1,0:T(8,128)(2,1)}, u32[]{:S(2)}) copy-start(bf16[512,2560]{1,0:T(8,128)(2,1)} %get-tuple-element.66) | copy-start | bytes 7864324
  241.4 3.0 copy-start.16
  254.9 13.4 %copy-start.6 = (bf16[512,2560]{1,0:T(8,128)(2,1)S(1)}, bf16[512,2560]{1,0:T(8,128)(2,1)}, u32[]{:S(2)}) copy-start(bf16[512,2560]{1,0:T(8,128)(2,1)} %multiply_convert_fusion) | copy-start | bytes 7864324
  267.1 1.3 copy-start.22
  289.3 17.3 %copy-start.23 = (bf16[512,1920]{1,0:T(8,128)(2,1)}, bf16[512,1920]{1,0:T(8,128)(2,1)S(1)}, u32[]{:S(2)}) copy-start(bf16[512,1920]{1,0:T(8,128)(2,1)S(1)} %get-tuple-element.100) | copy-start | bytes 5898244
  289.3 9.0 %copy-start.17 = (bf16[512,2560]{1,0:T(8,128)(2,1)S(1)}, bf16[512,2560]{1,0:T(8,128)(2,1)}, u32[]{:S(2)}) copy-start(bf16[512,2560]{1,0:T(8,128)(2,1)} %get-tuple-element.62) | copy-start | bytes 7864324
  289.3 17.3 %slice-start = ((s8[9830400]{0:T(1024)(128)(4,1)}), s8[4194304]{0:T(1024)(128)(4,1)S(1)}, s32[]{:S(2)}) async-start(s8[9830400]{0:T(1024)(128)(4,1)} %bitcast.47), calls=%async_computation.8 | async-start | bytes 8388608
  289.3 17.3 %slice-start.1 = ((s8[9830400]{0:T(1024)(128)(4,1)}), s8[4194304]{0:T(1024)(128)(4,1)S(1)}, s32[]{:S(2)}) async-start(s8[9830400]{0:T(1024)(128)(4,1)} %bitcast.47), calls=%async_computation.9 | async-start | bytes 8388608
  298.3 8.3 %slice-start.2 = ((s8[9830400]{0:T(1024)(128)(4,1)}), s8[1441792]{0:T(1024)(128)(4,1)S(1)}, s32[]{:S(2)}) async-start(s8[9830400]{0:T(1024)(128)(4,1)} %bitcast.47), calls=%async_computation.10 | async-start | bytes 2883584
  405.2 183.3 %reduce-scatter.6.cloned.1.call-start = ((), (), s32[]{:S(2)}) async-start(), calls=%async_computation.6 | async-start | bytes 11059200 | tf_op jit(solution)/shard_map/reduce_scatter | solution.py:1880
  415.1 241.6 %reduce-scatter.8.cloned.1.call-start = ((), (), s32[]{:S(2)}) async-start(), calls=%async_computation.7 | async-start | bytes 11059200 | tf_op jit(solution)/shard_map/reduce_scatter | solution.py:1868
  416.3 53.8 %copy-start.4 = (bf16[512,2560]{1,0:T(8,128)(2,1)S(1)}, bf16[512,2560]{1,0:T(8,128)(2,1)}, u32[]{:S(2)}) copy-start(bf16[512,2560]{1,0:T(8,128)(2,1)} %get-tuple-element.68.refs_0_) | copy-start | bytes 7864324
  416.3 53.8 %copy-start.19 = (bf16[512,640]{1,0:T(8,128)(2,1)S(1)}, bf16[512,640]{1,0:T(8,128)(2,1)}, u32[]{:S(2)}) copy-start(bf16[512,640]{1,0:T(8,128)(2,1)} %get-tuple-element.85) | copy-start | bytes 1966084
  470.2 4.2 copy-start.12
  470.2 4.2 copy-start.14
  470.2 4.9 copy-start.15
  470.2 4.9 copy-start.18
  480.7 98.2 %copy-start.8 = (bf16[320,1920]{1,0:T(8,128)(2,1)S(1)}, bf16[320,1920]{1,0:T(8,128)(2,1)}, u32[]{:S(2)}) copy-start(bf16[320,1920]{1,0:T(8,128)(2,1)} %get-tuple-element.93) | copy-start | bytes 3686404
  577.4 5.9 copy-start.11
  577.4 6.6 copy-start.10
  577.4 7.5 %copy-start.2 = (bf16[320,1280]{1,0:T(8,128)(2,1)S(1)}, bf16[320,1280]{1,0:T(8,128)(2,1)}, u32[]{:S(2)}) copy-start(bf16[320,1280]{1,0:T(8,128)(2,1)} %get-tuple-element.89) | copy-start | bytes 2457604
  580.5 5.7 copy-start
  588.5 71.0 %copy-start.7 = (f32[128,2560]{1,0:T(8,128)S(1)}, f32[128,2560]{1,0:T(8,128)}, u32[]{:S(2)}) copy-start(f32[128,2560]{1,0:T(8,128)} %get-tuple-element.137) | copy-start | bytes 3932164
Sparse Core Ops, SparseCore 0:
  76.0 60.7 all-gather.2
  138.6 92.3 all-gather.4
  405.3 54.7 reduce-scatter.3
  463.6 111.9 reduce-scatter.5
  579.0 77.5 reduce-scatter.7

commit v5 on v3

--- a/solution.py
+++ b/solution.py
@@ -1028,26 +1028,36 @@
     )(terms, tokens, gain, *mats)
 
 
-def middle_sums(n_dp, n_line, terms, after, gain, grad_in, mats):
+def middle_sums(n_dp, n_line, terms, after, gain, grad_in, mat, hidden, grad_up, product, down):
     rows, width = after.shape
-    count = len(mats)
-    block = mats[0].shape[0] // n_dp
-    per = len(ReducePlane.scratch(16, 128))
+    block = mat.shape[0] // n_dp
+    wide = grad_up.shape[1]
+    spread_rows = n_line * rows
 
     def kernel(*refs):
-        s, after_ref, gain_ref, g_ref = refs[:4]
-        srcs = refs[4 : 4 + count]
-        grad_after, gain_sum, spread = refs[4 + count : 7 + count]
-        results = refs[7 + count : 7 + 2 * count]
-        rest = refs[7 + 2 * count :]
-        scratch = rest[count * per :]
+        s, after_ref, gain_ref, g_ref, src = refs[:5]
+        hid_far, gu_far, pr_far, dw_far = refs[5:9]
+        grad_after, gain_sum, spread, result, up_far, feed_far = refs[9:15]
+        hid, gu, pr, dw, up_out, feed, sems = refs[15:22]
+        rest = refs[22:]
+        fetch = Fetch(
+            [
+                (hid_far, hid),
+                (gu_far, gu),
+                (pr_far, pr),
+                (dw_far, dw),
+                (feed, feed_far),
+                (up_out.at[0], up_far.at[pl.ds(0, width // 2)]),
+                (up_out.at[1], up_far.at[pl.ds(width // 2, width // 2)]),
+            ],
+            sems,
+        )
+        fetch.start(0, 1, 2, 3)
         place = Place(n_dp, n_line)
         place.meet()
-        planes = [
-            ReducePlane(place, srcs[i], rest[i * per : (i + 1) * per]) for i in range(count)
-        ]
-        for part in planes:
-            part.begin()
+        plane = ReducePlane(place, src, rest[:7])
+        scratch = rest[7:]
+        plane.begin()
         gain_sum[...] = jnp.zeros_like(gain_sum)
 
         def norm(c, here, total):
@@ -1059,27 +1069,78 @@
             first = pl.multiple_of(place.t * rows, 16) + c * total.shape[0]
             spread[pl.ds(pl.multiple_of(first, 16), total.shape[0])] = both.astype(jnp.bfloat16)
 
-        between = {0: planes[0].cores, 3: planes[1].cores, 5: planes[0].turn}
-        sum_rows_and_spread(place, s, scratch, norm, spread, between)
-        planes[1].turn()
-        for part, result in zip(planes, results):
-            part.finish(result)
-
+        def feed_part(i):
+            cols = pl.ds(i * (width // 4), width // 4)
+            feed[:, cols] = times_trans(pr[...], dw[cols]).astype(jnp.bfloat16)
+
+        def up_part(i):
+            cols = pl.ds(i * (width // 4), width // 4)
+            here = pl.ds((i % 2) * (width // 4), width // 4)
+            up_out[i // 2, here] = trans_times(hid[:, cols], gu[...]).astype(jnp.bfloat16)
+
+        def early():
+            plane.cores()
+            fetch.wait(0, 1)
+
+        def two():
+            up_part(0)
+
+        def three():
+            up_part(1)
+            fetch.start(5)
+
+        def four():
+            up_part(2)
+
+        def five():
+            up_part(3)
+            fetch.start(6)
+            fetch.wait(2, 3)
+
+        def six():
+            feed_part(0)
+
+        def seven():
+            plane.turn()
+            feed_part(1)
+
+        def eight():
+            feed_part(2)
+
+        def nine():
+            feed_part(3)
+            fetch.start(4)
+
+        steps = {1: early, 2: two, 3: three, 4: four, 5: five, 6: six, 7: seven, 8: eight, 9: nine}
+        sum_rows_and_spread(place, s, scratch, norm, spread, steps)
+        plane.finish(result)
+        fetch.wait(4, 5, 6)
+
+    low, full = jnp.bfloat16, jnp.float32
+    near, far = in_vmem(), in_any()
     return pl.pallas_call(
         kernel,
         out_shape=(
-            shaped((rows, width), jnp.float32),
-            shaped((1, width), jnp.float32),
-            shaped((n_line * rows, width), jnp.bfloat16),
-        )
-        + tuple(shaped((block, m.shape[1]), jnp.bfloat16) for m in mats),
-        in_specs=[in_vmem()] * 4 + [in_any()] * count,
-        out_specs=[in_vmem()] * (3 + count),
-        scratch_shapes=sum([ReducePlane.scratch(block, m.shape[1]) for m in mats], [])
+            shaped((rows, width), full),
+            shaped((1, width), full),
+            shaped((spread_rows, width), low),
+            shaped((block, mat.shape[1]), low),
+            shaped((width, wide), low),
+            shaped((spread_rows, width), low),
+        ),
+        in_specs=[near] * 4 + [far] * 5,
+        out_specs=[near] * 4 + [far] * 2,
+        scratch_shapes=[vmem_like(m) for m in (hidden, grad_up, product, down)]
+        + [
+            pltpu.VMEM((2, width // 2, wide), low),
+            pltpu.VMEM((spread_rows, width), low),
+            dma_sems(7),
+        ]
+        + ReducePlane.scratch(block, mat.shape[1])
         + line_scratch(n_line, rows // CHUNKS, width),
         compiler_params=comm_params(3),
         name="middle_sums",
-    )(terms, after, gain, grad_in, *mats)
+    )(terms, after, gain, grad_in, mat, hidden, grad_up, product, down)
 
 
 class Exchange:
@@ -1269,6 +1330,25 @@
         return pl.ds(pl.multiple_of(self.first + index * size, RIM), size)
 
 
+class Fetch:
+    def __init__(self, pairs, sems):
+        self.copies = [
+            pltpu.make_async_copy(src, dst, sems.at[i]) for i, (src, dst) in enumerate(pairs)
+        ]
+
+    def start(self, *which):
+        for i in which:
+            self.copies[i].start()
+
+    def wait(self, *which):
+        for i in which:
+            self.copies[i].wait()
+
+
+def vmem_like(array):
+    return pltpu.VMEM(array.shape, array.dtype)
+
+
 def recur_forward(
     n_dp,
     n_line,
@@ -1295,11 +1375,16 @@
     parts = 1
 
     def kernel(*refs):
-        (tok, cot_ref, plc, sto, wx, wy, wo, gain_ref, gw, cw, sp, fl) = refs[:12]
-        (hp, xext, y, conv_low, conv, pre_r, pre_i, rate, state, merged_st, terms, cot_all) = refs[
-            12:24
-        ]
-        (h, xf, local, cum, merged, agg, slots, hs, hr, es, er, el, gs, gr, gl) = refs[24:]
+        (tok_far, cot_ref, plc, sto, wx_far, wy_far, wo_far, gain_ref, gw, cw, sp, fl) = refs[:12]
+        far, cot_all = refs[12:23], refs[23]
+        tok, wx, wy, wo = refs[24:28]
+        results = refs[28:39]
+        hp, xext, y, conv_low, conv, pre_r, pre_i, rate, state, merged_st, terms = results
+        (h, xf, local, cum, merged, agg, slots, hs, hr, es, er, el, gs, gr, gl) = refs[39:54]
+        in_sems, out_sems = refs[54:]
+        fetch = Fetch(((tok_far, tok), (wx_far, wx), (wy_far, wy), (wo_far, wo)), in_sems)
+        store = Fetch(zip(results, far), out_sems)
+        fetch.start(0, 1, 2, 3)
         place = Place(n_dp, n_line)
         place.meet(True)
         swap = RimSwap(place, own)
@@ -1318,7 +1403,9 @@
             here = tile_rows(i, TILE)
             h[here] = rms_scale(tok[here].astype(jnp.float32), gain_ref[...]).astype(jnp.bfloat16)
 
+        fetch.wait(0)
         loop(rows // TILE, norm)
+        fetch.wait(1)
 
         def project(i):
             here = tile_rows(i, 128)
@@ -1326,6 +1413,7 @@
             xext[tile_rows(i, 128, 16)] = plain_dot(hp[here], wx[...]).astype(jnp.bfloat16)
 
         loop(rows // 128, project)
+        store.start(0)
         edge = remote(
             xext.at[pl.ds(rows, 16)],
             xext.at[pl.ds(0, 16)],
@@ -1341,10 +1429,13 @@
             here = tile_rows(i, 128)
             y[here] = plain_dot(hp[here], wy[...])
 
+        fetch.wait(2)
         loop(rows // 128, project_y)
+        store.start(2)
         edge.wait()
         top = xext[pl.ds(0, 16)]
         xext[pl.ds(0, 16)] = jnp.where(place.d > 0, top, jnp.zeros_like(top))
+        store.start(1)
 
         def widen(i):
             xf[tile_rows(i, TILE)] = xext[tile_rows(i, TILE)].astype(jnp.float32)
@@ -1362,6 +1453,7 @@
             conv_low[here, RIM : RIM + own] = total.astype(jnp.bfloat16)
 
         loop(rows // TILE, convolve)
+        store.start(4)
         rim = remote(
             conv_low.at[:, swap.edge],
             conv_low.at[:, swap.over_there],
@@ -1379,6 +1471,8 @@
             pre_r[:, cols] = plain_dot(conv_low[:, cols], gw[:, cols])
             pre_i[:, cols] = plain_dot(conv_low[:, cols], gw[:, other])
 
+        store.start(3, 5, 6)
+
         def drive(i):
             here = tile_rows(i, TILE)
             start = fl[tile_rows(i, TILE, 8)][:, 0:1] > 0.0
@@ -1388,6 +1482,7 @@
             put_lanes(local, here, conv[here] * jax.nn.sigmoid(pre_i[here, own_cols]) * scale)
 
         loop(rows // TILE, drive)
+        store.start(7)
         for line in lines:
             line.step(2)
         groups = own // LANES
@@ -1433,7 +1528,11 @@
             loop(chunk // TILE, settle)
             last = pl.ds(j * chunk + chunk - 1, 1)
             entry = take_lanes(local, last) + take_lanes(cum, last) * entry
+        store.start(8)
         merged_st[...] = plain_dot(sto[...], merged[...]).astype(jnp.bfloat16)
+
+        store.start(9)
+        fetch.wait(3)
 
         def mix(i):
             some = tile_rows(i, 512)
@@ -1445,27 +1544,31 @@
         for line in lines:
             line.finish()
         keep.wait()
+        store.start(10)
+        store.wait(*range(11))
 
     low, full = jnp.bfloat16, jnp.float32
+    results = (
+        shaped((rows, width), low),
+        shaped((rows + 16, own), low),
+        shaped((rows, own), full),
+        shaped((rows, wide), low),
+        shaped((rows, own), full),
+        shaped((rows, wide), full),
+        shaped((rows, wide), full),
+        shaped((own // LANES, rows, LANES), full),
+        shaped((rows + 8, own), full),
+        shaped((rows, own), low),
+        shaped((rows, width), low),
+    )
+    near, far = in_vmem(), in_any()
     return pl.pallas_call(
         kernel,
-        out_shape=(
-            shaped((rows, width), low),
-            shaped((rows + 16, own), low),
-            shaped((rows, own), full),
-            shaped((rows, wide), low),
-            shaped((rows, own), full),
-            shaped((rows, wide), full),
-            shaped((rows, wide), full),
-            shaped((own // LANES, rows, LANES), full),
-            shaped((rows + 8, own), full),
-            shaped((rows, own), low),
-            shaped((rows, width), low),
-            shaped((n_line * cot_rows, width), low),
-        ),
-        in_specs=[in_vmem(), in_any()] + [in_vmem()] * 10,
-        out_specs=[in_vmem()] * 11 + [in_any()],
-        scratch_shapes=[
+        out_shape=results + (shaped((n_line * cot_rows, width), low),),
+        in_specs=[far, far, near, near, far, far, far] + [near] * 5,
+        out_specs=[far] * 12,
+        scratch_shapes=[vmem_like(m) for m in (tok_all, x_full, y_full, out_full) + results]
+        + [
             pltpu.VMEM((rows, width), low),
             pltpu.VMEM((rows + 16, own), full),
             pltpu.VMEM((own // LANES, rows, LANES), full),
@@ -1481,6 +1584,8 @@
             dma_sems(parts, 2, n_line - 1),
             dma_sems(parts, 2, n_line - 1),
             pltpu.SemaphoreType.DMA,
+            dma_sems(4),
+            dma_sems(11),
         ],
         compiler_params=comm_params(5),
         name="recur_forward",
@@ -1515,6 +1620,7 @@
     slope,
     flags,
     kept,
+    weight_terms,
 ):
     rows, width = mixer_in.shape
     count, own = taps.shape
@@ -1524,15 +1630,38 @@
     chunk = rows // 8
 
     def kernel(*refs):
-        (mix, plc, sto, wx, wy, wo, gw, cw, sp, sg, fl) = refs[:11]
-        (xext, y, conv_low, conv, pre_r, pre_i, rate, state) = refs[11:19]
-        (gxy, gate_grads, tap_grads, decay_grad, terms) = refs[19:24]
-        (mp, gm, lam, reach, gp_r, gp_i, grad, spread, rim_out, rim_in, ret_out, ret_in) = refs[
-            24:36
-        ]
-        (tap_sums, decay_sums, ends, agg, slots, hs, hr, es, er, el) = refs[36:]
+        (mix_far, plc, sto, wx_far, wy_far, wo_far, gw, cw, sp, sg, fl) = refs[:11]
+        kept_far, weights = refs[11:19], refs[19]
+        (gxy_far, gate_grads, tap_grads, decay_grad, terms_far, weight_sum) = refs[20:26]
+        mix, wx, wy, wo = refs[26:30]
+        (xext, y, conv_low, conv, pre_r, pre_i, rate, state) = refs[30:38]
+        (gxy, mp, gm, lam, reach, gp_r, gp_i, grad, spread, rim_out, rim_in) = refs[38:49]
+        (ret_out, ret_in, tap_sums, decay_sums, ends, agg, slots) = refs[49:56]
+        (hs, hr, es, er, el, in_sems, out_sems) = refs[56:63]
+        terms = mix
+        fetch = Fetch(
+            [
+                (mix_far, mix),
+                (wo_far, wo),
+                (kept_far[1], y),
+                (kept_far[7], state),
+                (kept_far[6], rate),
+                (kept_far[4], pre_r),
+                (kept_far[5], pre_i),
+                (kept_far[3], conv),
+                (kept_far[2], conv_low),
+                (kept_far[0], xext),
+                (wx_far, wx),
+                (wy_far, wy),
+            ],
+            in_sems,
+        )
+        fetch.start(*range(12))
+        store = Fetch(((gxy, gxy_far), (terms, terms_far)), out_sems)
         place = Place(n_dp, n_line)
         place.meet(True)
+        plane = ReducePlane(place, weights, refs[63:])
+        plane.begin()
         swap = RimSwap(place, own)
         own_cols = pl.ds(RIM, own)
 
@@ -1541,6 +1670,7 @@
             mp[here] = plain_dot(plc[here], mix[...]).astype(jnp.bfloat16)
             gm[here] = plain_dot(mp[here], wo[...])
 
+        fetch.wait(0, 1)
         loop(rows // 128, project)
 
         def split(i):
@@ -1551,7 +1681,10 @@
             values = state[tile_rows(i, TILE, 8)]
             gxy[here, own:] = (grads * values * slope_y).astype(jnp.bfloat16)
 
+        fetch.wait(2, 3)
         loop(rows // TILE, split)
+        plane.cores()
+        fetch.wait(4)
         groups = own // LANES
 
         def scan(i, carry):
@@ -1585,6 +1718,7 @@
         for q in reversed(range(n_dp)):
             longer = slots[q, 1:2] + slots[q, 0:1] * entry
             entry = jnp.where(q > place.d, longer, entry)
+        fetch.wait(5, 6, 7)
         for ref in (tap_sums, decay_sums):
             ref[...] = jnp.zeros_like(ref)
         for ref in (gp_r, gp_i):
@@ -1656,6 +1790,7 @@
             (lax.rem(place.d + n_dp - 1, n_dp), place.t),
         )
         ret.start()
+        fetch.wait(8)
         for i in range(blocks):
             cols = swap.block(i, size)
             spread[0:size, cols] = trans_times(conv_low[:, cols], gp_r[:, cols])
@@ -1683,6 +1818,7 @@
                 total = total + jnp.concatenate([jnp.zeros((8, own), jnp.float32), added], axis=0)
             gxy[here, 0:own] = total.astype(jnp.bfloat16)
 
+        fetch.wait(9)
         loop(rows // TILE - 1, taps_back)
         ret.wait()
         taps_back(rows // TILE - 1, jnp.where(place.d < n_dp - 1, ret_in[...], 0.0))
@@ -1690,6 +1826,9 @@
         for k in range(count):
             tap_grads[k : k + 1] = jnp.sum(tap_sums[k], axis=0, keepdims=True)
 
+        store.start(0)
+        plane.turn()
+
         def restore(i):
             here = tile_rows(i, 128)
             mp[here, 0 : 2 * own] = plain_dot(sto[here], gxy[...]).astype(jnp.bfloat16)
@@ -1702,9 +1841,15 @@
                 times_trans(mp[:, 0:own], wx[some]) + times_trans(mp[:, own : 2 * own], wy[some])
             ).astype(jnp.bfloat16)
 
+        fetch.wait(10, 11)
         loop(width // 512, spread_back)
+        store.start(1)
+        plane.finish(weight_sum)
+        store.wait(0, 1)
 
     low, full = jnp.bfloat16, jnp.float32
+    block = weight_terms.shape[0] // n_dp
+    near, far = in_vmem(), in_any()
     return pl.pallas_call(
         kernel,
         out_shape=(
@@ -1713,10 +1858,13 @@
             shaped((8, own), full),
             shaped((1, own), full),
             shaped((rows, width), low),
+            shaped((block, weight_terms.shape[1]), low),
         ),
-        in_specs=[in_vmem()] * 19,
-        out_specs=[in_vmem()] * 5,
-        scratch_shapes=[
+        in_specs=[far, near, near, far, far, far] + [near] * 5 + [far] * 9,
+        out_specs=[far, near, near, near, far, near],
+        scratch_shapes=[vmem_like(m) for m in (mixer_in, x_full, y_full, out_full, *kept)]
+        + [
+            pltpu.VMEM((rows, 2 * own), low),
             pltpu.VMEM((rows, width), low),
             pltpu.VMEM((rows, own), full),
             pltpu.VMEM((own // LANES, rows, LANES), full),
@@ -1739,7 +1887,10 @@
             dma_sems(n_dp),
             dma_sems(n_dp),
             pltpu.SemaphoreType.DMA,
-        ],
+            dma_sems(12),
+            dma_sems(2),
+        ]
+        + ReducePlane.scratch(block, weight_terms.shape[1]),
         compiler_params=comm_params(6),
         name="recur_backward",
     )(
@@ -1755,6 +1906,7 @@
         slope,
         flags,
         *kept,
+        weight_terms,
     )
 
 
@@ -1824,8 +1976,8 @@
     ]
     columns += [jnp.zeros_like(starts)] * (8 - len(columns))
     flags = (jnp.stack(columns, axis=1) & inside[:, None]).astype(jnp.float32)
-    live_stored = (order_all + dp_index * row_count < ends[-1]).astype(jnp.float32)
     live_own = (token_order < ends[-1]).astype(jnp.float32)
+    grad_in_own = (cotangent.astype(jnp.float32) * live_own[:, None]).astype(jnp.bfloat16)
     soft = jax.nn.softplus(-decay_param).reshape(1, own_width)
     slope = jax.nn.sigmoid(-decay_param).reshape(1, own_width)
     zero_rim = jnp.zeros((block_size, RIM), jnp.bfloat16)
@@ -1843,11 +1995,11 @@
     def glu(gate_pre, up_pre):
         return gelu_tanh(gate_pre) * up_pre
 
-    hidden_place, *kept, merged_stored, mixer_terms, cot_all = recur_forward(
+    hidden_place, *kept, merged_stored, mixer_terms, down_in = recur_forward(
         n_dp,
         n_tensor,
         tok_all,
-        cotangent,
+        grad_in_own,
         to_place,
         to_stored,
         x_full,
@@ -1866,8 +2018,6 @@
     up_pre = plain_dot(hidden_two, up_full)
     glu_out, glu_pull = jax.vjp(glu, gate_pre, up_pre)
     product = glu_out.astype(jnp.bfloat16)
-    down_in = (cot_all.astype(jnp.float32) * live_stored[:, None]).astype(jnp.bfloat16)
-    grad_in_own = (cotangent.astype(jnp.float32) * live_own[:, None]).astype(jnp.bfloat16)
     grad_down = trans_times(down_in, product).astype(jnp.bfloat16)
     down_sum = lax.psum_scatter(grad_down, "dp", scatter_dimension=0, tiled=True)
     down_in, _ = lax.optimization_barrier((down_in, grad_down))
@@ -1876,23 +2026,31 @@
     grad_gate_pre = grad_gate_pre.astype(jnp.bfloat16)
     grad_up_pre = grad_up_pre.astype(jnp.bfloat16)
     grad_gate = trans_times(hidden_two, grad_gate_pre).astype(jnp.bfloat16)
-    grad_up = trans_times(hidden_two, grad_up_pre).astype(jnp.bfloat16)
     back_terms = (
         times_trans(grad_gate_pre, gate_full) + times_trans(grad_up_pre, up_full)
     ).astype(jnp.bfloat16)
-    feed_terms = times_trans(product, down_full).astype(jnp.bfloat16)
-    grad_after_own, second_part, mixer_in, gate_sum, up_sum = middle_sums(
-        n_dp, n_tensor, back_terms, after_own, second_gain, grad_in_own, (grad_gate, grad_up)
+    grad_after_own, second_part, mixer_in, gate_sum, grad_up, feed_terms = middle_sums(
+        n_dp,
+        n_tensor,
+        back_terms,
+        after_own,
+        second_gain,
+        grad_in_own,
+        grad_gate,
+        hidden_two,
+        grad_up_pre,
+        product,
+        down_full,
     )
     feed_out = lax.psum_scatter(
-        lax.optimization_barrier((feed_terms, mixer_in))[0],
+        feed_terms,
         "tensor",
         scatter_dimension=0,
         tiled=True,
     ).astype(jnp.float32)
     output = ((after_own + feed_out) * live_own[:, None]).astype(jnp.bfloat16)
 
-    grad_xy, gate_grads, tap_grads, decay_grad, one_terms = recur_backward(
+    grad_xy, gate_grads, tap_grads, decay_grad, one_terms, up_sum = recur_backward(
         n_dp,
         n_tensor,
         mixer_in,
@@ -1907,6 +2065,7 @@
         slope,
         flags,
         kept,
+        grad_up,
     )
     grad_out_mat = trans_times(mixer_in, merged_stored).astype(jnp.bfloat16)
     grad_xy_mat = trans_times(hidden_place, grad_xy).astype(jnp.bfloat16)

time: 606 us -> 577 us (0.952)
  matrix products: 91.1 us -> 74.7 us
  Pallas kernels: 456 us -> 441 us
    pallas_call x2, Pallas kernels: 177 us -> 143 us  [the longest x1 83.8 us: middle_sums(): pl.pallas_call(kernel, out_shape=(shaped((rows, width), full), shaped((1,...]
    pallas_call x1, Pallas kernels: 51.6 us -> 71.1 us  [recur_backward(): pl.pallas_call(kernel, out_shape=(shaped((rows, 2 * own), low), shaped((s...]
    dot_general x3 -> x2, matrix products: 26.3 us -> 16.2 us  [times_trans(): lax.dot_general(left, right, (((1,), (1,)), ((), ())), preferred_element_...]
    dot_general x5 -> x4, matrix products: 34.1 us -> 25.8 us  [trans_times(): lax.dot_general(left, right, (((0,), (0,)), ((), ())), preferred_element_...]
  transfers between devices with their start and end apart: 3 -> 3, of which waited for: 0 -> 0; matrix products, arithmetic and copies ran while one was open for 20% -> 18% of each run, Pallas kernels for 65% -> 66%
where the time goes in v5:
time: 577 us; the launch traced here: 570 us
  Pallas kernels  441 us (76%)
  matrix products  74.7 us (13%)
  other arithmetic  19.4 us (3%)
  local copies, waits for them, and re-layouts  19.1 us (3%)
  between operations  14.6 us (3%)
    pallas_call x1, Pallas kernels, middle_gather(): pl.pallas_call(kernel, out_shape=(shaped((rows, width), jnp.float32), sha...  95 us
    pallas_call x1, Pallas kernels, middle_sums(): pl.pallas_call(kernel, out_shape=(shaped((rows, width), full), shaped((1,...  83.8 us
    pallas_call x1, Pallas kernels, recur_backward(): pl.pallas_call(kernel, out_shape=(shaped((rows, 2 * own), low), shaped((s...  71.1 us
    pallas_call x1, Pallas kernels, last_sums(): pl.pallas_call(kernel, out_shape=(shaped((rows, width), jnp.float32), sha...  67.4 us
    pallas_call x1, Pallas kernels, first_gather(): pl.pallas_call(kernel, out_shape=tuple((shaped((n_dp * m.shape[0], m.shap...  65.1 us
    pallas_call x1, Pallas kernels, recur_forward(): pl.pallas_call(kernel, out_shape=results + (shaped((n_line * cot_rows, wi...  58.9 us
    dot_general x3, matrix products, plain_dot(): return jnp.dot(left, right, preferred_element_type=jnp.float32)  32.7 us
    dot_general x4, matrix products, trans_times(): lax.dot_general(left, right, (((0,), (0,)), ((), ())), preferred_element_...  25.8 us
  transfers between devices with their start and end apart: 3, of which 0 were waited for; matrix products, arithmetic and copies ran while one was open for 18% of the time, Pallas kernels for 66%

profile of v5, /device:TPU:0, one launch (start us, length us, event | category | flops | bytes accessed | tf_op | source)
XLA Modules:
  0.0 569.6 jit_solution(6816029707010596133)
XLA Ops:
  8.7 1.4 pad_maximum_fusion.refs_3_
  10.7 65.1 %first_gather.1 = (bf16[2560,640]{1,0:T(8,128)(2,1)}, bf16[2560,640]{1,0:T(8,128)(2,1)}, bf16[2560,640]{1,0:T(8,128)(2,1)}, bf16[256,1408]{1,0:T(8,128)(2,1)}, b...) custom-call(bf16[320,640]{1,0:T(8,128)(2,1)} %refs_0_.1, bf16[320,640]{1,0:T(8,128)(2,1)} %refs_1_.3, ...), custom_call_target="tpu_custom_call" | custom-call | tf_op jit(solution)/shard_map/first_gather/pallas_call | solution.py:896
  80.8 1.0 slice_dynamic-update-slice_fusion.1
  81.8 1.1 slice_dynamic-update-slice_fusion
  84.5 1.1 fusion.8
  85.6 1.0 multiply_convert_fusion.3.refs_1_.refs_3_
  86.6 58.9 %recur_forward.1 = (bf16[512,2560]{1,0:T(8,128)(2,1)}, bf16[528,640]{1,0:T(8,128)(2,1)}, f32[512,640]{1,0:T(8,128)}, bf16[512,896]{1,0:T(8,128)(2,1)}, f32[512,6...) custom-call(bf16[512,2560]{1,0:T(8,128)(2,1)} %get-tuple-element.56., ...), custom_call_target="tpu_custom_call" | custom-call | tf_op jit(solution)/shard_map/recur_forward/pallas_call | solution.py:1565
  145.5 95.0 %middle_gather.1 = (f32[128,2560]{1,0:T(8,128)}, bf16[512,2560]{1,0:T(8,128)(2,1)}, bf16[2560,1920]{1,0:T(8,128)(2,1)}, bf16[2560,1920]{1,0:T(8,128)(2,1)}) custom-call(bf16[512,2560]{1,0:T(8,128)(2,1)} %get-tuple-element.62.refs_0_, bf16[128,2560]{1,0:T(8,128)(2,1)} %refs_1_.5, f32[1,2560]{1,0:T(1,128)} %reshape.180.refs_2_, bf16[320,1920]{1,0:T(8,128)(2,1)} %refs_3_.1, ...), custom_call_target="tpu_custom_call" | custom-call | tf_op jit(solution)/shard_map/middle_gather/pallas_call | solution.py:1015
  240.5 10.3 %fusion.22 = f32[512,1920]{1,0:T(8,128)S(1)} fusion(bf16[512,2560]{1,0:T(8,128)(2,1)} %get-tuple-element.65.refs_5_, bf16[2560,1920]{1,0:T(8,128)(2,1)} %get-tuple-element.66), kind=kOutput, calls=%fused_computation.68 | convolution fusion | flops 5033164800 | bytes 16384000 | tf_op jit(solution)/shard_map/dot_general | solution.py:71
  250.8 7.9 %multiply_convert_fusion.1 = (bf16[512,1920]{1,0:T(8,128)(2,1)S(1)}, f32[512,1920]{1,0:T(8,128)}) fusion(f32[512,1920]{1,0:T(8,128)S(1)} %fusion.22, bf16[512,2560]{1,0:T(8,128)(2,1)S(1)} %copy-done.3, bf16[2560,1920]{1,0:T(8,128)(2,1)S(1)} %copy-done.12), kind=kOutput, calls=%fused_computation.15 | convolution fusion | flops 5042995200 | bytes 22282240 | tf_op jit(solution)/shard_map/dot_general | solution.py:71
  258.7 1.3 copy-done.4
  260.0 8.1 %convolution_convert_fusion.2 = bf16[2560,1920]{1,0:T(8,128)(2,1)} fusion(bf16[512,2560]{1,0:T(8,128)(2,1)S(1)} %copy-done.14, bf16[512,1920]{1,0:T(8,128)(2,1)S(1)} %get-tuple-element.120.refs_7_), kind=kOutput, calls=%fused_computation.2 | convolution fusion | flops 5038080000 | bytes 14417920 | tf_op jit(solution)/shard_map/dot_general | solution.py:81
  268.6 14.6 %multiply_convert_fusion = (bf16[512,1920]{1,0:T(8,128)(2,1)S(1)}, bf16[512,1920]{1,0:T(8,128)(2,1)S(1)}) fusion(f32[512,1920]{1,0:T(8,128)} %copy-done.19, f32[512,1920]{1,0:T(8,128)} %get-tuple-element.121, bf16[512,2560]{1,0:T(8,128)(2,1)} %get-tuple-element.68, bf16[2560,1920]{1,0:T(8,128)(2,1)} %all-gather.2.cloned.1.call-done.refs_8_), kind=kOutput, calls=%fused_computation.14 | convolution fusion | flops 5056757760 | bytes 24248320 | tf_op jit(solution)/shard_map/dot_general | solution.py:71
  283.2 9.2 %fusion.23 = f32[512,2560]{1,0:T(8,128)S(1)} fusion(bf16[512,1920]{1,0:T(8,128)(2,1)S(1)} %get-tuple-element.105, bf16[2560,1920]{1,0:T(8,128)(2,1)} %get-tuple-element.66), kind=kOutput, calls=%fused_computation.69 | convolution fusion | flops 5033164800 | bytes 17039360 | tf_op jit(solution)/shard_map/dot_general | solution.py:75
  292.5 8.1 %convolution_convert_fusion.1.refs_4_ = bf16[2560,1920]{1,0:T(8,128)(2,1)} fusion(bf16[512,2560]{1,0:T(8,128)(2,1)S(1)} %copy-done.3, bf16[512,1920]{1,0:T(8,128)(2,1)S(1)} %get-tuple-element.105), kind=kOutput, calls=%fused_computation.1 | convolution fusion | flops 5038080000 | bytes 14417920 | tf_op jit(solution)/shard_map/dot_general | solution.py:81
  300.6 7.0 %add_convert_fusion.refs_0_ = bf16[512,2560]{1,0:T(8,128)(2,1)} fusion(f32[512,2560]{1,0:T(8,128)S(1)} %fusion.23, bf16[512,1920]{1,0:T(8,128)(2,1)S(1)} %get-tuple-element.104.refs_6_, bf16[2560,1920]{1,0:T(8,128)(2,1)S(1)} %bitcast.43), kind=kOutput, calls=%fused_computation.5 | convolution fusion | flops 5035786240 | bytes 19660800 | tf_op jit(solution)/shard_map/dot_general | solution.py:75
  307.6 83.8 %middle_sums.1 = (f32[128,2560]{1,0:T(8,128)}, f32[1,2560]{1,0:T(1,128)}, bf16[512,2560]{1,0:T(8,128)(2,1)}, bf16[320,1920]{1,0:T(8,128)(2,1)}, bf16[2560,1920]{1,0:T(8,128)(2,1)}, /*index=5*/bf16[512,2560]{1,0:T(8,128)(2,1)}) custom-call(bf16[512,2560]{1,0:T(8,128)(2,1)} %add_convert_fusion.refs_0_, f32[128,2560]{1,0:T(8,128)} %get-tuple-element.63.refs_1_, ...), custom_call_target="tpu_custom_call" | custom-call | tf_op jit(solution)/shard_map/middle_sums/pallas_call | solution.py:1121
  392.0 2.9 convert_bitcast_fusion
  394.9 71.1 %recur_backward.1 = (bf16[512,1280]{1,0:T(8,128)(2,1)}, bf16[256,1280]{1,0:T(8,128)(2,1)}, f32[8,640]{1,0:T(8,128)}, f32[1,640]{1,0:T(1,128)}, bf16[512,2560]{1,0:T(8,128)(2,1)}, /*index=5*/bf16[320,1920]{1,0:T(8,128)(2,1)}) custom-call(bf16[512,2560]{1,0:T(8,128)(2,1)} %get-tuple-element.71.refs_0_, bf16[512,512]{1,0:T(8,128)(2,1)} %get-tuple-element.119.refs_2_.refs_1_, ...), custom_call_target="tpu_custom_call" | custom-call | tf_op jit(solution)/shard_map/recur_backward/pallas_call | solution.py:1853
  466.9 3.0 convert_element_type.116
  469.9 1.6 convert_element_type.115
  471.6 4.0 convolution_convert_fusion.3.refs_6_
  476.2 5.6 convolution_convert_fusion.refs_5_
  481.8 67.4 %last_sums.1 = (f32[128,2560]{1,0:T(8,128)}, f32[4,2560]{1,0:T(4,128)}, f32[2,2560]{1,0:T(2,128)}, bf16[320,1280]{1,0:T(8,128)(2,1)}, bf16[320,640]{1,0:T(8,128)(2,1)}, /*index=5*/bf16[32,1280]{1,0:T(8,128)(2,1)}) custom-call(bf16[512,2560]{1,0:T(8,128)(2,1)} %get-tuple-element.81.refs_0_, bf16[128,2560]{1,0:T(8,128)(2,1)} %refs_1_.5, ...), custom_call_target="tpu_custom_call" | custom-call | tf_op jit(solution)/shard_map/last_sums/pallas_call | solution.py:1234
  549.2 0.9 slice_reduce_fusion
  550.8 1.4 dynamic-slice_reduce_fusion
  552.2 1.3 slice_reduce_fusion.1
  553.5 1.5 fusion.20
  555.0 2.0 convert_bitcast_fusion.1
  557.0 2.4 fusion.19
  559.4 2.1 multiply_convert_fusion.2
  561.6 1.1 copy.44
  (91 shorter events, 11.9 us)
Async XLA Ops:
  7.2 75.7 %copy-start.18 = (s32[128]{0:T(128)S(1)}, s32[128]{0:T(128)}, u32[]{:S(2)}) copy-start(s32[128]{0:T(128)} %param.30) | copy-start | bytes 1540
  7.2 68.7 %copy-start.17 = (s32[3]{0:T(128)S(1)}, s32[3]{0:T(128)}, u32[]{:S(2)}) copy-start(s32[3]{0:T(128)} %param.29) | copy-start | bytes 40
  7.2 69.5 %copy-start.10 = (f32[640]{0:T(1024)S(1)}, f32[640]{0:T(1024)}, u32[]{:S(2)}) copy-start(f32[640]{0:T(1024)} %param.23) | copy-start | bytes 7684
  7.2 261.4 %all-gather.2.cloned.1.call-start = ((), (), s32[]{:S(2)}) async-start(), calls=%async_computation.2 | async-start | bytes 11059200 | tf_op jit(solution)/shard_map/all_gather | solution.py:1956
  10.7 74.9 %copy-start.8 = (bf16[128,2560]{1,0:T(8,128)(2,1)S(1)}, bf16[128,2560]{1,0:T(8,128)(2,1)}, u32[]{:S(2)}) copy-start(bf16[128,2560]{1,0:T(8,128)(2,1)} %param.31) | copy-start | bytes 1966084
  75.8 316.2 %reduce-scatter.5.cloned.1.call-start = ((), (), s32[]{:S(2)}) async-start(), calls=%async_computation.4 | async-start | bytes 11059200 | tf_op jit(solution)/shard_map/reduce_scatter | solution.py:2022
  82.9 3.7 copy-start.1
  240.5 10.3 %copy-start.3 = (bf16[512,2560]{1,0:T(8,128)(2,1)S(1)}, bf16[512,2560]{1,0:T(8,128)(2,1)}, u32[]{:S(2)}) copy-start(bf16[512,2560]{1,0:T(8,128)(2,1)} %get-tuple-element.65.refs_5_) | copy-start | bytes 7864324
  240.5 10.3 %copy-start.12 = (bf16[2560,1920]{1,0:T(8,128)(2,1)S(1)}, bf16[2560,1920]{1,0:T(8,128)(2,1)}, u32[]{:S(2)}) copy-start(bf16[2560,1920]{1,0:T(8,128)(2,1)} %get-tuple-element.67) | copy-start | bytes 29491204
  250.8 8.0 %copy-start.19 = (f32[512,1920]{1,0:T(8,128)}, f32[512,1920]{1,0:T(8,128)S(1)}, u32[]{:S(2)}) copy-start(f32[512,1920]{1,0:T(8,128)S(1)} %fusion.22) | copy-start | bytes 11796484
  250.8 9.2 %copy-start.14 = (bf16[512,2560]{1,0:T(8,128)(2,1)S(1)}, bf16[512,2560]{1,0:T(8,128)(2,1)}, u32[]{:S(2)}) copy-start(bf16[512,2560]{1,0:T(8,128)(2,1)} %get-tuple-element.68) | copy-start | bytes 7864324
  258.7 1.3 copy-start.4
  268.1 291.3 %reduce-scatter.3.cloned.1.call-start = ((), (), s32[]{:S(2)}) async-start(), calls=%async_computation.3 | async-start | bytes 3276800 | tf_op jit(solution)/shard_map/reduce_scatter | solution.py:2045
  283.2 17.4 %copy-start.5 = (bf16[512,1920]{1,0:T(8,128)(2,1)}, bf16[512,1920]{1,0:T(8,128)(2,1)S(1)}, u32[]{:S(2)}) copy-start(bf16[512,1920]{1,0:T(8,128)(2,1)S(1)} %get-tuple-element.104.refs_6_) | copy-start | bytes 5898244
  283.2 17.4 %slice-start = ((s8[9830400]{0:T(1024)(128)(4,1)}), s8[4194304]{0:T(1024)(128)(4,1)S(1)}, s32[]{:S(2)}) async-start(s8[9830400]{0:T(1024)(128)(4,1)} %bitcast.42), calls=%async_computation.5 | async-start | bytes 8388608
  283.2 17.4 %slice-start.1 = ((s8[9830400]{0:T(1024)(128)(4,1)}), s8[4194304]{0:T(1024)(128)(4,1)S(1)}, s32[]{:S(2)}) async-start(s8[9830400]{0:T(1024)(128)(4,1)} %bitcast.42), calls=%async_computation.6 | async-start | bytes 8388608
  292.4 8.1 %slice-start.2 = ((s8[9830400]{0:T(1024)(128)(4,1)}), s8[1441792]{0:T(1024)(128)(4,1)S(1)}, s32[]{:S(2)}) async-start(s8[9830400]{0:T(1024)(128)(4,1)} %bitcast.42), calls=%async_computation.7 | async-start | bytes 2883584
  466.0 3.9 copy-start.7
  466.9 4.7 copy-start.2
  466.9 4.7 copy-start.16
  471.5 4.0 copy-start.9
  471.5 4.0 copy-start.11
  471.5 4.7 copy-start.13
  471.5 4.7 copy-start.15
  549.2 10.2 %copy-start = (f32[128,2560]{1,0:T(8,128)S(1)}, f32[128,2560]{1,0:T(8,128)}, u32[]{:S(2)}) copy-start(f32[128,2560]{1,0:T(8,128)} %get-tuple-element.63.refs_1_) | copy-start | bytes 3932164
  555.0 6.6 %copy-start.6 = (f32[128,2560]{1,0:T(8,128)S(1)}, f32[128,2560]{1,0:T(8,128)}, u32[]{:S(2)}) copy-start(f32[128,2560]{1,0:T(8,128)} %get-tuple-element.141) | copy-start | bytes 3932164
Sparse Core Ops, SparseCore 0:
  76.0 60.9 all-gather.1
  268.3 90.6 reduce-scatter.4
  391.5 51.0 reduce-scatter.2

commit v6 on v5

--- a/solution.py
+++ b/solution.py
@@ -488,11 +488,47 @@
         pl.semaphore_wait(barrier, 3 + below.astype(jnp.int32) + above.astype(jnp.int32))
 
 
+class Fetch:
+    def __init__(self, pairs, sems):
+        self.copies = [
+            pltpu.make_async_copy(src, dst, sems.at[i]) for i, (src, dst) in enumerate(pairs)
+        ]
+
+    def start(self, *which):
+        for i in which:
+            self.copies[i].start()
+
+    def wait(self, *which):
+        for i in which:
+            self.copies[i].wait()
+
+
+def vmem_like(array):
+    return pltpu.VMEM(array.shape, array.dtype)
+
+
+class Kept:
+    def __init__(self, src, dst, held, sems):
+        self.there = pltpu.make_async_copy(src, held, sems.at[0])
+        self.back = pltpu.make_async_copy(held, dst, sems.at[1])
+
+    def begin(self):
+        self.there.start()
+
+    def turn(self):
+        self.there.wait()
+        self.back.start()
+
+    def finish(self):
+        self.back.wait()
+
+
 class GatherPlane:
-    def __init__(self, place, src, dst, send, recv, local):
+    def __init__(self, place, src, dst, send, recv, local, held):
         self.p, self.src, self.dst = place, src, dst
         self.rows = src.shape[0]
-        self.send, self.recv, self.local = send, recv, local
+        self.send, self.recv = send, recv
+        self.keep = Kept(src, self.block(0, 0), held, local)
 
     def block(self, fx, fy, fc=0, part=None):
         first = self.p.chip(fx, fy, fc) * self.rows
@@ -504,9 +540,6 @@
 
     def copy(self, i, src, dst, device):
         return remote(src, dst, self.send.at[i], self.recv.at[i], device)
-
-    def mine(self):
-        return pltpu.make_async_copy(self.src, self.block(0, 0), self.local)
 
     def outgoing(self, i):
         at, block = self.p.at, self.block
@@ -539,11 +572,12 @@
         self.copy(i, here, here, self.p.at(0, 0, 1)).wait_recv()
 
     def begin(self):
-        self.mine().start()
         for i in (0, 1, 2):
             self.outgoing(i).start()
+        self.keep.begin()
 
     def forward(self):
+        self.keep.turn()
         self.arrive(0)
         self.outgoing(3).start()
         self.arrive(1)
@@ -562,7 +596,7 @@
             self.arrive(i)
         for i in range(9):
             self.outgoing(i).wait_send()
-        self.mine().wait()
+        self.keep.finish()
 
 
 class GatherLine:
@@ -672,9 +706,7 @@
     def hand_on(self, way, j):
         term = self.own(self.last - j if way == 0 else j)
         self.copy(way, j, term).wait_recv()
-        self.stage[way, j] = (
-            term[...].astype(jnp.float32) + self.inbox[way, j].astype(jnp.float32)
-        ).astype(jnp.bfloat16)
+        self.stage[way, j] = term[...] + self.inbox[way, j]
         self.copy(way, j, self.stage.at[way, j]).start()
 
     def hop(self, k):
@@ -723,9 +755,7 @@
 
     def tile(i, carry):
         rows = pl.ds(pl.multiple_of(i * 16, 16), 16)
-        result[rows] = (
-            into[rows].astype(jnp.float32) + other[rows].astype(jnp.float32)
-        ).astype(result.dtype)
+        result[rows] = into[rows] + other[rows]
         return carry
 
     lax.fori_loop(0, into.shape[0] // 16, tile, None)
@@ -847,11 +877,12 @@
     def kernel(*refs):
         srcs, (c, e) = refs[:count], refs[count : count + 2]
         dsts, (c_out, e_out) = refs[count + 2 : 2 * count + 2], refs[2 * count + 2 : 2 * count + 4]
-        ps, pr, pl_sem, ls, lr, ll = refs[2 * count + 4 :]
+        ps, pr, pl_sem, ls, lr, ll = refs[2 * count + 4 : 2 * count + 10]
+        held = refs[2 * count + 10 :]
         place = Place(n_dp, n_line)
         place.meet()
         planes = [
-            GatherPlane(place, a, b, ps.at[i], pr.at[i], pl_sem.at[i])
+            GatherPlane(place, a, b, ps.at[i], pr.at[i], pl_sem.at[i], held[i])
             for i, (a, b) in enumerate(zip(srcs, dsts))
         ]
         rows = c.shape[0]
@@ -872,14 +903,16 @@
         copies = []
         for i, (src, dst) in enumerate(((c, c_out), (e, e_out))):
             own = dst.at[pl.ds(pl.multiple_of(place.t * src.shape[0], 8), src.shape[0])]
-            copies.append(pltpu.make_async_copy(src, own, ll.at[i]))
-            copies[i].start()
+            copies.append(Kept(src, own, held[count + i], ll.at[i]))
+            copies[i].begin()
         for line in lines:
             line.step(1)
         for part in late:
             part.begin()
         for part in early:
             part.forward()
+        for copy in copies:
+            copy.turn()
         for line in lines:
             line.step(2)
         for part in early:
@@ -891,7 +924,7 @@
         for part in lines + planes:
             part.finish()
         for copy in copies:
-            copy.wait()
+            copy.finish()
 
     return pl.pallas_call(
         kernel,
@@ -905,28 +938,30 @@
         scratch_shapes=[
             dma_sems(count, 9),
             dma_sems(count, 9),
-            dma_sems(count),
+            dma_sems(count, 2),
             dma_sems(parts + 1, 2, n_line - 1),
             dma_sems(parts + 1, 2, n_line - 1),
-            dma_sems(2),
-        ],
+            dma_sems(2, 2),
+        ]
+        + [vmem_like(m) for m in (*mats, rows_in, order)],
         compiler_params=comm_params(1),
         name="first_gather",
     )(*mats, rows_in, order)
 
 
 CHUNKS = 8
-
-
-def line_scratch(n_line, span, width):
+LAST_CHUNKS = 4
+
+
+def line_scratch(n_line, span, width, chunks):
     hops = n_line - 1
     return [
-        pltpu.VMEM((CHUNKS, 2, hops, span, width), jnp.bfloat16),
-        pltpu.VMEM((CHUNKS, 2, hops, span, width), jnp.bfloat16),
-        dma_sems(CHUNKS, 2, hops),
-        dma_sems(CHUNKS, 2, hops),
-        dma_sems(CHUNKS, 2, hops),
-        dma_sems(CHUNKS, 2, hops),
+        pltpu.VMEM((chunks, 2, hops, span, width), jnp.bfloat16),
+        pltpu.VMEM((chunks, 2, hops, span, width), jnp.bfloat16),
+        dma_sems(chunks, 2, hops),
+        dma_sems(chunks, 2, hops),
+        dma_sems(chunks, 2, hops),
+        dma_sems(chunks, 2, hops),
         pltpu.VMEM((span, width), jnp.float32),
     ]
 
@@ -988,11 +1023,12 @@
         after, hidden = refs[3 + count : 5 + count]
         dsts = refs[5 + count : 5 + 2 * count]
         ps, pr, pl_sem = refs[5 + 2 * count : 8 + 2 * count]
-        scratch = refs[8 + 2 * count :]
+        held = refs[8 + 2 * count : 8 + 3 * count]
+        scratch = refs[8 + 3 * count :]
         place = Place(n_dp, n_line)
         place.meet()
         planes = [
-            GatherPlane(place, a, b, ps.at[i], pr.at[i], pl_sem.at[i])
+            GatherPlane(place, a, b, ps.at[i], pr.at[i], pl_sem.at[i], held[i])
             for i, (a, b) in enumerate(zip(srcs, dsts))
         ]
         planes[0].begin()
@@ -1004,11 +1040,8 @@
             first = pl.multiple_of(place.t * rows, 16) + c * total.shape[0]
             hidden[pl.ds(pl.multiple_of(first, 16), total.shape[0])] = low
 
-        between = {4: planes[1].begin, 5: planes[0].forward}
+        between = {6: planes[0].forward, 9: planes[0].share}
         sum_rows_and_spread(place, s, scratch, norm, hidden, between)
-        planes[1].forward()
-        planes[0].share()
-        planes[1].share()
         for part in planes:
             part.finish()
 
@@ -1021,8 +1054,9 @@
         + tuple(shaped((n_dp * m.shape[0], m.shape[1]), m.dtype) for m in mats),
         in_specs=[in_vmem()] * 3 + [in_any()] * count,
         out_specs=[in_vmem()] * 2 + [in_any()] * count,
-        scratch_shapes=[dma_sems(count, 9), dma_sems(count, 9), dma_sems(count)]
-        + line_scratch(n_line, rows // CHUNKS, width),
+        scratch_shapes=[dma_sems(count, 9), dma_sems(count, 9), dma_sems(count, 2)]
+        + [vmem_like(m) for m in mats]
+        + line_scratch(n_line, rows // CHUNKS, width, CHUNKS),
         compiler_params=comm_params(2),
         name="middle_gather",
     )(terms, tokens, gain, *mats)
@@ -1137,7 +1171,7 @@
             dma_sems(7),
         ]
         + ReducePlane.scratch(block, mat.shape[1])
-        + line_scratch(n_line, rows // CHUNKS, width),
+        + line_scratch(n_line, rows // CHUNKS, width, CHUNKS),
         compiler_params=comm_params(3),
         name="middle_sums",
     )(terms, after, gain, grad_in, mat, hidden, grad_up, product, down)
@@ -1219,7 +1253,7 @@
             for part in planes:
                 part.turn()
 
-        sum_rows_and_spread(place, s, scratch, norm, None, {0: cores, 5: turn})
+        sum_rows_and_spread(place, s, scratch, norm, None, {1: cores, 3: turn})
         first = Exchange(place, "dp", own_first, slots_b, xs.at[1], xr.at[1], xl.at[1])
         first.begin()
         small_out[...] = early.finish()
@@ -1253,7 +1287,7 @@
             dma_sems(3, n_dp),
             dma_sems(3),
         ]
-        + line_scratch(n_line, rows // CHUNKS, width),
+        + line_scratch(n_line, rows // LAST_CHUNKS, width, LAST_CHUNKS),
         compiler_params=comm_params(4),
         name="last_sums",
     )(terms, tokens, gain, grad_after, small, *mats)
@@ -1328,25 +1362,6 @@
 
     def block(self, index, size):
         return pl.ds(pl.multiple_of(self.first + index * size, RIM), size)
-
-
-class Fetch:
-    def __init__(self, pairs, sems):
-        self.copies = [
-            pltpu.make_async_copy(src, dst, sems.at[i]) for i, (src, dst) in enumerate(pairs)
-        ]
-
-    def start(self, *which):
-        for i in which:
-            self.copies[i].start()
-
-    def wait(self, *which):
-        for i in which:
-            self.copies[i].wait()
-
-
-def vmem_like(array):
-    return pltpu.VMEM(array.shape, array.dtype)
 
 
 def recur_forward(
@@ -1381,7 +1396,7 @@
         results = refs[28:39]
         hp, xext, y, conv_low, conv, pre_r, pre_i, rate, state, merged_st, terms = results
         (h, xf, local, cum, merged, agg, slots, hs, hr, es, er, el, gs, gr, gl) = refs[39:54]
-        in_sems, out_sems = refs[54:]
+        in_sems, out_sems, cot_held = refs[54:]
         fetch = Fetch(((tok_far, tok), (wx_far, wx), (wy_far, wy), (wo_far, wo)), in_sems)
         store = Fetch(zip(results, far), out_sems)
         fetch.start(0, 1, 2, 3)
@@ -1389,8 +1404,8 @@
         place.meet(True)
         swap = RimSwap(place, own)
         own_cot = cot_all.at[pl.ds(pl.multiple_of(place.t * cot_rows, 16), cot_rows)]
-        keep = pltpu.make_async_copy(cot_ref, own_cot, gl)
-        keep.start()
+        keep = Kept(cot_ref, own_cot, cot_held, gl)
+        keep.begin()
         span = cot_rows // parts
         lines = [
             GatherLine(place, cot_all, cot_rows, c * span, span, gs.at[c], gr.at[c])
@@ -1422,6 +1437,7 @@
             (lax.rem(place.d + 1, n_dp), place.t),
         )
         edge.start()
+        keep.turn()
         for line in lines:
             line.step(1)
 
@@ -1543,7 +1559,7 @@
         loop(width // 512, mix)
         for line in lines:
             line.finish()
-        keep.wait()
+        keep.finish()
         store.start(10)
         store.wait(*range(11))
 
@@ -1583,9 +1599,10 @@
             pltpu.SemaphoreType.DMA,
             dma_sems(parts, 2, n_line - 1),
             dma_sems(parts, 2, n_line - 1),
-            pltpu.SemaphoreType.DMA,
+            dma_sems(2),
             dma_sems(4),
             dma_sems(11),
+            vmem_like(cot),
         ],
         compiler_params=comm_params(5),
         name="recur_forward",
@@ -1683,7 +1700,6 @@
 
         fetch.wait(2, 3)
         loop(rows // TILE, split)
-        plane.cores()
         fetch.wait(4)
         groups = own // LANES
 
@@ -1713,6 +1729,7 @@
         agg[1:2] = message
         swap_all = Exchange(place, "dp", agg, slots, es, er, el)
         swap_all.begin()
+        plane.cores()
         swap_all.wait()
         entry = jnp.zeros((1, own), jnp.float32)
         for q in reversed(range(n_dp)):
@@ -1953,9 +1970,9 @@
     x_full, y_full, out_full, minor_full, tok_all, order_full = first_gather(
         n_dp, n_tensor, (x_weight, y_weight, out_weight.T, minor), tokens, order_rows
     )
-    down_full = lax.all_gather(
-        lax.optimization_barrier((down_weight.T, tok_all))[0], "dp", axis=0, tiled=True
-    )
+    late_up, late_down, _ = lax.optimization_barrier((up_weight, down_weight.T, tok_all))
+    up_full = lax.all_gather(late_up, "dp", axis=0, tiled=True)
+    down_full = lax.all_gather(late_down, "dp", axis=0, tiled=True)
     order_all = order_full.reshape(n_tensor, 8, tok_rows)[:, 0].reshape(row_count)
     both_gates = minor_full[:, : 2 * own_width]
     gain_rows = minor_full[:, 2 * own_width :].reshape(n_dp, -1)
@@ -2011,8 +2028,8 @@
         soft,
         flags,
     )
-    after_own, hidden_two, gate_full, up_full = middle_gather(
-        n_dp, n_tensor, mixer_terms, tokens, second_gain, (gate_weight, up_weight)
+    after_own, hidden_two, gate_full = middle_gather(
+        n_dp, n_tensor, mixer_terms, tokens, second_gain, (gate_weight,)
     )
     gate_pre = plain_dot(hidden_two, gate_full)
     up_pre = plain_dot(hidden_two, up_full)

time: 577 us -> 578 us (level)
    pallas_call x1, Pallas kernels: 67.4 us -> 103 us  [last_sums(): pl.pallas_call(kernel, out_shape=(shaped((rows, width), jnp.float32), sha...]
    pallas_call x1, Pallas kernels: 71.1 us -> 56.3 us  [recur_backward(): pl.pallas_call(kernel, out_shape=(shaped((rows, 2 * own), low), shaped((s...]
    pallas_call x1, Pallas kernels: 65.1 us -> 51.6 us  [first_gather(): pl.pallas_call(kernel, out_shape=tuple((shaped((n_dp * m.shape[0], m.shap...]
    pallas_call x1, Pallas kernels: 95 us -> 87.2 us  [middle_gather(): pl.pallas_call(kernel, out_shape=(shaped((rows, width), jnp.float32), sha...]
  transfers between devices with their start and end apart: 3 -> 4, of which waited for: 0 -> 0; matrix products, arithmetic and copies ran while one was open for 18% -> 12% of each run, Pallas kernels for 66% -> 53%
where the time goes in v6:
time: 578 us; the launch traced here: 572 us
  Pallas kernels  440 us (76%)
  matrix products  79.1 us (14%)
  other arithmetic  19.5 us (3%)
  local copies, waits for them, and re-layouts  17.1 us (3%)
  between operations  14.6 us (3%)
    pallas_call x1, Pallas kernels, last_sums(): pl.pallas_call(kernel, out_shape=(shaped((rows, width), jnp.float32), sha...  103 us
    pallas_call x1, Pallas kernels, middle_gather(): pl.pallas_call(kernel, out_shape=(shaped((rows, width), jnp.float32), sha...  87.2 us
    pallas_call x1, Pallas kernels, middle_sums(): pl.pallas_call(kernel, out_shape=(shaped((rows, width), full), shaped((1,...  82.6 us
    pallas_call x1, Pallas kernels, recur_forward(): pl.pallas_call(kernel, out_shape=results + (shaped((n_line * cot_rows, wi...  58.8 us
    pallas_call x1, Pallas kernels, recur_backward(): pl.pallas_call(kernel, out_shape=(shaped((rows, 2 * own), low), shaped((s...  56.3 us
    pallas_call x1, Pallas kernels, first_gather(): pl.pallas_call(kernel, out_shape=tuple((shaped((n_dp * m.shape[0], m.shap...  51.6 us
    dot_general x3, matrix products, plain_dot(): return jnp.dot(left, right, preferred_element_type=jnp.float32)  36.8 us
    dot_general x4, matrix products, trans_times(): lax.dot_general(left, right, (((0,), (0,)), ((), ())), preferred_element_...  26.1 us
  transfers between devices with their start and end apart: 4, of which 0 were waited for; matrix products, arithmetic and copies ran while one was open for 12% of the time, Pallas kernels for 53%

profile of v6, /device:TPU:0, one launch (start us, length us, event | category | flops | bytes accessed | tf_op | source)
XLA Modules:
  0.0 571.5 jit_solution(4611739818221800762)
XLA Ops:
  8.7 1.4 pad_maximum_fusion.refs_3_
  10.7 51.6 %first_gather.1 = (bf16[2560,640]{1,0:T(8,128)(2,1)}, bf16[2560,640]{1,0:T(8,128)(2,1)}, bf16[2560,640]{1,0:T(8,128)(2,1)}, bf16[256,1408]{1,0:T(8,128)(2,1)}, b...) custom-call(bf16[320,640]{1,0:T(8,128)(2,1)} %refs_0_.1, bf16[320,640]{1,0:T(8,128)(2,1)} %refs_1_.3, ...), custom_call_target="tpu_custom_call" | custom-call | tf_op jit(solution)/shard_map/first_gather/pallas_call | solution.py:929
  65.7 0.8 slice.54
  69.0 0.8 and_convert_fusion.refs_11_.refs_10_
  69.8 1.1 fusion.8
  70.9 1.0 multiply_convert_fusion.3.refs_1_.refs_3_
  71.9 58.8 %recur_forward.1 = (bf16[512,2560]{1,0:T(8,128)(2,1)}, bf16[528,640]{1,0:T(8,128)(2,1)}, f32[512,640]{1,0:T(8,128)}, bf16[512,896]{1,0:T(8,128)(2,1)}, f32[512,6...) custom-call(bf16[512,2560]{1,0:T(8,128)(2,1)} %get-tuple-element.56., ...), custom_call_target="tpu_custom_call" | custom-call | tf_op jit(solution)/shard_map/recur_forward/pallas_call | solution.py:1581
  130.7 87.2 %middle_gather.1 = (f32[128,2560]{1,0:T(8,128)}, bf16[512,2560]{1,0:T(8,128)(2,1)}, bf16[2560,1920]{1,0:T(8,128)(2,1)}) custom-call(bf16[512,2560]{1,0:T(8,128)(2,1)} %get-tuple-element.62.refs_0_, bf16[128,2560]{1,0:T(8,128)(2,1)} %refs_1_.5, f32[1,2560]{1,0:T(1,128)} %reshape.180.refs_2_, bf16[320,1920]{1,0:T(8,128)(2,1)} %refs_3_.1), custom_call_target="tpu_custom_call" | custom-call | tf_op jit(solution)/shard_map/middle_gather/pallas_call | solution.py:1048
  218.0 11.4 %fusion.22 = f32[512,1920]{1,0:T(8,128)} fusion(bf16[512,2560]{1,0:T(8,128)(2,1)} %get-tuple-element.65.refs_5_, bf16[2560,1920]{1,0:T(8,128)(2,1)} %get-tuple-element.66), kind=kOutput, calls=%fused_computation.68 | convolution fusion | flops 5033164800 | bytes 16384000 | tf_op jit(solution)/shard_map/dot_general | solution.py:71
  229.4 11.7 %multiply_convert_fusion.1 = (bf16[512,1920]{1,0:T(8,128)(2,1)S(1)}, f32[512,1920]{1,0:T(8,128)}) fusion(f32[512,1920]{1,0:T(8,128)} %fusion.22, bf16[512,2560]{1,0:T(8,128)(2,1)S(1)} %copy-done.3, bf16[2560,1920]{1,0:T(8,128)(2,1)} %all-gather.3.cloned.1.call-done), kind=kOutput, calls=%fused_computation.15 | convolution fusion | flops 5042995200 | bytes 22282240 | tf_op jit(solution)/shard_map/dot_general | solution.py:71
  241.1 1.3 copy-done.4
  242.4 8.2 %convolution_convert_fusion.2 = bf16[2560,1920]{1,0:T(8,128)(2,1)} fusion(bf16[512,2560]{1,0:T(8,128)(2,1)S(1)} %copy-done.14, bf16[512,1920]{1,0:T(8,128)(2,1)S(1)} %get-tuple-element.120.refs_7_), kind=kOutput, calls=%fused_computation.2 | convolution fusion | flops 5038080000 | bytes 14417920 | tf_op jit(solution)/shard_map/dot_general | solution.py:81
  250.5 13.7 %multiply_convert_fusion = (bf16[512,1920]{1,0:T(8,128)(2,1)S(1)}, bf16[512,1920]{1,0:T(8,128)(2,1)S(1)}) fusion(f32[512,1920]{1,0:T(8,128)} %fusion.22, f32[512,1920]{1,0:T(8,128)} %get-tuple-element.121, bf16[512,2560]{1,0:T(8,128)(2,1)} %get-tuple-element.68, bf16[2560,1920]{1,0:T(8,128)(2,1)} %all-gather.5.cloned.1.call-done.refs_8_), kind=kOutput, calls=%fused_computation.14 | convolution fusion | flops 5056757760 | bytes 24248320 | tf_op jit(solution)/shard_map/dot_general | solution.py:71
  264.3 9.2 %fusion.23 = f32[512,2560]{1,0:T(8,128)S(1)} fusion(bf16[512,1920]{1,0:T(8,128)(2,1)S(1)} %get-tuple-element.105, bf16[2560,1920]{1,0:T(8,128)(2,1)} %get-tuple-element.66), kind=kOutput, calls=%fused_computation.69 | convolution fusion | flops 5033164800 | bytes 17039360 | tf_op jit(solution)/shard_map/dot_general | solution.py:75
  273.5 8.1 %convolution_convert_fusion.1.refs_4_ = bf16[2560,1920]{1,0:T(8,128)(2,1)} fusion(bf16[512,2560]{1,0:T(8,128)(2,1)S(1)} %copy-done.3, bf16[512,1920]{1,0:T(8,128)(2,1)S(1)} %get-tuple-element.105), kind=kOutput, calls=%fused_computation.1 | convolution fusion | flops 5038080000 | bytes 14417920 | tf_op jit(solution)/shard_map/dot_general | solution.py:81
  281.7 6.9 %add_convert_fusion.refs_0_ = bf16[512,2560]{1,0:T(8,128)(2,1)} fusion(f32[512,2560]{1,0:T(8,128)S(1)} %fusion.23, bf16[512,1920]{1,0:T(8,128)(2,1)S(1)} %get-tuple-element.104.refs_6_, bf16[2560,1920]{1,0:T(8,128)(2,1)S(1)} %bitcast.43), kind=kOutput, calls=%fused_computation.5 | convolution fusion | flops 5035786240 | bytes 19660800 | tf_op jit(solution)/shard_map/dot_general | solution.py:75
  288.6 82.6 %middle_sums.1 = (f32[128,2560]{1,0:T(8,128)}, f32[1,2560]{1,0:T(1,128)}, bf16[512,2560]{1,0:T(8,128)(2,1)}, bf16[320,1920]{1,0:T(8,128)(2,1)}, bf16[2560,1920]{1,0:T(8,128)(2,1)}, /*index=5*/bf16[512,2560]{1,0:T(8,128)(2,1)}) custom-call(bf16[512,2560]{1,0:T(8,128)(2,1)} %add_convert_fusion.refs_0_, f32[128,2560]{1,0:T(8,128)} %get-tuple-element.63.refs_1_, ...), custom_call_target="tpu_custom_call" | custom-call | tf_op jit(solution)/shard_map/middle_sums/pallas_call | solution.py:1155
  372.5 56.3 %recur_backward.1 = (bf16[512,1280]{1,0:T(8,128)(2,1)}, bf16[256,1280]{1,0:T(8,128)(2,1)}, f32[8,640]{1,0:T(8,128)}, f32[1,640]{1,0:T(1,128)}, bf16[512,2560]{1,0:T(8,128)(2,1)}, /*index=5*/bf16[320,1920]{1,0:T(8,128)(2,1)}) custom-call(bf16[512,2560]{1,0:T(8,128)(2,1)} %get-tuple-element.71.refs_0_, bf16[512,512]{1,0:T(8,128)(2,1)} %get-tuple-element.119.refs_2_.refs_1_, ...), custom_call_target="tpu_custom_call" | custom-call | tf_op jit(solution)/shard_map/recur_backward/pallas_call | solution.py:1870
  429.6 3.0 convert_element_type.116
  432.6 1.7 convert_element_type.115
  434.4 4.3 convolution_convert_fusion.3.refs_6_
  439.4 5.5 convolution_convert_fusion.refs_5_
  444.9 103.3 %last_sums.1 = (f32[128,2560]{1,0:T(8,128)}, f32[4,2560]{1,0:T(4,128)}, f32[2,2560]{1,0:T(2,128)}, bf16[320,1280]{1,0:T(8,128)(2,1)}, bf16[320,640]{1,0:T(8,128)(2,1)}, /*index=5*/bf16[32,1280]{1,0:T(8,128)(2,1)}) custom-call(bf16[512,2560]{1,0:T(8,128)(2,1)} %get-tuple-element.81.refs_0_, bf16[128,2560]{1,0:T(8,128)(2,1)} %refs_1_.5, ...), custom_call_target="tpu_custom_call" | custom-call | tf_op jit(solution)/shard_map/last_sums/pallas_call | solution.py:1268
  548.3 0.9 slice_reduce_fusion
  549.8 1.4 dynamic-slice_reduce_fusion
  551.2 1.3 slice_reduce_fusion.1
  552.5 1.5 fusion.20
  554.0 1.9 convert_bitcast_fusion.1
  556.0 2.4 fusion.19
  558.4 2.2 multiply_convert_fusion.2
  560.6 2.9 convert_bitcast_fusion
  563.5 1.1 copy.44
  (92 shorter events, 11.1 us)
Async XLA Ops:
  7.2 56.0 %copy-start.17 = (s32[3]{0:T(128)S(1)}, s32[3]{0:T(128)}, u32[]{:S(2)}) copy-start(s32[3]{0:T(128)} %param.29) | copy-start | bytes 40
  7.2 56.8 %copy-start.11 = (f32[640]{0:T(1024)S(1)}, f32[640]{0:T(1024)}, u32[]{:S(2)}) copy-start(f32[640]{0:T(1024)} %param.23) | copy-start | bytes 7684
  7.2 222.2 %all-gather.3.cloned.1.call-start = ((), (), s32[]{:S(2)}) async-start(), calls=%async_computation.2 | async-start | bytes 11059200 | tf_op jit(solution)/shard_map/all_gather | solution.py:1974
  10.7 57.5 %copy-start.18 = (s32[128]{0:T(128)S(1)}, s32[128]{0:T(128)}, u32[]{:S(2)}) copy-start(s32[128]{0:T(128)} %param.30) | copy-start | bytes 1540
  62.3 5.7 %copy-start.8 = (bf16[256,1408]{1,0:T(8,128)(2,1)S(1)}, bf16[256,1408]{1,0:T(8,128)(2,1)}, u32[]{:S(2)}) copy-start(bf16[256,1408]{1,0:T(8,128)(2,1)} %get-tuple-element.61) | copy-start | bytes 2162692
  62.4 8.6 %copy-start.9 = (bf16[128,2560]{1,0:T(8,128)(2,1)S(1)}, bf16[128,2560]{1,0:T(8,128)(2,1)}, u32[]{:S(2)}) copy-start(bf16[128,2560]{1,0:T(8,128)(2,1)} %param.31) | copy-start | bytes 1966084
  62.4 188.1 %all-gather.5.cloned.1.call-start = ((), (), s32[]{:S(2)}) async-start(), calls=%async_computation.3 | async-start | bytes 11059200 | tf_op jit(solution)/shard_map/all_gather | solution.py:1975
  63.1 495.2 %reduce-scatter.3.cloned.1.call-start = ((), (), s32[]{:S(2)}) async-start(), calls=%async_computation.4 | async-start | bytes 3276800 | tf_op jit(solution)/shard_map/reduce_scatter | solution.py:2062
  68.2 3.7 copy-start.1
  218.0 11.4 %copy-start.3 = (bf16[512,2560]{1,0:T(8,128)(2,1)S(1)}, bf16[512,2560]{1,0:T(8,128)(2,1)}, u32[]{:S(2)}) copy-start(bf16[512,2560]{1,0:T(8,128)(2,1)} %get-tuple-element.65.refs_5_) | copy-start | bytes 7864324
  229.4 13.0 %copy-start.14 = (bf16[512,2560]{1,0:T(8,128)(2,1)S(1)}, bf16[512,2560]{1,0:T(8,128)(2,1)}, u32[]{:S(2)}) copy-start(bf16[512,2560]{1,0:T(8,128)(2,1)} %get-tuple-element.68) | copy-start | bytes 7864324
  241.1 1.3 copy-start.4
  264.2 17.4 %copy-start.5 = (bf16[512,1920]{1,0:T(8,128)(2,1)}, bf16[512,1920]{1,0:T(8,128)(2,1)S(1)}, u32[]{:S(2)}) copy-start(bf16[512,1920]{1,0:T(8,128)(2,1)S(1)} %get-tuple-element.104.refs_6_) | copy-start | bytes 5898244
  264.3 17.4 %slice-start = ((s8[9830400]{0:T(1024)(128)(4,1)}), s8[4194304]{0:T(1024)(128)(4,1)S(1)}, s32[]{:S(2)}) async-start(s8[9830400]{0:T(1024)(128)(4,1)} %bitcast.42), calls=%async_computation.6 | async-start | bytes 8388608
  264.3 17.4 %slice-start.1 = ((s8[9830400]{0:T(1024)(128)(4,1)}), s8[4194304]{0:T(1024)(128)(4,1)S(1)}, s32[]{:S(2)}) async-start(s8[9830400]{0:T(1024)(128)(4,1)} %bitcast.42), calls=%async_computation.7 | async-start | bytes 8388608
  273.5 8.1 %slice-start.2 = ((s8[9830400]{0:T(1024)(128)(4,1)}), s8[1441792]{0:T(1024)(128)(4,1)S(1)}, s32[]{:S(2)}) async-start(s8[9830400]{0:T(1024)(128)(4,1)} %bitcast.42), calls=%async_computation.8 | async-start | bytes 2883584
  371.2 189.4 %reduce-scatter.5.cloned.1.call-start = ((), (), s32[]{:S(2)}) async-start(), calls=%async_computation.5 | async-start | bytes 11059200 | tf_op jit(solution)/shard_map/reduce_scatter | solution.py:2039
  428.7 3.9 copy-start.7
  429.6 4.8 copy-start.2
  429.6 4.8 copy-start.16
  434.4 4.3 copy-start.10
  434.4 4.3 copy-start.12
  434.4 5.0 copy-start.13
  434.4 5.0 copy-start.15
  548.3 10.1 %copy-start = (f32[128,2560]{1,0:T(8,128)S(1)}, f32[128,2560]{1,0:T(8,128)}, u32[]{:S(2)}) copy-start(f32[128,2560]{1,0:T(8,128)} %get-tuple-element.63.refs_1_) | copy-start | bytes 3932164
  558.4 5.1 copy-start.6
Sparse Core Ops, SparseCore 0:
  62.5 61.0 all-gather.2
  125.5 90.9 all-gather.4
  371.3 53.8 reduce-scatter.2
  428.6 102.2 reduce-scatter.4

commit v7 on v6

--- a/solution.py
+++ b/solution.py
@@ -660,10 +660,10 @@
 
 
 class ReduceLine:
-    def __init__(self, place, terms, rows, begin, span, stage, inbox, send, recv):
+    def __init__(self, place, terms, rows, begin, span, inbox, send, recv):
         self.p, self.terms, self.rows = place, terms, rows
         self.begin, self.span = begin, span
-        self.stage, self.inbox = stage, inbox
+        self.inbox = inbox
         self.send, self.recv = send, recv
         self.last = place.n_line - 1
 
@@ -706,8 +706,8 @@
     def hand_on(self, way, j):
         term = self.own(self.last - j if way == 0 else j)
         self.copy(way, j, term).wait_recv()
-        self.stage[way, j] = term[...] + self.inbox[way, j]
-        self.copy(way, j, self.stage.at[way, j]).start()
+        self.inbox[way, j] = term[...] + self.inbox[way, j]
+        self.copy(way, j, self.inbox.at[way, j]).start()
 
     def hop(self, k):
         t, last = self.p.t, self.last
@@ -729,12 +729,12 @@
         @pl.when(t > 0)
         def _():
             j = last - t
-            self.copy(0, j, self.stage.at[0, 0]).wait_recv()
+            self.copy(0, j, self.inbox.at[0, 0]).wait_recv()
             result[...] += self.inbox[0, j].astype(jnp.float32)
 
         @pl.when(t < last)
         def _():
-            self.copy(1, t, self.stage.at[0, 0]).wait_recv()
+            self.copy(1, t, self.inbox.at[0, 0]).wait_recv()
             result[...] += self.inbox[1, t].astype(jnp.float32)
 
     def finish(self):
@@ -743,11 +743,11 @@
 
             @pl.when((t > 0) & (t < last - j))
             def _():
-                self.copy(0, j, self.stage.at[0, j]).wait_send()
+                self.copy(0, j, self.inbox.at[0, j]).wait_send()
 
             @pl.when((t < last) & (t > j))
             def _():
-                self.copy(1, j, self.stage.at[1, j]).wait_send()
+                self.copy(1, j, self.inbox.at[1, j]).wait_send()
 
 
 def add_rows(into, other, result=None):
@@ -957,7 +957,6 @@
     hops = n_line - 1
     return [
         pltpu.VMEM((chunks, 2, hops, span, width), jnp.bfloat16),
-        pltpu.VMEM((chunks, 2, hops, span, width), jnp.bfloat16),
         dma_sems(chunks, 2, hops),
         dma_sems(chunks, 2, hops),
         dma_sems(chunks, 2, hops),
@@ -967,13 +966,13 @@
 
 
 def sum_rows_and_spread(place, terms, scratch, finish_rows, spread, between):
-    stage, inbox, rs, rr, gs, gr, total = scratch
+    inbox, rs, rr, gs, gr, total = scratch
     span = total.shape[0]
-    count = stage.shape[0]
+    count = inbox.shape[0]
     rows = span * count
     hops = place.n_line - 1
     sums = [
-        ReduceLine(place, terms, rows, c * span, span, stage.at[c], inbox.at[c], rs.at[c], rr.at[c])
+        ReduceLine(place, terms, rows, c * span, span, inbox.at[c], rs.at[c], rr.at[c])
         for c in range(count)
     ]
     gathers = []
@@ -1638,6 +1637,7 @@
     flags,
     kept,
     weight_terms,
+    row_terms,
 ):
     rows, width = mixer_in.shape
     count, own = taps.shape
@@ -1645,17 +1645,20 @@
     wide = own + 2 * RIM
     blocks = (wide - RIM) // size
     chunk = rows // 8
+    own_rows = rows // n_line
+    parts = 4
+    span = own_rows // parts
 
     def kernel(*refs):
         (mix_far, plc, sto, wx_far, wy_far, wo_far, gw, cw, sp, sg, fl) = refs[:11]
-        kept_far, weights = refs[11:19], refs[19]
-        (gxy_far, gate_grads, tap_grads, decay_grad, terms_far, weight_sum) = refs[20:26]
-        mix, wx, wy, wo = refs[26:30]
-        (xext, y, conv_low, conv, pre_r, pre_i, rate, state) = refs[30:38]
-        (gxy, mp, gm, lam, reach, gp_r, gp_i, grad, spread, rim_out, rim_in) = refs[38:49]
-        (ret_out, ret_in, tap_sums, decay_sums, ends, agg, slots) = refs[49:56]
-        (hs, hr, es, er, el, in_sems, out_sems) = refs[56:63]
-        terms = mix
+        kept_far, weights, feed_far = refs[11:19], refs[19], refs[20]
+        (gxy_far, gate_grads, tap_grads, decay_grad, terms_far, weight_sum, row_sum) = refs[21:28]
+        mix, wy, wo, feed = refs[28:32]
+        (xext, y, conv_low, conv, pre_r, pre_i, rate, state) = refs[32:40]
+        (gxy, mp, gm, lam, reach, gp_r, gp_i, grad, spread, rim_out, rim_in) = refs[40:51]
+        (ret_out, ret_in, tap_sums, decay_sums, ends, agg, slots) = refs[51:58]
+        (hs, hr, es, er, el, in_sems, out_sems, inbox, ls, lr, total) = refs[58:69]
+        terms, wx = mix, wo
         fetch = Fetch(
             [
                 (mix_far, mix),
@@ -1670,15 +1673,29 @@
                 (kept_far[0], xext),
                 (wx_far, wx),
                 (wy_far, wy),
+                (feed_far, feed),
             ],
             in_sems,
         )
-        fetch.start(*range(12))
+        fetch.start(12, *range(10), 11)
         store = Fetch(((gxy, gxy_far), (terms, terms_far)), out_sems)
         place = Place(n_dp, n_line)
         place.meet(True)
-        plane = ReducePlane(place, weights, refs[63:])
+        plane = ReducePlane(place, weights, refs[69:])
         plane.begin()
+        lines = [
+            ReduceLine(place, feed, own_rows, c * span, span, inbox.at[c], ls.at[c], lr.at[c])
+            for c in range(parts)
+        ]
+        early, late = lines[: parts // 2], lines[parts // 2 :]
+
+        def add_up(c):
+            lines[c].total(total)
+            row_sum[pl.ds(c * span, span)] = total[...].astype(jnp.bfloat16)
+
+        fetch.wait(12)
+        for line in early:
+            line.ends()
         swap = RimSwap(place, own)
         own_cols = pl.ds(RIM, own)
 
@@ -1689,6 +1706,7 @@
 
         fetch.wait(0, 1)
         loop(rows // 128, project)
+        fetch.start(10)
 
         def split(i):
             here = tile_rows(i, TILE)
@@ -1731,6 +1749,12 @@
         swap_all.begin()
         plane.cores()
         swap_all.wait()
+        for line in early:
+            line.sent()
+        for line in late:
+            line.ends()
+        for line in early:
+            line.hop(0)
         entry = jnp.zeros((1, own), jnp.float32)
         for q in reversed(range(n_dp)):
             longer = slots[q, 1:2] + slots[q, 0:1] * entry
@@ -1769,6 +1793,8 @@
 
             loop(chunk // TILE, back)
             entry = ends[1, j : j + 1] + ends[0, j : j + 1] * entry
+        for line in early:
+            line.hop(1)
         decay_grad[...] = rate_scale * sg[...] * jnp.sum(decay_sums[...], axis=0, keepdims=True)
 
         for i in range(blocks):
@@ -1845,6 +1871,12 @@
 
         store.start(0)
         plane.turn()
+        for c in range(parts // 2):
+            add_up(c)
+        for line in late:
+            line.sent()
+        for line in late:
+            line.hop(0)
 
         def restore(i):
             here = tile_rows(i, 128)
@@ -1861,7 +1893,13 @@
         fetch.wait(10, 11)
         loop(width // 512, spread_back)
         store.start(1)
+        for line in late:
+            line.hop(1)
         plane.finish(weight_sum)
+        for c in range(parts // 2, parts):
+            add_up(c)
+        for line in lines:
+            line.finish()
         store.wait(0, 1)
 
     low, full = jnp.bfloat16, jnp.float32
@@ -1876,10 +1914,11 @@
             shaped((1, own), full),
             shaped((rows, width), low),
             shaped((block, weight_terms.shape[1]), low),
+            shaped((own_rows, width), low),
         ),
-        in_specs=[far, near, near, far, far, far] + [near] * 5 + [far] * 9,
-        out_specs=[far, near, near, near, far, near],
-        scratch_shapes=[vmem_like(m) for m in (mixer_in, x_full, y_full, out_full, *kept)]
+        in_specs=[far, near, near, far, far, far] + [near] * 5 + [far] * 10,
+        out_specs=[far, near, near, near, far, near, near],
+        scratch_shapes=[vmem_like(m) for m in (mixer_in, y_full, out_full, row_terms, *kept)]
         + [
             pltpu.VMEM((rows, 2 * own), low),
             pltpu.VMEM((rows, width), low),
@@ -1904,8 +1943,12 @@
             dma_sems(n_dp),
             dma_sems(n_dp),
             pltpu.SemaphoreType.DMA,
-            dma_sems(12),
+            dma_sems(13),
             dma_sems(2),
+            pltpu.VMEM((parts, 2, n_line - 1, span, width), low),
+            dma_sems(parts, 2, n_line - 1),
+            dma_sems(parts, 2, n_line - 1),
+            pltpu.VMEM((span, width), full),
         ]
         + ReducePlane.scratch(block, weight_terms.shape[1]),
         compiler_params=comm_params(6),
@@ -1924,6 +1967,7 @@
         flags,
         *kept,
         weight_terms,
+        row_terms,
     )
 
 
@@ -2059,15 +2103,7 @@
         product,
         down_full,
     )
-    feed_out = lax.psum_scatter(
-        feed_terms,
-        "tensor",
-        scatter_dimension=0,
-        tiled=True,
-    ).astype(jnp.float32)
-    output = ((after_own + feed_out) * live_own[:, None]).astype(jnp.bfloat16)
-
-    grad_xy, gate_grads, tap_grads, decay_grad, one_terms, up_sum = recur_backward(
+    grad_xy, gate_grads, tap_grads, decay_grad, one_terms, up_sum, feed_out = recur_backward(
         n_dp,
         n_tensor,
         mixer_in,
@@ -2083,7 +2119,10 @@
         flags,
         kept,
         grad_up,
-    )
+        feed_terms,
+    )
+    output = (after_own + feed_out.astype(jnp.float32)) * live_own[:, None]
+    output = output.astype(jnp.bfloat16)
     grad_out_mat = trans_times(mixer_in, merged_stored).astype(jnp.bfloat16)
     grad_xy_mat = trans_times(hidden_place, grad_xy).astype(jnp.bfloat16)
     small = jnp.concatenate(

time: 578 us -> 571 us (0.988)
  Pallas kernels: 440 us -> 433 us
    pallas_call x1, Pallas kernels: 103 us -> 77 us  [last_sums(): pl.pallas_call(kernel, out_shape=(shaped((rows, width), jnp.float32), sha...]
    pallas_call x1, Pallas kernels: 56.3 us -> 76.7 us  [recur_backward(): pl.pallas_call(kernel, out_shape=(shaped((rows, 2 * own), low), shaped((s...]
  transfers between devices with their start and end apart: 4 -> 3, of which waited for: 0 -> 0; matrix products, arithmetic and copies ran while one was open for 12% -> 19% of each run, Pallas kernels for 53% -> 68%
where the time goes in v7:
time: 571 us; the launch traced here: 564 us
  Pallas kernels  433 us (76%)
  matrix products  80.6 us (14%)
  other arithmetic  18.1 us (3%)
  local copies, waits for them, and re-layouts  17.2 us (3%)
  between operations  14.6 us (3%)
    pallas_call x1, Pallas kernels, middle_gather(): pl.pallas_call(kernel, out_shape=(shaped((rows, width), jnp.float32), sha...  87.2 us
    pallas_call x1, Pallas kernels, middle_sums(): pl.pallas_call(kernel, out_shape=(shaped((rows, width), full), shaped((1,...  81.7 us
    pallas_call x1, Pallas kernels, last_sums(): pl.pallas_call(kernel, out_shape=(shaped((rows, width), jnp.float32), sha...  77 us
    pallas_call x1, Pallas kernels, recur_backward(): pl.pallas_call(kernel, out_shape=(shaped((rows, 2 * own), low), shaped((s...  76.7 us
    pallas_call x1, Pallas kernels, recur_forward(): pl.pallas_call(kernel, out_shape=results + (shaped((n_line * cot_rows, wi...  58.8 us
    pallas_call x1, Pallas kernels, first_gather(): pl.pallas_call(kernel, out_shape=tuple((shaped((n_dp * m.shape[0], m.shap...  51.6 us
    dot_general x3, matrix products, plain_dot(): return jnp.dot(left, right, preferred_element_type=jnp.float32)  38.6 us
    dot_general x4, matrix products, trans_times(): lax.dot_general(left, right, (((0,), (0,)), ((), ())), preferred_element_...  25.7 us
  transfers between devices with their start and end apart: 3, of which 0 were waited for; matrix products, arithmetic and copies ran while one was open for 19% of the time, Pallas kernels for 68%

profile of v7, /device:TPU:0, one launch (start us, length us, event | category | flops | bytes accessed | tf_op | source)
XLA Modules:
  0.0 564.3 jit_solution(12843596036203423345)
XLA Ops:
  8.7 1.4 pad_maximum_fusion.refs_3_
  10.7 51.6 %first_gather.1 = (bf16[2560,640]{1,0:T(8,128)(2,1)}, bf16[2560,640]{1,0:T(8,128)(2,1)}, bf16[2560,640]{1,0:T(8,128)(2,1)}, bf16[256,1408]{1,0:T(8,128)(2,1)}, b...) custom-call(bf16[320,640]{1,0:T(8,128)(2,1)} %refs_0_.1, bf16[320,640]{1,0:T(8,128)(2,1)} %refs_1_.3, ...), custom_call_target="tpu_custom_call" | custom-call | tf_op jit(solution)/shard_map/first_gather/pallas_call | solution.py:929
  65.7 0.8 slice.54
  69.0 0.8 and_convert_fusion.refs_11_.refs_10_
  69.8 1.1 fusion.8
  70.9 1.0 multiply_convert_fusion.3.refs_1_.refs_3_
  71.9 58.8 %recur_forward.1 = (bf16[512,2560]{1,0:T(8,128)(2,1)}, bf16[528,640]{1,0:T(8,128)(2,1)}, f32[512,640]{1,0:T(8,128)}, bf16[512,896]{1,0:T(8,128)(2,1)}, f32[512,6...) custom-call(bf16[512,2560]{1,0:T(8,128)(2,1)} %get-tuple-element.57., ...), custom_call_target="tpu_custom_call" | custom-call | tf_op jit(solution)/shard_map/recur_forward/pallas_call | solution.py:1580
  130.7 87.2 %middle_gather.1 = (f32[128,2560]{1,0:T(8,128)}, bf16[512,2560]{1,0:T(8,128)(2,1)}, bf16[2560,1920]{1,0:T(8,128)(2,1)}) custom-call(bf16[512,2560]{1,0:T(8,128)(2,1)} %get-tuple-element.63.refs_0_, bf16[128,2560]{1,0:T(8,128)(2,1)} %refs_1_.5, f32[1,2560]{1,0:T(1,128)} %reshape.180.refs_2_, bf16[320,1920]{1,0:T(8,128)(2,1)} %refs_3_.1), custom_call_target="tpu_custom_call" | custom-call | tf_op jit(solution)/shard_map/middle_gather/pallas_call | solution.py:1047
  218.0 11.4 %fusion.22 = f32[512,1920]{1,0:T(8,128)} fusion(bf16[512,2560]{1,0:T(8,128)(2,1)} %get-tuple-element.66.refs_5_, bf16[2560,1920]{1,0:T(8,128)(2,1)} %get-tuple-element.67), kind=kOutput, calls=%fused_computation.68 | convolution fusion | flops 5033164800 | bytes 16384000 | tf_op jit(solution)/shard_map/dot_general | solution.py:71
  229.4 11.7 %multiply_convert_fusion.1 = (bf16[512,1920]{1,0:T(8,128)(2,1)S(1)}, f32[512,1920]{1,0:T(8,128)}) fusion(f32[512,1920]{1,0:T(8,128)} %fusion.22, bf16[512,2560]{1,0:T(8,128)(2,1)S(1)} %copy-done.2, bf16[2560,1920]{1,0:T(8,128)(2,1)} %all-gather.3.cloned.1.call-done), kind=kOutput, calls=%fused_computation.15 | convolution fusion | flops 5042995200 | bytes 22282240 | tf_op jit(solution)/shard_map/dot_general | solution.py:71
  241.1 1.3 copy-done.4
  242.4 8.1 %convolution_convert_fusion.2 = bf16[2560,1920]{1,0:T(8,128)(2,1)} fusion(bf16[512,2560]{1,0:T(8,128)(2,1)S(1)} %copy-done.15, bf16[512,1920]{1,0:T(8,128)(2,1)S(1)} %get-tuple-element.122.refs_7_), kind=kOutput, calls=%fused_computation.2 | convolution fusion | flops 5038080000 | bytes 14417920 | tf_op jit(solution)/shard_map/dot_general | solution.py:81
  251.2 15.5 %multiply_convert_fusion = (bf16[512,1920]{1,0:T(8,128)(2,1)S(1)}, bf16[512,1920]{1,0:T(8,128)(2,1)S(1)}) fusion(f32[512,1920]{1,0:T(8,128)} %fusion.22, f32[512,1920]{1,0:T(8,128)} %get-tuple-element.123, bf16[512,2560]{1,0:T(8,128)(2,1)} %get-tuple-element.69, bf16[2560,1920]{1,0:T(8,128)(2,1)} %all-gather.5.cloned.1.call-done.refs_8_), kind=kOutput, calls=%fused_computation.14 | convolution fusion | flops 5056757760 | bytes 24248320 | tf_op jit(solution)/shard_map/dot_general | solution.py:71
  266.8 9.2 %fusion.23 = f32[512,2560]{1,0:T(8,128)S(1)} fusion(bf16[512,1920]{1,0:T(8,128)(2,1)S(1)} %get-tuple-element.107, bf16[2560,1920]{1,0:T(8,128)(2,1)} %get-tuple-element.67), kind=kOutput, calls=%fused_computation.69 | convolution fusion | flops 5033164800 | bytes 17039360 | tf_op jit(solution)/shard_map/dot_general | solution.py:75
  276.0 8.1 %convolution_convert_fusion.1.refs_4_ = bf16[2560,1920]{1,0:T(8,128)(2,1)} fusion(bf16[512,2560]{1,0:T(8,128)(2,1)S(1)} %copy-done.2, bf16[512,1920]{1,0:T(8,128)(2,1)S(1)} %get-tuple-element.107), kind=kOutput, calls=%fused_computation.1 | convolution fusion | flops 5038080000 | bytes 14417920 | tf_op jit(solution)/shard_map/dot_general | solution.py:81
  284.1 7.0 %add_convert_fusion.refs_0_ = bf16[512,2560]{1,0:T(8,128)(2,1)} fusion(f32[512,2560]{1,0:T(8,128)S(1)} %fusion.23, bf16[512,1920]{1,0:T(8,128)(2,1)S(1)} %get-tuple-element.106.refs_6_, bf16[2560,1920]{1,0:T(8,128)(2,1)S(1)} %bitcast.43), kind=kOutput, calls=%fused_computation.5 | convolution fusion | flops 5035786240 | bytes 19660800 | tf_op jit(solution)/shard_map/dot_general | solution.py:75
  291.1 81.7 %middle_sums.1 = (f32[128,2560]{1,0:T(8,128)}, f32[1,2560]{1,0:T(1,128)}, bf16[512,2560]{1,0:T(8,128)(2,1)}, bf16[320,1920]{1,0:T(8,128)(2,1)}, bf16[2560,1920]{1,0:T(8,128)(2,1)}, /*index=5*/bf16[512,2560]{1,0:T(8,128)(2,1)}) custom-call(bf16[512,2560]{1,0:T(8,128)(2,1)} %add_convert_fusion.refs_0_, f32[128,2560]{1,0:T(8,128)} %get-tuple-element.64.refs_1_, ...), custom_call_target="tpu_custom_call" | custom-call | tf_op jit(solution)/shard_map/middle_sums/pallas_call | solution.py:1154
  372.8 76.7 %recur_backward.1 = (bf16[512,1280]{1,0:T(8,128)(2,1)}, bf16[256,1280]{1,0:T(8,128)(2,1)}, f32[8,640]{1,0:T(8,128)}, f32[1,640]{1,0:T(1,128)}, bf16[512,2560]{1,...) custom-call(bf16[512,2560]{1,0:T(8,128)(2,1)} %get-tuple-element.71.refs_0_, ...), custom_call_target="tpu_custom_call" | custom-call | tf_op jit(solution)/shard_map/recur_backward/pallas_call | solution.py:1908
  450.4 3.0 convert_element_type.116
  453.4 1.6 convert_element_type.115
  455.1 3.9 convolution_convert_fusion.3.refs_6_
  459.7 5.5 convolution_convert_fusion.refs_5_
  465.2 77.0 %last_sums.1 = (f32[128,2560]{1,0:T(8,128)}, f32[4,2560]{1,0:T(4,128)}, f32[2,2560]{1,0:T(2,128)}, bf16[320,1280]{1,0:T(8,128)(2,1)}, bf16[320,640]{1,0:T(8,128)(2,1)}, /*index=5*/bf16[32,1280]{1,0:T(8,128)(2,1)}) custom-call(bf16[512,2560]{1,0:T(8,128)(2,1)} %get-tuple-element.83.refs_0_, bf16[128,2560]{1,0:T(8,128)(2,1)} %refs_1_.5, ...), custom_call_target="tpu_custom_call" | custom-call | tf_op jit(solution)/shard_map/last_sums/pallas_call | solution.py:1267
  542.3 1.0 slice_reduce_fusion
  543.8 1.4 dynamic-slice_reduce_fusion
  545.3 1.3 slice_reduce_fusion.1
  546.6 1.5 fusion.20
  548.0 1.9 convert_bitcast_fusion.1
  550.0 2.4 fusion.19
  552.4 1.0 multiply_convert_fusion.2
  553.4 2.9 convert_bitcast_fusion
  556.3 1.1 copy.44
  (91 shorter events, 10.5 us)
Async XLA Ops:
  7.2 56.0 %copy-start.18 = (s32[3]{0:T(128)S(1)}, s32[3]{0:T(128)}, u32[]{:S(2)}) copy-start(s32[3]{0:T(128)} %param.29) | copy-start | bytes 40
  7.2 56.8 %copy-start.12 = (f32[640]{0:T(1024)S(1)}, f32[640]{0:T(1024)}, u32[]{:S(2)}) copy-start(f32[640]{0:T(1024)} %param.23) | copy-start | bytes 7684
  7.2 222.2 %all-gather.3.cloned.1.call-start = ((), (), s32[]{:S(2)}) async-start(), calls=%async_computation.1 | async-start | bytes 11059200 | tf_op jit(solution)/shard_map/all_gather | solution.py:2018
  10.7 57.5 %copy-start.19 = (s32[128]{0:T(128)S(1)}, s32[128]{0:T(128)}, u32[]{:S(2)}) copy-start(s32[128]{0:T(128)} %param.30) | copy-start | bytes 1540
  62.3 5.7 %copy-start.8 = (bf16[256,1408]{1,0:T(8,128)(2,1)S(1)}, bf16[256,1408]{1,0:T(8,128)(2,1)}, u32[]{:S(2)}) copy-start(bf16[256,1408]{1,0:T(8,128)(2,1)} %get-tuple-element.62) | copy-start | bytes 2162692
  62.4 8.6 %copy-start.9 = (bf16[128,2560]{1,0:T(8,128)(2,1)S(1)}, bf16[128,2560]{1,0:T(8,128)(2,1)}, u32[]{:S(2)}) copy-start(bf16[128,2560]{1,0:T(8,128)(2,1)} %param.31) | copy-start | bytes 1966084
  62.4 188.8 %all-gather.5.cloned.1.call-start = ((), (), s32[]{:S(2)}) async-start(), calls=%async_computation.2 | async-start | bytes 11059200 | tf_op jit(solution)/shard_map/all_gather | solution.py:2019
  63.1 490.3 %reduce-scatter.2.cloned.1.call-start = ((), (), s32[]{:S(2)}) async-start(), calls=%async_computation.3 | async-start | bytes 11059200 | tf_op jit(solution)/shard_map/reduce_scatter | solution.py:2083
  68.2 3.7 copy-start.1
  218.0 11.4 %copy-start.2 = (bf16[512,2560]{1,0:T(8,128)(2,1)S(1)}, bf16[512,2560]{1,0:T(8,128)(2,1)}, u32[]{:S(2)}) copy-start(bf16[512,2560]{1,0:T(8,128)(2,1)} %get-tuple-element.66.refs_5_) | copy-start | bytes 7864324
  229.4 13.0 %copy-start.15 = (bf16[512,2560]{1,0:T(8,128)(2,1)S(1)}, bf16[512,2560]{1,0:T(8,128)(2,1)}, u32[]{:S(2)}) copy-start(bf16[512,2560]{1,0:T(8,128)(2,1)} %get-tuple-element.69) | copy-start | bytes 7864324
  241.1 1.3 copy-start.4
  266.7 17.4 %copy-start.5 = (bf16[512,1920]{1,0:T(8,128)(2,1)}, bf16[512,1920]{1,0:T(8,128)(2,1)S(1)}, u32[]{:S(2)}) copy-start(bf16[512,1920]{1,0:T(8,128)(2,1)S(1)} %get-tuple-element.106.refs_6_) | copy-start | bytes 5898244
  266.7 17.4 %slice-start = ((s8[9830400]{0:T(1024)(128)(4,1)}), s8[4194304]{0:T(1024)(128)(4,1)S(1)}, s32[]{:S(2)}) async-start(s8[9830400]{0:T(1024)(128)(4,1)} %bitcast.42), calls=%async_computation.4 | async-start | bytes 8388608
  266.7 17.4 %slice-start.1 = ((s8[9830400]{0:T(1024)(128)(4,1)}), s8[4194304]{0:T(1024)(128)(4,1)S(1)}, s32[]{:S(2)}) async-start(s8[9830400]{0:T(1024)(128)(4,1)} %bitcast.42), calls=%async_computation.5 | async-start | bytes 8388608
  276.0 8.1 %slice-start.2 = ((s8[9830400]{0:T(1024)(128)(4,1)}), s8[1441792]{0:T(1024)(128)(4,1)S(1)}, s32[]{:S(2)}) async-start(s8[9830400]{0:T(1024)(128)(4,1)} %bitcast.42), calls=%async_computation.6 | async-start | bytes 2883584
  449.5 3.9 copy-start.7
  450.4 4.7 copy-start.3
  450.4 4.7 copy-start.17
  455.0 4.0 copy-start.11
  455.0 4.0 copy-start.13
  455.0 4.6 copy-start.14
  455.1 4.6 copy-start.16
  542.2 10.1 %copy-start = (f32[128,2560]{1,0:T(8,128)S(1)}, f32[128,2560]{1,0:T(8,128)}, u32[]{:S(2)}) copy-start(f32[128,2560]{1,0:T(8,128)} %get-tuple-element.64.refs_1_) | copy-start | bytes 3932164
  542.3 10.1 %copy-start.10 = (bf16[128,2560]{1,0:T(8,128)(2,1)S(1)}, bf16[128,2560]{1,0:T(8,128)(2,1)}, u32[]{:S(2)}) copy-start(bf16[128,2560]{1,0:T(8,128)(2,1)} %get-tuple-element.82) | copy-start | bytes 1966084
  552.4 3.9 copy-start.6
Sparse Core Ops, SparseCore 0:
  62.5 61.0 all-gather.2
  125.5 90.9 all-gather.4
  250.7 89.6 reduce-scatter.1

commit v8 on v7

--- a/solution.py
+++ b/solution.py
@@ -950,7 +950,7 @@
 
 
 CHUNKS = 8
-LAST_CHUNKS = 4
+LAST_CHUNKS = 8
 
 
 def line_scratch(n_line, span, width, chunks):
@@ -1252,7 +1252,7 @@
             for part in planes:
                 part.turn()
 
-        sum_rows_and_spread(place, s, scratch, norm, None, {1: cores, 3: turn})
+        sum_rows_and_spread(place, s, scratch, norm, None, {0: cores, 5: turn})
         first = Exchange(place, "dp", own_first, slots_b, xs.at[1], xr.at[1], xl.at[1])
         first.begin()
         small_out[...] = early.finish()
@@ -1363,6 +1363,9 @@
         return pl.ds(pl.multiple_of(self.first + index * size, RIM), size)
 
 
+LATE_SHARE = 4
+
+
 def recur_forward(
     n_dp,
     n_line,
@@ -1385,7 +1388,7 @@
     wide = own + 2 * RIM
     blocks = (wide - RIM) // size
     chunk = rows // 8
-    cot_rows = cot.shape[0]
+    cot_rows = cot.shape[0] - cot.shape[0] // LATE_SHARE
     parts = 1
 
     def kernel(*refs):
@@ -1403,6 +1406,7 @@
         place.meet(True)
         swap = RimSwap(place, own)
         own_cot = cot_all.at[pl.ds(pl.multiple_of(place.t * cot_rows, 16), cot_rows)]
+        cot_ref = cot_ref.at[pl.ds(0, cot_rows)]
         keep = Kept(cot_ref, own_cot, cot_held, gl)
         keep.begin()
         span = cot_rows // parts
@@ -1601,7 +1605,7 @@
             dma_sems(2),
             dma_sems(4),
             dma_sems(11),
-            vmem_like(cot),
+            pltpu.VMEM((cot_rows, width), low),
         ],
         compiler_params=comm_params(5),
         name="recur_forward",
@@ -1687,15 +1691,19 @@
             ReduceLine(place, feed, own_rows, c * span, span, inbox.at[c], ls.at[c], lr.at[c])
             for c in range(parts)
         ]
-        early, late = lines[: parts // 2], lines[parts // 2 :]
+
+        def send(c):
+            if c > 0:
+                lines[c - 1].sent()
+            if c < parts:
+                lines[c].ends()
 
         def add_up(c):
             lines[c].total(total)
             row_sum[pl.ds(c * span, span)] = total[...].astype(jnp.bfloat16)
 
         fetch.wait(12)
-        for line in early:
-            line.ends()
+        send(0)
         swap = RimSwap(place, own)
         own_cols = pl.ds(RIM, own)
 
@@ -1718,6 +1726,8 @@
 
         fetch.wait(2, 3)
         loop(rows // TILE, split)
+        send(1)
+        lines[0].hop(0)
         fetch.wait(4)
         groups = own // LANES
 
@@ -1749,12 +1759,7 @@
         swap_all.begin()
         plane.cores()
         swap_all.wait()
-        for line in early:
-            line.sent()
-        for line in late:
-            line.ends()
-        for line in early:
-            line.hop(0)
+        lines[0].hop(1)
         entry = jnp.zeros((1, own), jnp.float32)
         for q in reversed(range(n_dp)):
             longer = slots[q, 1:2] + slots[q, 0:1] * entry
@@ -1792,9 +1797,12 @@
                 decay_sums[...] += inner[:8] + inner[8:]
 
             loop(chunk // TILE, back)
+            if j == 4:
+                send(2)
+                lines[1].hop(0)
             entry = ends[1, j : j + 1] + ends[0, j : j + 1] * entry
-        for line in early:
-            line.hop(1)
+        lines[1].hop(1)
+        add_up(0)
         decay_grad[...] = rate_scale * sg[...] * jnp.sum(decay_sums[...], axis=0, keepdims=True)
 
         for i in range(blocks):
@@ -1808,6 +1816,8 @@
                 rim_out[...] = spread[:, swap.beyond].astype(jnp.bfloat16)
                 rim = remote(rim_out, rim_in, hs.at[0], hr.at[0], swap.partner)
                 rim.start()
+        send(3)
+        lines[2].hop(0)
         rim.wait()
         shared = pl.ds(pl.multiple_of((1 - swap.odd) * (own - RIM), RIM), RIM)
 
@@ -1863,6 +1873,8 @@
 
         fetch.wait(9)
         loop(rows // TILE - 1, taps_back)
+        lines[2].hop(1)
+        add_up(1)
         ret.wait()
         taps_back(rows // TILE - 1, jnp.where(place.d < n_dp - 1, ret_in[...], 0.0))
         tap_grads[...] = jnp.zeros_like(tap_grads)
@@ -1871,12 +1883,8 @@
 
         store.start(0)
         plane.turn()
-        for c in range(parts // 2):
-            add_up(c)
-        for line in late:
-            line.sent()
-        for line in late:
-            line.hop(0)
+        send(4)
+        lines[3].hop(0)
 
         def restore(i):
             here = tile_rows(i, 128)
@@ -1893,11 +1901,10 @@
         fetch.wait(10, 11)
         loop(width // 512, spread_back)
         store.start(1)
-        for line in late:
-            line.hop(1)
+        lines[3].hop(1)
+        add_up(2)
         plane.finish(weight_sum)
-        for c in range(parts // 2, parts):
-            add_up(c)
+        add_up(3)
         for line in lines:
             line.finish()
         store.wait(0, 1)
@@ -1971,6 +1978,140 @@
     )
 
 
+def column_parts(width, size=768):
+    return [(c, min(size, width - c)) for c in range(0, width, size)]
+
+
+def feed_forward(n_dp, n_line, hidden, gate, up, down, grads, grad_own):
+    rows, width = hidden.shape
+    units = gate.shape[1]
+    own_rows = grad_own.shape[0]
+    ready = grads.shape[0] // n_line
+    late = own_rows - ready
+    part = width // 4
+
+    def kernel(*refs):
+        hid_far, wg_far, wu_far, wd_far, grads_far, own_far = refs[:6]
+        product_far, gup_far, back_far, gdown_far, ggate_far = refs[6:11]
+        hid, wg, wu, wd, grad, slope, branch, product, ggate, gup, stage, back = refs[11:23]
+        in_sems, out_sems, stage_sems, ls, lr = refs[23:]
+        place = Place(n_dp, n_line)
+        pairs = [(hid_far, hid), (wg_far, wg), (wu_far, wu), (wd_far, wd)]
+        pairs += [
+            (grads_far.at[pl.ds(q * ready, ready)], grad.at[pl.ds(q * own_rows, ready)])
+            for q in range(n_line)
+        ]
+        mine = pl.ds(pl.multiple_of(place.t * own_rows + ready, 16), late)
+        pairs.append((own_far.at[pl.ds(ready, late)], grad.at[mine]))
+        fetch = Fetch(pairs, in_sems)
+        fetch.start(*range(len(pairs)))
+        store = Fetch(((product, product_far), (gup, gup_far), (back, back_far)), out_sems)
+        place.meet()
+        line = GatherLine(place, grad, own_rows, ready, late, ls, lr)
+        line.step(0, own_far.at[pl.ds(ready, late)])
+        columns = column_parts(units)
+        fetch.wait(0, 1)
+        for c, size in columns:
+            cols = pl.ds(c, size)
+
+            def gates(i, cols=cols):
+                here = tile_rows(i, 256)
+                branch[here, cols] = plain_dot(hid[here], wg[:, cols])
+
+            loop(rows // 256, gates)
+        line.step(1)
+        fetch.wait(2)
+        for c, size in columns:
+            cols = pl.ds(c, size)
+
+            def ups(i, cols=cols):
+                here = tile_rows(i, 256)
+                value = plain_dot(hid[here], wu[:, cols])
+                active, bend = gelu_parts(branch[here, cols])
+                product[here, cols] = (active * value).astype(jnp.bfloat16)
+                branch[here, cols] = active
+                slope[here, cols] = bend * value
+
+            loop(rows // 256, ups)
+        store.start(0)
+        line.step(2)
+        fetch.wait(*range(4, len(pairs)))
+        line.finish()
+
+        def weight_rows(left, right, far, first):
+            for i in range(4):
+                some = pl.ds(i * part, part)
+                copy = pltpu.make_async_copy(
+                    stage.at[i % 2], far.at[some], stage_sems.at[first + i]
+                )
+                if i >= 2:
+                    pltpu.make_async_copy(
+                        stage.at[i % 2],
+                        far.at[pl.ds((i - 2) * part, part)],
+                        stage_sems.at[first + i - 2],
+                    ).wait()
+                stage[i % 2] = trans_times(left[:, some], right[...]).astype(jnp.bfloat16)
+                copy.start()
+            for i in (2, 3):
+                pltpu.make_async_copy(
+                    stage.at[i % 2], far.at[pl.ds(i * part, part)], stage_sems.at[first + i]
+                ).wait()
+
+        weight_rows(grad, product, gdown_far, 0)
+        fetch.wait(3)
+        for c, size in columns:
+            cols = pl.ds(c, size)
+
+            def backs(i, cols=cols):
+                here = tile_rows(i, 256)
+                value = plain_dot(grad[here], wd[:, cols])
+                ggate[here, cols] = (value * slope[here, cols]).astype(jnp.bfloat16)
+                gup[here, cols] = (value * branch[here, cols]).astype(jnp.bfloat16)
+
+            loop(rows // 256, backs)
+        store.start(1)
+        for i in range(4):
+            some = pl.ds(i * part, part)
+            back[:, some] = (
+                times_trans(ggate[...], wg[some]) + times_trans(gup[...], wu[some])
+            ).astype(jnp.bfloat16)
+        store.start(2)
+        weight_rows(hid, ggate, ggate_far, 4)
+        store.wait(0, 1, 2)
+
+    low, full = jnp.bfloat16, jnp.float32
+    return pl.pallas_call(
+        kernel,
+        out_shape=(
+            shaped((rows, units), low),
+            shaped((rows, units), low),
+            shaped((rows, width), low),
+            shaped((width, units), low),
+            shaped((width, units), low),
+        ),
+        in_specs=[in_any()] * 6,
+        out_specs=[in_any()] * 5,
+        scratch_shapes=[vmem_like(m) for m in (hidden, gate, up, down)]
+        + [
+            pltpu.VMEM((n_line * own_rows, width), low),
+            pltpu.VMEM((rows, units), full),
+            pltpu.VMEM((rows, units), full),
+            pltpu.VMEM((rows, units), low),
+            pltpu.VMEM((rows, units), low),
+            pltpu.VMEM((rows, units), low),
+            pltpu.VMEM((2, part, units), low),
+            pltpu.VMEM((rows, width), low),
+            dma_sems(5 + n_line),
+            dma_sems(3),
+            dma_sems(8),
+            dma_sems(2, n_line - 1),
+            dma_sems(2, n_line - 1),
+        ],
+        compiler_params=comm_params(7),
+        name="feed_forward",
+    )(hidden, gate, up, down, grads, grad_own)
+
+
 def matches(mesh):
     return mesh.shape["dp"] == 8 and mesh.shape["tensor"] == 4
 
@@ -2053,10 +2194,7 @@
         ],
         axis=1,
     )
-    def glu(gate_pre, up_pre):
-        return gelu_tanh(gate_pre) * up_pre
-
-    hidden_place, *kept, merged_stored, mixer_terms, down_in = recur_forward(
+    hidden_place, *kept, merged_stored, mixer_terms, grad_rows = recur_forward(
         n_dp,
         n_tensor,
         tok_all,
@@ -2075,21 +2213,17 @@
     after_own, hidden_two, gate_full = middle_gather(
         n_dp, n_tensor, mixer_terms, tokens, second_gain, (gate_weight,)
     )
-    gate_pre = plain_dot(hidden_two, gate_full)
-    up_pre = plain_dot(hidden_two, up_full)
-    glu_out, glu_pull = jax.vjp(glu, gate_pre, up_pre)
-    product = glu_out.astype(jnp.bfloat16)
-    grad_down = trans_times(down_in, product).astype(jnp.bfloat16)
+    product, grad_up_pre, back_terms, grad_down, grad_gate = feed_forward(
+        n_dp,
+        n_tensor,
+        hidden_two,
+        gate_full,
+        up_full,
+        down_full,
+        grad_rows,
+        grad_in_own,
+    )
     down_sum = lax.psum_scatter(grad_down, "dp", scatter_dimension=0, tiled=True)
-    down_in, _ = lax.optimization_barrier((down_in, grad_down))
-    grad_product = plain_dot(down_in, down_full)
-    grad_gate_pre, grad_up_pre = glu_pull(grad_product)
-    grad_gate_pre = grad_gate_pre.astype(jnp.bfloat16)
-    grad_up_pre = grad_up_pre.astype(jnp.bfloat16)
-    grad_gate = trans_times(hidden_two, grad_gate_pre).astype(jnp.bfloat16)
-    back_terms = (
-        times_trans(grad_gate_pre, gate_full) + times_trans(grad_up_pre, up_full)
-    ).astype(jnp.bfloat16)
     grad_after_own, second_part, mixer_in, gate_sum, grad_up, feed_terms = middle_sums(
         n_dp,
         n_tensor,

time: 571 us -> 538 us (0.942)
  matrix products: 80.6 us -> 9.49 us
  Pallas kernels: 433 us -> 468 us
    pallas_call x0 -> x1, Pallas kernels: none -> 59.9 us  [feed_forward(): pl.pallas_call(kernel, out_shape=(shaped((rows, units), low), shaped((row...]
    dot_general x5 -> x0, matrix products: 54.8 us -> none  [the longest x3 38.6 us: plain_dot(): return jnp.dot(left, right, preferred_element_type=jnp.float32)]
    dot_general x4 -> x2, matrix products: 25.7 us -> 9.49 us  [trans_times(): lax.dot_general(left, right, (((0,), (0,)), ((), ())), preferred_element_...]
    pallas_call x1, Pallas kernels: 76.7 us -> 62.5 us  [recur_backward(): pl.pallas_call(kernel, out_shape=(shaped((rows, 2 * own), low), shaped((s...]
    pallas_call x1, Pallas kernels: 77 us -> 67.4 us  [last_sums(): pl.pallas_call(kernel, out_shape=(shaped((rows, width), jnp.float32), sha...]
    pallas_call x1, Pallas kernels: 58.8 us -> 50.3 us  [recur_forward(): pl.pallas_call(kernel, out_shape=results + (shaped((n_line * cot_rows, wi...]
    pallas_call x1, Pallas kernels: 81.7 us -> 88.2 us  [middle_sums(): pl.pallas_call(kernel, out_shape=(shaped((rows, width), full), shaped((1,...]
  transfers between devices with their start and end apart: 3 -> 3, of which waited for: 0 -> 1; matrix products, arithmetic and copies ran while one was open for 19% -> 7% of each run, Pallas kernels for 68% -> 67%
where the time goes in v8:
time: 538 us; the launch traced here: 531 us
  Pallas kernels  468 us (87%)
  other arithmetic  18.1 us (3%)
  local copies, waits for them, and re-layouts  16.2 us (3%)
  between operations  14.5 us (3%)
  matrix products  9.49 us (2%)
    pallas_call x1, Pallas kernels, middle_sums(): pl.pallas_call(kernel, out_shape=(shaped((rows, width), full), shaped((1,...  88.2 us
    pallas_call x1, Pallas kernels, middle_gather(): pl.pallas_call(kernel, out_shape=(shaped((rows, width), jnp.float32), sha...  87.7 us
    pallas_call x1, Pallas kernels, last_sums(): pl.pallas_call(kernel, out_shape=(shaped((rows, width), jnp.float32), sha...  67.4 us
    pallas_call x1, Pallas kernels, recur_backward(): pl.pallas_call(kernel, out_shape=(shaped((rows, 2 * own), low), shaped((s...  62.5 us
    pallas_call x1, Pallas kernels, feed_forward(): pl.pallas_call(kernel, out_shape=(shaped((rows, units), low), shaped((row...  59.9 us
    pallas_call x1, Pallas kernels, first_gather(): pl.pallas_call(kernel, out_shape=tuple((shaped((n_dp * m.shape[0], m.shap...  51.6 us
    pallas_call x1, Pallas kernels, recur_forward(): pl.pallas_call(kernel, out_shape=results + (shaped((n_line * cot_rows, wi...  50.3 us
  transfers between devices with their start and end apart: 3, of which 1 were waited for; matrix products, arithmetic and copies ran while one was open for 7% of the time, Pallas kernels for 67%

profile of v8, /device:TPU:0, one launch (start us, length us, event | category | flops | bytes accessed | tf_op | source)
XLA Modules:
  0.0 530.5 jit_solution(5795717594403427167)
XLA Ops:
  7.9 0.8 fusion.7
  8.7 1.4 pad_maximum_fusion.refs_3_
  10.7 51.6 %first_gather.1 = (bf16[2560,640]{1,0:T(8,128)(2,1)}, bf16[2560,640]{1,0:T(8,128)(2,1)}, bf16[2560,640]{1,0:T(8,128)(2,1)}, bf16[256,1408]{1,0:T(8,128)(2,1)}, b...) custom-call(bf16[320,640]{1,0:T(8,128)(2,1)} %refs_0_.1, bf16[320,640]{1,0:T(8,128)(2,1)} %refs_1_.3, ...), custom_call_target="tpu_custom_call" | custom-call | tf_op jit(solution)/shard_map/first_gather/pallas_call | solution.py:929
  62.5 0.7 all-gather.5.cloned.1.call-update
  65.0 0.7 slice.68
  67.4 0.7 compare_convert_fusion
  68.1 0.8 and_convert_fusion.refs_11_.refs_10_
  69.0 1.1 fusion.1
  70.1 1.0 multiply_convert_fusion.1.refs_1_.refs_5_.refs_3_
  71.1 50.3 %recur_forward.1 = (bf16[512,2560]{1,0:T(8,128)(2,1)}, bf16[528,640]{1,0:T(8,128)(2,1)}, f32[512,640]{1,0:T(8,128)}, bf16[512,896]{1,0:T(8,128)(2,1)}, f32[512,6...) custom-call(bf16[512,2560]{1,0:T(8,128)(2,1)} %get-tuple-element.61., ...), custom_call_target="tpu_custom_call" | custom-call | tf_op jit(solution)/shard_map/recur_forward/pallas_call | solution.py:1584
  121.4 87.7 %middle_gather.1 = (f32[128,2560]{1,0:T(8,128)}, bf16[512,2560]{1,0:T(8,128)(2,1)}, bf16[2560,1920]{1,0:T(8,128)(2,1)}) custom-call(bf16[512,2560]{1,0:T(8,128)(2,1)} %get-tuple-element.67.refs_0_, bf16[128,2560]{1,0:T(8,128)(2,1)} %refs_1_.5, f32[1,2560]{1,0:T(1,128)} %reshape.180.refs_2_, bf16[320,1920]{1,0:T(8,128)(2,1)} %refs_3_.1), custom_call_target="tpu_custom_call" | custom-call | tf_op jit(solution)/shard_map/middle_gather/pallas_call | solution.py:1047
  209.2 3.7 all-gather.5.cloned.1.call-done.refs_3_.refs_8_
  212.9 59.9 %feed_forward.1 = (bf16[512,1920]{1,0:T(8,128)(2,1)}, bf16[512,1920]{1,0:T(8,128)(2,1)}, bf16[512,2560]{1,0:T(8,128)(2,1)}, bf16[2560,1920]{1,0:T(8,128)(2,1)}, bf16[2560,1920]{1,0:T(8,128)(2,1)}) custom-call(bf16[512,2560]{1,0:T(8,128)(2,1)} %get-tuple-element.69.refs_0_.refs_5_, bf16[2560,1920]{1,0:T(8,128)(2,1)} %get-tuple-element.70.refs_1_, ...), custom_call_target="tpu_custom_call" | custom-call | tf_op jit(solution)/shard_map/feed_forward/pallas_call | solution.py:2083
  273.5 88.2 %middle_sums.1 = (f32[128,2560]{1,0:T(8,128)}, f32[1,2560]{1,0:T(1,128)}, bf16[512,2560]{1,0:T(8,128)(2,1)}, bf16[320,1920]{1,0:T(8,128)(2,1)}, bf16[2560,1920]{1,0:T(8,128)(2,1)}, /*index=5*/bf16[512,2560]{1,0:T(8,128)(2,1)}) custom-call(bf16[512,2560]{1,0:T(8,128)(2,1)} %get-tuple-element.74.refs_0_, f32[128,2560]{1,0:T(8,128)} %get-tuple-element.68.refs_1_, ...), custom_call_target="tpu_custom_call" | custom-call | tf_op jit(solution)/shard_map/middle_sums/pallas_call | solution.py:1154
  361.7 62.5 %recur_backward.1 = (bf16[512,1280]{1,0:T(8,128)(2,1)}, bf16[256,1280]{1,0:T(8,128)(2,1)}, f32[8,640]{1,0:T(8,128)}, f32[1,640]{1,0:T(1,128)}, bf16[512,2560]{1,...) custom-call(bf16[512,2560]{1,0:T(8,128)(2,1)} %get-tuple-element.78.refs_0_, ...), custom_call_target="tpu_custom_call" | custom-call | tf_op jit(solution)/shard_map/recur_backward/pallas_call | solution.py:1915
  424.3 0.8 slice_bitcast_fusion
  425.1 2.9 convert_element_type.92
  428.0 1.6 convert_element_type.91
  429.6 1.0 copy-done.2
  430.8 4.0 convolution_convert_fusion.1.refs_6_
  434.7 0.7 fusion.2.refs_4_
  435.4 5.5 %convolution_convert_fusion.refs_5_ = bf16[2560,1280]{1,0:T(8,128)(2,1)} fusion(bf16[512,2560]{1,0:T(8,128)(2,1)S(1)} %copy-done.11, bf16[512,1280]{1,0:T(8,128)(2,1)S(1)} %copy-done.12), kind=kOutput, calls=%fused_computation | convolution fusion | flops 3358720000 | bytes 10485760 | tf_op jit(solution)/shard_map/dot_general | solution.py:81
  441.0 67.4 %last_sums.1 = (f32[128,2560]{1,0:T(8,128)}, f32[4,2560]{1,0:T(4,128)}, f32[2,2560]{1,0:T(2,128)}, bf16[320,1280]{1,0:T(8,128)(2,1)}, bf16[320,640]{1,0:T(8,128)(2,1)}, /*index=5*/bf16[32,1280]{1,0:T(8,128)(2,1)}) custom-call(bf16[512,2560]{1,0:T(8,128)(2,1)} %get-tuple-element.90.refs_0_, bf16[128,2560]{1,0:T(8,128)(2,1)} %refs_1_.5, ...), custom_call_target="tpu_custom_call" | custom-call | tf_op jit(solution)/shard_map/last_sums/pallas_call | solution.py:1267
  508.4 1.0 slice_reduce_fusion
  510.0 1.4 dynamic-slice_reduce_fusion
  511.4 1.3 slice_reduce_fusion.1
  512.7 1.5 fusion.13
  514.2 1.9 convert_bitcast_fusion.1
  516.1 2.4 fusion.12
  518.5 1.0 multiply_convert_fusion
  519.5 3.0 convert_bitcast_fusion
  522.5 1.1 copy.44
  (70 shorter events, 6.3 us)
Async XLA Ops:
  7.2 56.0 %copy-start.14 = (s32[3]{0:T(128)S(1)}, s32[3]{0:T(128)}, u32[]{:S(2)}) copy-start(s32[3]{0:T(128)} %param.29) | copy-start | bytes 40
  7.2 56.8 %copy-start.9 = (f32[640]{0:T(1024)S(1)}, f32[640]{0:T(1024)}, u32[]{:S(2)}) copy-start(f32[640]{0:T(1024)} %param.23) | copy-start | bytes 7684
  7.2 202.0 %all-gather.3.cloned.1.call-start = ((), (), s32[]{:S(2)}) async-start(), calls=%async_computation.1 | async-start | bytes 11059200 | tf_op jit(solution)/shard_map/all_gather | solution.py:2159
  62.3 3.4 copy-start.5
  62.4 5.1 copy-start.15
  62.4 7.7 %copy-start.6 = (bf16[128,2560]{1,0:T(8,128)(2,1)S(1)}, bf16[128,2560]{1,0:T(8,128)(2,1)}, u32[]{:S(2)}) copy-start(bf16[128,2560]{1,0:T(8,128)(2,1)} %param.31) | copy-start | bytes 1966084
  62.4 150.4 %all-gather.5.cloned.1.call-start = ((), (), s32[]{:S(2)}) async-start(), calls=%async_computation.2 | async-start | bytes 11059200 | tf_op jit(solution)/shard_map/all_gather | solution.py:2160
  63.2 456.4 %reduce-scatter.2.cloned.1.call-start = ((), (), s32[]{:S(2)}) async-start(), calls=%async_computation.3 | async-start | bytes 11059200 | tf_op jit(solution)/shard_map/reduce_scatter | solution.py:2226
  67.4 3.7 copy-start.1
  424.2 3.7 copy-start.4
  428.0 2.6 copy-start.2
  428.0 2.8 copy-start.13
  430.7 4.0 copy-start.8
  430.8 4.0 copy-start.10
  430.8 4.7 copy-start.11
  430.8 4.7 copy-start.12
  508.4 10.1 %copy-start = (f32[128,2560]{1,0:T(8,128)S(1)}, f32[128,2560]{1,0:T(8,128)}, u32[]{:S(2)}) copy-start(f32[128,2560]{1,0:T(8,128)} %get-tuple-element.68.refs_1_) | copy-start | bytes 3932164
  508.4 10.1 %copy-start.7 = (bf16[128,2560]{1,0:T(8,128)(2,1)S(1)}, bf16[128,2560]{1,0:T(8,128)(2,1)}, u32[]{:S(2)}) copy-start(bf16[128,2560]{1,0:T(8,128)(2,1)} %get-tuple-element.89) | copy-start | bytes 1966084
  519.5 3.0 copy-start.3
Sparse Core Ops, SparseCore 0:
  62.5 61.2 all-gather.2
  125.7 87.0 all-gather.4
  273.0 102.5 reduce-scatter.1

commit v9 on v8

--- a/solution.py
+++ b/solution.py
@@ -1061,18 +1061,20 @@
     )(terms, tokens, gain, *mats)
 
 
-def middle_sums(n_dp, n_line, terms, after, gain, grad_in, mat, hidden, grad_up, product, down):
+def middle_sums(
+    n_dp, n_line, terms, after, gain, grad_in, grad_gate, hidden, grad_up, product, down
+):
     rows, width = after.shape
-    block = mat.shape[0] // n_dp
+    block = width // n_dp
     wide = grad_up.shape[1]
     spread_rows = n_line * rows
 
     def kernel(*refs):
-        s, after_ref, gain_ref, g_ref, src = refs[:5]
+        s, after_ref, gain_ref, g_ref, gg_far = refs[:5]
         hid_far, gu_far, pr_far, dw_far = refs[5:9]
-        grad_after, gain_sum, spread, result, up_far, feed_far = refs[9:15]
-        hid, gu, pr, dw, up_out, feed, sems = refs[15:22]
-        rest = refs[22:]
+        grad_after, gain_sum, spread, result, up_far, feed_far, gate_far = refs[9:16]
+        hid, gu, pr, dw, gg, up_out, feed, sems = refs[16:24]
+        rest = refs[24:]
         fetch = Fetch(
             [
                 (hid_far, hid),
@@ -1082,15 +1084,17 @@
                 (feed, feed_far),
                 (up_out.at[0], up_far.at[pl.ds(0, width // 2)]),
                 (up_out.at[1], up_far.at[pl.ds(width // 2, width // 2)]),
+                (gg_far, gg),
+                (up_out.at[0], gate_far.at[pl.ds(0, width // 2)]),
+                (up_out.at[1], gate_far.at[pl.ds(width // 2, width // 2)]),
             ],
             sems,
         )
-        fetch.start(0, 1, 2, 3)
+        fetch.start(0, 7, 1, 2, 3)
         place = Place(n_dp, n_line)
         place.meet()
-        plane = ReducePlane(place, src, rest[:7])
+        plane = ReducePlane(place, gate_far, rest[:7])
         scratch = rest[7:]
-        plane.begin()
         gain_sum[...] = jnp.zeros_like(gain_sum)
 
         def norm(c, here, total):
@@ -1106,27 +1110,37 @@
             cols = pl.ds(i * (width // 4), width // 4)
             feed[:, cols] = times_trans(pr[...], dw[cols]).astype(jnp.bfloat16)
 
-        def up_part(i):
+        def rows_part(right, i):
             cols = pl.ds(i * (width // 4), width // 4)
             here = pl.ds((i % 2) * (width // 4), width // 4)
-            up_out[i // 2, here] = trans_times(hid[:, cols], gu[...]).astype(jnp.bfloat16)
-
-        def early():
+            up_out[i // 2, here] = trans_times(hid[:, cols], right[...]).astype(jnp.bfloat16)
+
+        def zero():
+            fetch.wait(0, 7)
+            rows_part(gg, 0)
+            rows_part(gg, 1)
+            fetch.start(8)
+
+        def one():
+            rows_part(gg, 2)
+            rows_part(gg, 3)
+            fetch.start(9)
+
+        def two():
+            fetch.wait(1, 8, 9)
+            plane.begin()
+            rows_part(gu, 0)
+
+        def three():
             plane.cores()
-            fetch.wait(0, 1)
-
-        def two():
-            up_part(0)
-
-        def three():
-            up_part(1)
+            rows_part(gu, 1)
             fetch.start(5)
 
         def four():
-            up_part(2)
+            rows_part(gu, 2)
 
         def five():
-            up_part(3)
+            rows_part(gu, 3)
             fetch.start(6)
             fetch.wait(2, 3)
 
@@ -1144,7 +1158,7 @@
             feed_part(3)
             fetch.start(4)
 
-        steps = {1: early, 2: two, 3: three, 4: four, 5: five, 6: six, 7: seven, 8: eight, 9: nine}
+        steps = dict(enumerate((zero, one, two, three, four, five, six, seven, eight, nine)))
         sum_rows_and_spread(place, s, scratch, norm, spread, steps)
         plane.finish(result)
         fetch.wait(4, 5, 6)
@@ -1157,23 +1171,24 @@
             shaped((rows, width), full),
             shaped((1, width), full),
             shaped((spread_rows, width), low),
-            shaped((block, mat.shape[1]), low),
+            shaped((block, wide), low),
             shaped((width, wide), low),
             shaped((spread_rows, width), low),
+            shaped((width, wide), low),
         ),
         in_specs=[near] * 4 + [far] * 5,
-        out_specs=[near] * 4 + [far] * 2,
-        scratch_shapes=[vmem_like(m) for m in (hidden, grad_up, product, down)]
+        out_specs=[near] * 4 + [far] * 3,
+        scratch_shapes=[vmem_like(m) for m in (hidden, grad_up, product, down, grad_gate)]
         + [
             pltpu.VMEM((2, width // 2, wide), low),
             pltpu.VMEM((spread_rows, width), low),
-            dma_sems(7),
+            dma_sems(10),
         ]
-        + ReducePlane.scratch(block, mat.shape[1])
+        + ReducePlane.scratch(block, wide)
         + line_scratch(n_line, rows // CHUNKS, width, CHUNKS),
         compiler_params=comm_params(3),
         name="middle_sums",
-    )(terms, after, gain, grad_in, mat, hidden, grad_up, product, down)
+    )(terms, after, gain, grad_in, grad_gate, hidden, grad_up, product, down)
 
 
 class Exchange:
@@ -1625,6 +1640,34 @@
     )
 
 
+class RowProducts:
+    def __init__(self, left, right, far, stage, sems):
+        self.left, self.right, self.far, self.stage, self.sems = left, right, far, stage, sems
+        self.part = stage.shape[1]
+        self.count = far.shape[0] // self.part
+
+    def slot(self, i):
+        return self.stage.at[i % 2, :, pl.ds(0, self.far.shape[1])]
+
+    def copy(self, i):
+        some = pl.ds(i * self.part, self.part)
+        return pltpu.make_async_copy(self.slot(i), self.far.at[some], self.sems.at[i])
+
+    def run(self):
+        for i in range(self.count):
+            if i >= 2:
+                self.copy(i - 2).wait()
+            some = pl.ds(i * self.part, self.part)
+            self.slot(i)[...] = trans_times(self.left[:, some], self.right[...]).astype(
+                jnp.bfloat16
+            )
+            self.copy(i).start()
+
+    def finish(self):
+        self.copy(self.count - 2).wait()
+        self.copy(self.count - 1).wait()
+
+
 def recur_backward(
     n_dp,
     n_line,
@@ -1642,6 +1685,8 @@
     kept,
     weight_terms,
     row_terms,
+    hidden_place,
+    merged_stored,
 ):
     rows, width = mixer_in.shape
     count, own = taps.shape
@@ -1655,14 +1700,16 @@
 
     def kernel(*refs):
         (mix_far, plc, sto, wx_far, wy_far, wo_far, gw, cw, sp, sg, fl) = refs[:11]
-        kept_far, weights, feed_far = refs[11:19], refs[19], refs[20]
-        (gxy_far, gate_grads, tap_grads, decay_grad, terms_far, weight_sum, row_sum) = refs[21:28]
-        mix, wy, wo, feed = refs[28:32]
-        (xext, y, conv_low, conv, pre_r, pre_i, rate, state) = refs[32:40]
-        (gxy, mp, gm, lam, reach, gp_r, gp_i, grad, spread, rim_out, rim_in) = refs[40:51]
-        (ret_out, ret_in, tap_sums, decay_sums, ends, agg, slots) = refs[51:58]
-        (hs, hr, es, er, el, in_sems, out_sems, inbox, ls, lr, total) = refs[58:69]
-        terms, wx = mix, wo
+        kept_far, weights, feed_far, hp_far, merged_far = refs[11:19], *refs[19:23]
+        (gate_grads, tap_grads, decay_grad, terms_far, weight_sum, row_sum) = refs[23:29]
+        out_far, xy_far = refs[29:31]
+        mix, wy, wo, feed, merged = refs[31:36]
+        (xext, y, conv_low, conv, pre_r, pre_i, rate, state) = refs[36:44]
+        (gxy, mp, gm, lam, reach, gp_r, gp_i, grad, spread, rim_out, rim_in) = refs[44:55]
+        (ret_out, ret_in, tap_sums, decay_sums, ends, agg, slots) = refs[55:62]
+        (hs, hr, es, er, el, in_sems, out_sems, inbox, ls, lr, total) = refs[62:73]
+        stage, stage_sems = refs[73:75]
+        hp, terms, wx = mix, mix, wo
         fetch = Fetch(
             [
                 (mix_far, mix),
@@ -1678,14 +1725,18 @@
                 (wx_far, wx),
                 (wy_far, wy),
                 (feed_far, feed),
+                (merged_far, merged),
+                (hp_far, hp),
             ],
             in_sems,
         )
-        fetch.start(12, *range(10), 11)
-        store = Fetch(((gxy, gxy_far), (terms, terms_far)), out_sems)
+        fetch.start(12, 0, 1, 13)
+        store = Fetch(((terms, terms_far),), out_sems)
+        out_rows = RowProducts(mix, merged, out_far, stage, stage_sems.at[0])
+        xy_rows = RowProducts(hp, gxy, xy_far, stage, stage_sems.at[1])
         place = Place(n_dp, n_line)
         place.meet(True)
-        plane = ReducePlane(place, weights, refs[69:])
+        plane = ReducePlane(place, weights, refs[75:])
         plane.begin()
         lines = [
             ReduceLine(place, feed, own_rows, c * span, span, inbox.at[c], ls.at[c], lr.at[c])
@@ -1704,6 +1755,7 @@
 
         fetch.wait(12)
         send(0)
+        fetch.start(*range(2, 10), 11)
         swap = RimSwap(place, own)
         own_cols = pl.ds(RIM, own)
 
@@ -1715,6 +1767,9 @@
         fetch.wait(0, 1)
         loop(rows // 128, project)
         fetch.start(10)
+        fetch.wait(13)
+        out_rows.run()
+        fetch.start(14)
 
         def split(i):
             here = tile_rows(i, TILE)
@@ -1881,8 +1936,10 @@
         for k in range(count):
             tap_grads[k : k + 1] = jnp.sum(tap_sums[k], axis=0, keepdims=True)
 
-        store.start(0)
+        fetch.wait(14)
+        out_rows.finish()
         plane.turn()
+        xy_rows.run()
         send(4)
         lines[3].hop(0)
 
@@ -1900,14 +1957,15 @@
 
         fetch.wait(10, 11)
         loop(width // 512, spread_back)
-        store.start(1)
+        store.start(0)
         lines[3].hop(1)
         add_up(2)
         plane.finish(weight_sum)
         add_up(3)
         for line in lines:
             line.finish()
-        store.wait(0, 1)
+        xy_rows.finish()
+        store.wait(0)
 
     low, full = jnp.bfloat16, jnp.float32
     block = weight_terms.shape[0] // n_dp
@@ -1915,17 +1973,20 @@
     return pl.pallas_call(
         kernel,
         out_shape=(
-            shaped((rows, 2 * own), low),
             shaped((size, 2 * own), low),
             shaped((8, own), full),
             shaped((1, own), full),
             shaped((rows, width), low),
             shaped((block, weight_terms.shape[1]), low),
             shaped((own_rows, width), low),
+            shaped((width, own), low),
+            shaped((width, 2 * own), low),
         ),
-        in_specs=[far, near, near, far, far, far] + [near] * 5 + [far] * 10,
-        out_specs=[far, near, near, near, far, near, near],
-        scratch_shapes=[vmem_like(m) for m in (mixer_in, y_full, out_full, row_terms, *kept)]
+        in_specs=[far, near, near, far, far, far] + [near] * 5 + [far] * 12,
+        out_specs=[near, near, near, far, near, near, far, far],
+        scratch_shapes=[
+            vmem_like(m) for m in (mixer_in, y_full, out_full, row_terms, merged_stored, *kept)
+        ]
         + [
             pltpu.VMEM((rows, 2 * own), low),
             pltpu.VMEM((rows, width), low),
@@ -1950,12 +2011,14 @@
             dma_sems(n_dp),
             dma_sems(n_dp),
             pltpu.SemaphoreType.DMA,
-            dma_sems(13),
-            dma_sems(2),
+            dma_sems(15),
+            dma_sems(1),
             pltpu.VMEM((parts, 2, n_line - 1, span, width), low),
             dma_sems(parts, 2, n_line - 1),
             dma_sems(parts, 2, n_line - 1),
             pltpu.VMEM((span, width), full),
+            pltpu.VMEM((2, width // 5, 2 * own), low),
+            dma_sems(2, 5),
         ]
         + ReducePlane.scratch(block, weight_terms.shape[1]),
         compiler_params=comm_params(6),
@@ -1975,6 +2038,8 @@
         *kept,
         weight_terms,
         row_terms,
+        hidden_place,
+        merged_stored,
     )
 
 
@@ -1992,7 +2057,7 @@
 
     def kernel(*refs):
         hid_far, wg_far, wu_far, wd_far, grads_far, own_far = refs[:6]
-        product_far, gup_far, back_far, gdown_far, ggate_far = refs[6:11]
+        product_far, gup_far, back_far, gdown_far, gg_far = refs[6:11]
         hid, wg, wu, wd, grad, slope, branch, product, ggate, gup, stage, back = refs[11:23]
         in_sems, out_sems, stage_sems, ls, lr = refs[23:]
         place = Place(n_dp, n_line)
@@ -2005,7 +2070,9 @@
         pairs.append((own_far.at[pl.ds(ready, late)], grad.at[mine]))
         fetch = Fetch(pairs, in_sems)
         fetch.start(*range(len(pairs)))
-        store = Fetch(((product, product_far), (gup, gup_far), (back, back_far)), out_sems)
+        store = Fetch(
+            ((product, product_far), (gup, gup_far), (back, back_far), (ggate, gg_far)), out_sems
+        )
         place.meet()
         line = GatherLine(place, grad, own_rows, ready, late, ls, lr)
         line.step(0, own_far.at[pl.ds(ready, late)])
@@ -2038,26 +2105,8 @@
         fetch.wait(*range(4, len(pairs)))
         line.finish()
 
-        def weight_rows(left, right, far, first):
-            for i in range(4):
-                some = pl.ds(i * part, part)
-                copy = pltpu.make_async_copy(
-                    stage.at[i % 2], far.at[some], stage_sems.at[first + i]
-                )
-                if i >= 2:
-                    pltpu.make_async_copy(
-                        stage.at[i % 2],
-                        far.at[pl.ds((i - 2) * part, part)],
-                        stage_sems.at[first + i - 2],
-                    ).wait()
-                stage[i % 2] = trans_times(left[:, some], right[...]).astype(jnp.bfloat16)
-                copy.start()
-            for i in (2, 3):
-                pltpu.make_async_copy(
-                    stage.at[i % 2], far.at[pl.ds(i * part, part)], stage_sems.at[first + i]
-                ).wait()
-
-        weight_rows(grad, product, gdown_far, 0)
+        down_rows = RowProducts(grad, product, gdown_far, stage, stage_sems)
+        down_rows.run()
         fetch.wait(3)
         for c, size in columns:
             cols = pl.ds(c, size)
@@ -2069,15 +2118,15 @@
                 gup[here, cols] = (value * branch[here, cols]).astype(jnp.bfloat16)
 
             loop(rows // 256, backs)
-        store.start(1)
+        store.start(1, 3)
         for i in range(4):
             some = pl.ds(i * part, part)
             back[:, some] = (
                 times_trans(ggate[...], wg[some]) + times_trans(gup[...], wu[some])
             ).astype(jnp.bfloat16)
         store.start(2)
-        weight_rows(hid, ggate, ggate_far, 4)
-        store.wait(0, 1, 2)
+        down_rows.finish()
+        store.wait(0, 1, 2, 3)
 
     low, full = jnp.bfloat16, jnp.float32
     return pl.pallas_call(
@@ -2087,7 +2136,7 @@
             shaped((rows, units), low),
             shaped((rows, width), low),
             shaped((width, units), low),
-            shaped((width, units), low),
+            shaped((rows, units), low),
         ),
         in_specs=[in_any()] * 6,
         out_specs=[in_any()] * 5,
@@ -2102,8 +2151,8 @@
             pltpu.VMEM((2, part, units), low),
             pltpu.VMEM((rows, width), low),
             dma_sems(5 + n_line),
-            dma_sems(3),
-            dma_sems(8),
+            dma_sems(4),
+            dma_sems(4),
             dma_sems(2, n_line - 1),
             dma_sems(2, n_line - 1),
         ],
@@ -2213,7 +2262,7 @@
     after_own, hidden_two, gate_full = middle_gather(
         n_dp, n_tensor, mixer_terms, tokens, second_gain, (gate_weight,)
     )
-    product, grad_up_pre, back_terms, grad_down, grad_gate = feed_forward(
+    product, grad_up_pre, back_terms, grad_down, grad_gate_pre = feed_forward(
         n_dp,
         n_tensor,
         hidden_two,
@@ -2224,20 +2273,29 @@
         grad_in_own,
     )
     down_sum = lax.psum_scatter(grad_down, "dp", scatter_dimension=0, tiled=True)
-    grad_after_own, second_part, mixer_in, gate_sum, grad_up, feed_terms = middle_sums(
+    grad_after_own, second_part, mixer_in, gate_sum, grad_up, feed_terms, _ = middle_sums(
         n_dp,
         n_tensor,
         back_terms,
         after_own,
         second_gain,
         grad_in_own,
-        grad_gate,
+        grad_gate_pre,
         hidden_two,
         grad_up_pre,
         product,
         down_full,
     )
-    grad_xy, gate_grads, tap_grads, decay_grad, one_terms, up_sum, feed_out = recur_backward(
+    (
+        gate_grads,
+        tap_grads,
+        decay_grad,
+        one_terms,
+        up_sum,
+        feed_out,
+        grad_out_mat,
+        grad_xy_mat,
+    ) = recur_backward(
         n_dp,
         n_tensor,
         mixer_in,
@@ -2254,11 +2312,11 @@
         kept,
         grad_up,
         feed_terms,
+        hidden_place,
+        merged_stored,
     )
     output = (after_own + feed_out.astype(jnp.float32)) * live_own[:, None]
     output = output.astype(jnp.bfloat16)
-    grad_out_mat = trans_times(mixer_in, merged_stored).astype(jnp.bfloat16)
-    grad_xy_mat = trans_times(hidden_place, grad_xy).astype(jnp.bfloat16)
     small = jnp.concatenate(
         [
             second_part,

time: 538 us -> 537 us (level)
  Pallas kernels: 468 us -> 481 us
  matrix products: 9.49 us -> 0 us
    pallas_call x1, Pallas kernels: 88.2 us -> 106 us  [middle_sums(): pl.pallas_call(kernel, out_shape=(shaped((rows, width), full), shaped((1,...]
    dot_general x2 -> x0, matrix products: 9.49 us -> none  [trans_times(): lax.dot_general(left, right, (((0,), (0,)), ((), ())), preferred_element_...]
    pallas_call x1, Pallas kernels: 59.9 us -> 52.3 us  [feed_forward(): pl.pallas_call(kernel, out_shape=(shaped((rows, units), low), shaped((row...]
  transfers between devices with their start and end apart: 3 -> 3, of which waited for: 1 -> 1; matrix products, arithmetic and copies ran while one was open for 7% -> 4% of each run, Pallas kernels for 67% -> 71%
where the time goes in v9:
time: 537 us; the launch traced here: 530 us
  Pallas kernels  481 us (90%)
  other arithmetic  16.5 us (3%)
  between operations  14.5 us (3%)
  local copies, waits for them, and re-layouts  13 us (2%)
    pallas_call x1, Pallas kernels, middle_sums(): pl.pallas_call(kernel, out_shape=(shaped((rows, width), full), shaped((1,...  106 us
    pallas_call x1, Pallas kernels, middle_gather(): pl.pallas_call(kernel, out_shape=(shaped((rows, width), jnp.float32), sha...  87.6 us
    pallas_call x1, Pallas kernels, last_sums(): pl.pallas_call(kernel, out_shape=(shaped((rows, width), jnp.float32), sha...  66.8 us
    pallas_call x1, Pallas kernels, recur_backward(): pl.pallas_call(kernel, out_shape=(shaped((size, 2 * own), low), shaped((8...  66.7 us
    pallas_call x1, Pallas kernels, feed_forward(): pl.pallas_call(kernel, out_shape=(shaped((rows, units), low), shaped((row...  52.3 us
    pallas_call x1, Pallas kernels, first_gather(): pl.pallas_call(kernel, out_shape=tuple((shaped((n_dp * m.shape[0], m.shap...  51.6 us
    pallas_call x1, Pallas kernels, recur_forward(): pl.pallas_call(kernel, out_shape=results + (shaped((n_line * cot_rows, wi...  50.3 us
  transfers between devices with their start and end apart: 3, of which 1 were waited for; matrix products, arithmetic and copies ran while one was open for 4% of the time, Pallas kernels for 71%

profile of v9, /device:TPU:0, one launch (start us, length us, event | category | flops | bytes accessed | tf_op | source)
XLA Modules:
  0.0 529.9 jit_solution(9685877792229596203)
XLA Ops:
  7.2 0.7 broadcast_subtract_fusion
  7.9 0.8 fusion.7
  8.7 1.4 pad_maximum_fusion.refs_3_
  10.7 51.6 %first_gather.1 = (bf16[2560,640]{1,0:T(8,128)(2,1)}, bf16[2560,640]{1,0:T(8,128)(2,1)}, bf16[2560,640]{1,0:T(8,128)(2,1)}, bf16[256,1408]{1,0:T(8,128)(2,1)}, b...) custom-call(bf16[320,640]{1,0:T(8,128)(2,1)} %refs_0_.1, bf16[320,640]{1,0:T(8,128)(2,1)} %refs_1_.3, ...), custom_call_target="tpu_custom_call" | custom-call | tf_op jit(solution)/shard_map/first_gather/pallas_call | solution.py:929
  62.4 0.7 all-gather.5.cloned.1.call-update
  65.0 0.7 slice.68
  65.9 0.7 reshape.180.refs_2_
  66.5 0.7 reshape.179.refs_7_.refs_2_
  67.4 0.7 compare_convert_fusion
  68.1 0.8 and_convert_fusion.refs_11_.refs_10_
  68.9 1.1 fusion.1
  70.1 1.0 multiply_convert_fusion.1.refs_1_.refs_5_.refs_3_
  71.1 50.3 %recur_forward.1 = (bf16[512,2560]{1,0:T(8,128)(2,1)}, bf16[528,640]{1,0:T(8,128)(2,1)}, f32[512,640]{1,0:T(8,128)}, bf16[512,896]{1,0:T(8,128)(2,1)}, f32[512,6...) custom-call(bf16[512,2560]{1,0:T(8,128)(2,1)} %get-tuple-element.62., ...), custom_call_target="tpu_custom_call" | custom-call | tf_op jit(solution)/shard_map/recur_forward/pallas_call | solution.py:1599
  121.4 87.6 %middle_gather.1 = (f32[128,2560]{1,0:T(8,128)}, bf16[512,2560]{1,0:T(8,128)(2,1)}, bf16[2560,1920]{1,0:T(8,128)(2,1)}) custom-call(bf16[512,2560]{1,0:T(8,128)(2,1)} %get-tuple-element.68.refs_0_, bf16[128,2560]{1,0:T(8,128)(2,1)} %refs_1_.5, f32[1,2560]{1,0:T(1,128)} %reshape.180.refs_2_, bf16[320,1920]{1,0:T(8,128)(2,1)} %refs_3_.1), custom_call_target="tpu_custom_call" | custom-call | tf_op jit(solution)/shard_map/middle_gather/pallas_call | solution.py:1047
  209.1 3.7 all-gather.5.cloned.1.call-done.refs_3_.refs_8_
  212.8 52.3 %feed_forward.1 = (bf16[512,1920]{1,0:T(8,128)(2,1)}, bf16[512,1920]{1,0:T(8,128)(2,1)}, bf16[512,2560]{1,0:T(8,128)(2,1)}, bf16[2560,1920]{1,0:T(8,128)(2,1)}, bf16[512,1920]{1,0:T(8,128)(2,1)}) custom-call(bf16[512,2560]{1,0:T(8,128)(2,1)} %get-tuple-element.70.refs_0_.refs_5_, bf16[2560,1920]{1,0:T(8,128)(2,1)} %get-tuple-element.71.refs_1_, ...), custom_call_target="tpu_custom_call" | custom-call | tf_op jit(solution)/shard_map/feed_forward/pallas_call | solution.py:2132
  265.9 105.9 %middle_sums.1 = (f32[128,2560]{1,0:T(8,128)}, f32[1,2560]{1,0:T(1,128)}, bf16[512,2560]{1,0:T(8,128)(2,1)}, bf16[320,1920]{1,0:T(8,128)(2,1)}, bf16[2560,1920]{...) custom-call(bf16[512,2560]{1,0:T(8,128)(2,1)} %get-tuple-element.75.refs_0_, ...), custom_call_target="tpu_custom_call" | custom-call | tf_op jit(solution)/shard_map/middle_sums/pallas_call | solution.py:1168
  371.8 66.7 %recur_backward.1 = (bf16[256,1280]{1,0:T(8,128)(2,1)}, f32[8,640]{1,0:T(8,128)}, f32[1,640]{1,0:T(1,128)}, bf16[512,2560]{1,0:T(8,128)(2,1)}, bf16[320,1920]{1,...) custom-call(bf16[512,2560]{1,0:T(8,128)(2,1)} %get-tuple-element.79.refs_0_, ...), custom_call_target="tpu_custom_call" | custom-call | tf_op jit(solution)/shard_map/recur_backward/pallas_call | solution.py:1973
  438.5 0.7 slice_bitcast_fusion
  439.3 1.4 fusion.2.refs_4_
  440.6 66.8 %last_sums.1 = (f32[128,2560]{1,0:T(8,128)}, f32[4,2560]{1,0:T(4,128)}, f32[2,2560]{1,0:T(2,128)}, bf16[320,1280]{1,0:T(8,128)(2,1)}, bf16[320,640]{1,0:T(8,128)(2,1)}, /*index=5*/bf16[32,1280]{1,0:T(8,128)(2,1)}) custom-call(bf16[512,2560]{1,0:T(8,128)(2,1)} %get-tuple-element.93.refs_0_, bf16[128,2560]{1,0:T(8,128)(2,1)} %refs_1_.5, ...), custom_call_target="tpu_custom_call" | custom-call | tf_op jit(solution)/shard_map/last_sums/pallas_call | solution.py:1282
  507.5 0.9 slice_reduce_fusion
  509.0 1.6 convert_element_type.84
  510.6 1.6 convert_element_type.83
  512.2 1.4 dynamic-slice_reduce_fusion
  513.6 1.3 slice_reduce_fusion.1
  515.0 0.7 fusion.13
  515.6 0.9 convert_bitcast_fusion.1
  516.6 1.3 fusion.12
  517.9 1.0 multiply_convert_fusion
  518.9 3.0 convert_bitcast_fusion
  521.9 1.1 copy.44
  (66 shorter events, 4.1 us)
Async XLA Ops:
  7.2 201.9 %all-gather.3.cloned.1.call-start = ((), (), s32[]{:S(2)}) async-start(), calls=%async_computation.1 | async-start | bytes 11059200 | tf_op jit(solution)/shard_map/all_gather | solution.py:2208
  10.7 52.5 %copy-start.13 = (s32[3]{0:T(128)S(1)}, s32[3]{0:T(128)}, u32[]{:S(2)}) copy-start(s32[3]{0:T(128)} %param.29) | copy-start | bytes 40
  10.7 53.3 %copy-start.12 = (f32[640]{0:T(1024)S(1)}, f32[640]{0:T(1024)}, u32[]{:S(2)}) copy-start(f32[640]{0:T(1024)} %param.23) | copy-start | bytes 7684
  62.3 3.4 copy-start.6
  62.4 5.0 copy-start.14
  62.4 150.5 %all-gather.5.cloned.1.call-start = ((), (), s32[]{:S(2)}) async-start(), calls=%async_computation.2 | async-start | bytes 11059200 | tf_op jit(solution)/shard_map/all_gather | solution.py:2209
  63.1 6.9 %copy-start.7 = (bf16[128,2560]{1,0:T(8,128)(2,1)S(1)}, bf16[128,2560]{1,0:T(8,128)(2,1)}, u32[]{:S(2)}) copy-start(bf16[128,2560]{1,0:T(8,128)(2,1)} %param.31) | copy-start | bytes 1966084
  63.1 455.8 %reduce-scatter.2.cloned.1.call-start = ((), (), s32[]{:S(2)}) async-start(), calls=%async_computation.3 | async-start | bytes 11059200 | tf_op jit(solution)/shard_map/reduce_scatter | solution.py:2275
  67.4 3.7 copy-start.1
  371.8 67.5 %copy-start.11 = (f32[1,2560]{1,0:T(1,128)S(1)}, f32[1,2560]{1,0:T(1,128)}, u32[]{:S(2)}) copy-start(f32[1,2560]{1,0:T(1,128)} %get-tuple-element.95) | copy-start | bytes 30724
  440.6 68.4 %copy-start.5 = (bf16[320,1920]{1,0:T(8,128)(2,1)S(1)}, bf16[320,1920]{1,0:T(8,128)(2,1)}, u32[]{:S(2)}) copy-start(bf16[320,1920]{1,0:T(8,128)(2,1)} %get-tuple-element.108) | copy-start | bytes 3686404
  507.5 3.1 copy-start.4
  510.6 4.3 copy-start.10
  510.6 5.0 copy-start.9
  510.6 6.0 %copy-start.2 = (bf16[320,1280]{1,0:T(8,128)(2,1)S(1)}, bf16[320,1280]{1,0:T(8,128)(2,1)}, u32[]{:S(2)}) copy-start(bf16[320,1280]{1,0:T(8,128)(2,1)} %get-tuple-element.103) | copy-start | bytes 2457604
  515.6 2.2 copy-start
  515.6 2.2 copy-start.8
  518.9 3.0 copy-start.3
Sparse Core Ops, SparseCore 0:
  62.5 61.2 all-gather.2
  125.7 87.0 all-gather.4
  265.3 107.6 reduce-scatter.1

commit v10 on v9

--- a/solution.py
+++ b/solution.py
@@ -1039,7 +1039,13 @@
             first = pl.multiple_of(place.t * rows, 16) + c * total.shape[0]
             hidden[pl.ds(pl.multiple_of(first, 16), total.shape[0])] = low
 
-        between = {6: planes[0].forward, 9: planes[0].share}
+        between = {
+            2: planes[1].begin,
+            6: planes[0].forward,
+            8: planes[1].forward,
+            9: planes[0].share,
+            10: planes[1].share,
+        }
         sum_rows_and_spread(place, s, scratch, norm, hidden, between)
         for part in planes:
             part.finish()
@@ -1062,39 +1068,39 @@
 
 
 def middle_sums(
-    n_dp, n_line, terms, after, gain, grad_in, grad_gate, hidden, grad_up, product, down
+    n_dp, n_line, terms, after, gain, grad_in, mat, hidden, grad_up, product, down, down_rest
 ):
     rows, width = after.shape
-    block = width // n_dp
+    block = mat.shape[0] // n_dp
     wide = grad_up.shape[1]
     spread_rows = n_line * rows
 
     def kernel(*refs):
-        s, after_ref, gain_ref, g_ref, gg_far = refs[:5]
-        hid_far, gu_far, pr_far, dw_far = refs[5:9]
-        grad_after, gain_sum, spread, result, up_far, feed_far, gate_far = refs[9:16]
-        hid, gu, pr, dw, gg, up_out, feed, sems = refs[16:24]
-        rest = refs[24:]
+        s, after_ref, gain_ref, g_ref, src = refs[:5]
+        hid_far, gu_far, pr_far, dw_far, dw_rest = refs[5:10]
+        grad_after, gain_sum, spread, result, up_far, feed_far = refs[10:16]
+        hid, gu, pr, dw, up_out, feed, sems = refs[16:23]
+        rest = refs[23:]
+        cut = dw_far.shape[1]
         fetch = Fetch(
             [
                 (hid_far, hid),
                 (gu_far, gu),
                 (pr_far, pr),
-                (dw_far, dw),
+                (dw_far, dw.at[:, pl.ds(0, cut)]),
                 (feed, feed_far),
                 (up_out.at[0], up_far.at[pl.ds(0, width // 2)]),
                 (up_out.at[1], up_far.at[pl.ds(width // 2, width // 2)]),
-                (gg_far, gg),
-                (up_out.at[0], gate_far.at[pl.ds(0, width // 2)]),
-                (up_out.at[1], gate_far.at[pl.ds(width // 2, width // 2)]),
+                (dw_rest, dw.at[:, pl.ds(cut, wide - cut)]),
             ],
             sems,
         )
-        fetch.start(0, 7, 1, 2, 3)
+        fetch.start(0, 1, 2, 3, 7)
         place = Place(n_dp, n_line)
         place.meet()
-        plane = ReducePlane(place, gate_far, rest[:7])
+        plane = ReducePlane(place, src, rest[:7])
         scratch = rest[7:]
+        plane.begin()
         gain_sum[...] = jnp.zeros_like(gain_sum)
 
         def norm(c, here, total):
@@ -1110,39 +1116,29 @@
             cols = pl.ds(i * (width // 4), width // 4)
             feed[:, cols] = times_trans(pr[...], dw[cols]).astype(jnp.bfloat16)
 
-        def rows_part(right, i):
+        def up_part(i):
             cols = pl.ds(i * (width // 4), width // 4)
             here = pl.ds((i % 2) * (width // 4), width // 4)
-            up_out[i // 2, here] = trans_times(hid[:, cols], right[...]).astype(jnp.bfloat16)
-
-        def zero():
-            fetch.wait(0, 7)
-            rows_part(gg, 0)
-            rows_part(gg, 1)
-            fetch.start(8)
-
-        def one():
-            rows_part(gg, 2)
-            rows_part(gg, 3)
-            fetch.start(9)
+            up_out[i // 2, here] = trans_times(hid[:, cols], gu[...]).astype(jnp.bfloat16)
+
+        def early():
+            plane.cores()
+            fetch.wait(0, 1)
 
         def two():
-            fetch.wait(1, 8, 9)
-            plane.begin()
-            rows_part(gu, 0)
+            up_part(0)
 
         def three():
-            plane.cores()
-            rows_part(gu, 1)
+            up_part(1)
             fetch.start(5)
 
         def four():
-            rows_part(gu, 2)
+            up_part(2)
 
         def five():
-            rows_part(gu, 3)
+            up_part(3)
             fetch.start(6)
-            fetch.wait(2, 3)
+            fetch.wait(2, 3, 7)
 
         def six():
             feed_part(0)
@@ -1158,7 +1154,7 @@
             feed_part(3)
             fetch.start(4)
 
-        steps = dict(enumerate((zero, one, two, three, four, five, six, seven, eight, nine)))
+        steps = {1: early, 2: two, 3: three, 4: four, 5: five, 6: six, 7: seven, 8: eight, 9: nine}
         sum_rows_and_spread(place, s, scratch, norm, spread, steps)
         plane.finish(result)
         fetch.wait(4, 5, 6)
@@ -1171,24 +1167,23 @@
             shaped((rows, width), full),
             shaped((1, width), full),
             shaped((spread_rows, width), low),
-            shaped((block, wide), low),
+            shaped((block, mat.shape[1]), low),
             shaped((width, wide), low),
             shaped((spread_rows, width), low),
-            shaped((width, wide), low),
         ),
-        in_specs=[near] * 4 + [far] * 5,
-        out_specs=[near] * 4 + [far] * 3,
-        scratch_shapes=[vmem_like(m) for m in (hidden, grad_up, product, down, grad_gate)]
+        in_specs=[near] * 4 + [far] * 6,
+        out_specs=[near] * 4 + [far] * 2,
+        scratch_shapes=[vmem_like(m) for m in (hidden, grad_up, product, mat)]
         + [
             pltpu.VMEM((2, width // 2, wide), low),
             pltpu.VMEM((spread_rows, width), low),
-            dma_sems(10),
+            dma_sems(8),
         ]
-        + ReducePlane.scratch(block, wide)
+        + ReducePlane.scratch(block, mat.shape[1])
         + line_scratch(n_line, rows // CHUNKS, width, CHUNKS),
         compiler_params=comm_params(3),
         name="middle_sums",
-    )(terms, after, gain, grad_in, grad_gate, hidden, grad_up, product, down)
+    )(terms, after, gain, grad_in, mat, hidden, grad_up, product, down, down_rest)
 
 
 class Exchange:
@@ -1407,19 +1402,24 @@
     parts = 1
 
     def kernel(*refs):
-        (tok_far, cot_ref, plc, sto, wx_far, wy_far, wo_far, gain_ref, gw, cw, sp, fl) = refs[:12]
-        far, cot_all = refs[12:23], refs[23]
-        tok, wx, wy, wo = refs[24:28]
-        results = refs[28:39]
+        (tok_far, cot_ref, plc, sto, wx_far, wy_far, wo_far, gain_ref, gates_in, cw, sp, fl) = refs[:12]
+        far, gw, cot_all = refs[12:23], refs[23], refs[24]
+        tok, wx, wy, wo = refs[25:29]
+        results = refs[29:40]
         hp, xext, y, conv_low, conv, pre_r, pre_i, rate, state, merged_st, terms = results
-        (h, xf, local, cum, merged, agg, slots, hs, hr, es, er, el, gs, gr, gl) = refs[39:54]
-        in_sems, out_sems, cot_held = refs[54:]
+        (h, xf, local, cum, merged, agg, slots, hs, hr, es, er, el, gs, gr, gl) = refs[40:55]
+        in_sems, out_sems, cot_held = refs[55:]
         fetch = Fetch(((tok_far, tok), (wx_far, wx), (wy_far, wy), (wo_far, wo)), in_sems)
         store = Fetch(zip(results, far), out_sems)
         fetch.start(0, 1, 2, 3)
         place = Place(n_dp, n_line)
         place.meet(True)
         swap = RimSwap(place, own)
+        for side in range(2):
+            first = side * wide
+            gw[:, first : first + RIM] = jnp.zeros((size, RIM), jnp.bfloat16)
+            gw[:, first + RIM : first + RIM + own] = gates_in[:, side * own : (side + 1) * own]
+            gw[:, first + RIM + own : first + wide] = jnp.zeros((size, RIM), jnp.bfloat16)
         own_cot = cot_all.at[pl.ds(pl.multiple_of(place.t * cot_rows, 16), cot_rows)]
         cot_ref = cot_ref.at[pl.ds(0, cot_rows)]
         keep = Kept(cot_ref, own_cot, cot_held, gl)
@@ -1598,9 +1598,10 @@
     near, far = in_vmem(), in_any()
     return pl.pallas_call(
         kernel,
-        out_shape=results + (shaped((n_line * cot_rows, width), low),),
+        out_shape=results
+        + (shaped((size, 2 * wide), low), shaped((n_line * cot_rows, width), low)),
         in_specs=[far, far, near, near, far, far, far] + [near] * 5,
-        out_specs=[far] * 12,
+        out_specs=[far] * 11 + [near, far],
         scratch_shapes=[vmem_like(m) for m in (tok_all, x_full, y_full, out_full) + results]
         + [
             pltpu.VMEM((rows, width), low),
@@ -2047,7 +2048,7 @@
     return [(c, min(size, width - c)) for c in range(0, width, size)]
 
 
-def feed_forward(n_dp, n_line, hidden, gate, up, down, grads, grad_own):
+def feed_forward(n_dp, n_line, hidden, gate, up, down, down_rest, grads, grad_own):
     rows, width = hidden.shape
     units = gate.shape[1]
     own_rows = grad_own.shape[0]
@@ -2056,12 +2057,19 @@
     part = width // 4
 
     def kernel(*refs):
-        hid_far, wg_far, wu_far, wd_far, grads_far, own_far = refs[:6]
-        product_far, gup_far, back_far, gdown_far, gg_far = refs[6:11]
-        hid, wg, wu, wd, grad, slope, branch, product, ggate, gup, stage, back = refs[11:23]
-        in_sems, out_sems, stage_sems, ls, lr = refs[23:]
+        hid_far, wg_far, wu_far, wd_far, wd_rest, grads_far, own_far = refs[:7]
+        product_far, gup_far, back_far, gdown_far, ggate_far = refs[7:12]
+        hid, wg, wu, wd, grad, slope, branch, product, ggate, gup, stage, back = refs[12:24]
+        in_sems, out_sems, stage_sems, ls, lr = refs[24:]
         place = Place(n_dp, n_line)
-        pairs = [(hid_far, hid), (wg_far, wg), (wu_far, wu), (wd_far, wd)]
+        cut = wd_far.shape[1]
+        pairs = [
+            (hid_far, hid),
+            (wg_far, wg),
+            (wu_far, wu),
+            (wd_far, wd.at[:, pl.ds(0, cut)]),
+            (wd_rest, wd.at[:, pl.ds(cut, units - cut)]),
+        ]
         pairs += [
             (grads_far.at[pl.ds(q * ready, ready)], grad.at[pl.ds(q * own_rows, ready)])
             for q in range(n_line)
@@ -2070,9 +2078,7 @@
         pairs.append((own_far.at[pl.ds(ready, late)], grad.at[mine]))
         fetch = Fetch(pairs, in_sems)
         fetch.start(*range(len(pairs)))
-        store = Fetch(
-            ((product, product_far), (gup, gup_far), (back, back_far), (ggate, gg_far)), out_sems
-        )
+        store = Fetch(((product, product_far), (gup, gup_far), (back, back_far)), out_sems)
         place.meet()
         line = GatherLine(place, grad, own_rows, ready, late, ls, lr)
         line.step(0, own_far.at[pl.ds(ready, late)])
@@ -2102,12 +2108,12 @@
             loop(rows // 256, ups)
         store.start(0)
         line.step(2)
-        fetch.wait(*range(4, len(pairs)))
+        fetch.wait(*range(5, len(pairs)))
         line.finish()
 
-        down_rows = RowProducts(grad, product, gdown_far, stage, stage_sems)
+        down_rows = RowProducts(grad, product, gdown_far, stage, stage_sems.at[0])
         down_rows.run()
-        fetch.wait(3)
+        fetch.wait(3, 4)
         for c, size in columns:
             cols = pl.ds(c, size)
 
@@ -2118,7 +2124,7 @@
                 gup[here, cols] = (value * branch[here, cols]).astype(jnp.bfloat16)
 
             loop(rows // 256, backs)
-        store.start(1, 3)
+        store.start(1)
         for i in range(4):
             some = pl.ds(i * part, part)
             back[:, some] = (
@@ -2126,7 +2132,10 @@
             ).astype(jnp.bfloat16)
         store.start(2)
         down_rows.finish()
-        store.wait(0, 1, 2, 3)
+        gate_rows = RowProducts(hid, ggate, ggate_far, stage, stage_sems.at[1])
+        gate_rows.run()
+        gate_rows.finish()
+        store.wait(0, 1, 2)
 
     low, full = jnp.bfloat16, jnp.float32
     return pl.pallas_call(
@@ -2136,11 +2145,11 @@
             shaped((rows, units), low),
             shaped((rows, width), low),
             shaped((width, units), low),
-            shaped((rows, units), low),
+            shaped((width, units), low),
         ),
-        in_specs=[in_any()] * 6,
+        in_specs=[in_any()] * 7,
         out_specs=[in_any()] * 5,
-        scratch_shapes=[vmem_like(m) for m in (hidden, gate, up, down)]
+        scratch_shapes=[vmem_like(m) for m in (hidden, gate, up, gate)]
         + [
             pltpu.VMEM((n_line * own_rows, width), low),
             pltpu.VMEM((rows, units), full),
@@ -2150,15 +2159,15 @@
             pltpu.VMEM((rows, units), low),
             pltpu.VMEM((2, part, units), low),
             pltpu.VMEM((rows, width), low),
-            dma_sems(5 + n_line),
-            dma_sems(4),
-            dma_sems(4),
+            dma_sems(6 + n_line),
+            dma_sems(3),
+            dma_sems(2, 4),
             dma_sems(2, n_line - 1),
             dma_sems(2, n_line - 1),
         ],
         compiler_params=comm_params(7),
         name="feed_forward",
-    )(hidden, gate, up, down, grads, grad_own)
+    )(hidden, gate, up, down, down_rest, grads, grad_own)
 
 
 def matches(mesh):
@@ -2204,15 +2213,15 @@
     x_full, y_full, out_full, minor_full, tok_all, order_full = first_gather(
         n_dp, n_tensor, (x_weight, y_weight, out_weight.T, minor), tokens, order_rows
     )
-    late_up, late_down, _ = lax.optimization_barrier((up_weight, down_weight.T, tok_all))
+    down_rows = down_weight.T
+    cut = 2 * down_rows.shape[1] // 3
+    late_up, late_down, _ = lax.optimization_barrier((up_weight, down_rows[:, :cut], tok_all))
     up_full = lax.all_gather(late_up, "dp", axis=0, tiled=True)
     down_full = lax.all_gather(late_down, "dp", axis=0, tiled=True)
     order_all = order_full.reshape(n_tensor, 8, tok_rows)[:, 0].reshape(row_count)
-    both_gates = minor_full[:, : 2 * own_width]
     gain_rows = minor_full[:, 2 * own_width :].reshape(n_dp, -1)
     first_gain = gain_rows[:, :dp_width].reshape(1, width).astype(jnp.float32)
     second_gain = gain_rows[:, dp_width : 2 * dp_width].reshape(1, width).astype(jnp.float32)
-    block_size = both_gates.shape[0]
     row_index = jnp.arange(row_count, dtype=jnp.int32)
     hits = row_index[:, None] == order_all[None, :]
     to_place = hits.astype(jnp.bfloat16)
@@ -2231,19 +2240,7 @@
     grad_in_own = (cotangent.astype(jnp.float32) * live_own[:, None]).astype(jnp.bfloat16)
     soft = jax.nn.softplus(-decay_param).reshape(1, own_width)
     slope = jax.nn.sigmoid(-decay_param).reshape(1, own_width)
-    zero_rim = jnp.zeros((block_size, RIM), jnp.bfloat16)
-    gates_wide = jnp.concatenate(
-        [
-            zero_rim,
-            both_gates[:, :own_width],
-            zero_rim,
-            zero_rim,
-            both_gates[:, own_width:],
-            zero_rim,
-        ],
-        axis=1,
-    )
-    hidden_place, *kept, merged_stored, mixer_terms, grad_rows = recur_forward(
+    hidden_place, *kept, merged_stored, mixer_terms, gates_wide, grad_rows = recur_forward(
         n_dp,
         n_tensor,
         tok_all,
@@ -2254,37 +2251,39 @@
         y_full,
         out_full,
         first_gain,
-        gates_wide,
+        minor_full,
         conv_weight,
         soft,
         flags,
     )
-    after_own, hidden_two, gate_full = middle_gather(
-        n_dp, n_tensor, mixer_terms, tokens, second_gain, (gate_weight,)
-    )
-    product, grad_up_pre, back_terms, grad_down, grad_gate_pre = feed_forward(
+    after_own, hidden_two, gate_full, down_rest = middle_gather(
+        n_dp, n_tensor, mixer_terms, tokens, second_gain, (gate_weight, down_rows[:, cut:])
+    )
+    product, grad_up_pre, back_terms, grad_down, grad_gate = feed_forward(
         n_dp,
         n_tensor,
         hidden_two,
         gate_full,
         up_full,
         down_full,
+        down_rest,
         grad_rows,
         grad_in_own,
     )
     down_sum = lax.psum_scatter(grad_down, "dp", scatter_dimension=0, tiled=True)
-    grad_after_own, second_part, mixer_in, gate_sum, grad_up, feed_terms, _ = middle_sums(
+    grad_after_own, second_part, mixer_in, gate_sum, grad_up, feed_terms = middle_sums(
         n_dp,
         n_tensor,
         back_terms,
         after_own,
         second_gain,
         grad_in_own,
-        grad_gate_pre,
+        grad_gate,
         hidden_two,
         grad_up_pre,
         product,
         down_full,
+        down_rest,
     )
     (
         gate_grads,

time: 537 us -> 535 us (level)
    pallas_call x1, Pallas kernels: 106 us -> 88 us  [middle_sums(): pl.pallas_call(kernel, out_shape=(shaped((rows, width), full), shaped((1,...]
    pallas_call x1, Pallas kernels: 87.6 us -> 96.3 us  [middle_gather(): pl.pallas_call(kernel, out_shape=(shaped((rows, width), jnp.float32), sha...]
    pallas_call x1, Pallas kernels: 52.3 us -> 58.9 us  [feed_forward(): pl.pallas_call(kernel, out_shape=(shaped((rows, units), low), shaped((row...]
  transfers between devices with their start and end apart: 3 -> 3, of which waited for: 1 -> 0; matrix products, arithmetic and copies ran while one was open for 4% -> 5% of each run, Pallas kernels for 71% -> 70%
where the time goes in v10:
time: 535 us; the launch traced here: 527 us
  Pallas kernels  478 us (89%)
  local copies, waits for them, and re-layouts  17.6 us (3%)
  other arithmetic  16.4 us (3%)
  between operations  14.4 us (3%)
    pallas_call x1, Pallas kernels, middle_gather(): pl.pallas_call(kernel, out_shape=(shaped((rows, width), jnp.float32), sha...  96.3 us
    pallas_call x1, Pallas kernels, middle_sums(): pl.pallas_call(kernel, out_shape=(shaped((rows, width), full), shaped((1,...  88 us
    pallas_call x1, Pallas kernels, last_sums(): pl.pallas_call(kernel, out_shape=(shaped((rows, width), jnp.float32), sha...  67.2 us
    pallas_call x1, Pallas kernels, recur_backward(): pl.pallas_call(kernel, out_shape=(shaped((size, 2 * own), low), shaped((8...  65.3 us
    pallas_call x1, Pallas kernels, feed_forward(): pl.pallas_call(kernel, out_shape=(shaped((rows, units), low), shaped((row...  58.9 us
    pallas_call x1, Pallas kernels, first_gather(): pl.pallas_call(kernel, out_shape=tuple((shaped((n_dp * m.shape[0], m.shap...  51.6 us
    pallas_call x1, Pallas kernels, recur_forward(): pl.pallas_call(kernel, out_shape=results + (shaped((size, 2 * wide), low)...  50.9 us
  transfers between devices with their start and end apart: 3, of which 0 were waited for; matrix products, arithmetic and copies ran while one was open for 5% of the time, Pallas kernels for 70%

profile of v10, /device:TPU:0, one launch (start us, length us, event | category | flops | bytes accessed | tf_op | source)
XLA Modules:
  0.0 527.5 jit_solution(8692558680486608893)
XLA Ops:
  7.2 2.1 slice.69
  10.0 0.8 fusion.7
  10.7 1.4 pad_maximum_fusion.refs_3_
  12.8 51.6 %first_gather.1 = (bf16[2560,640]{1,0:T(8,128)(2,1)}, bf16[2560,640]{1,0:T(8,128)(2,1)}, bf16[2560,640]{1,0:T(8,128)(2,1)}, bf16[256,1408]{1,0:T(8,128)(2,1)}, b...) custom-call(bf16[320,640]{1,0:T(8,128)(2,1)} %refs_0_.1, bf16[320,640]{1,0:T(8,128)(2,1)} %refs_1_.3, ...), custom_call_target="tpu_custom_call" | custom-call | tf_op jit(solution)/shard_map/first_gather/pallas_call | solution.py:929
  64.5 0.7 all-gather.3.cloned.1.call-update
  65.3 1.8 slice.68.refs_4_
  68.9 0.7 slice.65
  69.6 0.8 slice.51
  70.5 0.7 reshape.180.refs_2_
  71.2 0.7 reshape.179.refs_7_.refs_2_
  72.6 0.8 and_convert_fusion.refs_11_.refs_10_
  73.4 1.1 fusion.1
  74.5 1.0 multiply_convert_fusion.1.refs_1_.refs_6_.refs_3_
  75.6 50.9 %recur_forward.1 = (bf16[512,2560]{1,0:T(8,128)(2,1)}, bf16[528,640]{1,0:T(8,128)(2,1)}, f32[512,640]{1,0:T(8,128)}, bf16[512,896]{1,0:T(8,128)(2,1)}, f32[512,6...) custom-call(bf16[512,2560]{1,0:T(8,128)(2,1)} %get-tuple-element.64., ...), custom_call_target="tpu_custom_call" | custom-call | tf_op jit(solution)/shard_map/recur_forward/pallas_call | solution.py:1599
  126.5 96.3 %middle_gather.1 = (f32[128,2560]{1,0:T(8,128)}, bf16[512,2560]{1,0:T(8,128)(2,1)}, bf16[2560,1920]{1,0:T(8,128)(2,1)}, bf16[2560,640]{1,0:T(8,128)(2,1)}) custom-call(bf16[512,2560]{1,0:T(8,128)(2,1)} %get-tuple-element.70.refs_0_, bf16[128,2560]{1,0:T(8,128)(2,1)} %refs_1_.5, f32[1,2560]{1,0:T(1,128)} %reshape.180.refs_2_, bf16[320,1920]{1,0:T(8,128)(2,1)} %refs_3_.1, ...), custom_call_target="tpu_custom_call" | custom-call | tf_op jit(solution)/shard_map/middle_gather/pallas_call | solution.py:1053
  222.8 58.9 %feed_forward.1 = (bf16[512,1920]{1,0:T(8,128)(2,1)}, bf16[512,1920]{1,0:T(8,128)(2,1)}, bf16[512,2560]{1,0:T(8,128)(2,1)}, bf16[2560,1920]{1,0:T(8,128)(2,1)}, bf16[2560,1920]{1,0:T(8,128)(2,1)}) custom-call(bf16[512,2560]{1,0:T(8,128)(2,1)} %get-tuple-element.72.refs_0_.refs_5_, bf16[2560,1920]{1,0:T(8,128)(2,1)} %get-tuple-element.73.refs_1_, ...), custom_call_target="tpu_custom_call" | custom-call | tf_op jit(solution)/shard_map/feed_forward/pallas_call | solution.py:2141
  282.4 88.0 %middle_sums.1 = (f32[128,2560]{1,0:T(8,128)}, f32[1,2560]{1,0:T(1,128)}, bf16[512,2560]{1,0:T(8,128)(2,1)}, bf16[320,1920]{1,0:T(8,128)(2,1)}, bf16[2560,1920]{1,0:T(8,128)(2,1)}, /*index=5*/bf16[512,2560]{1,0:T(8,128)(2,1)}) custom-call(bf16[512,2560]{1,0:T(8,128)(2,1)} %get-tuple-element.78.refs_0_, f32[128,2560]{1,0:T(8,128)} %get-tuple-element.71.refs_1_, ...), custom_call_target="tpu_custom_call" | custom-call | tf_op jit(solution)/shard_map/middle_sums/pallas_call | solution.py:1164
  370.4 65.3 %recur_backward.1 = (bf16[256,1280]{1,0:T(8,128)(2,1)}, f32[8,640]{1,0:T(8,128)}, f32[1,640]{1,0:T(1,128)}, bf16[512,2560]{1,0:T(8,128)(2,1)}, bf16[320,1920]{1,...) custom-call(bf16[512,2560]{1,0:T(8,128)(2,1)} %get-tuple-element.82.refs_0_, ...), custom_call_target="tpu_custom_call" | custom-call | tf_op jit(solution)/shard_map/recur_backward/pallas_call | solution.py:1974
  435.8 0.7 slice_bitcast_fusion
  436.5 1.4 fusion.2.refs_4_
  437.9 67.2 %last_sums.1 = (f32[128,2560]{1,0:T(8,128)}, f32[4,2560]{1,0:T(4,128)}, f32[2,2560]{1,0:T(2,128)}, bf16[320,1280]{1,0:T(8,128)(2,1)}, bf16[320,640]{1,0:T(8,128)(2,1)}, /*index=5*/bf16[32,1280]{1,0:T(8,128)(2,1)}) custom-call(bf16[512,2560]{1,0:T(8,128)(2,1)} %get-tuple-element.97.refs_0_, bf16[128,2560]{1,0:T(8,128)(2,1)} %refs_1_.5, ...), custom_call_target="tpu_custom_call" | custom-call | tf_op jit(solution)/shard_map/last_sums/pallas_call | solution.py:1277
  505.1 0.9 slice_reduce_fusion
  506.6 1.6 convert_element_type.84
  508.2 1.6 convert_element_type.83
  509.8 1.4 dynamic-slice_reduce_fusion
  511.2 1.3 slice_reduce_fusion.1
  512.5 0.7 fusion.13
  513.2 0.9 convert_bitcast_fusion.1
  514.2 1.3 fusion.12
  515.4 1.0 multiply_convert_fusion
  516.5 3.0 convert_bitcast_fusion
  519.5 1.1 copy.40
  (59 shorter events, 5.3 us)
Async XLA Ops:
  7.2 215.6 %all-gather.5.cloned.1.call-start = ((), (), s32[]{:S(2)}) async-start(), calls=%async_computation.2 | async-start | bytes 7372800 | tf_op jit(solution)/shard_map/all_gather | solution.py:2220
  12.8 54.3 %copy-start.11 = (s32[3]{0:T(128)S(1)}, s32[3]{0:T(128)}, u32[]{:S(2)}) copy-start(s32[3]{0:T(128)} %param.29) | copy-start | bytes 40
  12.8 55.0 %copy-start.10 = (f32[640]{0:T(1024)S(1)}, f32[640]{0:T(1024)}, u32[]{:S(2)}) copy-start(f32[640]{0:T(1024)} %param.23) | copy-start | bytes 7684
  64.4 7.5 %copy-start.12 = (s32[128]{0:T(128)S(1)}, s32[128]{0:T(128)}, u32[]{:S(2)}) copy-start(s32[128]{0:T(128)} %param.30) | copy-start | bytes 1540
  64.5 10.1 %copy-start.5 = (bf16[128,2560]{1,0:T(8,128)(2,1)S(1)}, bf16[128,2560]{1,0:T(8,128)(2,1)}, u32[]{:S(2)}) copy-start(bf16[128,2560]{1,0:T(8,128)(2,1)} %param.31) | copy-start | bytes 1966084
  64.5 158.3 %all-gather.3.cloned.1.call-start = ((), (), s32[]{:S(2)}) async-start(), calls=%async_computation.1 | async-start | bytes 11059200 | tf_op jit(solution)/shard_map/all_gather | solution.py:2219
  65.2 451.3 %reduce-scatter.2.cloned.1.call-start = ((), (), s32[]{:S(2)}) async-start(), calls=%async_computation.3 | async-start | bytes 11059200 | tf_op jit(solution)/shard_map/reduce_scatter | solution.py:2273
  370.4 66.1 %copy-start.9 = (f32[1,2560]{1,0:T(1,128)S(1)}, f32[1,2560]{1,0:T(1,128)}, u32[]{:S(2)}) copy-start(f32[1,2560]{1,0:T(1,128)} %get-tuple-element.99) | copy-start | bytes 30724
  437.9 68.7 %copy-start.4 = (bf16[320,1920]{1,0:T(8,128)(2,1)S(1)}, bf16[320,1920]{1,0:T(8,128)(2,1)}, u32[]{:S(2)}) copy-start(bf16[320,1920]{1,0:T(8,128)(2,1)} %get-tuple-element.112) | copy-start | bytes 3686404
  505.1 3.1 copy-start.3
  508.2 4.3 copy-start.8
  508.2 5.0 copy-start.7
  508.2 6.0 %copy-start.1 = (bf16[320,1280]{1,0:T(8,128)(2,1)S(1)}, bf16[320,1280]{1,0:T(8,128)(2,1)}, u32[]{:S(2)}) copy-start(bf16[320,1280]{1,0:T(8,128)(2,1)} %get-tuple-element.107) | copy-start | bytes 2457604
  513.2 2.2 copy-start
  513.2 2.2 copy-start.6
  516.5 3.0 copy-start.2
Sparse Core Ops, SparseCore 0:
  64.6 46.9 all-gather.4
  113.4 95.8 all-gather.2
  281.8 103.5 reduce-scatter.1

commit v11 on v10

--- a/solution.py
+++ b/solution.py
@@ -1039,13 +1039,7 @@
             first = pl.multiple_of(place.t * rows, 16) + c * total.shape[0]
             hidden[pl.ds(pl.multiple_of(first, 16), total.shape[0])] = low
 
-        between = {
-            2: planes[1].begin,
-            6: planes[0].forward,
-            8: planes[1].forward,
-            9: planes[0].share,
-            10: planes[1].share,
-        }
+        between = {6: planes[0].forward, 9: planes[0].share}
         sum_rows_and_spread(place, s, scratch, norm, hidden, between)
         for part in planes:
             part.finish()
@@ -1067,9 +1061,7 @@
     )(terms, tokens, gain, *mats)
 
 
-def middle_sums(
-    n_dp, n_line, terms, after, gain, grad_in, mat, hidden, grad_up, product, down, down_rest
-):
+def middle_sums(n_dp, n_line, terms, after, gain, grad_in, mat, hidden, grad_up, product, down):
     rows, width = after.shape
     block = mat.shape[0] // n_dp
     wide = grad_up.shape[1]
@@ -1077,25 +1069,23 @@
 
     def kernel(*refs):
         s, after_ref, gain_ref, g_ref, src = refs[:5]
-        hid_far, gu_far, pr_far, dw_far, dw_rest = refs[5:10]
-        grad_after, gain_sum, spread, result, up_far, feed_far = refs[10:16]
-        hid, gu, pr, dw, up_out, feed, sems = refs[16:23]
-        rest = refs[23:]
-        cut = dw_far.shape[1]
+        hid_far, gu_far, pr_far, dw_far = refs[5:9]
+        grad_after, gain_sum, spread, result, up_far, feed_far = refs[9:15]
+        hid, gu, pr, dw, up_out, feed, sems = refs[15:22]
+        rest = refs[22:]
         fetch = Fetch(
             [
                 (hid_far, hid),
                 (gu_far, gu),
                 (pr_far, pr),
-                (dw_far, dw.at[:, pl.ds(0, cut)]),
+                (dw_far, dw),
                 (feed, feed_far),
                 (up_out.at[0], up_far.at[pl.ds(0, width // 2)]),
                 (up_out.at[1], up_far.at[pl.ds(width // 2, width // 2)]),
-                (dw_rest, dw.at[:, pl.ds(cut, wide - cut)]),
             ],
             sems,
         )
-        fetch.start(0, 1, 2, 3, 7)
+        fetch.start(0, 1, 2, 3)
         place = Place(n_dp, n_line)
         place.meet()
         plane = ReducePlane(place, src, rest[:7])
@@ -1138,7 +1128,7 @@
         def five():
             up_part(3)
             fetch.start(6)
-            fetch.wait(2, 3, 7)
+            fetch.wait(2, 3)
 
         def six():
             feed_part(0)
@@ -1171,19 +1161,19 @@
             shaped((width, wide), low),
             shaped((spread_rows, width), low),
         ),
-        in_specs=[near] * 4 + [far] * 6,
+        in_specs=[near] * 4 + [far] * 5,
         out_specs=[near] * 4 + [far] * 2,
-        scratch_shapes=[vmem_like(m) for m in (hidden, grad_up, product, mat)]
+        scratch_shapes=[vmem_like(m) for m in (hidden, grad_up, product, down)]
         + [
             pltpu.VMEM((2, width // 2, wide), low),
             pltpu.VMEM((spread_rows, width), low),
-            dma_sems(8),
+            dma_sems(7),
         ]
         + ReducePlane.scratch(block, mat.shape[1])
         + line_scratch(n_line, rows // CHUNKS, width, CHUNKS),
         compiler_params=comm_params(3),
         name="middle_sums",
-    )(terms, after, gain, grad_in, mat, hidden, grad_up, product, down, down_rest)
+    )(terms, after, gain, grad_in, mat, hidden, grad_up, product, down)
 
 
 class Exchange:
@@ -1222,17 +1212,17 @@
         return total
 
 
-def last_sums(n_dp, n_line, terms, tokens, gain, grad_after, small, mats):
+def last_sums(n_dp, n_line, terms, tokens, gain, grad_after, second, small, mats):
     rows, width = tokens.shape
     count = len(mats)
     per = len(ReducePlane.scratch(16, 128))
 
     def kernel(*refs):
-        s, tok, gain_ref, g_ref, small_ref = refs[:5]
-        srcs = refs[5 : 5 + count]
-        grad_tok, small_out, first_out = refs[5 + count : 8 + count]
-        results = refs[8 + count : 8 + 2 * count]
-        rest = refs[8 + 2 * count :]
+        s, tok, gain_ref, g_ref, second_ref, small_ref = refs[:6]
+        srcs = refs[6 : 6 + count]
+        grad_tok, small_out, first_out = refs[6 + count : 9 + count]
+        results = refs[9 + count : 9 + 2 * count]
+        rest = refs[9 + 2 * count :]
         own_first, row_sum = rest[count * per : count * per + 2]
         slots_a, slots_b, slots_c, slots_d = rest[count * per + 2 : count * per + 6]
         xs, xr, xl = rest[count * per + 6 : count * per + 9]
@@ -1246,6 +1236,8 @@
             part.begin()
         early = Exchange(place, "dp", small_ref, slots_a, xs.at[0], xr.at[0], xl.at[0])
         early.begin()
+        gain = Exchange(place, "dp", second_ref, slots_d, xs.at[3], xr.at[3], xl.at[3])
+        gain.begin()
         own_first[...] = jnp.zeros_like(own_first)
 
         def norm(c, here, total):
@@ -1266,7 +1258,7 @@
         first = Exchange(place, "dp", own_first, slots_b, xs.at[1], xr.at[1], xl.at[1])
         first.begin()
         small_out[...] = early.finish()
-        row_sum[0:1] = small_out[0:1]
+        row_sum[0:1] = gain.finish()
         row_sum[1:2] = first.finish()
         both = Exchange(place, "tensor", row_sum, slots_c, xs.at[2], xr.at[2], xl.at[2])
         both.begin()
@@ -1282,7 +1274,7 @@
             shaped((2, width), jnp.float32),
         )
         + tuple(shaped((m.shape[0] // n_dp, m.shape[1]), jnp.bfloat16) for m in mats),
-        in_specs=[in_vmem()] * 5 + [in_any()] * count,
+        in_specs=[in_vmem()] * 6 + [in_any()] * count,
         out_specs=[in_vmem()] * (3 + count),
         scratch_shapes=sum([ReducePlane.scratch(m.shape[0] // n_dp, m.shape[1]) for m in mats], [])
         + [
@@ -1291,15 +1283,15 @@
             pltpu.VMEM((n_dp,) + small.shape, jnp.float32),
             pltpu.VMEM((n_dp, 1, width), jnp.float32),
             pltpu.VMEM((n_line, 2, width), jnp.float32),
-            pltpu.VMEM((1, width), jnp.float32),
-            dma_sems(3, n_dp),
-            dma_sems(3, n_dp),
-            dma_sems(3),
+            pltpu.VMEM((n_dp, 1, width), jnp.float32),
+            dma_sems(4, n_dp),
+            dma_sems(4, n_dp),
+            dma_sems(4),
         ]
         + line_scratch(n_line, rows // LAST_CHUNKS, width, LAST_CHUNKS),
         compiler_params=comm_params(4),
         name="last_sums",
-    )(terms, tokens, gain, grad_after, small, *mats)
+    )(terms, tokens, gain, grad_after, second, small, *mats)
 
 
 def loop(count, body, unroll=1):
@@ -1702,14 +1694,14 @@
     def kernel(*refs):
         (mix_far, plc, sto, wx_far, wy_far, wo_far, gw, cw, sp, sg, fl) = refs[:11]
         kept_far, weights, feed_far, hp_far, merged_far = refs[11:19], *refs[19:23]
-        (gate_grads, tap_grads, decay_grad, terms_far, weight_sum, row_sum) = refs[23:29]
-        out_far, xy_far = refs[29:31]
-        mix, wy, wo, feed, merged = refs[31:36]
-        (xext, y, conv_low, conv, pre_r, pre_i, rate, state) = refs[36:44]
-        (gxy, mp, gm, lam, reach, gp_r, gp_i, grad, spread, rim_out, rim_in) = refs[44:55]
-        (ret_out, ret_in, tap_sums, decay_sums, ends, agg, slots) = refs[55:62]
-        (hs, hr, es, er, el, in_sems, out_sems, inbox, ls, lr, total) = refs[62:73]
-        stage, stage_sems = refs[73:75]
+        (gate_grads, tap_grads, terms_far, weight_sum, row_sum) = refs[23:28]
+        out_far, xy_far = refs[28:30]
+        mix, wy, wo, feed, merged = refs[30:35]
+        (xext, y, conv_low, conv, pre_r, pre_i, rate, state) = refs[35:43]
+        (gxy, mp, gm, lam, reach, gp_r, gp_i, grad, spread, rim_out, rim_in) = refs[43:54]
+        (ret_out, ret_in, tap_sums, decay_sums, ends, agg, slots) = refs[54:61]
+        (hs, hr, es, er, el, in_sems, out_sems, inbox, ls, lr, total) = refs[61:72]
+        stage, stage_sems = refs[72:74]
         hp, terms, wx = mix, mix, wo
         fetch = Fetch(
             [
@@ -1737,7 +1729,7 @@
         xy_rows = RowProducts(hp, gxy, xy_far, stage, stage_sems.at[1])
         place = Place(n_dp, n_line)
         place.meet(True)
-        plane = ReducePlane(place, weights, refs[75:])
+        plane = ReducePlane(place, weights, refs[74:])
         plane.begin()
         lines = [
             ReduceLine(place, feed, own_rows, c * span, span, inbox.at[c], ls.at[c], lr.at[c])
@@ -1859,7 +1851,6 @@
             entry = ends[1, j : j + 1] + ends[0, j : j + 1] * entry
         lines[1].hop(1)
         add_up(0)
-        decay_grad[...] = rate_scale * sg[...] * jnp.sum(decay_sums[...], axis=0, keepdims=True)
 
         for i in range(blocks):
             index = lax.rem(i + 2 - 2 * swap.odd, blocks)
@@ -1936,6 +1927,9 @@
         tap_grads[...] = jnp.zeros_like(tap_grads)
         for k in range(count):
             tap_grads[k : k + 1] = jnp.sum(tap_sums[k], axis=0, keepdims=True)
+        tap_grads[count : count + 1] = (
+            rate_scale * sg[...] * jnp.sum(decay_sums[...], axis=0, keepdims=True)
+        )
 
         fetch.wait(14)
         out_rows.finish()
@@ -1976,7 +1970,6 @@
         out_shape=(
             shaped((size, 2 * own), low),
             shaped((8, own), full),
-            shaped((1, own), full),
             shaped((rows, width), low),
             shaped((block, weight_terms.shape[1]), low),
             shaped((own_rows, width), low),
@@ -1984,7 +1977,7 @@
             shaped((width, 2 * own), low),
         ),
         in_specs=[far, near, near, far, far, far] + [near] * 5 + [far] * 12,
-        out_specs=[near, near, near, far, near, near, far, far],
+        out_specs=[near, near, far, near, near, far, far],
         scratch_shapes=[
             vmem_like(m) for m in (mixer_in, y_full, out_full, row_terms, merged_stored, *kept)
         ]
@@ -2048,7 +2041,7 @@
     return [(c, min(size, width - c)) for c in range(0, width, size)]
 
 
-def feed_forward(n_dp, n_line, hidden, gate, up, down, down_rest, grads, grad_own):
+def feed_forward(n_dp, n_line, hidden, gate, up, down, grads, grad_own):
     rows, width = hidden.shape
     units = gate.shape[1]
     own_rows = grad_own.shape[0]
@@ -2057,19 +2050,12 @@
     part = width // 4
 
     def kernel(*refs):
-        hid_far, wg_far, wu_far, wd_far, wd_rest, grads_far, own_far = refs[:7]
-        product_far, gup_far, back_far, gdown_far, ggate_far = refs[7:12]
-        hid, wg, wu, wd, grad, slope, branch, product, ggate, gup, stage, back = refs[12:24]
-        in_sems, out_sems, stage_sems, ls, lr = refs[24:]
+        hid_far, wg_far, wu_far, wd_far, grads_far, own_far = refs[:6]
+        product_far, gup_far, back_far, gdown_far, ggate_far = refs[6:11]
+        hid, wg, wu, wd, grad, slope, branch, product, ggate, gup, stage, back = refs[11:23]
+        in_sems, out_sems, stage_sems, ls, lr = refs[23:]
         place = Place(n_dp, n_line)
-        cut = wd_far.shape[1]
-        pairs = [
-            (hid_far, hid),
-            (wg_far, wg),
-            (wu_far, wu),
-            (wd_far, wd.at[:, pl.ds(0, cut)]),
-            (wd_rest, wd.at[:, pl.ds(cut, units - cut)]),
-        ]
+        pairs = [(hid_far, hid), (wg_far, wg), (wu_far, wu), (wd_far, wd)]
         pairs += [
             (grads_far.at[pl.ds(q * ready, ready)], grad.at[pl.ds(q * own_rows, ready)])
             for q in range(n_line)
@@ -2108,12 +2094,12 @@
             loop(rows // 256, ups)
         store.start(0)
         line.step(2)
-        fetch.wait(*range(5, len(pairs)))
+        fetch.wait(*range(4, len(pairs)))
         line.finish()
 
         down_rows = RowProducts(grad, product, gdown_far, stage, stage_sems.at[0])
         down_rows.run()
-        fetch.wait(3, 4)
+        fetch.wait(3)
         for c, size in columns:
             cols = pl.ds(c, size)
 
@@ -2147,9 +2133,9 @@
             shaped((width, units), low),
             shaped((width, units), low),
         ),
-        in_specs=[in_any()] * 7,
+        in_specs=[in_any()] * 6,
         out_specs=[in_any()] * 5,
-        scratch_shapes=[vmem_like(m) for m in (hidden, gate, up, gate)]
+        scratch_shapes=[vmem_like(m) for m in (hidden, gate, up, down)]
         + [
             pltpu.VMEM((n_line * own_rows, width), low),
             pltpu.VMEM((rows, units), full),
@@ -2159,7 +2145,7 @@
             pltpu.VMEM((rows, units), low),
             pltpu.VMEM((2, part, units), low),
             pltpu.VMEM((rows, width), low),
-            dma_sems(6 + n_line),
+            dma_sems(5 + n_line),
             dma_sems(3),
             dma_sems(2, 4),
             dma_sems(2, n_line - 1),
@@ -2167,7 +2153,7 @@
         ],
         compiler_params=comm_params(7),
         name="feed_forward",
-    )(hidden, gate, up, down, down_rest, grads, grad_own)
+    )(hidden, gate, up, down, grads, grad_own)
 
 
 def matches(mesh):
@@ -2213,9 +2199,7 @@
     x_full, y_full, out_full, minor_full, tok_all, order_full = first_gather(
         n_dp, n_tensor, (x_weight, y_weight, out_weight.T, minor), tokens, order_rows
     )
-    down_rows = down_weight.T
-    cut = 2 * down_rows.shape[1] // 3
-    late_up, late_down, _ = lax.optimization_barrier((up_weight, down_rows[:, :cut], tok_all))
+    late_up, late_down, _ = lax.optimization_barrier((up_weight, down_weight.T, tok_all))
     up_full = lax.all_gather(late_up, "dp", axis=0, tiled=True)
     down_full = lax.all_gather(late_down, "dp", axis=0, tiled=True)
     order_all = order_full.reshape(n_tensor, 8, tok_rows)[:, 0].reshape(row_count)
@@ -2256,8 +2240,8 @@
         soft,
         flags,
     )
-    after_own, hidden_two, gate_full, down_rest = middle_gather(
-        n_dp, n_tensor, mixer_terms, tokens, second_gain, (gate_weight, down_rows[:, cut:])
+    after_own, hidden_two, gate_full = middle_gather(
+        n_dp, n_tensor, mixer_terms, tokens, second_gain, (gate_weight,)
     )
     product, grad_up_pre, back_terms, grad_down, grad_gate = feed_forward(
         n_dp,
@@ -2266,7 +2250,6 @@
         gate_full,
         up_full,
         down_full,
-        down_rest,
         grad_rows,
         grad_in_own,
     )
@@ -2283,12 +2266,10 @@
         grad_up_pre,
         product,
         down_full,
-        down_rest,
     )
     (
         gate_grads,
         tap_grads,
-        decay_grad,
         one_terms,
         up_sum,
         feed_out,
@@ -2316,15 +2297,6 @@
     )
     output = (after_own + feed_out.astype(jnp.float32)) * live_own[:, None]
     output = output.astype(jnp.bfloat16)
-    small = jnp.concatenate(
-        [
-            second_part,
-            tap_grads[:kernel_taps].reshape(1, -1),
-            jnp.pad(decay_grad, ((0, 0), (0, width - own_width))),
-            jnp.zeros((1, width), jnp.float32),
-        ],
-        axis=0,
-    )
     grad_tokens, small_sum, gain_sums, xy_sum, out_sum, gates_sum = last_sums(
         n_dp,
         n_tensor,
@@ -2332,7 +2304,8 @@
         tokens,
         first_gain,
         grad_after_own,
-        small,
+        second_part,
+        tap_grads,
         (grad_xy_mat, grad_out_mat, gate_grads),
     )
     xy_sum, gates_sum = xy_sum.astype(jnp.float32), gates_sum.astype(jnp.float32)
@@ -2343,10 +2316,10 @@
         own_gains[1],
         xy_sum[:, :own_width],
         xy_sum[:, own_width:],
-        small_sum[1].reshape(kernel_taps, own_width),
+        small_sum[:kernel_taps],
         gates_sum[:, :own_width],
         gates_sum[:, own_width:],
-        small_sum[2, :own_width],
+        small_sum[kernel_taps],
         out_sum.astype(jnp.float32).T,
         own_gains[0],
         gate_sum.astype(jnp.float32),

time: 535 us -> 522 us (0.976)
  Pallas kernels: 478 us -> 471 us
    pallas_call x1, Pallas kernels: 96.3 us -> 88.4 us  [middle_gather(): pl.pallas_call(kernel, out_shape=(shaped((rows, width), jnp.float32), sha...]
  transfers between devices with their start and end apart: 3 -> 3, of which waited for: 0 -> 1; matrix products, arithmetic and copies ran while one was open for 5% -> 4% of each run, Pallas kernels for 70% -> 70%
where the time goes in v11:
time: 522 us; the launch traced here: 515 us
  Pallas kernels  471 us (90%)
  other arithmetic  15.1 us (3%)
  between operations  14.4 us (3%)
  local copies, waits for them, and re-layouts  12.8 us (2%)
    pallas_call x1, Pallas kernels, middle_gather(): pl.pallas_call(kernel, out_shape=(shaped((rows, width), jnp.float32), sha...  88.4 us
    pallas_call x1, Pallas kernels, middle_sums(): pl.pallas_call(kernel, out_shape=(shaped((rows, width), full), shaped((1,...  88 us
    pallas_call x1, Pallas kernels, last_sums(): pl.pallas_call(kernel, out_shape=(shaped((rows, width), jnp.float32), sha...  67.7 us
    pallas_call x1, Pallas kernels, recur_backward(): pl.pallas_call(kernel, out_shape=(shaped((size, 2 * own), low), shaped((8...  65.4 us
    pallas_call x1, Pallas kernels, feed_forward(): pl.pallas_call(kernel, out_shape=(shaped((rows, units), low), shaped((row...  58.6 us
    pallas_call x1, Pallas kernels, first_gather(): pl.pallas_call(kernel, out_shape=tuple((shaped((n_dp * m.shape[0], m.shap...  51.6 us
    pallas_call x1, Pallas kernels, recur_forward(): pl.pallas_call(kernel, out_shape=results + (shaped((size, 2 * wide), low)...  51.1 us
  transfers between devices with their start and end apart: 3, of which 1 were waited for; matrix products, arithmetic and copies ran while one was open for 4% of the time, Pallas kernels for 70%

profile of v11, /device:TPU:0, one launch (start us, length us, event | category | flops | bytes accessed | tf_op | source)
XLA Modules:
  0.0 515.3 jit_solution(12446984642337745772)
XLA Ops:
  7.2 0.7 broadcast_subtract_fusion
  7.9 0.8 fusion.5
  8.7 1.4 pad_maximum_fusion.refs_3_
  10.1 0.6 broadcast_in_dim.2.refs_5_
  10.7 51.6 %first_gather.1 = (bf16[2560,640]{1,0:T(8,128)(2,1)}, bf16[2560,640]{1,0:T(8,128)(2,1)}, bf16[2560,640]{1,0:T(8,128)(2,1)}, bf16[256,1408]{1,0:T(8,128)(2,1)}, b...) custom-call(bf16[320,640]{1,0:T(8,128)(2,1)} %refs_0_.1, bf16[320,640]{1,0:T(8,128)(2,1)} %refs_1_.3, ...), custom_call_target="tpu_custom_call" | custom-call | tf_op jit(solution)/shard_map/first_gather/pallas_call | solution.py:929
  62.4 0.7 all-gather.5.cloned.1.call-update
  65.0 0.7 slice.53
  65.7 0.8 slice.42
  66.7 0.7 reshape.176.refs_2_
  67.4 0.7 reshape.175.refs_7_.refs_2_
  68.0 0.6 compare_convert_fusion
  68.7 0.8 and_convert_fusion.refs_11_.refs_10_
  69.5 1.1 fusion.1
  70.7 1.0 multiply_convert_fusion.1.refs_1_.refs_5_.refs_3_
  71.7 51.1 %recur_forward.1 = (bf16[512,2560]{1,0:T(8,128)(2,1)}, bf16[528,640]{1,0:T(8,128)(2,1)}, f32[512,640]{1,0:T(8,128)}, bf16[512,896]{1,0:T(8,128)(2,1)}, f32[512,6...) custom-call(bf16[512,2560]{1,0:T(8,128)(2,1)} %get-tuple-element.62., ...), custom_call_target="tpu_custom_call" | custom-call | tf_op jit(solution)/shard_map/recur_forward/pallas_call | solution.py:1591
  122.8 88.4 %middle_gather.1 = (f32[128,2560]{1,0:T(8,128)}, bf16[512,2560]{1,0:T(8,128)(2,1)}, bf16[2560,1920]{1,0:T(8,128)(2,1)}) custom-call(bf16[512,2560]{1,0:T(8,128)(2,1)} %get-tuple-element.68.refs_0_, bf16[128,2560]{1,0:T(8,128)(2,1)} %refs_1_.5, f32[1,2560]{1,0:T(1,128)} %reshape.176.refs_2_, bf16[320,1920]{1,0:T(8,128)(2,1)} %refs_3_.1), custom_call_target="tpu_custom_call" | custom-call | tf_op jit(solution)/shard_map/middle_gather/pallas_call | solution.py:1047
  211.3 1.4 all-gather.5.cloned.1.call-done.refs_3_.refs_8_
  212.6 58.6 %feed_forward.1 = (bf16[512,1920]{1,0:T(8,128)(2,1)}, bf16[512,1920]{1,0:T(8,128)(2,1)}, bf16[512,2560]{1,0:T(8,128)(2,1)}, bf16[2560,1920]{1,0:T(8,128)(2,1)}, bf16[2560,1920]{1,0:T(8,128)(2,1)}) custom-call(bf16[512,2560]{1,0:T(8,128)(2,1)} %get-tuple-element.70.refs_0_.refs_5_, bf16[2560,1920]{1,0:T(8,128)(2,1)} %get-tuple-element.71.refs_1_, ...), custom_call_target="tpu_custom_call" | custom-call | tf_op jit(solution)/shard_map/feed_forward/pallas_call | solution.py:2127
  271.9 88.0 %middle_sums.1 = (f32[128,2560]{1,0:T(8,128)}, f32[1,2560]{1,0:T(1,128)}, bf16[512,2560]{1,0:T(8,128)(2,1)}, bf16[320,1920]{1,0:T(8,128)(2,1)}, bf16[2560,1920]{1,0:T(8,128)(2,1)}, /*index=5*/bf16[512,2560]{1,0:T(8,128)(2,1)}) custom-call(bf16[512,2560]{1,0:T(8,128)(2,1)} %get-tuple-element.75.refs_0_, f32[128,2560]{1,0:T(8,128)} %get-tuple-element.69.refs_1_, ...), custom_call_target="tpu_custom_call" | custom-call | tf_op jit(solution)/shard_map/middle_sums/pallas_call | solution.py:1154
  359.9 65.4 %recur_backward.1 = (bf16[256,1280]{1,0:T(8,128)(2,1)}, f32[8,640]{1,0:T(8,128)}, bf16[512,2560]{1,0:T(8,128)(2,1)}, bf16[320,1920]{1,0:T(8,128)(2,1)}, bf16[128...) custom-call(bf16[512,2560]{1,0:T(8,128)(2,1)} %get-tuple-element.79.refs_0_, ...), custom_call_target="tpu_custom_call" | custom-call | tf_op jit(solution)/shard_map/recur_backward/pallas_call | solution.py:1968
  425.2 67.7 %last_sums.1 = (f32[128,2560]{1,0:T(8,128)}, f32[8,640]{1,0:T(8,128)}, f32[2,2560]{1,0:T(2,128)}, bf16[320,1280]{1,0:T(8,128)(2,1)}, bf16[320,640]{1,0:T(8,128)(2,1)}, /*index=5*/bf16[32,1280]{1,0:T(8,128)(2,1)}) custom-call(bf16[512,2560]{1,0:T(8,128)(2,1)} %get-tuple-element.94.refs_0_, bf16[128,2560]{1,0:T(8,128)(2,1)} %refs_1_.5, ...), custom_call_target="tpu_custom_call" | custom-call | tf_op jit(solution)/shard_map/last_sums/pallas_call | solution.py:1269
  492.9 1.4 slice.48
  494.3 1.6 convert_element_type.82
  496.0 1.6 convert_element_type.81
  497.6 1.4 dynamic-slice_reduce_fusion
  499.0 1.3 slice_reduce_fusion
  500.3 0.7 fusion.11
  501.0 0.9 convert_bitcast_fusion.1
  501.9 1.3 fusion.10
  503.2 1.0 multiply_convert_fusion
  504.2 3.0 convert_bitcast_fusion
  507.2 1.1 copy.39
  (50 shorter events, 2.7 us)
Async XLA Ops:
  7.2 204.1 %all-gather.3.cloned.1.call-start = ((), (), s32[]{:S(2)}) async-start(), calls=%async_computation.1 | async-start | bytes 11059200 | tf_op jit(solution)/shard_map/all_gather | solution.py:2203
  10.7 52.5 %copy-start.10 = (s32[3]{0:T(128)S(1)}, s32[3]{0:T(128)}, u32[]{:S(2)}) copy-start(s32[3]{0:T(128)} %param.29) | copy-start | bytes 40
  10.7 53.2 %copy-start.9 = (f32[640]{0:T(1024)S(1)}, f32[640]{0:T(1024)}, u32[]{:S(2)}) copy-start(f32[640]{0:T(1024)} %param.23) | copy-start | bytes 7684
  62.3 5.7 %copy-start.11 = (s32[128]{0:T(128)S(1)}, s32[128]{0:T(128)}, u32[]{:S(2)}) copy-start(s32[128]{0:T(128)} %param.30) | copy-start | bytes 1540
  62.3 8.3 %copy-start.5 = (bf16[128,2560]{1,0:T(8,128)(2,1)S(1)}, bf16[128,2560]{1,0:T(8,128)(2,1)}, u32[]{:S(2)}) copy-start(bf16[128,2560]{1,0:T(8,128)(2,1)} %param.31) | copy-start | bytes 1966084
  62.4 150.3 %all-gather.5.cloned.1.call-start = ((), (), s32[]{:S(2)}) async-start(), calls=%async_computation.2 | async-start | bytes 11059200 | tf_op jit(solution)/shard_map/all_gather | solution.py:2204
  63.1 441.1 %reduce-scatter.2.cloned.1.call-start = ((), (), s32[]{:S(2)}) async-start(), calls=%async_computation.3 | async-start | bytes 11059200 | tf_op jit(solution)/shard_map/reduce_scatter | solution.py:2256
  425.2 69.1 %copy-start.4 = (bf16[320,1920]{1,0:T(8,128)(2,1)S(1)}, bf16[320,1920]{1,0:T(8,128)(2,1)}, u32[]{:S(2)}) copy-start(bf16[320,1920]{1,0:T(8,128)(2,1)} %get-tuple-element.108) | copy-start | bytes 3686404
  492.9 3.0 copy-start.3
  495.9 4.4 copy-start.8
  495.9 5.0 copy-start.7
  495.9 6.0 %copy-start.1 = (bf16[320,1280]{1,0:T(8,128)(2,1)S(1)}, bf16[320,1280]{1,0:T(8,128)(2,1)}, u32[]{:S(2)}) copy-start(bf16[320,1280]{1,0:T(8,128)(2,1)} %get-tuple-element.103) | copy-start | bytes 2457604
  501.0 2.2 copy-start
  501.0 2.2 copy-start.6
  504.2 3.0 copy-start.2
Sparse Core Ops, SparseCore 0:
  62.5 61.2 all-gather.2
  125.7 86.9 all-gather.4
  271.4 103.5 reduce-scatter.1

commit v12 on v11

--- a/solution.py
+++ b/solution.py
@@ -809,13 +809,13 @@
             dst = self.last.at[i - 8]
         return remote(src, dst, self.send.at[i], self.recv.at[i], to)
 
-    def begin(self):
-        for k in (3, 1, 2, 0):
+    def begin(self, which=(3, 1, 2, 0)):
+        for k in which:
             self.copy(k).start()
             self.load(k).start()
 
-    def cores(self):
-        for k in (3, 1, 2, 0):
+    def cores(self, which=(3, 1, 2, 0)):
+        for k in which:
             self.load(k).wait()
             self.copy(k).wait_recv()
             add_rows(self.held.at[k], self.near.at[k])
@@ -1730,7 +1730,7 @@
         place = Place(n_dp, n_line)
         place.meet(True)
         plane = ReducePlane(place, weights, refs[74:])
-        plane.begin()
+        plane.begin((3,))
         lines = [
             ReduceLine(place, feed, own_rows, c * span, span, inbox.at[c], ls.at[c], lr.at[c])
             for c in range(parts)
@@ -1758,6 +1758,8 @@
             gm[here] = plain_dot(mp[here], wo[...])
 
         fetch.wait(0, 1)
+        plane.cores((3,))
+        plane.begin((1, 2, 0))
         loop(rows // 128, project)
         fetch.start(10)
         fetch.wait(13)
@@ -1805,7 +1807,7 @@
         agg[1:2] = message
         swap_all = Exchange(place, "dp", agg, slots, es, er, el)
         swap_all.begin()
-        plane.cores()
+        plane.cores((1, 2, 0))
         swap_all.wait()
         lines[0].hop(1)
         entry = jnp.zeros((1, own), jnp.float32)
@@ -1890,6 +1892,7 @@
             (lax.rem(place.d + n_dp - 1, n_dp), place.t),
         )
         ret.start()
+        plane.turn()
         fetch.wait(8)
         for i in range(blocks):
             cols = swap.block(i, size)
@@ -1933,7 +1936,6 @@
 
         fetch.wait(14)
         out_rows.finish()
-        plane.turn()
         xy_rows.run()
         send(4)
         lines[3].hop(0)
@@ -2199,8 +2201,8 @@
     x_full, y_full, out_full, minor_full, tok_all, order_full = first_gather(
         n_dp, n_tensor, (x_weight, y_weight, out_weight.T, minor), tokens, order_rows
     )
-    late_up, late_down, _ = lax.optimization_barrier((up_weight, down_weight.T, tok_all))
-    up_full = lax.all_gather(late_up, "dp", axis=0, tiled=True)
+    late_down, _ = lax.optimization_barrier((down_weight.T, tok_all))
+    up_full = lax.all_gather(up_weight, "dp", axis=0, tiled=True)
     down_full = lax.all_gather(late_down, "dp", axis=0, tiled=True)
     order_all = order_full.reshape(n_tensor, 8, tok_rows)[:, 0].reshape(row_count)
     gain_rows = minor_full[:, 2 * own_width :].reshape(n_dp, -1)

time: 522 us -> 544 us (1.042)
  Pallas kernels: 471 us -> 493 us
    pallas_call x1, Pallas kernels: 51.6 us -> 80.9 us  [first_gather(): pl.pallas_call(kernel, out_shape=tuple((shaped((n_dp * m.shape[0], m.shap...]
    pallas_call x1, Pallas kernels: 88.4 us -> 81.3 us  [middle_gather(): pl.pallas_call(kernel, out_shape=(shaped((rows, width), jnp.float32), sha...]
    pallas_call x1, Pallas kernels: 65.4 us -> 71.1 us  [recur_backward(): pl.pallas_call(kernel, out_shape=(shaped((size, 2 * own), low), shaped((8...]
  transfers between devices with their start and end apart: 3 -> 3, of which waited for: 1 -> 0; matrix products, arithmetic and copies ran while one was open for 4% -> 4% of each run, Pallas kernels for 70% -> 82%
where the time goes in v12:
time: 544 us; the launch traced here: 536 us
  Pallas kernels  493 us (91%)
  other arithmetic  15.1 us (3%)
  between operations  14.4 us (3%)
  local copies, waits for them, and re-layouts  12.8 us (2%)
    pallas_call x1, Pallas kernels, middle_sums(): pl.pallas_call(kernel, out_shape=(shaped((rows, width), full), shaped((1,...  87 us
    pallas_call x1, Pallas kernels, middle_gather(): pl.pallas_call(kernel, out_shape=(shaped((rows, width), jnp.float32), sha...  81.3 us
    pallas_call x1, Pallas kernels, first_gather(): pl.pallas_call(kernel, out_shape=tuple((shaped((n_dp * m.shape[0], m.shap...  80.9 us
    pallas_call x1, Pallas kernels, recur_backward(): pl.pallas_call(kernel, out_shape=(shaped((size, 2 * own), low), shaped((8...  71.1 us
    pallas_call x1, Pallas kernels, last_sums(): pl.pallas_call(kernel, out_shape=(shaped((rows, width), jnp.float32), sha...  67.2 us
    pallas_call x1, Pallas kernels, feed_forward(): pl.pallas_call(kernel, out_shape=(shaped((rows, units), low), shaped((row...  55.5 us
    pallas_call x1, Pallas kernels, recur_forward(): pl.pallas_call(kernel, out_shape=results + (shaped((size, 2 * wide), low)...  50.3 us
  transfers between devices with their start and end apart: 3, of which 0 were waited for; matrix products, arithmetic and copies ran while one was open for 4% of the time, Pallas kernels for 82%

profile of v12, /device:TPU:0, one launch (start us, length us, event | category | flops | bytes accessed | tf_op | source)
XLA Modules:
  0.0 536.4 jit_solution(13824209746176580563)
XLA Ops:
  7.2 0.7 all-gather.3.cloned.1.call-update
  8.0 0.8 fusion.5
  8.8 0.7 broadcast_subtract_fusion
  9.4 1.5 pad_maximum_fusion.refs_3_
  10.9 0.6 broadcast_in_dim.2.refs_5_
  11.5 80.9 %first_gather.1 = (bf16[2560,640]{1,0:T(8,128)(2,1)}, bf16[2560,640]{1,0:T(8,128)(2,1)}, bf16[2560,640]{1,0:T(8,128)(2,1)}, bf16[256,1408]{1,0:T(8,128)(2,1)}, b...) custom-call(bf16[320,640]{1,0:T(8,128)(2,1)} %refs_0_.1, bf16[320,640]{1,0:T(8,128)(2,1)} %refs_1_.3, ...), custom_call_target="tpu_custom_call" | custom-call | tf_op jit(solution)/shard_map/first_gather/pallas_call | solution.py:929
  93.2 0.6 reshape.173.refs_10_.refs_8_
  94.3 0.7 slice.53
  95.0 0.8 slice.42
  95.9 0.7 reshape.176.refs_2_
  96.6 0.7 reshape.175.refs_7_.refs_2_
  97.3 0.6 compare_convert_fusion
  98.0 0.8 and_convert_fusion.refs_11_.refs_10_
  98.8 1.1 fusion.1
  99.9 1.0 multiply_convert_fusion.1.refs_1_.refs_5_.refs_3_
  100.9 50.3 %recur_forward.1 = (bf16[512,2560]{1,0:T(8,128)(2,1)}, bf16[528,640]{1,0:T(8,128)(2,1)}, f32[512,640]{1,0:T(8,128)}, bf16[512,896]{1,0:T(8,128)(2,1)}, f32[512,6...) custom-call(bf16[512,2560]{1,0:T(8,128)(2,1)} %get-tuple-element.61., ...), custom_call_target="tpu_custom_call" | custom-call | tf_op jit(solution)/shard_map/recur_forward/pallas_call | solution.py:1591
  151.3 81.3 %middle_gather.1 = (f32[128,2560]{1,0:T(8,128)}, bf16[512,2560]{1,0:T(8,128)(2,1)}, bf16[2560,1920]{1,0:T(8,128)(2,1)}) custom-call(bf16[512,2560]{1,0:T(8,128)(2,1)} %get-tuple-element.67.refs_0_, bf16[128,2560]{1,0:T(8,128)(2,1)} %refs_1_.5, f32[1,2560]{1,0:T(1,128)} %reshape.176.refs_2_, bf16[320,1920]{1,0:T(8,128)(2,1)} %refs_3_.1), custom_call_target="tpu_custom_call" | custom-call | tf_op jit(solution)/shard_map/middle_gather/pallas_call | solution.py:1047
  232.7 55.5 %feed_forward.1 = (bf16[512,1920]{1,0:T(8,128)(2,1)}, bf16[512,1920]{1,0:T(8,128)(2,1)}, bf16[512,2560]{1,0:T(8,128)(2,1)}, bf16[2560,1920]{1,0:T(8,128)(2,1)}, bf16[2560,1920]{1,0:T(8,128)(2,1)}) custom-call(bf16[512,2560]{1,0:T(8,128)(2,1)} %get-tuple-element.69.refs_0_.refs_5_, bf16[2560,1920]{1,0:T(8,128)(2,1)} %get-tuple-element.70.refs_1_, ...), custom_call_target="tpu_custom_call" | custom-call | tf_op jit(solution)/shard_map/feed_forward/pallas_call | solution.py:2129
  288.8 87.0 %middle_sums.1 = (f32[128,2560]{1,0:T(8,128)}, f32[1,2560]{1,0:T(1,128)}, bf16[512,2560]{1,0:T(8,128)(2,1)}, bf16[320,1920]{1,0:T(8,128)(2,1)}, bf16[2560,1920]{1,0:T(8,128)(2,1)}, /*index=5*/bf16[512,2560]{1,0:T(8,128)(2,1)}) custom-call(bf16[512,2560]{1,0:T(8,128)(2,1)} %get-tuple-element.73.refs_0_, f32[128,2560]{1,0:T(8,128)} %get-tuple-element.68.refs_1_, ...), custom_call_target="tpu_custom_call" | custom-call | tf_op jit(solution)/shard_map/middle_sums/pallas_call | solution.py:1154
  375.7 71.1 %recur_backward.1 = (bf16[256,1280]{1,0:T(8,128)(2,1)}, f32[8,640]{1,0:T(8,128)}, bf16[512,2560]{1,0:T(8,128)(2,1)}, bf16[320,1920]{1,0:T(8,128)(2,1)}, bf16[128...) custom-call(bf16[512,2560]{1,0:T(8,128)(2,1)} %get-tuple-element.77.refs_0_, ...), custom_call_target="tpu_custom_call" | custom-call | tf_op jit(solution)/shard_map/recur_backward/pallas_call | solution.py:1970
  446.9 67.2 %last_sums.1 = (f32[128,2560]{1,0:T(8,128)}, f32[8,640]{1,0:T(8,128)}, f32[2,2560]{1,0:T(2,128)}, bf16[320,1280]{1,0:T(8,128)(2,1)}, bf16[320,640]{1,0:T(8,128)(2,1)}, /*index=5*/bf16[32,1280]{1,0:T(8,128)(2,1)}) custom-call(bf16[512,2560]{1,0:T(8,128)(2,1)} %get-tuple-element.92.refs_0_, bf16[128,2560]{1,0:T(8,128)(2,1)} %refs_1_.5, ...), custom_call_target="tpu_custom_call" | custom-call | tf_op jit(solution)/shard_map/last_sums/pallas_call | solution.py:1269
  514.0 1.4 slice.48
  515.5 1.6 convert_element_type.82
  517.1 1.6 convert_element_type.81
  518.7 1.4 dynamic-slice_reduce_fusion
  520.1 1.3 slice_reduce_fusion
  521.4 0.7 fusion.11
  522.1 0.9 convert_bitcast_fusion.1
  523.1 1.3 fusion.10
  524.3 1.0 multiply_convert_fusion
  525.4 3.0 convert_bitcast_fusion
  528.4 1.1 copy.39
  (50 shorter events, 2.1 us)
Async XLA Ops:
  7.2 225.4 %all-gather.3.cloned.1.call-start = ((), (), s32[]{:S(2)}) async-start(), calls=%async_computation.1 | async-start | bytes 11059200 | tf_op jit(solution)/shard_map/all_gather | solution.py:2205
  7.9 84.5 %copy-start.10 = (s32[3]{0:T(128)S(1)}, s32[3]{0:T(128)}, u32[]{:S(2)}) copy-start(s32[3]{0:T(128)} %param.29) | copy-start | bytes 40
  7.9 85.3 %copy-start.9 = (f32[640]{0:T(1024)S(1)}, f32[640]{0:T(1024)}, u32[]{:S(2)}) copy-start(f32[640]{0:T(1024)} %param.23) | copy-start | bytes 7684
  7.9 224.7 %all-gather.5.cloned.1.call-start = ((), (), s32[]{:S(2)}) async-start(), calls=%async_computation.2 | async-start | bytes 11059200 | tf_op jit(solution)/shard_map/all_gather | solution.py:2206
  9.4 87.9 %copy-start.11 = (s32[128]{0:T(128)S(1)}, s32[128]{0:T(128)}, u32[]{:S(2)}) copy-start(s32[128]{0:T(128)} %param.30) | copy-start | bytes 1540
  92.4 7.6 %copy-start.5 = (bf16[128,2560]{1,0:T(8,128)(2,1)S(1)}, bf16[128,2560]{1,0:T(8,128)(2,1)}, u32[]{:S(2)}) copy-start(bf16[128,2560]{1,0:T(8,128)(2,1)} %param.31) | copy-start | bytes 1966084
  92.4 433.0 %reduce-scatter.2.cloned.1.call-start = ((), (), s32[]{:S(2)}) async-start(), calls=%async_computation.3 | async-start | bytes 11059200 | tf_op jit(solution)/shard_map/reduce_scatter | solution.py:2258
  446.9 68.6 %copy-start.4 = (bf16[320,1920]{1,0:T(8,128)(2,1)S(1)}, bf16[320,1920]{1,0:T(8,128)(2,1)}, u32[]{:S(2)}) copy-start(bf16[320,1920]{1,0:T(8,128)(2,1)} %get-tuple-element.106) | copy-start | bytes 3686404
  514.0 3.0 copy-start.3
  517.1 4.4 copy-start.8
  517.1 5.0 copy-start.7
  517.1 6.0 %copy-start.1 = (bf16[320,1280]{1,0:T(8,128)(2,1)S(1)}, bf16[320,1280]{1,0:T(8,128)(2,1)}, u32[]{:S(2)}) copy-start(bf16[320,1280]{1,0:T(8,128)(2,1)} %get-tuple-element.101) | copy-start | bytes 2457604
  522.1 2.2 copy-start
  522.1 2.2 copy-start.6
  525.4 3.0 copy-start.2
Sparse Core Ops, SparseCore 0:
  9.9 90.7 all-gather.2
  102.6 66.2 all-gather.4
  288.3 106.9 reduce-scatter.1

commit v13 on v11

--- a/solution.py
+++ b/solution.py
@@ -1039,7 +1039,7 @@
             first = pl.multiple_of(place.t * rows, 16) + c * total.shape[0]
             hidden[pl.ds(pl.multiple_of(first, 16), total.shape[0])] = low
 
-        between = {6: planes[0].forward, 9: planes[0].share}
+        between = {7: planes[0].forward, 10: planes[0].share}
         sum_rows_and_spread(place, s, scratch, norm, hidden, between)
         for part in planes:
             part.finish()
@@ -1085,12 +1085,12 @@
             ],
             sems,
         )
-        fetch.start(0, 1, 2, 3)
         place = Place(n_dp, n_line)
         place.meet()
         plane = ReducePlane(place, src, rest[:7])
         scratch = rest[7:]
         plane.begin()
+        fetch.start(0, 1, 2, 3)
         gain_sum[...] = jnp.zeros_like(gain_sum)
 
         def norm(c, here, total):
@@ -1112,7 +1112,6 @@
             up_out[i // 2, here] = trans_times(hid[:, cols], gu[...]).astype(jnp.bfloat16)
 
         def early():
-            plane.cores()
             fetch.wait(0, 1)
 
         def two():
@@ -1144,7 +1143,7 @@
             feed_part(3)
             fetch.start(4)
 
-        steps = {1: early, 2: two, 3: three, 4: four, 5: five, 6: six, 7: seven, 8: eight, 9: nine}
+        steps = {0: plane.cores, 1: early, 2: two, 3: three, 4: four, 5: five, 6: six, 7: seven, 8: eight, 9: nine}
         sum_rows_and_spread(place, s, scratch, norm, spread, steps)
         plane.finish(result)
         fetch.wait(4, 5, 6)
@@ -1403,7 +1402,7 @@
         in_sems, out_sems, cot_held = refs[55:]
         fetch = Fetch(((tok_far, tok), (wx_far, wx), (wy_far, wy), (wo_far, wo)), in_sems)
         store = Fetch(zip(results, far), out_sems)
-        fetch.start(0, 1, 2, 3)
+        fetch.start(0, 1)
         place = Place(n_dp, n_line)
         place.meet(True)
         swap = RimSwap(place, own)
@@ -1423,6 +1422,7 @@
         ]
         for c, line in enumerate(lines):
             line.step(0, cot_ref.at[pl.ds(c * span, span)])
+        fetch.start(2, 3)
 
         def norm(i):
             here = tile_rows(i, TILE)

time: 522 us -> 527 us (level)
  Pallas kernels: 471 us -> 477 us
    pallas_call x1, Pallas kernels: 88.4 us -> 95.2 us  [middle_gather(): pl.pallas_call(kernel, out_shape=(shaped((rows, width), jnp.float32), sha...]
  transfers between devices with their start and end apart: 3 -> 3, of which waited for: 1 -> 0; matrix products, arithmetic and copies ran while one was open for 4% -> 4% of each run, Pallas kernels for 70% -> 71%
where the time goes in v13:
time: 527 us; the launch traced here: 520 us
  Pallas kernels  477 us (91%)
  other arithmetic  15.1 us (3%)
  between operations  14.4 us (3%)
  local copies, waits for them, and re-layouts  12.8 us (2%)
    pallas_call x1, Pallas kernels, middle_gather(): pl.pallas_call(kernel, out_shape=(shaped((rows, width), jnp.float32), sha...  95.2 us
    pallas_call x1, Pallas kernels, middle_sums(): pl.pallas_call(kernel, out_shape=(shaped((rows, width), full), shaped((1,...  89.1 us
    pallas_call x1, Pallas kernels, last_sums(): pl.pallas_call(kernel, out_shape=(shaped((rows, width), jnp.float32), sha...  67.5 us
    pallas_call x1, Pallas kernels, recur_backward(): pl.pallas_call(kernel, out_shape=(shaped((size, 2 * own), low), shaped((8...  66.4 us
    pallas_call x1, Pallas kernels, feed_forward(): pl.pallas_call(kernel, out_shape=(shaped((rows, units), low), shaped((row...  56.2 us
    pallas_call x1, Pallas kernels, first_gather(): pl.pallas_call(kernel, out_shape=tuple((shaped((n_dp * m.shape[0], m.shap...  51.6 us
    pallas_call x1, Pallas kernels, recur_forward(): pl.pallas_call(kernel, out_shape=results + (shaped((size, 2 * wide), low)...  51.1 us
  transfers between devices with their start and end apart: 3, of which 0 were waited for; matrix products, arithmetic and copies ran while one was open for 4% of the time, Pallas kernels for 71%

profile of v13, /device:TPU:0, one launch (start us, length us, event | category | flops | bytes accessed | tf_op | source)
XLA Modules:
  0.0 520.2 jit_solution(6703099597406049826)
XLA Ops:
  7.2 0.7 broadcast_subtract_fusion
  7.9 0.8 fusion.5
  8.7 1.4 pad_maximum_fusion.refs_3_
  10.1 0.6 broadcast_in_dim.2.refs_5_
  10.7 51.6 %first_gather.1 = (bf16[2560,640]{1,0:T(8,128)(2,1)}, bf16[2560,640]{1,0:T(8,128)(2,1)}, bf16[2560,640]{1,0:T(8,128)(2,1)}, bf16[256,1408]{1,0:T(8,128)(2,1)}, b...) custom-call(bf16[320,640]{1,0:T(8,128)(2,1)} %refs_0_.1, bf16[320,640]{1,0:T(8,128)(2,1)} %refs_1_.3, ...), custom_call_target="tpu_custom_call" | custom-call | tf_op jit(solution)/shard_map/first_gather/pallas_call | solution.py:929
  62.4 0.7 all-gather.5.cloned.1.call-update
  64.0 0.6 reshape.173.refs_10_.refs_8_
  65.0 0.7 slice.53
  65.7 0.8 slice.42
  66.7 0.7 reshape.176.refs_2_
  67.4 0.7 reshape.175.refs_7_.refs_2_
  68.0 0.6 compare_convert_fusion
  68.7 0.8 and_convert_fusion.refs_11_.refs_10_
  69.5 1.1 fusion.1
  70.7 1.0 multiply_convert_fusion.1.refs_1_.refs_5_.refs_3_
  71.7 51.1 %recur_forward.1 = (bf16[512,2560]{1,0:T(8,128)(2,1)}, bf16[528,640]{1,0:T(8,128)(2,1)}, f32[512,640]{1,0:T(8,128)}, bf16[512,896]{1,0:T(8,128)(2,1)}, f32[512,6...) custom-call(bf16[512,2560]{1,0:T(8,128)(2,1)} %get-tuple-element.62., ...), custom_call_target="tpu_custom_call" | custom-call | tf_op jit(solution)/shard_map/recur_forward/pallas_call | solution.py:1591
  122.8 95.2 %middle_gather.1 = (f32[128,2560]{1,0:T(8,128)}, bf16[512,2560]{1,0:T(8,128)(2,1)}, bf16[2560,1920]{1,0:T(8,128)(2,1)}) custom-call(bf16[512,2560]{1,0:T(8,128)(2,1)} %get-tuple-element.68.refs_0_, bf16[128,2560]{1,0:T(8,128)(2,1)} %refs_1_.5, f32[1,2560]{1,0:T(1,128)} %reshape.176.refs_2_, bf16[320,1920]{1,0:T(8,128)(2,1)} %refs_3_.1), custom_call_target="tpu_custom_call" | custom-call | tf_op jit(solution)/shard_map/middle_gather/pallas_call | solution.py:1047
  218.0 56.2 %feed_forward.1 = (bf16[512,1920]{1,0:T(8,128)(2,1)}, bf16[512,1920]{1,0:T(8,128)(2,1)}, bf16[512,2560]{1,0:T(8,128)(2,1)}, bf16[2560,1920]{1,0:T(8,128)(2,1)}, bf16[2560,1920]{1,0:T(8,128)(2,1)}) custom-call(bf16[512,2560]{1,0:T(8,128)(2,1)} %get-tuple-element.70.refs_0_.refs_5_, bf16[2560,1920]{1,0:T(8,128)(2,1)} %get-tuple-element.71.refs_1_, ...), custom_call_target="tpu_custom_call" | custom-call | tf_op jit(solution)/shard_map/feed_forward/pallas_call | solution.py:2127
  274.9 89.1 %middle_sums.1 = (f32[128,2560]{1,0:T(8,128)}, f32[1,2560]{1,0:T(1,128)}, bf16[512,2560]{1,0:T(8,128)(2,1)}, bf16[320,1920]{1,0:T(8,128)(2,1)}, bf16[2560,1920]{1,0:T(8,128)(2,1)}, /*index=5*/bf16[512,2560]{1,0:T(8,128)(2,1)}) custom-call(bf16[512,2560]{1,0:T(8,128)(2,1)} %get-tuple-element.75.refs_0_, f32[128,2560]{1,0:T(8,128)} %get-tuple-element.69.refs_1_, ...), custom_call_target="tpu_custom_call" | custom-call | tf_op jit(solution)/shard_map/middle_sums/pallas_call | solution.py:1153
  363.9 66.4 %recur_backward.1 = (bf16[256,1280]{1,0:T(8,128)(2,1)}, f32[8,640]{1,0:T(8,128)}, bf16[512,2560]{1,0:T(8,128)(2,1)}, bf16[320,1920]{1,0:T(8,128)(2,1)}, bf16[128...) custom-call(bf16[512,2560]{1,0:T(8,128)(2,1)} %get-tuple-element.79.refs_0_, ...), custom_call_target="tpu_custom_call" | custom-call | tf_op jit(solution)/shard_map/recur_backward/pallas_call | solution.py:1968
  430.3 67.5 %last_sums.1 = (f32[128,2560]{1,0:T(8,128)}, f32[8,640]{1,0:T(8,128)}, f32[2,2560]{1,0:T(2,128)}, bf16[320,1280]{1,0:T(8,128)(2,1)}, bf16[320,640]{1,0:T(8,128)(2,1)}, /*index=5*/bf16[32,1280]{1,0:T(8,128)(2,1)}) custom-call(bf16[512,2560]{1,0:T(8,128)(2,1)} %get-tuple-element.94.refs_0_, bf16[128,2560]{1,0:T(8,128)(2,1)} %refs_1_.5, ...), custom_call_target="tpu_custom_call" | custom-call | tf_op jit(solution)/shard_map/last_sums/pallas_call | solution.py:1268
  497.8 1.4 slice.48
  499.2 1.6 convert_element_type.82
  500.9 1.6 convert_element_type.81
  502.5 1.4 dynamic-slice_reduce_fusion
  503.9 1.3 slice_reduce_fusion
  505.2 0.7 fusion.11
  505.9 0.9 convert_bitcast_fusion.1
  506.8 1.3 fusion.10
  508.1 1.0 multiply_convert_fusion
  509.2 3.0 convert_bitcast_fusion
  512.1 1.1 copy.39
  (50 shorter events, 2.1 us)
Async XLA Ops:
  7.2 210.8 %all-gather.3.cloned.1.call-start = ((), (), s32[]{:S(2)}) async-start(), calls=%async_computation.1 | async-start | bytes 11059200 | tf_op jit(solution)/shard_map/all_gather | solution.py:2203
  10.7 52.5 %copy-start.10 = (s32[3]{0:T(128)S(1)}, s32[3]{0:T(128)}, u32[]{:S(2)}) copy-start(s32[3]{0:T(128)} %param.29) | copy-start | bytes 40
  10.7 53.2 %copy-start.9 = (f32[640]{0:T(1024)S(1)}, f32[640]{0:T(1024)}, u32[]{:S(2)}) copy-start(f32[640]{0:T(1024)} %param.23) | copy-start | bytes 7684
  62.3 5.7 %copy-start.11 = (s32[128]{0:T(128)S(1)}, s32[128]{0:T(128)}, u32[]{:S(2)}) copy-start(s32[128]{0:T(128)} %param.30) | copy-start | bytes 1540
  62.3 8.3 %copy-start.5 = (bf16[128,2560]{1,0:T(8,128)(2,1)S(1)}, bf16[128,2560]{1,0:T(8,128)(2,1)}, u32[]{:S(2)}) copy-start(bf16[128,2560]{1,0:T(8,128)(2,1)} %param.31) | copy-start | bytes 1966084
  62.4 155.6 %all-gather.5.cloned.1.call-start = ((), (), s32[]{:S(2)}) async-start(), calls=%async_computation.2 | async-start | bytes 11059200 | tf_op jit(solution)/shard_map/all_gather | solution.py:2204
  63.1 446.0 %reduce-scatter.2.cloned.1.call-start = ((), (), s32[]{:S(2)}) async-start(), calls=%async_computation.3 | async-start | bytes 11059200 | tf_op jit(solution)/shard_map/reduce_scatter | solution.py:2256
  430.3 68.9 %copy-start.4 = (bf16[320,1920]{1,0:T(8,128)(2,1)S(1)}, bf16[320,1920]{1,0:T(8,128)(2,1)}, u32[]{:S(2)}) copy-start(bf16[320,1920]{1,0:T(8,128)(2,1)} %get-tuple-element.108) | copy-start | bytes 3686404
  497.8 3.0 copy-start.3
  500.8 4.4 copy-start.8
  500.9 5.0 copy-start.7
  500.9 6.0 %copy-start.1 = (bf16[320,1280]{1,0:T(8,128)(2,1)S(1)}, bf16[320,1280]{1,0:T(8,128)(2,1)}, u32[]{:S(2)}) copy-start(bf16[320,1280]{1,0:T(8,128)(2,1)} %get-tuple-element.103) | copy-start | bytes 2457604
  505.9 2.2 copy-start
  505.9 2.2 copy-start.6
  509.1 3.0 copy-start.2
Sparse Core Ops, SparseCore 0:
  62.5 61.2 all-gather.2
  125.7 88.0 all-gather.4
  274.4 91.3 reduce-scatter.1

commit v14 on v11

--- a/solution.py
+++ b/solution.py
@@ -1039,7 +1039,7 @@
             first = pl.multiple_of(place.t * rows, 16) + c * total.shape[0]
             hidden[pl.ds(pl.multiple_of(first, 16), total.shape[0])] = low
 
-        between = {6: planes[0].forward, 9: planes[0].share}
+        between = {5: planes[0].forward, 8: planes[0].share}
         sum_rows_and_spread(place, s, scratch, norm, hidden, between)
         for part in planes:
             part.finish()
@@ -1131,10 +1131,10 @@
             fetch.wait(2, 3)
 
         def six():
+            plane.turn()
             feed_part(0)
 
         def seven():
-            plane.turn()
             feed_part(1)
 
         def eight():

time: 522 us -> 519 us (level)
  Pallas kernels: 471 us -> 464 us
    pallas_call x1, Pallas kernels: 88.4 us -> 82.4 us  [middle_gather(): pl.pallas_call(kernel, out_shape=(shaped((rows, width), jnp.float32), sha...]
  transfers between devices with their start and end apart: 3 -> 3, of which waited for: 1 -> 1; matrix products, arithmetic and copies ran while one was open for 4% -> 4% of each run, Pallas kernels for 70% -> 69%
where the time goes in v14:
time: 519 us; the launch traced here: 512 us
  Pallas kernels  464 us (89%)
  other arithmetic  15.1 us (3%)
  between operations  14.4 us (3%)
  local copies, waits for them, and re-layouts  12.8 us (2%)
  waiting for transfers between devices  6.09 us (1%)
    pallas_call x1, Pallas kernels, middle_sums(): pl.pallas_call(kernel, out_shape=(shaped((rows, width), full), shaped((1,...  87.1 us
    pallas_call x1, Pallas kernels, middle_gather(): pl.pallas_call(kernel, out_shape=(shaped((rows, width), jnp.float32), sha...  82.4 us
    pallas_call x1, Pallas kernels, last_sums(): pl.pallas_call(kernel, out_shape=(shaped((rows, width), jnp.float32), sha...  67.2 us
    pallas_call x1, Pallas kernels, recur_backward(): pl.pallas_call(kernel, out_shape=(shaped((size, 2 * own), low), shaped((8...  65.8 us
    pallas_call x1, Pallas kernels, feed_forward(): pl.pallas_call(kernel, out_shape=(shaped((rows, units), low), shaped((row...  58.3 us
    pallas_call x1, Pallas kernels, first_gather(): pl.pallas_call(kernel, out_shape=tuple((shaped((n_dp * m.shape[0], m.shap...  51.6 us
    pallas_call x1, Pallas kernels, recur_forward(): pl.pallas_call(kernel, out_shape=results + (shaped((size, 2 * wide), low)...  51.1 us
  transfers between devices with their start and end apart: 3, of which 1 were waited for; matrix products, arithmetic and copies ran while one was open for 4% of the time, Pallas kernels for 69%

profile of v14, /device:TPU:0, one launch (start us, length us, event | category | flops | bytes accessed | tf_op | source)
XLA Modules:
  0.0 512.0 jit_solution(4431250784373092244)
XLA Ops:
  7.2 0.7 broadcast_subtract_fusion
  7.9 0.8 fusion.5
  8.7 1.4 pad_maximum_fusion.refs_3_
  10.1 0.6 broadcast_in_dim.2.refs_5_
  10.7 51.6 %first_gather.1 = (bf16[2560,640]{1,0:T(8,128)(2,1)}, bf16[2560,640]{1,0:T(8,128)(2,1)}, bf16[2560,640]{1,0:T(8,128)(2,1)}, bf16[256,1408]{1,0:T(8,128)(2,1)}, b...) custom-call(bf16[320,640]{1,0:T(8,128)(2,1)} %refs_0_.1, bf16[320,640]{1,0:T(8,128)(2,1)} %refs_1_.3, ...), custom_call_target="tpu_custom_call" | custom-call | tf_op jit(solution)/shard_map/first_gather/pallas_call | solution.py:929
  62.4 0.7 all-gather.5.cloned.1.call-update
  65.0 0.7 slice.53
  65.7 0.8 slice.42
  66.7 0.7 reshape.176.refs_2_
  67.4 0.7 reshape.175.refs_7_.refs_2_
  68.0 0.6 compare_convert_fusion
  68.7 0.8 and_convert_fusion.refs_11_.refs_10_
  69.5 1.1 fusion.1
  70.7 1.0 multiply_convert_fusion.1.refs_1_.refs_5_.refs_3_
  71.7 51.1 %recur_forward.1 = (bf16[512,2560]{1,0:T(8,128)(2,1)}, bf16[528,640]{1,0:T(8,128)(2,1)}, f32[512,640]{1,0:T(8,128)}, bf16[512,896]{1,0:T(8,128)(2,1)}, f32[512,6...) custom-call(bf16[512,2560]{1,0:T(8,128)(2,1)} %get-tuple-element.62., ...), custom_call_target="tpu_custom_call" | custom-call | tf_op jit(solution)/shard_map/recur_forward/pallas_call | solution.py:1591
  122.8 82.4 %middle_gather.1 = (f32[128,2560]{1,0:T(8,128)}, bf16[512,2560]{1,0:T(8,128)(2,1)}, bf16[2560,1920]{1,0:T(8,128)(2,1)}) custom-call(bf16[512,2560]{1,0:T(8,128)(2,1)} %get-tuple-element.68.refs_0_, bf16[128,2560]{1,0:T(8,128)(2,1)} %refs_1_.5, f32[1,2560]{1,0:T(1,128)} %reshape.176.refs_2_, bf16[320,1920]{1,0:T(8,128)(2,1)} %refs_3_.1), custom_call_target="tpu_custom_call" | custom-call | tf_op jit(solution)/shard_map/middle_gather/pallas_call | solution.py:1047
  205.3 5.3 %all-gather.5.cloned.1.call-done.refs_3_.refs_8_ = bf16[2560,1920]{1,0:T(8,128)(2,1)} async-done(((bf16[320,1920]{1,0:T(8,128)(2,1)}), bf16[2560,1920]{1,0:T(8,128)(2,1)}) %all-gather.5.cloned.1.call-update) | async-done | bytes 9830416 | tf_op jit(solution)/shard_map/all_gather | solution.py:2204
  210.6 58.3 %feed_forward.1 = (bf16[512,1920]{1,0:T(8,128)(2,1)}, bf16[512,1920]{1,0:T(8,128)(2,1)}, bf16[512,2560]{1,0:T(8,128)(2,1)}, bf16[2560,1920]{1,0:T(8,128)(2,1)}, bf16[2560,1920]{1,0:T(8,128)(2,1)}) custom-call(bf16[512,2560]{1,0:T(8,128)(2,1)} %get-tuple-element.70.refs_0_.refs_5_, bf16[2560,1920]{1,0:T(8,128)(2,1)} %get-tuple-element.71.refs_1_, ...), custom_call_target="tpu_custom_call" | custom-call | tf_op jit(solution)/shard_map/feed_forward/pallas_call | solution.py:2127
  269.5 87.1 %middle_sums.1 = (f32[128,2560]{1,0:T(8,128)}, f32[1,2560]{1,0:T(1,128)}, bf16[512,2560]{1,0:T(8,128)(2,1)}, bf16[320,1920]{1,0:T(8,128)(2,1)}, bf16[2560,1920]{1,0:T(8,128)(2,1)}, /*index=5*/bf16[512,2560]{1,0:T(8,128)(2,1)}) custom-call(bf16[512,2560]{1,0:T(8,128)(2,1)} %get-tuple-element.75.refs_0_, f32[128,2560]{1,0:T(8,128)} %get-tuple-element.69.refs_1_, ...), custom_call_target="tpu_custom_call" | custom-call | tf_op jit(solution)/shard_map/middle_sums/pallas_call | solution.py:1154
  356.6 65.8 %recur_backward.1 = (bf16[256,1280]{1,0:T(8,128)(2,1)}, f32[8,640]{1,0:T(8,128)}, bf16[512,2560]{1,0:T(8,128)(2,1)}, bf16[320,1920]{1,0:T(8,128)(2,1)}, bf16[128...) custom-call(bf16[512,2560]{1,0:T(8,128)(2,1)} %get-tuple-element.79.refs_0_, ...), custom_call_target="tpu_custom_call" | custom-call | tf_op jit(solution)/shard_map/recur_backward/pallas_call | solution.py:1968
  422.5 67.2 %last_sums.1 = (f32[128,2560]{1,0:T(8,128)}, f32[8,640]{1,0:T(8,128)}, f32[2,2560]{1,0:T(2,128)}, bf16[320,1280]{1,0:T(8,128)(2,1)}, bf16[320,640]{1,0:T(8,128)(2,1)}, /*index=5*/bf16[32,1280]{1,0:T(8,128)(2,1)}) custom-call(bf16[512,2560]{1,0:T(8,128)(2,1)} %get-tuple-element.94.refs_0_, bf16[128,2560]{1,0:T(8,128)(2,1)} %refs_1_.5, ...), custom_call_target="tpu_custom_call" | custom-call | tf_op jit(solution)/shard_map/last_sums/pallas_call | solution.py:1269
  489.6 1.4 slice.48
  491.1 1.6 convert_element_type.82
  492.7 1.6 convert_element_type.81
  494.3 1.4 dynamic-slice_reduce_fusion
  495.7 1.3 slice_reduce_fusion
  497.0 0.7 fusion.11
  497.7 0.9 convert_bitcast_fusion.1
  498.7 1.3 fusion.10
  499.9 1.0 multiply_convert_fusion
  501.0 3.0 convert_bitcast_fusion
  504.0 1.1 copy.39
  (50 shorter events, 2.7 us)
Async XLA Ops:
  7.2 198.1 %all-gather.3.cloned.1.call-start = ((), (), s32[]{:S(2)}) async-start(), calls=%async_computation.1 | async-start | bytes 11059200 | tf_op jit(solution)/shard_map/all_gather | solution.py:2203
  10.7 52.5 %copy-start.10 = (s32[3]{0:T(128)S(1)}, s32[3]{0:T(128)}, u32[]{:S(2)}) copy-start(s32[3]{0:T(128)} %param.29) | copy-start | bytes 40
  10.7 53.2 %copy-start.9 = (f32[640]{0:T(1024)S(1)}, f32[640]{0:T(1024)}, u32[]{:S(2)}) copy-start(f32[640]{0:T(1024)} %param.23) | copy-start | bytes 7684
  62.3 5.7 %copy-start.11 = (s32[128]{0:T(128)S(1)}, s32[128]{0:T(128)}, u32[]{:S(2)}) copy-start(s32[128]{0:T(128)} %param.30) | copy-start | bytes 1540
  62.3 8.3 %copy-start.5 = (bf16[128,2560]{1,0:T(8,128)(2,1)S(1)}, bf16[128,2560]{1,0:T(8,128)(2,1)}, u32[]{:S(2)}) copy-start(bf16[128,2560]{1,0:T(8,128)(2,1)} %param.31) | copy-start | bytes 1966084
  62.4 148.2 %all-gather.5.cloned.1.call-start = ((), (), s32[]{:S(2)}) async-start(), calls=%async_computation.2 | async-start | bytes 11059200 | tf_op jit(solution)/shard_map/all_gather | solution.py:2204
  63.1 437.8 %reduce-scatter.2.cloned.1.call-start = ((), (), s32[]{:S(2)}) async-start(), calls=%async_computation.3 | async-start | bytes 11059200 | tf_op jit(solution)/shard_map/reduce_scatter | solution.py:2256
  422.4 68.6 %copy-start.4 = (bf16[320,1920]{1,0:T(8,128)(2,1)S(1)}, bf16[320,1920]{1,0:T(8,128)(2,1)}, u32[]{:S(2)}) copy-start(bf16[320,1920]{1,0:T(8,128)(2,1)} %get-tuple-element.108) | copy-start | bytes 3686404
  489.6 3.0 copy-start.3
  492.7 4.4 copy-start.8
  492.7 5.0 copy-start.7
  492.7 6.0 %copy-start.1 = (bf16[320,1280]{1,0:T(8,128)(2,1)S(1)}, bf16[320,1280]{1,0:T(8,128)(2,1)}, u32[]{:S(2)}) copy-start(bf16[320,1280]{1,0:T(8,128)(2,1)} %get-tuple-element.103) | copy-start | bytes 2457604
  497.7 2.2 copy-start
  497.7 2.2 copy-start.6
  501.0 3.0 copy-start.2
Sparse Core Ops, SparseCore 0:
  62.5 61.2 all-gather.2
  125.7 84.8 all-gather.4
  269.0 104.0 reduce-scatter.1

commit v15 on v14

--- a/solution.py
+++ b/solution.py
@@ -1126,12 +1126,12 @@
             up_part(2)
 
         def five():
+            plane.turn()
             up_part(3)
             fetch.start(6)
             fetch.wait(2, 3)
 
         def six():
-            plane.turn()
             feed_part(0)
 
         def seven():
@@ -1254,7 +1254,7 @@
             for part in planes:
                 part.turn()
 
-        sum_rows_and_spread(place, s, scratch, norm, None, {0: cores, 5: turn})
+        sum_rows_and_spread(place, s, scratch, norm, None, {0: cores, 4: turn})
         first = Exchange(place, "dp", own_first, slots_b, xs.at[1], xr.at[1], xl.at[1])
         first.begin()
         small_out[...] = early.finish()

time: 519 us -> 527 us (1.015)
  Pallas kernels: 464 us -> 471 us
    pallas_call x1, Pallas kernels: 87.1 us -> 93.4 us  [middle_sums(): pl.pallas_call(kernel, out_shape=(shaped((rows, width), full), shaped((1,...]
  transfers between devices with their start and end apart: 3 -> 3, of which waited for: 1 -> 1; matrix products, arithmetic and copies ran while one was open for 4% -> 4% of each run, Pallas kernels for 69% -> 70%
where the time goes in v15:
time: 527 us; the launch traced here: 519 us
  Pallas kernels  471 us (89%)
  other arithmetic  15.1 us (3%)
  between operations  14.4 us (3%)
  local copies, waits for them, and re-layouts  12.8 us (2%)
  waiting for transfers between devices  6.09 us (1%)
    pallas_call x1, Pallas kernels, middle_sums(): pl.pallas_call(kernel, out_shape=(shaped((rows, width), full), shaped((1,...  93.4 us
    pallas_call x1, Pallas kernels, middle_gather(): pl.pallas_call(kernel, out_shape=(shaped((rows, width), jnp.float32), sha...  82.4 us
    pallas_call x1, Pallas kernels, last_sums(): pl.pallas_call(kernel, out_shape=(shaped((rows, width), jnp.float32), sha...  68.4 us
    pallas_call x1, Pallas kernels, recur_backward(): pl.pallas_call(kernel, out_shape=(shaped((size, 2 * own), low), shaped((8...  65.7 us
    pallas_call x1, Pallas kernels, feed_forward(): pl.pallas_call(kernel, out_shape=(shaped((rows, units), low), shaped((row...  58.3 us
    pallas_call x1, Pallas kernels, first_gather(): pl.pallas_call(kernel, out_shape=tuple((shaped((n_dp * m.shape[0], m.shap...  51.6 us
    pallas_call x1, Pallas kernels, recur_forward(): pl.pallas_call(kernel, out_shape=results + (shaped((size, 2 * wide), low)...  51.1 us
  transfers between devices with their start and end apart: 3, of which 1 were waited for; matrix products, arithmetic and copies ran while one was open for 4% of the time, Pallas kernels for 70%

profile of v15, /device:TPU:0, one launch (start us, length us, event | category | flops | bytes accessed | tf_op | source)
XLA Modules:
  0.0 519.4 jit_solution(1363715923631790829)
XLA Ops:
  7.2 0.7 broadcast_subtract_fusion
  7.9 0.8 fusion.5
  8.7 1.4 pad_maximum_fusion.refs_3_
  10.1 0.6 broadcast_in_dim.2.refs_5_
  10.7 51.6 %first_gather.1 = (bf16[2560,640]{1,0:T(8,128)(2,1)}, bf16[2560,640]{1,0:T(8,128)(2,1)}, bf16[2560,640]{1,0:T(8,128)(2,1)}, bf16[256,1408]{1,0:T(8,128)(2,1)}, b...) custom-call(bf16[320,640]{1,0:T(8,128)(2,1)} %refs_0_.1, bf16[320,640]{1,0:T(8,128)(2,1)} %refs_1_.3, ...), custom_call_target="tpu_custom_call" | custom-call | tf_op jit(solution)/shard_map/first_gather/pallas_call | solution.py:929
  62.4 0.7 all-gather.5.cloned.1.call-update
  65.0 0.7 slice.53
  65.7 0.8 slice.42
  66.7 0.7 reshape.176.refs_2_
  67.4 0.7 reshape.175.refs_7_.refs_2_
  68.0 0.6 compare_convert_fusion
  68.7 0.8 and_convert_fusion.refs_11_.refs_10_
  69.5 1.1 fusion.1
  70.7 1.0 multiply_convert_fusion.1.refs_1_.refs_5_.refs_3_
  71.7 51.1 %recur_forward.1 = (bf16[512,2560]{1,0:T(8,128)(2,1)}, bf16[528,640]{1,0:T(8,128)(2,1)}, f32[512,640]{1,0:T(8,128)}, bf16[512,896]{1,0:T(8,128)(2,1)}, f32[512,6...) custom-call(bf16[512,2560]{1,0:T(8,128)(2,1)} %get-tuple-element.62., ...), custom_call_target="tpu_custom_call" | custom-call | tf_op jit(solution)/shard_map/recur_forward/pallas_call | solution.py:1591
  122.8 82.4 %middle_gather.1 = (f32[128,2560]{1,0:T(8,128)}, bf16[512,2560]{1,0:T(8,128)(2,1)}, bf16[2560,1920]{1,0:T(8,128)(2,1)}) custom-call(bf16[512,2560]{1,0:T(8,128)(2,1)} %get-tuple-element.68.refs_0_, bf16[128,2560]{1,0:T(8,128)(2,1)} %refs_1_.5, f32[1,2560]{1,0:T(1,128)} %reshape.176.refs_2_, bf16[320,1920]{1,0:T(8,128)(2,1)} %refs_3_.1), custom_call_target="tpu_custom_call" | custom-call | tf_op jit(solution)/shard_map/middle_gather/pallas_call | solution.py:1047
  205.3 5.3 %all-gather.5.cloned.1.call-done.refs_3_.refs_8_ = bf16[2560,1920]{1,0:T(8,128)(2,1)} async-done(((bf16[320,1920]{1,0:T(8,128)(2,1)}), bf16[2560,1920]{1,0:T(8,128)(2,1)}) %all-gather.5.cloned.1.call-update) | async-done | bytes 9830416 | tf_op jit(solution)/shard_map/all_gather | solution.py:2204
  210.6 58.3 %feed_forward.1 = (bf16[512,1920]{1,0:T(8,128)(2,1)}, bf16[512,1920]{1,0:T(8,128)(2,1)}, bf16[512,2560]{1,0:T(8,128)(2,1)}, bf16[2560,1920]{1,0:T(8,128)(2,1)}, bf16[2560,1920]{1,0:T(8,128)(2,1)}) custom-call(bf16[512,2560]{1,0:T(8,128)(2,1)} %get-tuple-element.70.refs_0_.refs_5_, bf16[2560,1920]{1,0:T(8,128)(2,1)} %get-tuple-element.71.refs_1_, ...), custom_call_target="tpu_custom_call" | custom-call | tf_op jit(solution)/shard_map/feed_forward/pallas_call | solution.py:2127
  269.5 93.4 %middle_sums.1 = (f32[128,2560]{1,0:T(8,128)}, f32[1,2560]{1,0:T(1,128)}, bf16[512,2560]{1,0:T(8,128)(2,1)}, bf16[320,1920]{1,0:T(8,128)(2,1)}, bf16[2560,1920]{1,0:T(8,128)(2,1)}, /*index=5*/bf16[512,2560]{1,0:T(8,128)(2,1)}) custom-call(bf16[512,2560]{1,0:T(8,128)(2,1)} %get-tuple-element.75.refs_0_, f32[128,2560]{1,0:T(8,128)} %get-tuple-element.69.refs_1_, ...), custom_call_target="tpu_custom_call" | custom-call | tf_op jit(solution)/shard_map/middle_sums/pallas_call | solution.py:1154
  362.9 65.7 %recur_backward.1 = (bf16[256,1280]{1,0:T(8,128)(2,1)}, f32[8,640]{1,0:T(8,128)}, bf16[512,2560]{1,0:T(8,128)(2,1)}, bf16[320,1920]{1,0:T(8,128)(2,1)}, bf16[128...) custom-call(bf16[512,2560]{1,0:T(8,128)(2,1)} %get-tuple-element.79.refs_0_, ...), custom_call_target="tpu_custom_call" | custom-call | tf_op jit(solution)/shard_map/recur_backward/pallas_call | solution.py:1968
  428.6 68.4 %last_sums.1 = (f32[128,2560]{1,0:T(8,128)}, f32[8,640]{1,0:T(8,128)}, f32[2,2560]{1,0:T(2,128)}, bf16[320,1280]{1,0:T(8,128)(2,1)}, bf16[320,640]{1,0:T(8,128)(2,1)}, /*index=5*/bf16[32,1280]{1,0:T(8,128)(2,1)}) custom-call(bf16[512,2560]{1,0:T(8,128)(2,1)} %get-tuple-element.94.refs_0_, bf16[128,2560]{1,0:T(8,128)(2,1)} %refs_1_.5, ...), custom_call_target="tpu_custom_call" | custom-call | tf_op jit(solution)/shard_map/last_sums/pallas_call | solution.py:1269
  497.1 1.4 slice.48
  498.5 1.6 convert_element_type.82
  500.1 1.6 convert_element_type.81
  501.7 1.4 dynamic-slice_reduce_fusion
  503.2 1.3 slice_reduce_fusion
  504.5 0.7 fusion.11
  505.2 0.9 convert_bitcast_fusion.1
  506.1 1.3 fusion.10
  507.4 1.0 multiply_convert_fusion
  508.4 3.0 convert_bitcast_fusion
  511.4 1.1 copy.39
  (50 shorter events, 2.7 us)
Async XLA Ops:
  7.2 198.1 %all-gather.3.cloned.1.call-start = ((), (), s32[]{:S(2)}) async-start(), calls=%async_computation.1 | async-start | bytes 11059200 | tf_op jit(solution)/shard_map/all_gather | solution.py:2203
  10.7 52.5 %copy-start.10 = (s32[3]{0:T(128)S(1)}, s32[3]{0:T(128)}, u32[]{:S(2)}) copy-start(s32[3]{0:T(128)} %param.29) | copy-start | bytes 40
  10.7 53.2 %copy-start.9 = (f32[640]{0:T(1024)S(1)}, f32[640]{0:T(1024)}, u32[]{:S(2)}) copy-start(f32[640]{0:T(1024)} %param.23) | copy-start | bytes 7684
  62.3 5.7 %copy-start.11 = (s32[128]{0:T(128)S(1)}, s32[128]{0:T(128)}, u32[]{:S(2)}) copy-start(s32[128]{0:T(128)} %param.30) | copy-start | bytes 1540
  62.3 8.3 %copy-start.5 = (bf16[128,2560]{1,0:T(8,128)(2,1)S(1)}, bf16[128,2560]{1,0:T(8,128)(2,1)}, u32[]{:S(2)}) copy-start(bf16[128,2560]{1,0:T(8,128)(2,1)} %param.31) | copy-start | bytes 1966084
  62.4 148.2 %all-gather.5.cloned.1.call-start = ((), (), s32[]{:S(2)}) async-start(), calls=%async_computation.2 | async-start | bytes 11059200 | tf_op jit(solution)/shard_map/all_gather | solution.py:2204
  63.1 445.3 %reduce-scatter.2.cloned.1.call-start = ((), (), s32[]{:S(2)}) async-start(), calls=%async_computation.3 | async-start | bytes 11059200 | tf_op jit(solution)/shard_map/reduce_scatter | solution.py:2256
  428.6 69.9 %copy-start.4 = (bf16[320,1920]{1,0:T(8,128)(2,1)S(1)}, bf16[320,1920]{1,0:T(8,128)(2,1)}, u32[]{:S(2)}) copy-start(bf16[320,1920]{1,0:T(8,128)(2,1)} %get-tuple-element.108) | copy-start | bytes 3686404
  497.1 3.0 copy-start.3
  500.1 4.4 copy-start.8
  500.1 5.0 copy-start.7
  500.1 6.0 %copy-start.1 = (bf16[320,1280]{1,0:T(8,128)(2,1)S(1)}, bf16[320,1280]{1,0:T(8,128)(2,1)}, u32[]{:S(2)}) copy-start(bf16[320,1280]{1,0:T(8,128)(2,1)} %get-tuple-element.103) | copy-start | bytes 2457604
  505.2 2.2 copy-start
  505.2 2.2 copy-start.6
  508.4 3.0 copy-start.2
Sparse Core Ops, SparseCore 0:
  62.5 61.2 all-gather.2
  125.7 84.8 all-gather.4
  269.0 104.0 reduce-scatter.1

commit v16 on v14

--- a/solution.py
+++ b/solution.py
@@ -1365,7 +1365,7 @@
         return pl.ds(pl.multiple_of(self.first + index * size, RIM), size)
 
 
-LATE_SHARE = 4
+LATE_SHARE = 8
 
 
 def recur_forward(

time: 519 us -> 521 us (level)
  transfers between devices with their start and end apart: 3 -> 3, of which waited for: 1 -> 1; matrix products, arithmetic and copies ran while one was open for 4% -> 4% of each run, Pallas kernels for 69% -> 70%
where the time goes in v16:
time: 521 us; the launch traced here: 514 us
  Pallas kernels  469 us (90%)
  other arithmetic  15.1 us (3%)
  between operations  14.4 us (3%)
  local copies, waits for them, and re-layouts  12.8 us (2%)
    pallas_call x1, Pallas kernels, middle_sums(): pl.pallas_call(kernel, out_shape=(shaped((rows, width), full), shaped((1,...  87.9 us
    pallas_call x1, Pallas kernels, middle_gather(): pl.pallas_call(kernel, out_shape=(shaped((rows, width), jnp.float32), sha...  84.5 us
    pallas_call x1, Pallas kernels, last_sums(): pl.pallas_call(kernel, out_shape=(shaped((rows, width), jnp.float32), sha...  67.3 us
    pallas_call x1, Pallas kernels, recur_backward(): pl.pallas_call(kernel, out_shape=(shaped((size, 2 * own), low), shaped((8...  65.9 us
    pallas_call x1, Pallas kernels, feed_forward(): pl.pallas_call(kernel, out_shape=(shaped((rows, units), low), shaped((row...  56.8 us
    pallas_call x1, Pallas kernels, recur_forward(): pl.pallas_call(kernel, out_shape=results + (shaped((size, 2 * wide), low)...  54.6 us
    pallas_call x1, Pallas kernels, first_gather(): pl.pallas_call(kernel, out_shape=tuple((shaped((n_dp * m.shape[0], m.shap...  51.6 us
  transfers between devices with their start and end apart: 3, of which 1 were waited for; matrix products, arithmetic and copies ran while one was open for 4% of the time, Pallas kernels for 70%

profile of v16, /device:TPU:0, one launch (start us, length us, event | category | flops | bytes accessed | tf_op | source)
XLA Modules:
  0.0 513.8 jit_solution(17834216332299613676)
XLA Ops:
  7.2 0.7 broadcast_subtract_fusion
  7.9 0.8 fusion.5
  8.7 1.4 pad_maximum_fusion.refs_3_
  10.1 0.6 broadcast_in_dim.2.refs_5_
  10.7 51.6 %first_gather.1 = (bf16[2560,640]{1,0:T(8,128)(2,1)}, bf16[2560,640]{1,0:T(8,128)(2,1)}, bf16[2560,640]{1,0:T(8,128)(2,1)}, bf16[256,1408]{1,0:T(8,128)(2,1)}, b...) custom-call(bf16[320,640]{1,0:T(8,128)(2,1)} %refs_0_.1, bf16[320,640]{1,0:T(8,128)(2,1)} %refs_1_.3, ...), custom_call_target="tpu_custom_call" | custom-call | tf_op jit(solution)/shard_map/first_gather/pallas_call | solution.py:929
  62.4 0.7 all-gather.5.cloned.1.call-update
  65.0 0.7 slice.53
  65.7 0.8 slice.42
  66.7 0.7 reshape.176.refs_2_
  67.4 0.7 reshape.175.refs_7_.refs_2_
  68.0 0.6 compare_convert_fusion
  68.7 0.8 and_convert_fusion.refs_11_.refs_10_
  69.5 1.1 fusion.1
  70.7 1.0 multiply_convert_fusion.1.refs_1_.refs_5_.refs_3_
  71.7 54.6 %recur_forward.1 = (bf16[512,2560]{1,0:T(8,128)(2,1)}, bf16[528,640]{1,0:T(8,128)(2,1)}, f32[512,640]{1,0:T(8,128)}, bf16[512,896]{1,0:T(8,128)(2,1)}, f32[512,6...) custom-call(bf16[512,2560]{1,0:T(8,128)(2,1)} %get-tuple-element.62., ...), custom_call_target="tpu_custom_call" | custom-call | tf_op jit(solution)/shard_map/recur_forward/pallas_call | solution.py:1591
  126.3 84.5 %middle_gather.1 = (f32[128,2560]{1,0:T(8,128)}, bf16[512,2560]{1,0:T(8,128)(2,1)}, bf16[2560,1920]{1,0:T(8,128)(2,1)}) custom-call(bf16[512,2560]{1,0:T(8,128)(2,1)} %get-tuple-element.68.refs_0_, bf16[128,2560]{1,0:T(8,128)(2,1)} %refs_1_.5, f32[1,2560]{1,0:T(1,128)} %reshape.176.refs_2_, bf16[320,1920]{1,0:T(8,128)(2,1)} %refs_3_.1), custom_call_target="tpu_custom_call" | custom-call | tf_op jit(solution)/shard_map/middle_gather/pallas_call | solution.py:1047
  210.9 2.0 all-gather.5.cloned.1.call-done.refs_3_.refs_8_
  212.8 56.8 %feed_forward.1 = (bf16[512,1920]{1,0:T(8,128)(2,1)}, bf16[512,1920]{1,0:T(8,128)(2,1)}, bf16[512,2560]{1,0:T(8,128)(2,1)}, bf16[2560,1920]{1,0:T(8,128)(2,1)}, bf16[2560,1920]{1,0:T(8,128)(2,1)}) custom-call(bf16[512,2560]{1,0:T(8,128)(2,1)} %get-tuple-element.70.refs_0_.refs_5_, bf16[2560,1920]{1,0:T(8,128)(2,1)} %get-tuple-element.71.refs_1_, ...), custom_call_target="tpu_custom_call" | custom-call | tf_op jit(solution)/shard_map/feed_forward/pallas_call | solution.py:2127
  270.2 87.9 %middle_sums.1 = (f32[128,2560]{1,0:T(8,128)}, f32[1,2560]{1,0:T(1,128)}, bf16[512,2560]{1,0:T(8,128)(2,1)}, bf16[320,1920]{1,0:T(8,128)(2,1)}, bf16[2560,1920]{1,0:T(8,128)(2,1)}, /*index=5*/bf16[512,2560]{1,0:T(8,128)(2,1)}) custom-call(bf16[512,2560]{1,0:T(8,128)(2,1)} %get-tuple-element.75.refs_0_, f32[128,2560]{1,0:T(8,128)} %get-tuple-element.69.refs_1_, ...), custom_call_target="tpu_custom_call" | custom-call | tf_op jit(solution)/shard_map/middle_sums/pallas_call | solution.py:1154
  358.1 65.9 %recur_backward.1 = (bf16[256,1280]{1,0:T(8,128)(2,1)}, f32[8,640]{1,0:T(8,128)}, bf16[512,2560]{1,0:T(8,128)(2,1)}, bf16[320,1920]{1,0:T(8,128)(2,1)}, bf16[128...) custom-call(bf16[512,2560]{1,0:T(8,128)(2,1)} %get-tuple-element.79.refs_0_, ...), custom_call_target="tpu_custom_call" | custom-call | tf_op jit(solution)/shard_map/recur_backward/pallas_call | solution.py:1968
  424.1 67.3 %last_sums.1 = (f32[128,2560]{1,0:T(8,128)}, f32[8,640]{1,0:T(8,128)}, f32[2,2560]{1,0:T(2,128)}, bf16[320,1280]{1,0:T(8,128)(2,1)}, bf16[320,640]{1,0:T(8,128)(2,1)}, /*index=5*/bf16[32,1280]{1,0:T(8,128)(2,1)}) custom-call(bf16[512,2560]{1,0:T(8,128)(2,1)} %get-tuple-element.94.refs_0_, bf16[128,2560]{1,0:T(8,128)(2,1)} %refs_1_.5, ...), custom_call_target="tpu_custom_call" | custom-call | tf_op jit(solution)/shard_map/last_sums/pallas_call | solution.py:1269
  491.5 1.4 slice.48
  492.9 1.6 convert_element_type.82
  494.5 1.6 convert_element_type.81
  496.1 1.4 dynamic-slice_reduce_fusion
  497.5 1.3 slice_reduce_fusion
  498.9 0.7 fusion.11
  499.5 0.9 convert_bitcast_fusion.1
  500.5 1.3 fusion.10
  501.8 1.0 multiply_convert_fusion
  502.8 3.0 convert_bitcast_fusion
  505.8 1.1 copy.39
  (50 shorter events, 2.7 us)
Async XLA Ops:
  7.2 203.7 %all-gather.3.cloned.1.call-start = ((), (), s32[]{:S(2)}) async-start(), calls=%async_computation.1 | async-start | bytes 11059200 | tf_op jit(solution)/shard_map/all_gather | solution.py:2203
  10.7 52.5 %copy-start.10 = (s32[3]{0:T(128)S(1)}, s32[3]{0:T(128)}, u32[]{:S(2)}) copy-start(s32[3]{0:T(128)} %param.29) | copy-start | bytes 40
  10.7 53.2 %copy-start.9 = (f32[640]{0:T(1024)S(1)}, f32[640]{0:T(1024)}, u32[]{:S(2)}) copy-start(f32[640]{0:T(1024)} %param.23) | copy-start | bytes 7684
  62.3 5.7 %copy-start.11 = (s32[128]{0:T(128)S(1)}, s32[128]{0:T(128)}, u32[]{:S(2)}) copy-start(s32[128]{0:T(128)} %param.30) | copy-start | bytes 1540
  62.3 8.3 %copy-start.5 = (bf16[128,2560]{1,0:T(8,128)(2,1)S(1)}, bf16[128,2560]{1,0:T(8,128)(2,1)}, u32[]{:S(2)}) copy-start(bf16[128,2560]{1,0:T(8,128)(2,1)} %param.31) | copy-start | bytes 1966084
  62.4 150.4 %all-gather.5.cloned.1.call-start = ((), (), s32[]{:S(2)}) async-start(), calls=%async_computation.2 | async-start | bytes 11059200 | tf_op jit(solution)/shard_map/all_gather | solution.py:2204
  63.1 439.7 %reduce-scatter.2.cloned.1.call-start = ((), (), s32[]{:S(2)}) async-start(), calls=%async_computation.3 | async-start | bytes 11059200 | tf_op jit(solution)/shard_map/reduce_scatter | solution.py:2256
  424.1 68.8 %copy-start.4 = (bf16[320,1920]{1,0:T(8,128)(2,1)S(1)}, bf16[320,1920]{1,0:T(8,128)(2,1)}, u32[]{:S(2)}) copy-start(bf16[320,1920]{1,0:T(8,128)(2,1)} %get-tuple-element.108) | copy-start | bytes 3686404
  491.4 3.0 copy-start.3
  494.5 4.4 copy-start.8
  494.5 5.0 copy-start.7
  494.5 6.0 %copy-start.1 = (bf16[320,1280]{1,0:T(8,128)(2,1)S(1)}, bf16[320,1280]{1,0:T(8,128)(2,1)}, u32[]{:S(2)}) copy-start(bf16[320,1280]{1,0:T(8,128)(2,1)} %get-tuple-element.103) | copy-start | bytes 2457604
  499.5 2.2 copy-start
  499.5 2.2 copy-start.6
  502.8 3.0 copy-start.2
Sparse Core Ops, SparseCore 0:
  62.5 61.2 all-gather.2
  125.7 87.1 all-gather.4
  269.8 104.8 reduce-scatter.1
